TPU v7x, 1024 devices: a whole 4x8x16 slice. The times are simulated.
1024 devices in a mesh: row: 16 (over z), col: 32 (over x, y_hi, core), narrow: 2 (over y_lo).
Axes of the slice: x: 4, y: 8 (y_hi: 4, y_lo: 2; y = y_hi * 2 + y_lo), z: 16, core: 2. Of those that a mesh axis runs over, the one named last changes fastest.
Arguments:
- a_tiles: bfloat16 [12288, 12288], P('row', 'col'), may hold values from -0.375 to 0.375
- p_tiles: bfloat16 [12288, 3072], P('row'), may hold values from -0.4375 to 0.4375
- a_mask: int32 [64, 64], P('row', 'col'), may hold values 0 or 1
- p_mask: int32 [64, 16], P('row'), may hold values 0 or 1
Outputs:
- coarse: float32 [3072, 3072], P('row', ('col', 'narrow'))
Inputs may be any that keep to these rules, and one draw needn't show every extreme that they name: `a_mask`: 0 or 1 for every block tile of the operator. `p_mask`: 0 or 1 for every block tile of the prolongator.
All inputs are finite; a program needn't handle non-finite values.
Results may differ from a plain program's by a relative error of at most 0.0003.
Values may be sent and summed in bfloat16 or wider, within the bound.
No kernel may reach another device: no remote copies, remote signals or barrier semaphores. Data moves between devices by JAX's collectives and lax.ppermute only.
A program may use at most 64 MiB of HBM per device.

v0:
```python
import jax
import jax.numpy as jnp
from jax import lax
from jax.sharding import PartitionSpec as P

TILE = 192


def from_root(block, axis, source):
    block = jnp.where(lax.axis_index(axis) == source, block, jnp.zeros_like(block))
    return lax.psum(block, axis)


def masked(tiles, mask):
    height, breadth = tiles.shape
    shaped = tiles.reshape(height // TILE, TILE, breadth // TILE, TILE)
    return (shaped * mask.astype(jnp.bfloat16)[:, None, :, None]).reshape(height, breadth)


def local(a_tiles, p_tiles, a_mask, p_mask):
    a_masked = masked(a_tiles, a_mask)
    p_masked = masked(p_tiles, p_mask)
    fine_rows, col_rows = a_tiles.shape
    coarse_width = p_tiles.shape[1]
    col_total = lax.axis_size("col")
    col_index = lax.axis_index("col")
    narrow_index = lax.axis_index("narrow")
    owner = col_index * col_rows // fine_rows
    offset = col_index * col_rows % fine_rows
    slab = coarse_width // (2 * col_total)
    partner = lax.dynamic_slice_in_dim(p_masked, offset, col_rows, 0)
    partner = lax.dynamic_index_in_dim(
        partner.reshape(col_rows, col_total, 2, slab), narrow_index, 2, keepdims=False
    )
    partner = from_root(partner.reshape(col_rows, col_total * slab), "row", owner)
    picked = partner
    product_flip = lax.psum_scatter(
        lax.dot_general(
            picked, a_masked, (((0,), (1,)), ((), ())), preferred_element_type=jnp.float32
        ),
        "col",
        scatter_dimension=0,
        tiled=True,
    )
    picked = p_masked.astype(jnp.float32)
    return lax.psum_scatter(
        lax.dot_general(
            picked,
            product_flip,
            (((0,), (1,)), ((), ())),
            precision=lax.Precision.HIGHEST,
            preferred_element_type=jnp.float32,
        ),
        "row",
        scatter_dimension=0,
        tiled=True,
    )


def solution(mesh):
    return jax.shard_map(
        local,
        mesh=mesh,
        in_specs=(P("row", "col"), P("row", None), P("row", "col"), P("row", None)),
        out_specs=P("row", ("col", "narrow")),
        check_vma=False,
    )
```

profile of v0, /device:TPU:6, one launch (start us, length us, event | category | flops | bytes accessed | tf_op | source)
XLA Modules:
  0.0 411.6 jit_solution(8098235685807334337)
XLA Ops:
  6.5 0.0 all-reduce.2.cloned.1.call-start
  6.5 0.7 convert_element_type.7
  7.2 0.1 copy.9
  7.3 4.3 %mul.26 = bf16[4,192,16,192]{1,0,3,2:T(4,128)(2,1)} broadcast(bf16[4,16]{0,1:T(8,128)(2,1)S(1)} %copy.9), dimensions={0,2} | broadcast | bytes 4718720 | tf_op jit(solution)/shard_map/mul | solution.py:17
  11.7 11.6 %mul.27 = bf16[768,3072]{0,1:T(8,128)(2,1)} reshape(bf16[4,192,16,192]{1,0,3,2:T(4,128)(2,1)} %mul.26) | data formatting | bytes 9437184 | tf_op jit(solution)/shard_map/mul | solution.py:17
  23.2 6.6 %copy.10 = bf16[768,3072]{0,1:T(8,128)(2,1)} copy(bf16[768,3072]{1,0:T(8,128)(2,1)} %param.5) | data formatting | bytes 9437184 | tf_op args[1]
  29.9 5.0 %mul.28 = bf16[768,3072]{0,1:T(8,128)(2,1)S(1)} multiply(bf16[768,3072]{0,1:T(8,128)(2,1)} %copy.10, bf16[768,3072]{0,1:T(8,128)(2,1)} %mul.27) | non-fusion elementwise | flops 2359296 | bytes 14155776 | tf_op jit(solution)/shard_map/mul | solution.py:17
  34.9 0.0 copy-start
  34.9 2.1 copy-done
  37.0 1.3 constant_dynamic-slice_fusion
  38.3 0.0 copy-start.2
  38.3 0.0 copy-start.1
  38.4 1.2 dynamic-slice_select_fusion
  39.5 0.0 all-reduce.2.cloned.1.call-update
  39.6 0.0 reduce-scatter.5.cloned.1.call-start
  39.6 0.0 copy-done.2
  39.6 0.1 copy.11
  39.7 0.5 mul.30
  40.2 0.4 mul.31
  40.6 153.6 %all-reduce.2.cloned.1.call-done = bf16[384,1536]{0,1:T(8,128)(2,1)} async-done(((bf16[384,1536]{0,1:T(8,128)(2,1)}), bf16[384,1536]{0,1:T(8,128)(2,1)}) %all-reduce.2.cloned.1.call-update) | async-done | bytes 1179664 | tf_op jit(solution)/shard_map/psum | solution.py:11
  194.2 0.0 copy-done.1
  194.2 4.9 %fusion = f32[1536,768]{1,0:T(8,128)} fusion(bf16[384,1536]{0,1:T(8,128)(2,1)} %all-reduce.2.cloned.1.call-done, bf16[768,384]{1,0:T(8,128)(2,1)S(1)} %copy-done.1, bf16[768,384]{1,0:T(8,128)(2,1)S(1)} %mul.31), kind=kOutput, calls=%fused_computation.1 | convolution fusion | flops 906264576 | bytes 7077888 | tf_op jit(solution)/shard_map/dot_general | solution.py:38
  199.1 0.0 reduce-scatter.5.cloned.1.call-update
  199.1 0.2 reduce-scatter.7.cloned.1.call-start
  199.4 121.7 %reduce-scatter.5.cloned.1.call-done = f32[48,768]{1,0:T(8,128)} async-done(((f32[1536,768]{1,0:T(8,128)}), f32[48,768]{1,0:T(8,128)}) %reduce-scatter.5.cloned.1.call-update) | async-done | bytes 147472 | tf_op jit(solution)/shard_map/reduce_scatter | solution.py:37
  321.1 7.3 %fusion.2 = f32[3072,48]{1,0:T(8,128)} fusion(bf16[768,3072]{0,1:T(8,128)(2,1)} %copy-done, f32[48,768]{1,0:T(8,128)} %reduce-scatter.5.cloned.1.call-done), kind=kOutput, calls=%fused_computation.4 | convolution fusion | flops 1358954496 | bytes 5455872
  328.4 0.0 reduce-scatter.7.cloned.1.call-update
  328.4 75.1 %reduce-scatter.7.cloned.1.call-done = f32[192,48]{1,0:T(8,128)} async-done(((f32[3072,48]{1,0:T(8,128)}), f32[192,48]{1,0:T(8,128)}) %reduce-scatter.7.cloned.1.call-update) | async-done | bytes 36880
  403.5 1.6 copy.13
  (1 shorter events, 0.0 us)
Async XLA Ops:
  6.5 187.7 %all-reduce.2.cloned.1.call-start = ((), (), s32[]{:S(2)}) async-start(), calls=%async_computation.2 | async-start | bytes 2359296 | tf_op jit(solution)/shard_map/psum | solution.py:11
  34.9 2.1 copy-start
  38.3 1.3 copy-start.2
  38.3 155.9 %copy-start.1 = (bf16[768,384]{1,0:T(8,128)(2,1)S(1)}, bf16[768,384]{1,0:T(8,128)(2,1)}, u32[]{:S(2)}) copy-start(bf16[768,384]{1,0:T(8,128)(2,1)} %param.4) | copy-start | bytes 1769476
  39.6 281.5 %reduce-scatter.5.cloned.1.call-start = ((), (), s32[]{:S(2)}) async-start(), calls=%async_computation.3 | async-start | bytes 4866048 | tf_op jit(solution)/shard_map/reduce_scatter | solution.py:37
  199.1 204.4 %reduce-scatter.7.cloned.1.call-start = ((), (), s32[]{:S(2)}) async-start(), calls=%async_computation.4 | async-start | bytes 1671168
Sparse Core Ops, SparseCore 0:
  39.7 154.5 all-reduce.1
  200.0 121.0 reduce-scatter.4
  328.5 74.9 reduce-scatter.6
where the time goes:
time: 412 us
  waiting for transfers between devices  350 us (85%)
  local copies, waits for them, and re-layouts  28.7 us (7%)
  between operations  13.2 us (3%)
  matrix products  12.2 us (3%)
  other arithmetic  6.83 us (2%)
    psum x1, waiting for transfers between devices, from_root(): return lax.psum(block, axis)  154 us
    reduce_scatter x1, waiting for transfers between devices, local(): lax.psum_scatter(lax.dot_general(picked, a_masked, (((0,), (1,)), ((), ()...  122 us
    unnamed x4, waiting for transfers between devices  75.2 us
    mul x4, local copies, waits for them, and re-layouts, masked(): shaped * mask.astype(jnp.bfloat16)[:, None, :, None]  16.8 us
    unnamed x8, local copies, waits for them, and re-layouts  10.4 us
  transfers between devices with their start and end apart: 3, of which 3 were waited for; matrix products, arithmetic and copies ran while one was open for 0% of the time, Pallas kernels for 0%

commit v1 on v0

v1 whole, which is shorter than its diff:
```python
import jax
import jax.numpy as jnp
from jax import lax
from jax.experimental import pallas as pl
from jax.experimental.pallas import tpu as pltpu
from jax.sharding import Mesh
from jax.sharding import PartitionSpec as P

TILE = 192
WIDE = 48
ROWS = 768
HALF = 384
FINE = 12288
COARSE = 3072
PLANES = 16
LIMIT = 32766.0
STEPS = 128.0
CODED = 80
VMEM = 48 * 1024 * 1024
F32 = jnp.float32
BF16 = jnp.bfloat16


def params():
    return pltpu.CompilerParams(vmem_limit_bytes=VMEM)


def dot_last(left, right):
    return lax.dot_general(left, right, (((1,), (1,)), ((), ())), preferred_element_type=F32)


def slice_kernel(place, mask, first, second, out):
    offset = place[1]
    tile = place[2]
    row = lax.broadcasted_iota(jnp.int32, (WIDE, 128), 0)
    lane = lax.broadcasted_iota(jnp.int32, (WIDE, 128), 1)
    pick_first = (lane == row + offset).astype(F32).astype(BF16)
    pick_second = (lane + 128 == row + offset).astype(F32).astype(BF16)
    picked = dot_last(pick_first, first[...]) + dot_last(pick_second, second[...])
    fine = lax.broadcasted_iota(jnp.int32, (1, ROWS), 1)
    present = jnp.zeros((1, ROWS), F32)
    for i in range(ROWS // TILE):
        inside = (fine >= i * TILE) & (fine < (i + 1) * TILE)
        present = jnp.where(inside, mask[i, tile].astype(F32), present)
    out[...] = (picked * present).astype(BF16)


def own_columns(p_tiles, p_mask, index):
    start = index * WIDE
    block = jnp.minimum(start // 128, COARSE // 128 - 2)
    place = jnp.stack([block, start - block * 128, start // TILE]).astype(jnp.int32)
    return pl.pallas_call(
        slice_kernel,
        out_shape=jax.ShapeDtypeStruct((WIDE, ROWS), BF16),
        grid_spec=pltpu.PrefetchScalarGridSpec(
            num_scalar_prefetch=2,
            grid=(1,),
            in_specs=[
                pl.BlockSpec((ROWS, 128), lambda g, place, mask: (0, place[0])),
                pl.BlockSpec((ROWS, 128), lambda g, place, mask: (0, place[0] + 1)),
            ],
            out_specs=pl.BlockSpec((WIDE, ROWS), lambda g, place, mask: (0, 0)),
        ),
        compiler_params=params(),
        name="own_columns",
    )(place, p_mask, p_tiles, p_tiles)


def mask_kernel(mask, tiles, out):
    width = tiles.shape[1]
    first = pl.program_id(0) * (width // TILE)
    lane = lax.broadcasted_iota(jnp.int32, (1, width), 1)
    for i in range(ROWS // TILE):
        present = jnp.zeros((1, width), F32)
        for k in range(width // TILE):
            inside = (lane >= k * TILE) & (lane < (k + 1) * TILE)
            present = jnp.where(inside, mask[i, first + k].astype(F32), present)
        rows = pl.ds(i * TILE, TILE)
        out[rows, :] = tiles[rows, :] * present.astype(BF16)


def masked(tiles, mask, width):
    height, breadth = tiles.shape
    return pl.pallas_call(
        mask_kernel,
        out_shape=jax.ShapeDtypeStruct((height, breadth), BF16),
        grid_spec=pltpu.PrefetchScalarGridSpec(
            num_scalar_prefetch=1,
            grid=(breadth // width,),
            in_specs=[pl.BlockSpec((height, width), lambda g, mask: (0, g))],
            out_specs=pl.BlockSpec((height, width), lambda g, mask: (0, g)),
        ),
        compiler_params=params(),
        name="masked_tiles",
    )(mask, tiles)


def product_kernel(place, columns, *refs):
    blocks, out = refs[:-1], refs[-1]
    total = jnp.zeros((4 * WIDE, ROWS), F32)
    for b, block in enumerate(blocks):
        plane = place[b]
        half = pl.multiple_of(place[8 + b] * HALF, HALF)
        left = columns[:, pl.ds(plane, 1), :, pl.ds(half, HALF)].reshape(4 * WIDE, HALF)
        total = total + dot_last(left, block[...])
    out[...] = total.reshape(4, WIDE, ROWS)


def product(columns, blocks, place):
    return pl.pallas_call(
        product_kernel,
        out_shape=jax.ShapeDtypeStruct((4, WIDE, ROWS), F32),
        in_specs=[pl.BlockSpec(memory_space=pltpu.SMEM)]
        + [pl.BlockSpec(memory_space=pltpu.VMEM)] * (1 + len(blocks)),
        out_specs=pl.BlockSpec(memory_space=pltpu.VMEM),
        compiler_params=params(),
        name="product",
    )(place, columns, *blocks)


def pack(values):
    tail = values[:, 128:]
    return jnp.concatenate(
        [values[:, :128], jnp.concatenate([tail[:24], tail[24:]], axis=1)], axis=0
    )


def coarse_kernel(parts, tiles, out, terms):
    @pl.when(pl.program_id(0) == 0)
    def _():
        whole = (parts[0] + parts[1]) + (parts[2] + parts[3])
        high = whole.astype(BF16)
        rest = whole - high.astype(F32)
        middle = rest.astype(BF16)
        low = (rest - middle.astype(F32)).astype(BF16)
        terms[...] = jnp.concatenate([high, middle, low], axis=0)

    full = jnp.dot(terms[...], tiles[...], preferred_element_type=F32)
    full = (full[2 * WIDE :] + full[WIDE : 2 * WIDE]) + full[:WIDE]
    for k in range(out.shape[0]):
        chunk = full[:, k * TILE : (k + 1) * TILE]
        most = jnp.maximum(jnp.max(jnp.abs(chunk), axis=0, keepdims=True), 1e-33)
        code = jnp.ceil(jnp.log2(most) * STEPS) + 1.0
        factor = LIMIT * jnp.exp2(code * (-1.0 / STEPS))
        values = pack(jnp.round(chunk * factor))
        scales = pack(jnp.broadcast_to(code, (WIDE, TILE)))
        coded = jnp.concatenate([values, scales[:1], scales[48:49], jnp.zeros((6, 128), F32)], axis=0)
        out[k] = coded.astype(jnp.int32).astype(jnp.int16)


def coarse_parts(parts, p_masked):
    width = COARSE // 4
    return pl.pallas_call(
        coarse_kernel,
        out_shape=jax.ShapeDtypeStruct((PLANES, CODED, 128), jnp.int16),
        grid=(4,),
        in_specs=[
            pl.BlockSpec((4, WIDE, ROWS), lambda g: (0, 0, 0)),
            pl.BlockSpec((ROWS, width), lambda g: (0, g)),
        ],
        out_specs=pl.BlockSpec((width // TILE, CODED, 128), lambda g: (g, 0, 0)),
        scratch_shapes=[pltpu.VMEM((3 * WIDE, ROWS), BF16)],
        compiler_params=params(),
        name="coarse_parts",
    )(parts, p_masked)


def sum_kernel(coded, out):
    total = jnp.zeros((72, 128), F32)
    for z in range(PLANES):
        block = coded[z].astype(jnp.int32).astype(F32)
        scale = jnp.exp2(block[72:80] * (1.0 / STEPS)) * (1.0 / LIMIT)
        factor = jnp.concatenate(
            [jnp.broadcast_to(scale[:1], (48, 128)), jnp.broadcast_to(scale[1:2], (24, 128))], axis=0
        )
        total = total + block[:72] * factor
    out[:, :128] = total[:48]
    out[:24, 128:] = total[48:, :64]
    out[24:, 128:] = total[48:, 64:]


def summed(coded):
    return pl.pallas_call(
        sum_kernel,
        out_shape=jax.ShapeDtypeStruct((WIDE, TILE), F32),
        in_specs=[pl.BlockSpec(memory_space=pltpu.VMEM)],
        out_specs=pl.BlockSpec(memory_space=pltpu.VMEM),
        compiler_params=params(),
        name="summed",
    )(coded)


def along_y(near):
    pairs = []
    for y in range(8):
        source = (y + near) % 8 if y % 2 else (y - near) % 8
        for core in range(2):
            pairs.append((((source // 2) * 2 + core) * 2 + source % 2, ((y // 2) * 2 + core) * 2 + y % 2))
    return pairs


def local(a_tiles, p_tiles, a_mask, p_mask):
    yh, core, yl = lax.axis_index("yh"), lax.axis_index("core"), lax.axis_index("yl")
    index = ((lax.axis_index("x") * 4 + yh) * 2 + core) * 2 + yl

    mine = own_columns(p_tiles, p_mask, index)
    gathered = lax.all_gather(mine, ("zh", "zl"))

    a_tiles, mine = lax.optimization_barrier((a_tiles, mine))
    own = masked(a_tiles, a_mask, HALF)
    ys = ("yh", "core", "yl")
    sign = 2 * yl - 1
    blocks = [own] + [lax.ppermute(own, ys, along_y(d)) for d in (1, -2, 3)]
    planes = [yh, yh + sign, yh - sign, yh + 2]
    blocks = blocks + [lax.ppermute(block, "core", [(0, 1), (1, 0)]) for block in blocks]
    planes = jnp.stack(planes + planes) % 4
    halves = jnp.stack([core] * 4 + [1 - core] * 4)
    place = jnp.concatenate([planes, halves]).astype(jnp.int32)

    p_tiles, own = lax.optimization_barrier((p_tiles, own))
    p_masked = masked(p_tiles, p_mask, COARSE // 4)

    columns = lax.all_to_all(gathered, "x", 0, 0, tiled=True).reshape(4, 4, WIDE, ROWS)
    parts = lax.all_to_all(product(columns, blocks, place), "x", 0, 0, tiled=True)
    coded = lax.all_to_all(coarse_parts(parts, p_masked), ("zh", "zl"), 0, 0, tiled=True)
    return summed(coded).T


def solution(mesh):
    fine = Mesh(mesh.devices.reshape(4, 4, 4, 4, 2, 2), ("zh", "zl", "x", "yh", "core", "yl"))
    z, col = ("zh", "zl"), ("x", "yh", "core")
    return jax.shard_map(
        local,
        mesh=fine,
        in_specs=(P(z, col), P(z, None), P(z, col), P(z, None)),
        out_specs=P(z, col + ("yl",)),
        check_vma=False,
    )
```

time: 412 us -> 170 us (0.41)
  waiting for transfers between devices: 350 us -> 71.8 us
  starting transfers between devices: 0.27 us -> 33.2 us
  blocking collectives: 0 us -> 28 us
  local copies, waits for them, and re-layouts: 28.7 us -> 7.74 us
  Pallas kernels: 0 us -> 13.6 us
  matrix products: 12.2 us -> 0 us
  other arithmetic: 6.83 us -> 0.09 us
    psum x1 -> x0, waiting for transfers between devices: 154 us -> none  [from_root(): return lax.psum(block, axis)]
    reduce_scatter x1 -> x0, waiting for transfers between devices: 122 us -> none  [local(): lax.psum_scatter(lax.dot_general(picked, a_masked, (((0,), (1,)), ((), ()...]
    unnamed x4 -> x1, waiting for transfers between devices: 75.2 us -> 0.02 us
    all_gather x0 -> x1, waiting for transfers between devices: none -> 67.6 us  [local(): gathered = lax.all_gather(mine, ('zh', 'zl'))]
    all_to_all x0 -> x1, blocking collectives: none -> 28 us  [local(): lax.all_to_all(coarse_parts(parts, p_masked), ('zh', 'zl'), 0, 0, tiled=T...]
    ppermute x0 -> x7, starting transfers between devices: none -> 23.4 us  [the longest x3 14.8 us: local(): blocks = [own] + [lax.ppermute(own, ys, along_y(d)) for d in (1, -2, 3)]]
    mul x4 -> x0, local copies, waits for them, and re-layouts: 16.8 us -> none  [masked(): shaped * mask.astype(jnp.bfloat16)[:, None, :, None]]
    pallas_call x0 -> x6, Pallas kernels: none -> 13.6 us  [the longest x2 4.53 us: masked(): pl.pallas_call(mask_kernel, out_shape=jax.ShapeDtypeStruct((height, bread...]
  transfers between devices with their start and end apart: 3 -> 10, of which waited for: 3 -> 3; matrix products, arithmetic and copies ran while one was open for 0% -> 0% of each run, Pallas kernels for 0% -> 3%
where the time goes in v1:
time: 170 us; the launch traced here: 168 us
  waiting for transfers between devices  71.8 us (42%)
  starting transfers between devices  33.2 us (20%)
  blocking collectives  28 us (16%)
  Pallas kernels  13.6 us (8%)
  between operations  13.5 us (8%)
  local copies, waits for them, and re-layouts  7.74 us (5%)
    all_gather x1, waiting for transfers between devices, local(): gathered = lax.all_gather(mine, ('zh', 'zl'))  67.6 us
    all_to_all x1, blocking collectives, local(): lax.all_to_all(coarse_parts(parts, p_masked), ('zh', 'zl'), 0, 0, tiled=T...  28 us
    ppermute x3, starting transfers between devices, local(): blocks = [own] + [lax.ppermute(own, ys, along_y(d)) for d in (1, -2, 3)]  14.8 us
    ppermute x4, starting transfers between devices, local(): lax.ppermute(block, 'core', [(0, 1), (1, 0)])  8.64 us
    unnamed x15, local copies, waits for them, and re-layouts  7.57 us
    all_to_all x1, starting transfers between devices, local(): lax.all_to_all(gathered, 'x', 0, 0, tiled=True).reshape(4, 4, WIDE, ROWS)  4.95 us
    all_to_all x1, starting transfers between devices, local(): lax.all_to_all(product(columns, blocks, place), 'x', 0, 0, tiled=True)  4.81 us
    pallas_call x2, Pallas kernels, masked(): pl.pallas_call(mask_kernel, out_shape=jax.ShapeDtypeStruct((height, bread...  4.53 us
  transfers between devices with their start and end apart: 10, of which 3 were waited for; matrix products, arithmetic and copies ran while one was open for 0% of the time, Pallas kernels for 3%

profile of v1, /device:TPU:6, one launch (start us, length us, event | category | flops | bytes accessed | tf_op | source)
XLA Modules:
  0.0 167.9 jit_solution(4710787192073706829)
XLA Ops:
  6.5 0.1 pad_add_fusion.place
  6.6 2.3 %copy-done = bf16[768,3072]{1,0:T(8,128)(2,1)S(1)} copy-done((bf16[768,3072]{1,0:T(8,128)(2,1)S(1)}, bf16[768,3072]{1,0:T(8,128)(2,1)}, u32[]{:S(2)}) %copy-start) | copy-done | bytes 4718616
  9.0 0.7 copy-done.4
  9.6 1.5 own_columns.1
  11.1 0.0 all-gather.3.cloned.1.call-update
  11.2 0.1 copy.5.mask
  11.2 0.6 masked_tiles.2.refs_0_
  11.9 6.9 %collective-permute-start.2 = (bf16[768,384]{1,0:T(8,128)(2,1)S(1)}, bf16[768,384]{1,0:T(8,128)(2,1)S(1)}, u32[]{:S(2)}, u32[]{:S(2)}) collective-permute-start(bf16[768,384]{1,0:T(8,128)(2,1)S(1)} %masked_tiles.2.refs_0_), channel_id=1, source_target_pairs={{9,0},{11,2},{8,1},{10,3},{13,4},{15,6},{12,5},{14,7},{1,8},{3,10}... | collective-permute-start | bytes 1769480 | tf_op jit(solution)/shard_map/ppermute | solution.py:213
  18.8 3.1 %collective-permute-start.1 = (bf16[768,384]{1,0:T(8,128)(2,1)S(1)}, bf16[768,384]{1,0:T(8,128)(2,1)S(1)}, u32[]{:S(2)}, u32[]{:S(2)}) collective-permute-start(bf16[768,384]{1,0:T(8,128)(2,1)S(1)} %masked_tiles.2.refs_0_), channel_id=1, source_target_pairs={{4,0},{6,2},{13,1},{15,3},{8,4},{10,6},{1,5},{3,7},{12,8},{14,10},... | collective-permute-start | bytes 1769480 | tf_op jit(solution)/shard_map/ppermute | solution.py:213
  22.0 4.7 %collective-permute-start = (bf16[768,384]{1,0:T(8,128)(2,1)S(1)}, bf16[768,384]{1,0:T(8,128)(2,1)S(1)}, u32[]{:S(2)}, u32[]{:S(2)}) collective-permute-start(bf16[768,384]{1,0:T(8,128)(2,1)S(1)} %masked_tiles.2.refs_0_), channel_id=1, source_target_pairs={{13,0},{15,2},{4,1},{6,3},{1,4},{3,6},{8,5},{10,7},{5,8},{7,10},{1... | collective-permute-start | bytes 1769480 | tf_op jit(solution)/shard_map/ppermute | solution.py:213
  26.7 67.6 %all-gather.3.cloned.1.call-done = bf16[768,768]{1,0:T(8,128)(2,1)} async-done(((bf16[48,768]{1,0:T(8,128)(2,1)}), bf16[768,768]{1,0:T(8,128)(2,1)}) %all-gather.3.cloned.1.call-update) | async-done | bytes 1179664 | tf_op jit(solution)/shard_map/all_gather | solution.py:207
  94.3 4.9 %all-to-all-start = ((bf16[16,48,768]{2,1,0:T(8,128)(2,1)}), bf16[16,48,768]{2,1,0:T(8,128)(2,1)}, u32[]{:S(2)}, u32[]{:S(2)}) async-start(bf16[16,48,768]{2,1,0:T(8,128)(2,1)} %bitcast.12), calls=%async_computation | async-start | bytes 2359296 | tf_op jit(solution)/shard_map/all_to_all | solution.py:223
  99.3 1.9 %collective-permute-start.3 = (bf16[768,384]{1,0:T(8,128)(2,1)S(1)}, bf16[768,384]{1,0:T(8,128)(2,1)S(1)}, u32[]{:S(2)}, u32[]{:S(2)}) collective-permute-start(bf16[768,384]{1,0:T(8,128)(2,1)S(1)} %masked_tiles.2.refs_0_), channel_id=1, source_target_pairs={{0,2},{2,0},{1,3},{3,1},{4,6},{6,4},{5,7},{7,5},{8,10},{10,8},{9,1... | collective-permute-start | bytes 1769480 | tf_op jit(solution)/shard_map/ppermute | solution.py:215
  101.2 0.0 collective-permute-done.2.refs_3_
  101.2 2.4 %collective-permute-start.6 = (bf16[768,384]{1,0:T(8,128)(2,1)S(1)}, bf16[768,384]{1,0:T(8,128)(2,1)S(1)}, u32[]{:S(2)}, u32[]{:S(2)}) collective-permute-start(bf16[768,384]{1,0:T(8,128)(2,1)S(1)} %collective-permute-done.2.refs_3_), channel_id=1, source_target_pairs={{0,2},{2,0},{1,3},{3,1},{4,6},{6,4},{5,7},{7,5},{8,10},{10,8},{9,1... | collective-permute-start | bytes 1769480 | tf_op jit(solution)/shard_map/ppermute | solution.py:215
  103.6 0.0 collective-permute-done.1.refs_2_
  103.6 1.9 %collective-permute-start.5 = (bf16[768,384]{1,0:T(8,128)(2,1)S(1)}, bf16[768,384]{1,0:T(8,128)(2,1)}, u32[]{:S(2)}, u32[]{:S(2)}) collective-permute-start(bf16[768,384]{1,0:T(8,128)(2,1)S(1)} %collective-permute-done.1.refs_2_), channel_id=1, source_target_pairs={{0,2},{2,0},{1,3},{3,1},{4,6},{6,4},{5,7},{7,5},{8,10},{10,8},{9,1... | collective-permute-start | bytes 1769480 | tf_op jit(solution)/shard_map/ppermute | solution.py:215
  105.6 2.4 %collective-permute-start.4 = (bf16[768,384]{1,0:T(8,128)(2,1)S(1)}, bf16[768,384]{1,0:T(8,128)(2,1)}, u32[]{:S(2)}, u32[]{:S(2)}) collective-permute-start(bf16[768,384]{1,0:T(8,128)(2,1)S(1)} %collective-permute-done.refs_1_), channel_id=1, source_target_pairs={{0,2},{2,0},{1,3},{3,1},{4,6},{6,4},{5,7},{7,5},{8,10},{10,8},{9,1... | collective-permute-start | bytes 1769480 | tf_op jit(solution)/shard_map/ppermute | solution.py:215
  108.0 0.1 stack.47
  108.1 0.1 concatenate.3.place
  108.2 0.0 collective-permute-done.3.refs_4_
  108.2 1.5 collective-permute-done.4.refs_5_
  109.7 0.0 all-to-all-done
  109.7 4.1 %product.1 = f32[4,48,768]{2,1,0:T(8,128)} custom-call(s32[16]{0:T(128)S(1)} %concatenate.3.place, bf16[4,4,48,768]{3,2,1,0:T(8,128)(2,1)} %bitcast.10.columns, bf16[768,384]{1,0:T(8,128)(2,1)S(1)} %masked_tiles.2.refs_0_, bf16[768,384]{1,0:T(8,128)(2,1)S(1)} %collective-permute-done.refs_1_, bf16[768,384]{1,0:T(8,128)(2,1)S(1)} %collective-permute-done.1.refs_2_, ...), custom_call_target="tpu_custom_call" | custom-call | tf_op jit(solution)/shard_map/product/pallas_call | solution.py:110
  113.9 4.8 %all-to-all-start.1 = ((f32[4,48,768]{2,1,0:T(8,128)}), f32[4,48,768]{2,1,0:T(8,128)S(1)}, u32[]{:S(2)}, u32[]{:S(2)}) async-start(f32[4,48,768]{2,1,0:T(8,128)} %product.1), calls=%async_computation.1 | async-start | bytes 1179648 | tf_op jit(solution)/shard_map/all_to_all | solution.py:224
  118.7 3.9 %masked_tiles.3.tiles = bf16[768,3072]{1,0:T(8,128)(2,1)S(1)} custom-call(s32[4,16]{1,0:T(4,128)S(1)} %copy-done.5, bf16[768,3072]{1,0:T(8,128)(2,1)} %tiles.1), custom_call_target="tpu_custom_call" | custom-call | tf_op jit(solution)/shard_map/masked_tiles/pallas_call | solution.py:84
  122.6 2.1 %copy-done.1 = bf16[768,3072]{1,0:T(8,128)(2,1)} copy-done((bf16[768,3072]{1,0:T(8,128)(2,1)}, bf16[768,3072]{1,0:T(8,128)(2,1)S(1)}, u32[]{:S(2)}) %copy-start.1) | copy-done | bytes 4718616
  124.7 2.6 %all-to-all-done.1.parts = f32[4,48,768]{2,1,0:T(8,128)S(1)} async-done(((f32[4,48,768]{2,1,0:T(8,128)}), f32[4,48,768]{2,1,0:T(8,128)S(1)}, u32[]{:S(2)}, u32[]{:S(2)}) %all-to-all-start.1) | async-done | bytes 589856 | tf_op jit(solution)/shard_map/all_to_all | solution.py:224
  127.3 2.3 %copy-done.2 = bf16[768,3072]{1,0:T(8,128)(2,1)S(1)} copy-done((bf16[768,3072]{1,0:T(8,128)(2,1)S(1)}, bf16[768,3072]{1,0:T(8,128)(2,1)}, u32[]{:S(2)}) %copy-start.2) | copy-done | bytes 4718616
  129.6 2.7 %coarse_parts.1 = s16[16,80,128]{2,1,0:T(8,128)(2,1)S(1)} custom-call(f32[4,48,768]{2,1,0:T(8,128)S(1)} %all-to-all-done.1.parts, bf16[768,3072]{1,0:T(8,128)(2,1)S(1)} %copy-done.2), custom_call_target="tpu_custom_call" | custom-call | tf_op jit(solution)/shard_map/coarse_parts/pallas_call | solution.py:153
  132.4 28.0 %all_to_all.15.coded = s16[16,80,128]{2,1,0:T(8,128)(2,1)S(1)} all-to-all(s16[16,80,128]{2,1,0:T(8,128)(2,1)S(1)} %coarse_parts.1), channel_id=1, replica_groups=mesh['zh'=4,'zl'=4,'x'=4,'yh'=4,'core'=2,'yl'=2] {'zh','zl'}, dimensions={0} | all-to-all | bytes 655360 | tf_op jit(solution)/shard_map/all_to_all | solution.py:225
  160.3 0.7 summed.1
  (15 shorter events, 0.0 us)
Async XLA Ops:
  6.5 87.8 %all-gather.3.cloned.1.call-start = ((), (), s32[]{:S(2)}) async-start(), calls=%async_computation.3 | async-start | bytes 1253376 | tf_op jit(solution)/shard_map/all_gather | solution.py:207
  6.6 2.3 %copy-start = (bf16[768,3072]{1,0:T(8,128)(2,1)S(1)}, bf16[768,3072]{1,0:T(8,128)(2,1)}, u32[]{:S(2)}) copy-start(bf16[768,3072]{1,0:T(8,128)(2,1)} %tiles.1) | copy-start | bytes 14155780
  9.0 0.7 copy-start.4
  9.6 1.5 copy-start.6
  9.6 1.6 copy-start.3
  11.9 89.3 %collective-permute-start.2 = (bf16[768,384]{1,0:T(8,128)(2,1)S(1)}, bf16[768,384]{1,0:T(8,128)(2,1)S(1)}, u32[]{:S(2)}, u32[]{:S(2)}) collective-permute-start(bf16[768,384]{1,0:T(8,128)(2,1)S(1)} %masked_tiles.2.refs_0_), channel_id=1, source_target_pairs={{9,0},{11,2},{8,1},{10,3},{13,4},{15,6},{12,5},{14,7},{1,8},{3,10}... | collective-permute-start | bytes 1769480 | tf_op jit(solution)/shard_map/ppermute | solution.py:213
  18.8 84.8 %collective-permute-start.1 = (bf16[768,384]{1,0:T(8,128)(2,1)S(1)}, bf16[768,384]{1,0:T(8,128)(2,1)S(1)}, u32[]{:S(2)}, u32[]{:S(2)}) collective-permute-start(bf16[768,384]{1,0:T(8,128)(2,1)S(1)} %masked_tiles.2.refs_0_), channel_id=1, source_target_pairs={{4,0},{6,2},{13,1},{15,3},{8,4},{10,6},{1,5},{3,7},{12,8},{14,10},... | collective-permute-start | bytes 1769480 | tf_op jit(solution)/shard_map/ppermute | solution.py:213
  22.0 83.6 %collective-permute-start = (bf16[768,384]{1,0:T(8,128)(2,1)S(1)}, bf16[768,384]{1,0:T(8,128)(2,1)S(1)}, u32[]{:S(2)}, u32[]{:S(2)}) collective-permute-start(bf16[768,384]{1,0:T(8,128)(2,1)S(1)} %masked_tiles.2.refs_0_), channel_id=1, source_target_pairs={{13,0},{15,2},{4,1},{6,3},{1,4},{3,6},{8,5},{10,7},{5,8},{7,10},{1... | collective-permute-start | bytes 1769480 | tf_op jit(solution)/shard_map/ppermute | solution.py:213
  94.3 24.4 %copy-start.5 = (s32[4,16]{1,0:T(4,128)S(1)}, s32[4,16]{1,0:T(4,128)}, u32[]{:S(2)}) copy-start(s32[4,16]{1,0:T(4,128)} %mask.4) | copy-start | bytes 772
  94.3 15.4 %all-to-all-start = ((bf16[16,48,768]{2,1,0:T(8,128)(2,1)}), bf16[16,48,768]{2,1,0:T(8,128)(2,1)}, u32[]{:S(2)}, u32[]{:S(2)}) async-start(bf16[16,48,768]{2,1,0:T(8,128)(2,1)} %bitcast.12), calls=%async_computation | async-start | bytes 2359296 | tf_op jit(solution)/shard_map/all_to_all | solution.py:223
  99.3 8.9 %collective-permute-start.3 = (bf16[768,384]{1,0:T(8,128)(2,1)S(1)}, bf16[768,384]{1,0:T(8,128)(2,1)S(1)}, u32[]{:S(2)}, u32[]{:S(2)}) collective-permute-start(bf16[768,384]{1,0:T(8,128)(2,1)S(1)} %masked_tiles.2.refs_0_), channel_id=1, source_target_pairs={{0,2},{2,0},{1,3},{3,1},{4,6},{6,4},{5,7},{7,5},{8,10},{10,8},{9,1... | collective-permute-start | bytes 1769480 | tf_op jit(solution)/shard_map/ppermute | solution.py:215
  101.2 7.0 %collective-permute-start.6 = (bf16[768,384]{1,0:T(8,128)(2,1)S(1)}, bf16[768,384]{1,0:T(8,128)(2,1)S(1)}, u32[]{:S(2)}, u32[]{:S(2)}) collective-permute-start(bf16[768,384]{1,0:T(8,128)(2,1)S(1)} %collective-permute-done.2.refs_3_), channel_id=1, source_target_pairs={{0,2},{2,0},{1,3},{3,1},{4,6},{6,4},{5,7},{7,5},{8,10},{10,8},{9,1... | collective-permute-start | bytes 1769480 | tf_op jit(solution)/shard_map/ppermute | solution.py:215
  103.6 4.6 %collective-permute-start.5 = (bf16[768,384]{1,0:T(8,128)(2,1)S(1)}, bf16[768,384]{1,0:T(8,128)(2,1)}, u32[]{:S(2)}, u32[]{:S(2)}) collective-permute-start(bf16[768,384]{1,0:T(8,128)(2,1)S(1)} %collective-permute-done.1.refs_2_), channel_id=1, source_target_pairs={{0,2},{2,0},{1,3},{3,1},{4,6},{6,4},{5,7},{7,5},{8,10},{10,8},{9,1... | collective-permute-start | bytes 1769480 | tf_op jit(solution)/shard_map/ppermute | solution.py:215
  105.6 4.2 %collective-permute-start.4 = (bf16[768,384]{1,0:T(8,128)(2,1)S(1)}, bf16[768,384]{1,0:T(8,128)(2,1)}, u32[]{:S(2)}, u32[]{:S(2)}) collective-permute-start(bf16[768,384]{1,0:T(8,128)(2,1)S(1)} %collective-permute-done.refs_1_), channel_id=1, source_target_pairs={{0,2},{2,0},{1,3},{3,1},{4,6},{6,4},{5,7},{7,5},{8,10},{10,8},{9,1... | collective-permute-start | bytes 1769480 | tf_op jit(solution)/shard_map/ppermute | solution.py:215
  113.9 13.4 %all-to-all-start.1 = ((f32[4,48,768]{2,1,0:T(8,128)}), f32[4,48,768]{2,1,0:T(8,128)S(1)}, u32[]{:S(2)}, u32[]{:S(2)}) async-start(f32[4,48,768]{2,1,0:T(8,128)} %product.1), calls=%async_computation.1 | async-start | bytes 1179648 | tf_op jit(solution)/shard_map/all_to_all | solution.py:224
  122.6 2.1 %copy-start.1 = (bf16[768,3072]{1,0:T(8,128)(2,1)}, bf16[768,3072]{1,0:T(8,128)(2,1)S(1)}, u32[]{:S(2)}) copy-start(bf16[768,3072]{1,0:T(8,128)(2,1)S(1)} %masked_tiles.3.tiles) | copy-start | bytes 14155780
  127.3 2.3 %copy-start.2 = (bf16[768,3072]{1,0:T(8,128)(2,1)S(1)}, bf16[768,3072]{1,0:T(8,128)(2,1)}, u32[]{:S(2)}) copy-start(bf16[768,3072]{1,0:T(8,128)(2,1)} %copy-done.1) | copy-start | bytes 14155780
Sparse Core Ops, SparseCore 0:
  11.3 83.0 all-gather.2

commit v2 on v1

--- a/solution.py
+++ b/solution.py
@@ -17,6 +17,8 @@
 STEPS = 128.0
 CODED = 80
 VMEM = 48 * 1024 * 1024
+MOST_VMEM = 62 * 1024 * 1024
+SWAP = [(0, 1), (1, 0)]
 F32 = jnp.float32
 BF16 = jnp.bfloat16
 
@@ -29,41 +31,43 @@
     return lax.dot_general(left, right, (((1,), (1,)), ((), ())), preferred_element_type=F32)
 
 
-def slice_kernel(place, mask, first, second, out):
-    offset = place[1]
-    tile = place[2]
+def slice_kernel(place, mask, *refs):
+    views, out = refs[:4], refs[4]
     row = lax.broadcasted_iota(jnp.int32, (WIDE, 128), 0)
     lane = lax.broadcasted_iota(jnp.int32, (WIDE, 128), 1)
-    pick_first = (lane == row + offset).astype(F32).astype(BF16)
-    pick_second = (lane + 128 == row + offset).astype(F32).astype(BF16)
-    picked = dot_last(pick_first, first[...]) + dot_last(pick_second, second[...])
+    pick_first = (lane == row + place[1]).astype(F32).astype(BF16)
+    pick_second = (lane + 128 == row + place[1]).astype(F32).astype(BF16)
     fine = lax.broadcasted_iota(jnp.int32, (1, ROWS), 1)
-    present = jnp.zeros((1, ROWS), F32)
-    for i in range(ROWS // TILE):
-        inside = (fine >= i * TILE) & (fine < (i + 1) * TILE)
-        present = jnp.where(inside, mask[i, tile].astype(F32), present)
-    out[...] = (picked * present).astype(BF16)
-
-
-def own_columns(p_tiles, p_mask, index):
-    start = index * WIDE
-    block = jnp.minimum(start // 128, COARSE // 128 - 2)
-    place = jnp.stack([block, start - block * 128, start // TILE]).astype(jnp.int32)
+    for n in range(2):
+        first, second = views[2 * n], views[2 * n + 1]
+        picked = dot_last(pick_first, first[...]) + dot_last(pick_second, second[...])
+        present = jnp.zeros((1, ROWS), F32)
+        for i in range(ROWS // TILE):
+            inside = (fine >= i * TILE) & (fine < (i + 1) * TILE)
+            present = jnp.where(inside, mask[i, place[2] + 4 * n].astype(F32), present)
+        out[n] = (picked * present).astype(BF16)
+
+
+def two_slices(p_tiles, p_mask, first, rest):
+    start = rest * WIDE
+    block = jnp.minimum(start // 128, 4)
+    place = jnp.stack([6 * first + block, start - block * 128, 4 * first + start // TILE])
+
+    def view(shift):
+        return pl.BlockSpec((ROWS, 128), lambda g, place, mask: (0, place[0] + shift))
+
     return pl.pallas_call(
         slice_kernel,
-        out_shape=jax.ShapeDtypeStruct((WIDE, ROWS), BF16),
+        out_shape=jax.ShapeDtypeStruct((2, WIDE, ROWS), BF16),
         grid_spec=pltpu.PrefetchScalarGridSpec(
             num_scalar_prefetch=2,
             grid=(1,),
-            in_specs=[
-                pl.BlockSpec((ROWS, 128), lambda g, place, mask: (0, place[0])),
-                pl.BlockSpec((ROWS, 128), lambda g, place, mask: (0, place[0] + 1)),
-            ],
-            out_specs=pl.BlockSpec((WIDE, ROWS), lambda g, place, mask: (0, 0)),
+            in_specs=[view(0), view(1), view(6), view(7)],
+            out_specs=pl.BlockSpec((2, WIDE, ROWS), lambda g, place, mask: (0, 0, 0)),
         ),
-        compiler_params=params(),
-        name="own_columns",
-    )(place, p_mask, p_tiles, p_tiles)
+        compiler_params=pltpu.CompilerParams(vmem_limit_bytes=MOST_VMEM),
+        name="two_slices",
+    )(place.astype(jnp.int32), p_mask, p_tiles, p_tiles, p_tiles, p_tiles)
 
 
 def mask_kernel(mask, tiles, out):
@@ -95,27 +99,57 @@
     )(mask, tiles)
 
 
-def product_kernel(place, columns, *refs):
-    blocks, out = refs[:-1], refs[-1]
+def collect_kernel(place, near, far, whole, lower, upper):
+    @pl.when(place[0] < 2)
+    def _():
+        lower[...], upper[...] = near[...], far[...]
+
+    @pl.when(place[0] >= 2)
+    def _():
+        lower[...], upper[...] = far[...], near[...]
+
+    whole[:2], whole[2:] = lower[...], upper[...]
+
+
+def collect(near, far, zh):
+    return pl.pallas_call(
+        collect_kernel,
+        out_shape=[jax.ShapeDtypeStruct((n, WIDE, ROWS), BF16) for n in (4, 2, 2)],
+        in_specs=[pl.BlockSpec(memory_space=pltpu.SMEM)]
+        + [pl.BlockSpec(memory_space=pltpu.VMEM)] * 2,
+        out_specs=[pl.BlockSpec(memory_space=pltpu.VMEM)] * 3,
+        compiler_params=params(),
+        name="collect",
+    )(zh.reshape(1).astype(jnp.int32), near, far)
+
+
+def product_kernel(place, slab, above, below, lower, upper, *refs):
+    blocks, out, columns = refs[:-2], refs[-2], refs[-1]
+    zl = place[16]
+    columns[(zl + 2) % 4] = slab[...]
+    columns[(zl + 3) % 4] = above[...]
+    columns[(zl + 1) % 4] = below[...]
+    columns[zl, :2] = lower[...]
+    columns[zl, 2:] = upper[...]
     total = jnp.zeros((4 * WIDE, ROWS), F32)
     for b, block in enumerate(blocks):
-        plane = place[b]
         half = pl.multiple_of(place[8 + b] * HALF, HALF)
-        left = columns[:, pl.ds(plane, 1), :, pl.ds(half, HALF)].reshape(4 * WIDE, HALF)
+        left = columns[place[b], :, :, pl.ds(half, HALF)].reshape(4 * WIDE, HALF)
         total = total + dot_last(left, block[...])
     out[...] = total.reshape(4, WIDE, ROWS)
 
 
-def product(columns, blocks, place):
+def product(slabs, blocks, place):
     return pl.pallas_call(
         product_kernel,
         out_shape=jax.ShapeDtypeStruct((4, WIDE, ROWS), F32),
         in_specs=[pl.BlockSpec(memory_space=pltpu.SMEM)]
-        + [pl.BlockSpec(memory_space=pltpu.VMEM)] * (1 + len(blocks)),
+        + [pl.BlockSpec(memory_space=pltpu.VMEM)] * (len(slabs) + len(blocks)),
         out_specs=pl.BlockSpec(memory_space=pltpu.VMEM),
+        scratch_shapes=[pltpu.VMEM((4, 4, WIDE, ROWS), BF16)],
         compiler_params=params(),
         name="product",
-    )(place, columns, *blocks)
+    )(place, *slabs, *blocks)
 
 
 def pack(values):
@@ -125,7 +159,7 @@
     )
 
 
-def coarse_kernel(parts, tiles, out, terms):
+def coarse_kernel(mask, parts, tiles, out, terms, present):
     @pl.when(pl.program_id(0) == 0)
     def _():
         whole = (parts[0] + parts[1]) + (parts[2] + parts[3])
@@ -135,7 +169,8 @@
         low = (rest - middle.astype(F32)).astype(BF16)
         terms[...] = jnp.concatenate([high, middle, low], axis=0)
 
-    full = jnp.dot(terms[...], tiles[...], preferred_element_type=F32)
+    mask_kernel(mask, tiles, present)
+    full = jnp.dot(terms[...], present[...], preferred_element_type=F32)
     full = (full[2 * WIDE :] + full[WIDE : 2 * WIDE]) + full[:WIDE]
     for k in range(out.shape[0]):
         chunk = full[:, k * TILE : (k + 1) * TILE]
@@ -148,21 +183,24 @@
         out[k] = coded.astype(jnp.int32).astype(jnp.int16)
 
 
-def coarse_parts(parts, p_masked):
+def coarse_parts(parts, p_tiles, p_mask):
     width = COARSE // 4
     return pl.pallas_call(
         coarse_kernel,
         out_shape=jax.ShapeDtypeStruct((PLANES, CODED, 128), jnp.int16),
-        grid=(4,),
-        in_specs=[
-            pl.BlockSpec((4, WIDE, ROWS), lambda g: (0, 0, 0)),
-            pl.BlockSpec((ROWS, width), lambda g: (0, g)),
-        ],
-        out_specs=pl.BlockSpec((width // TILE, CODED, 128), lambda g: (g, 0, 0)),
-        scratch_shapes=[pltpu.VMEM((3 * WIDE, ROWS), BF16)],
+        grid_spec=pltpu.PrefetchScalarGridSpec(
+            num_scalar_prefetch=1,
+            grid=(4,),
+            in_specs=[
+                pl.BlockSpec((4, WIDE, ROWS), lambda g, mask: (0, 0, 0)),
+                pl.BlockSpec((ROWS, width), lambda g, mask: (0, g)),
+            ],
+            out_specs=pl.BlockSpec((width // TILE, CODED, 128), lambda g, mask: (g, 0, 0)),
+            scratch_shapes=[pltpu.VMEM((3 * WIDE, ROWS), BF16), pltpu.VMEM((ROWS, width), BF16)],
+        ),
         compiler_params=params(),
         name="coarse_parts",
-    )(parts, p_masked)
+    )(p_mask, parts, p_tiles)
 
 
 def sum_kernel(coded, out):
@@ -199,30 +237,49 @@
     return pairs
 
 
+def swapped(turn):
+    return [
+        ((zh * 4 + zl) * 4 + x, ((x + turn) % 4 * 4 + (zl + 2) % 4) * 4 + zh)
+        for zh in range(4)
+        for zl in range(4)
+        for x in range(4)
+    ]
+
+
+def around(near):
+    return [((z + near) % PLANES, z) for z in range(PLANES)]
+
+
 def local(a_tiles, p_tiles, a_mask, p_mask):
+    zh, zl, x = lax.axis_index("zh"), lax.axis_index("zl"), lax.axis_index("x")
     yh, core, yl = lax.axis_index("yh"), lax.axis_index("core"), lax.axis_index("yl")
-    index = ((lax.axis_index("x") * 4 + yh) * 2 + core) * 2 + yl
-
-    mine = own_columns(p_tiles, p_mask, index)
-    gathered = lax.all_gather(mine, ("zh", "zl"))
-
+    z, ys = ("zh", "zl"), ("yh", "core", "yl")
+
+    mine = two_slices(p_tiles, p_mask, x // 2 * 2, (yh * 2 + core) * 2 + yl)
+    near, far = [lax.ppermute(mine, z + ("x",), swapped(turn)) for turn in (0, 2)]
     a_tiles, mine = lax.optimization_barrier((a_tiles, mine))
     own = masked(a_tiles, a_mask, HALF)
-    ys = ("yh", "core", "yl")
+    first, second = [lax.ppermute(own, ys, along_y(near_by)) for near_by in (1, -2)]
+    other = [lax.ppermute(own, "core", SWAP)]
+
+    slab, lower, upper = collect(near, far, zh)
+    slab, lower, upper, own, first, second, other = lax.optimization_barrier(
+        (slab, lower, upper, own, first, second, other)
+    )
+    slabs = [slab, lax.ppermute(slab, z, around(1)), lax.ppermute(slab, z, around(-1))]
+    slabs += [lax.ppermute(lower, z, around(2)), lax.ppermute(upper, z, around(-2))]
+    third = lax.ppermute(own, ys, along_y(3))
+    other += [lax.ppermute(block, "core", SWAP) for block in (first, second, third)]
+
     sign = 2 * yl - 1
-    blocks = [own] + [lax.ppermute(own, ys, along_y(d)) for d in (1, -2, 3)]
+    blocks = [own, first, second, third] + other
     planes = [yh, yh + sign, yh - sign, yh + 2]
-    blocks = blocks + [lax.ppermute(block, "core", [(0, 1), (1, 0)]) for block in blocks]
     planes = jnp.stack(planes + planes) % 4
     halves = jnp.stack([core] * 4 + [1 - core] * 4)
-    place = jnp.concatenate([planes, halves]).astype(jnp.int32)
-
-    p_tiles, own = lax.optimization_barrier((p_tiles, own))
-    p_masked = masked(p_tiles, p_mask, COARSE // 4)
-
-    columns = lax.all_to_all(gathered, "x", 0, 0, tiled=True).reshape(4, 4, WIDE, ROWS)
-    parts = lax.all_to_all(product(columns, blocks, place), "x", 0, 0, tiled=True)
-    coded = lax.all_to_all(coarse_parts(parts, p_masked), ("zh", "zl"), 0, 0, tiled=True)
+    place = jnp.concatenate([planes, halves, zl.reshape(1)]).astype(jnp.int32)
+
+    parts = lax.all_to_all(product(slabs, blocks, place), "x", 0, 0, tiled=True)
+    coded = lax.all_to_all(coarse_parts(parts, p_tiles, p_mask), z, 0, 0, tiled=True)
     return summed(coded).T
 
 

time: 170 us -> 172 us (1.012)
  starting transfers between devices: 33.2 us -> 61.7 us
  waiting for transfers between devices: 71.8 us -> 51.4 us
  between operations: 13.5 us -> 0.2 us
  blocking collectives: 28 us -> 39.8 us
  local copies, waits for them, and re-layouts: 7.74 us -> 4.08 us
    all_gather x1 -> x0, waiting for transfers between devices: 67.6 us -> none  [local(): gathered = lax.all_gather(mine, ('zh', 'zl'))]
    ppermute x7 -> x13, waiting for transfers between devices: 1.53 us -> 51.4 us  [the longest x1 21 us: local(): third = lax.ppermute(own, ys, along_y(3))]
    ppermute x7 -> x13, starting transfers between devices: 23.4 us -> 61.7 us  [the longest x2 23.9 us: local(): lax.ppermute(mine, z + ('x',), swapped(turn))]
    all_to_all x1 -> x2, blocking collectives: 28 us -> 39.8 us  [the longest x1 26.9 us: local(): lax.all_to_all(coarse_parts(parts, p_tiles, p_mask), z, 0, 0, tiled=True)]
    all_to_all x2 -> x0, starting transfers between devices: 9.76 us -> none  [the longest x1 4.95 us: local(): lax.all_to_all(gathered, 'x', 0, 0, tiled=True).reshape(4, 4, WIDE, ROWS)]
    pallas_call x2 -> x1, Pallas kernels: 4.53 us -> 0.62 us  [masked(): pl.pallas_call(mask_kernel, out_shape=jax.ShapeDtypeStruct((height, bread...]
    unnamed x15 -> x17, local copies, waits for them, and re-layouts: 7.57 us -> 3.91 us
    all_to_all x2 -> x0, waiting for transfers between devices: 2.59 us -> none  [the longest x1 2.59 us: local(): lax.all_to_all(product(columns, blocks, place), 'x', 0, 0, tiled=True)]
  transfers between devices with their start and end apart: 10 -> 13, of which waited for: 3 -> 6; matrix products, arithmetic and copies ran while one was open for 0% -> 0% of each run, Pallas kernels for 3% -> 0%
where the time goes in v2:
time: 172 us; the launch traced here: 170 us
  starting transfers between devices  61.7 us (36%)
  waiting for transfers between devices  51.4 us (30%)
  blocking collectives  39.8 us (23%)
  Pallas kernels  12 us (7%)
  local copies, waits for them, and re-layouts  4.08 us (2%)
    all_to_all x1, blocking collectives, local(): lax.all_to_all(coarse_parts(parts, p_tiles, p_mask), z, 0, 0, tiled=True)  26.9 us
    ppermute x2, starting transfers between devices, local(): lax.ppermute(mine, z + ('x',), swapped(turn))  23.9 us
    ppermute x1, waiting for transfers between devices, local(): third = lax.ppermute(own, ys, along_y(3))  21 us
    ppermute x2, waiting for transfers between devices, local(): lax.ppermute(mine, z + ('x',), swapped(turn))  19.3 us
    all_to_all x1, blocking collectives, local(): parts = lax.all_to_all(product(slabs, blocks, place), 'x', 0, 0, tiled=True)  12.9 us
    ppermute x2, starting transfers between devices, local(): lax.ppermute(own, ys, along_y(near_by))  8.09 us
    ppermute x1, starting transfers between devices, local(): lax.ppermute(slab, z, around(-1))  7.6 us
    ppermute x3, starting transfers between devices, local(): lax.ppermute(block, 'core', SWAP)  6.24 us
  transfers between devices with their start and end apart: 13, of which 6 were waited for; matrix products, arithmetic and copies ran while one was open for 0% of the time, Pallas kernels for 0%

profile of v2, /device:TPU:6, one launch (start us, length us, event | category | flops | bytes accessed | tf_op | source)
XLA Modules:
  0.0 169.7 jit_solution(1852540968628013634)
XLA Ops:
  0.0 0.8 copy.5.mask
  1.3 3.1 %two_slices.1 = bf16[2,48,768]{2,1,0:T(8,128)(2,1)} custom-call(s32[3]{0:T(128)} %pad_add_fusion.place, s32[4,16]{1,0:T(4,128)} %mask.4, bf16[768,3072]{1,0:T(8,128)(2,1)} %tiles.2, bf16[768,3072]{1,0:T(8,128)(2,1)} %tiles.2, bf16[768,3072]{1,0:T(8,128)(2,1)} %tiles.2, bf16[768,3072]{1,0:T(8,128)(2,1)} %tiles.2), custom_call_target="tpu_custom_call" | custom-call | tf_op jit(solution)/shard_map/two_slices/pallas_call | solution.py:59
  4.4 0.6 masked_tiles.1.refs_0_
  5.1 1.9 %collective-permute-start.4 = (bf16[768,384]{1,0:T(8,128)(2,1)S(1)}, bf16[768,384]{1,0:T(8,128)(2,1)S(1)}, u32[]{:S(2)}, u32[]{:S(2)}) collective-permute-start(bf16[768,384]{1,0:T(8,128)(2,1)S(1)} %masked_tiles.1.refs_0_), channel_id=1, source_target_pairs={{0,2},{2,0},{1,3},{3,1},{4,6},{6,4},{5,7},{7,5},{8,10},{10,8},{9,1... | collective-permute-start | bytes 1769480 | tf_op jit(solution)/shard_map/ppermute | solution.py:263
  7.0 6.2 %collective-permute-start.3 = (bf16[768,384]{1,0:T(8,128)(2,1)S(1)}, bf16[768,384]{1,0:T(8,128)(2,1)S(1)}, u32[]{:S(2)}, u32[]{:S(2)}) collective-permute-start(bf16[768,384]{1,0:T(8,128)(2,1)S(1)} %masked_tiles.1.refs_0_), channel_id=1, source_target_pairs={{4,0},{6,2},{13,1},{15,3},{8,4},{10,6},{1,5},{3,7},{12,8},{14,10},... | collective-permute-start | bytes 1769480 | tf_op jit(solution)/shard_map/ppermute | solution.py:262
  13.2 1.9 %collective-permute-start.2 = (bf16[768,384]{1,0:T(8,128)(2,1)S(1)}, bf16[768,384]{1,0:T(8,128)(2,1)S(1)}, u32[]{:S(2)}, u32[]{:S(2)}) collective-permute-start(bf16[768,384]{1,0:T(8,128)(2,1)S(1)} %masked_tiles.1.refs_0_), channel_id=1, source_target_pairs={{13,0},{15,2},{4,1},{6,3},{1,4},{3,6},{8,5},{10,7},{5,8},{7,10},{1... | collective-permute-start | bytes 1769480 | tf_op jit(solution)/shard_map/ppermute | solution.py:262
  15.1 14.4 %collective-permute-start.1 = (bf16[2,48,768]{2,1,0:T(8,128)(2,1)}, bf16[2,48,768]{2,1,0:T(8,128)(2,1)S(1)}, u32[]{:S(2)}, u32[]{:S(2)}) collective-permute-start(bf16[2,48,768]{2,1,0:T(8,128)(2,1)} %two_slices.1), channel_id=1, source_target_pairs={{0,640},{16,896},{32,128},{48,384},{64,704},{80,960},{96,192},{112... | collective-permute-start | bytes 442376 | tf_op jit(solution)/shard_map/ppermute | solution.py:259
  29.6 9.5 %collective-permute-start = (bf16[2,48,768]{2,1,0:T(8,128)(2,1)}, bf16[2,48,768]{2,1,0:T(8,128)(2,1)S(1)}, u32[]{:S(2)}, u32[]{:S(2)}) collective-permute-start(bf16[2,48,768]{2,1,0:T(8,128)(2,1)} %two_slices.1), channel_id=1, source_target_pairs={{0,128},{16,384},{32,640},{48,896},{64,192},{80,448},{96,704},{112... | collective-permute-start | bytes 442376 | tf_op jit(solution)/shard_map/ppermute | solution.py:259
  39.1 11.7 %collective-permute-done.1.far = bf16[2,48,768]{2,1,0:T(8,128)(2,1)S(1)} collective-permute-done((bf16[2,48,768]{2,1,0:T(8,128)(2,1)}, bf16[2,48,768]{2,1,0:T(8,128)(2,1)S(1)}, u32[]{:S(2)}, u32[]{:S(2)}) %collective-permute-start.1) | collective-permute-done | bytes 147488 | tf_op jit(solution)/shard_map/ppermute | solution.py:259
  50.7 7.6 %collective-permute-done.near = bf16[2,48,768]{2,1,0:T(8,128)(2,1)S(1)} collective-permute-done((bf16[2,48,768]{2,1,0:T(8,128)(2,1)}, bf16[2,48,768]{2,1,0:T(8,128)(2,1)S(1)}, u32[]{:S(2)}, u32[]{:S(2)}) %collective-permute-start) | collective-permute-done | bytes 147488 | tf_op jit(solution)/shard_map/ppermute | solution.py:259
  58.4 0.8 collect.1
  59.1 5.2 %collective-permute-start.9 = (bf16[768,384]{1,0:T(8,128)(2,1)S(1)}, bf16[768,384]{1,0:T(8,128)(2,1)S(1)}, u32[]{:S(2)}, u32[]{:S(2)}) collective-permute-start(bf16[768,384]{1,0:T(8,128)(2,1)S(1)} %masked_tiles.1.refs_0_), channel_id=1, source_target_pairs={{9,0},{11,2},{8,1},{10,3},{13,4},{15,6},{12,5},{14,7},{1,8},{3,10}... | collective-permute-start | bytes 1769480 | tf_op jit(solution)/shard_map/ppermute | solution.py:271
  64.4 1.9 %collective-permute-start.10 = (bf16[768,384]{1,0:T(8,128)(2,1)S(1)}, bf16[768,384]{1,0:T(8,128)(2,1)}, u32[]{:S(2)}, u32[]{:S(2)}) collective-permute-start(bf16[768,384]{1,0:T(8,128)(2,1)S(1)} %collective-permute-done.2.refs_1_), channel_id=1, source_target_pairs={{0,2},{2,0},{1,3},{3,1},{4,6},{6,4},{5,7},{7,5},{8,10},{10,8},{9,1... | collective-permute-start | bytes 1769480 | tf_op jit(solution)/shard_map/ppermute | solution.py:272
  66.3 2.4 %collective-permute-start.11 = (bf16[768,384]{1,0:T(8,128)(2,1)S(1)}, bf16[768,384]{1,0:T(8,128)(2,1)}, u32[]{:S(2)}, u32[]{:S(2)}) collective-permute-start(bf16[768,384]{1,0:T(8,128)(2,1)S(1)} %collective-permute-done.3.refs_2_), channel_id=1, source_target_pairs={{0,2},{2,0},{1,3},{3,1},{4,6},{6,4},{5,7},{7,5},{8,10},{10,8},{9,1... | collective-permute-start | bytes 1769480 | tf_op jit(solution)/shard_map/ppermute | solution.py:272
  68.7 21.0 %collective-permute-done.9.refs_3_ = bf16[768,384]{1,0:T(8,128)(2,1)S(1)} collective-permute-done((bf16[768,384]{1,0:T(8,128)(2,1)S(1)}, bf16[768,384]{1,0:T(8,128)(2,1)S(1)}, u32[]{:S(2)}, u32[]{:S(2)}) %collective-permute-start.9) | collective-permute-done | bytes 589856 | tf_op jit(solution)/shard_map/ppermute | solution.py:271
  89.7 1.9 %collective-permute-start.12 = (bf16[768,384]{1,0:T(8,128)(2,1)S(1)}, bf16[768,384]{1,0:T(8,128)(2,1)}, u32[]{:S(2)}, u32[]{:S(2)}) collective-permute-start(bf16[768,384]{1,0:T(8,128)(2,1)S(1)} %collective-permute-done.9.refs_3_), channel_id=1, source_target_pairs={{0,2},{2,0},{1,3},{3,1},{4,6},{6,4},{5,7},{7,5},{8,10},{10,8},{9,1... | collective-permute-start | bytes 1769480 | tf_op jit(solution)/shard_map/ppermute | solution.py:272
  91.6 1.9 %collective-permute-start.7 = (bf16[2,48,768]{2,1,0:T(8,128)(2,1)S(1)}, bf16[2,48,768]{2,1,0:T(8,128)(2,1)S(1)}, u32[]{:S(2)}, u32[]{:S(2)}) collective-permute-start(bf16[2,48,768]{2,1,0:T(8,128)(2,1)S(1)} %get-tuple-element.21), channel_id=1, source_target_pairs={{128,0},{192,64},{256,128},{320,192},{384,256},{448,320},{512,384}... | collective-permute-start | bytes 442376 | tf_op jit(solution)/shard_map/ppermute | solution.py:270
  93.6 4.8 %collective-permute-start.8 = (bf16[2,48,768]{2,1,0:T(8,128)(2,1)S(1)}, bf16[2,48,768]{2,1,0:T(8,128)(2,1)S(1)}, u32[]{:S(2)}, u32[]{:S(2)}) collective-permute-start(bf16[2,48,768]{2,1,0:T(8,128)(2,1)S(1)} %get-tuple-element.22), channel_id=1, source_target_pairs={{896,0},{960,64},{0,128},{64,192},{128,256},{192,320},{256,384},{3... | collective-permute-start | bytes 442376 | tf_op jit(solution)/shard_map/ppermute | solution.py:270
  98.4 2.4 %collective-permute-done.7.lower = bf16[2,48,768]{2,1,0:T(8,128)(2,1)S(1)} collective-permute-done((bf16[2,48,768]{2,1,0:T(8,128)(2,1)S(1)}, bf16[2,48,768]{2,1,0:T(8,128)(2,1)S(1)}, u32[]{:S(2)}, u32[]{:S(2)}) %collective-permute-start.7) | collective-permute-done | bytes 147488 | tf_op jit(solution)/shard_map/ppermute | solution.py:270
  100.8 0.7 copy-done.1
  101.5 7.6 %collective-permute-start.6 = (bf16[4,48,768]{2,1,0:T(8,128)(2,1)}, bf16[4,48,768]{2,1,0:T(8,128)(2,1)}, u32[]{:S(2)}, u32[]{:S(2)}) collective-permute-start(bf16[4,48,768]{2,1,0:T(8,128)(2,1)} %get-tuple-element.20.slab), channel_id=1, source_target_pairs={{960,0},{0,64},{64,128},{128,192},{192,256},{256,320},{320,384},{3... | collective-permute-start | bytes 884744 | tf_op jit(solution)/shard_map/ppermute | solution.py:269
  109.1 0.7 copy-done.3
  109.7 1.9 %collective-permute-start.5 = (bf16[4,48,768]{2,1,0:T(8,128)(2,1)}, bf16[4,48,768]{2,1,0:T(8,128)(2,1)}, u32[]{:S(2)}, u32[]{:S(2)}) collective-permute-start(bf16[4,48,768]{2,1,0:T(8,128)(2,1)} %get-tuple-element.20.slab), channel_id=1, source_target_pairs={{64,0},{128,64},{192,128},{256,192},{320,256},{384,320},{448,384},... | collective-permute-start | bytes 884744 | tf_op jit(solution)/shard_map/ppermute | solution.py:269
  111.9 4.8 %collective-permute-done.6.below = bf16[4,48,768]{2,1,0:T(8,128)(2,1)} collective-permute-done((bf16[4,48,768]{2,1,0:T(8,128)(2,1)}, bf16[4,48,768]{2,1,0:T(8,128)(2,1)}, u32[]{:S(2)}, u32[]{:S(2)}) %collective-permute-start.6) | collective-permute-done | bytes 294944 | tf_op jit(solution)/shard_map/ppermute | solution.py:269
  116.7 3.9 %collective-permute-done.5.above = bf16[4,48,768]{2,1,0:T(8,128)(2,1)} collective-permute-done((bf16[4,48,768]{2,1,0:T(8,128)(2,1)}, bf16[4,48,768]{2,1,0:T(8,128)(2,1)}, u32[]{:S(2)}, u32[]{:S(2)}) %collective-permute-start.5) | collective-permute-done | bytes 294944 | tf_op jit(solution)/shard_map/ppermute | solution.py:269
  120.5 0.9 copy-done.2
  121.4 0.9 copy-done.4
  122.4 3.4 %product.1 = f32[4,48,768]{2,1,0:T(8,128)S(1)} custom-call(s32[17]{0:T(128)S(1)} %concatenate.3.place, bf16[4,48,768]{2,1,0:T(8,128)(2,1)} %get-tuple-element.20.slab, bf16[4,48,768]{2,1,0:T(8,128)(2,1)} %collective-permute-done.5.above, bf16[4,48,768]{2,1,0:T(8,128)(2,1)} %collective-permute-done.6.below, bf16[2,48,768]{2,1,0:T(8,128)(2,1)S(1)} %copy-done.2, ...), custom_call_target="tpu_custom_call" | custom-call | tf_op jit(solution)/shard_map/product/pallas_call | solution.py:143
  125.8 12.9 %all_to_all.10.parts = f32[4,48,768]{2,1,0:T(8,128)S(1)} all-to-all(f32[4,48,768]{2,1,0:T(8,128)S(1)} %product.1), channel_id=1, replica_groups=mesh['zh'=4,'zl'=4,'x'=4,'yh'=4,'core'=2,'yl'=2] {'x'}, dimensions={0} | all-to-all | bytes 1179648 | tf_op jit(solution)/shard_map/all_to_all | solution.py:281
  138.7 3.4 %coarse_parts.1 = s16[16,80,128]{2,1,0:T(8,128)(2,1)S(1)} custom-call(s32[4,16]{1,0:T(4,128)S(1)} %copy-done.5, f32[4,48,768]{2,1,0:T(8,128)S(1)} %all_to_all.10.parts, bf16[768,3072]{1,0:T(8,128)(2,1)S(1)} %bitcast.13), custom_call_target="tpu_custom_call" | custom-call | tf_op jit(solution)/shard_map/coarse_parts/pallas_call | solution.py:188
  142.0 26.9 %all_to_all.11.coded = s16[16,80,128]{2,1,0:T(8,128)(2,1)S(1)} all-to-all(s16[16,80,128]{2,1,0:T(8,128)(2,1)S(1)} %coarse_parts.1), channel_id=1, replica_groups=mesh['zh'=4,'zl'=4,'x'=4,'yh'=4,'core'=2,'yl'=2] {'zh','zl'}, dimensions={0} | all-to-all | bytes 655360 | tf_op jit(solution)/shard_map/all_to_all | solution.py:282
  168.9 0.7 summed.1
  (24 shorter events, 0.8 us)
Async XLA Ops:
  1.3 3.1 %copy-start = (bf16[768,384]{1,0:T(8,128)(2,1)S(1)}, bf16[768,384]{1,0:T(8,128)(2,1)}, u32[]{:S(2)}) copy-start(bf16[768,384]{1,0:T(8,128)(2,1)} %tiles.1) | copy-start | bytes 1769476
  4.4 134.2 %slice-start = ((s8[4718592]{0:T(1024)(128)(4,1)}), s8[524288]{0:T(1024)(128)(4,1)S(1)}, s32[]{:S(2)}) async-start(s8[4718592]{0:T(1024)(128)(4,1)} %bitcast.12), calls=%async_computation.2 | async-start | bytes 1048576
  4.4 134.2 %copy-start.5 = (s32[4,16]{1,0:T(4,128)S(1)}, s32[4,16]{1,0:T(4,128)}, u32[]{:S(2)}) copy-start(s32[4,16]{1,0:T(4,128)} %mask.4) | copy-start | bytes 772
  5.1 54.1 %collective-permute-start.4 = (bf16[768,384]{1,0:T(8,128)(2,1)S(1)}, bf16[768,384]{1,0:T(8,128)(2,1)S(1)}, u32[]{:S(2)}, u32[]{:S(2)}) collective-permute-start(bf16[768,384]{1,0:T(8,128)(2,1)S(1)} %masked_tiles.1.refs_0_), channel_id=1, source_target_pairs={{0,2},{2,0},{1,3},{3,1},{4,6},{6,4},{5,7},{7,5},{8,10},{10,8},{9,1... | collective-permute-start | bytes 1769480 | tf_op jit(solution)/shard_map/ppermute | solution.py:263
  7.0 52.1 %collective-permute-start.3 = (bf16[768,384]{1,0:T(8,128)(2,1)S(1)}, bf16[768,384]{1,0:T(8,128)(2,1)S(1)}, u32[]{:S(2)}, u32[]{:S(2)}) collective-permute-start(bf16[768,384]{1,0:T(8,128)(2,1)S(1)} %masked_tiles.1.refs_0_), channel_id=1, source_target_pairs={{4,0},{6,2},{13,1},{15,3},{8,4},{10,6},{1,5},{3,7},{12,8},{14,10},... | collective-permute-start | bytes 1769480 | tf_op jit(solution)/shard_map/ppermute | solution.py:262
  13.2 46.0 %collective-permute-start.2 = (bf16[768,384]{1,0:T(8,128)(2,1)S(1)}, bf16[768,384]{1,0:T(8,128)(2,1)S(1)}, u32[]{:S(2)}, u32[]{:S(2)}) collective-permute-start(bf16[768,384]{1,0:T(8,128)(2,1)S(1)} %masked_tiles.1.refs_0_), channel_id=1, source_target_pairs={{13,0},{15,2},{4,1},{6,3},{1,4},{3,6},{8,5},{10,7},{5,8},{7,10},{1... | collective-permute-start | bytes 1769480 | tf_op jit(solution)/shard_map/ppermute | solution.py:262
  15.1 35.6 %collective-permute-start.1 = (bf16[2,48,768]{2,1,0:T(8,128)(2,1)}, bf16[2,48,768]{2,1,0:T(8,128)(2,1)S(1)}, u32[]{:S(2)}, u32[]{:S(2)}) collective-permute-start(bf16[2,48,768]{2,1,0:T(8,128)(2,1)} %two_slices.1), channel_id=1, source_target_pairs={{0,640},{16,896},{32,128},{48,384},{64,704},{80,960},{96,192},{112... | collective-permute-start | bytes 442376 | tf_op jit(solution)/shard_map/ppermute | solution.py:259
  29.6 28.8 %collective-permute-start = (bf16[2,48,768]{2,1,0:T(8,128)(2,1)}, bf16[2,48,768]{2,1,0:T(8,128)(2,1)S(1)}, u32[]{:S(2)}, u32[]{:S(2)}) collective-permute-start(bf16[2,48,768]{2,1,0:T(8,128)(2,1)} %two_slices.1), channel_id=1, source_target_pairs={{0,128},{16,384},{32,640},{48,896},{64,192},{80,448},{96,704},{112... | collective-permute-start | bytes 442376 | tf_op jit(solution)/shard_map/ppermute | solution.py:259
  59.1 30.6 %collective-permute-start.9 = (bf16[768,384]{1,0:T(8,128)(2,1)S(1)}, bf16[768,384]{1,0:T(8,128)(2,1)S(1)}, u32[]{:S(2)}, u32[]{:S(2)}) collective-permute-start(bf16[768,384]{1,0:T(8,128)(2,1)S(1)} %masked_tiles.1.refs_0_), channel_id=1, source_target_pairs={{9,0},{11,2},{8,1},{10,3},{13,4},{15,6},{12,5},{14,7},{1,8},{3,10}... | collective-permute-start | bytes 1769480 | tf_op jit(solution)/shard_map/ppermute | solution.py:271
  64.4 56.2 %collective-permute-start.10 = (bf16[768,384]{1,0:T(8,128)(2,1)S(1)}, bf16[768,384]{1,0:T(8,128)(2,1)}, u32[]{:S(2)}, u32[]{:S(2)}) collective-permute-start(bf16[768,384]{1,0:T(8,128)(2,1)S(1)} %collective-permute-done.2.refs_1_), channel_id=1, source_target_pairs={{0,2},{2,0},{1,3},{3,1},{4,6},{6,4},{5,7},{7,5},{8,10},{10,8},{9,1... | collective-permute-start | bytes 1769480 | tf_op jit(solution)/shard_map/ppermute | solution.py:272
  66.3 54.2 %collective-permute-start.11 = (bf16[768,384]{1,0:T(8,128)(2,1)S(1)}, bf16[768,384]{1,0:T(8,128)(2,1)}, u32[]{:S(2)}, u32[]{:S(2)}) collective-permute-start(bf16[768,384]{1,0:T(8,128)(2,1)S(1)} %collective-permute-done.3.refs_2_), channel_id=1, source_target_pairs={{0,2},{2,0},{1,3},{3,1},{4,6},{6,4},{5,7},{7,5},{8,10},{10,8},{9,1... | collective-permute-start | bytes 1769480 | tf_op jit(solution)/shard_map/ppermute | solution.py:272
  89.7 30.8 %collective-permute-start.12 = (bf16[768,384]{1,0:T(8,128)(2,1)S(1)}, bf16[768,384]{1,0:T(8,128)(2,1)}, u32[]{:S(2)}, u32[]{:S(2)}) collective-permute-start(bf16[768,384]{1,0:T(8,128)(2,1)S(1)} %collective-permute-done.9.refs_3_), channel_id=1, source_target_pairs={{0,2},{2,0},{1,3},{3,1},{4,6},{6,4},{5,7},{7,5},{8,10},{10,8},{9,1... | collective-permute-start | bytes 1769480 | tf_op jit(solution)/shard_map/ppermute | solution.py:272
  91.6 9.1 %collective-permute-start.7 = (bf16[2,48,768]{2,1,0:T(8,128)(2,1)S(1)}, bf16[2,48,768]{2,1,0:T(8,128)(2,1)S(1)}, u32[]{:S(2)}, u32[]{:S(2)}) collective-permute-start(bf16[2,48,768]{2,1,0:T(8,128)(2,1)S(1)} %get-tuple-element.21), channel_id=1, source_target_pairs={{128,0},{192,64},{256,128},{320,192},{384,256},{448,320},{512,384}... | collective-permute-start | bytes 442376 | tf_op jit(solution)/shard_map/ppermute | solution.py:270
  93.6 15.5 %collective-permute-start.8 = (bf16[2,48,768]{2,1,0:T(8,128)(2,1)S(1)}, bf16[2,48,768]{2,1,0:T(8,128)(2,1)S(1)}, u32[]{:S(2)}, u32[]{:S(2)}) collective-permute-start(bf16[2,48,768]{2,1,0:T(8,128)(2,1)S(1)} %get-tuple-element.22), channel_id=1, source_target_pairs={{896,0},{960,64},{0,128},{64,192},{128,256},{192,320},{256,384},{3... | collective-permute-start | bytes 442376 | tf_op jit(solution)/shard_map/ppermute | solution.py:270
  100.8 0.7 copy-start.1
  101.5 15.2 %collective-permute-start.6 = (bf16[4,48,768]{2,1,0:T(8,128)(2,1)}, bf16[4,48,768]{2,1,0:T(8,128)(2,1)}, u32[]{:S(2)}, u32[]{:S(2)}) collective-permute-start(bf16[4,48,768]{2,1,0:T(8,128)(2,1)} %get-tuple-element.20.slab), channel_id=1, source_target_pairs={{960,0},{0,64},{64,128},{128,192},{192,256},{256,320},{320,384},{3... | collective-permute-start | bytes 884744 | tf_op jit(solution)/shard_map/ppermute | solution.py:269
  109.1 0.7 copy-start.3
  109.7 10.8 %collective-permute-start.5 = (bf16[4,48,768]{2,1,0:T(8,128)(2,1)}, bf16[4,48,768]{2,1,0:T(8,128)(2,1)}, u32[]{:S(2)}, u32[]{:S(2)}) collective-permute-start(bf16[4,48,768]{2,1,0:T(8,128)(2,1)} %get-tuple-element.20.slab), channel_id=1, source_target_pairs={{64,0},{128,64},{192,128},{256,192},{320,256},{384,320},{448,384},... | collective-permute-start | bytes 884744 | tf_op jit(solution)/shard_map/ppermute | solution.py:269
  111.9 26.8 %slice-start.1 = ((s8[4718592]{0:T(1024)(128)(4,1)}), s8[4194304]{0:T(1024)(128)(4,1)S(1)}, s32[]{:S(2)}) async-start(s8[4718592]{0:T(1024)(128)(4,1)} %bitcast.12), calls=%async_computation.3 | async-start | bytes 8388608
  120.5 0.9 copy-start.2
  121.4 0.9 copy-start.4

commit v3 on v2

--- a/solution.py
+++ b/solution.py
@@ -259,20 +259,17 @@
     near, far = [lax.ppermute(mine, z + ("x",), swapped(turn)) for turn in (0, 2)]
     a_tiles, mine = lax.optimization_barrier((a_tiles, mine))
     own = masked(a_tiles, a_mask, HALF)
-    first, second = [lax.ppermute(own, ys, along_y(near_by)) for near_by in (1, -2)]
-    other = [lax.ppermute(own, "core", SWAP)]
+    blocks = [own] + [lax.ppermute(own, ys, along_y(near_by)) for near_by in (1, -2, 3)]
 
     slab, lower, upper = collect(near, far, zh)
-    slab, lower, upper, own, first, second, other = lax.optimization_barrier(
-        (slab, lower, upper, own, first, second, other)
-    )
-    slabs = [slab, lax.ppermute(slab, z, around(1)), lax.ppermute(slab, z, around(-1))]
-    slabs += [lax.ppermute(lower, z, around(2)), lax.ppermute(upper, z, around(-2))]
-    third = lax.ppermute(own, ys, along_y(3))
-    other += [lax.ppermute(block, "core", SWAP) for block in (first, second, third)]
+    slab, lower, upper, blocks = lax.optimization_barrier((slab, lower, upper, blocks))
+    beside = [lax.ppermute(slab, z, around(1)), lax.ppermute(slab, z, around(-1))]
+    halves = [lax.ppermute(lower, z, around(2)), lax.ppermute(upper, z, around(-2))]
+    halves, blocks = lax.optimization_barrier((halves, blocks))
+    blocks += [lax.ppermute(block, "core", SWAP) for block in blocks]
+    slabs = [slab] + beside + halves
 
     sign = 2 * yl - 1
-    blocks = [own, first, second, third] + other
     planes = [yh, yh + sign, yh - sign, yh + 2]
     planes = jnp.stack(planes + planes) % 4
     halves = jnp.stack([core] * 4 + [1 - core] * 4)

time: 172 us -> 163 us (0.948)
  waiting for transfers between devices: 51.4 us -> 35.4 us
  starting transfers between devices: 61.7 us -> 72.8 us
  blocking collectives: 39.8 us -> 34.4 us
    ppermute x5 -> x4, waiting for transfers between devices: 21 us -> 0.01 us  [local(): blocks += [lax.ppermute(block, 'core', SWAP) for block in blocks]]
    ppermute x1, starting transfers between devices: 1.92 us -> 18.2 us  [local(): lax.ppermute(lower, z, around(2))]
    ppermute x1, waiting for transfers between devices: 0.01 us -> 6.81 us  [local(): lax.ppermute(upper, z, around(-2))]
    ppermute x2 -> x3, starting transfers between devices: 8.09 us -> 14.8 us  [local(): lax.ppermute(own, ys, along_y(near_by))]
    ppermute x1, waiting for transfers between devices: 3.86 us -> 9 us  [local(): lax.ppermute(slab, z, around(1))]
    ppermute x1, waiting for transfers between devices: 4.77 us -> 0.01 us  [local(): lax.ppermute(slab, z, around(-1))]
    ppermute x5 -> x4, starting transfers between devices: 13.4 us -> 8.64 us  [local(): blocks += [lax.ppermute(block, 'core', SWAP) for block in blocks]]
    all_to_all x1, blocking collectives: 26.9 us -> 22.4 us  [local(): lax.all_to_all(coarse_parts(parts, p_tiles, p_mask), z, 0, 0, tiled=True)]
where the time goes in v3:
time: 163 us; the launch traced here: 161 us
  starting transfers between devices  72.8 us (45%)
  waiting for transfers between devices  35.4 us (22%)
  blocking collectives  34.4 us (21%)
  Pallas kernels  11.9 us (7%)
  local copies, waits for them, and re-layouts  5.76 us (4%)
    ppermute x2, starting transfers between devices, local(): lax.ppermute(mine, z + ('x',), swapped(turn))  23.9 us
    all_to_all x1, blocking collectives, local(): lax.all_to_all(coarse_parts(parts, p_tiles, p_mask), z, 0, 0, tiled=True)  22.4 us
    ppermute x1, starting transfers between devices, local(): lax.ppermute(lower, z, around(2))  18.2 us
    ppermute x2, waiting for transfers between devices, local(): lax.ppermute(mine, z + ('x',), swapped(turn))  18.1 us
    ppermute x3, starting transfers between devices, local(): lax.ppermute(own, ys, along_y(near_by))  14.8 us
    all_to_all x1, blocking collectives, local(): parts = lax.all_to_all(product(slabs, blocks, place), 'x', 0, 0, tiled=True)  12 us
    ppermute x1, waiting for transfers between devices, local(): lax.ppermute(slab, z, around(1))  9 us
    ppermute x4, starting transfers between devices, local(): blocks += [lax.ppermute(block, 'core', SWAP) for block in blocks]  8.64 us
  transfers between devices with their start and end apart: 13, of which 6 were waited for; matrix products, arithmetic and copies ran while one was open for 0% of the time, Pallas kernels for 0%

profile of v3, /device:TPU:6, one launch (start us, length us, event | category | flops | bytes accessed | tf_op | source)
XLA Modules:
  0.0 161.1 jit_solution(16315834837037269197)
XLA Ops:
  0.0 0.8 copy.5.mask
  1.4 3.1 %two_slices.1 = bf16[2,48,768]{2,1,0:T(8,128)(2,1)} custom-call(s32[3]{0:T(128)} %pad_add_fusion.place, s32[4,16]{1,0:T(4,128)} %mask.4, bf16[768,3072]{1,0:T(8,128)(2,1)} %tiles.2, bf16[768,3072]{1,0:T(8,128)(2,1)} %tiles.2, bf16[768,3072]{1,0:T(8,128)(2,1)} %tiles.2, bf16[768,3072]{1,0:T(8,128)(2,1)} %tiles.2), custom_call_target="tpu_custom_call" | custom-call | tf_op jit(solution)/shard_map/two_slices/pallas_call | solution.py:59
  5.1 7.0 %collective-permute-start.4 = (bf16[768,384]{1,0:T(8,128)(2,1)S(1)}, bf16[768,384]{1,0:T(8,128)(2,1)S(1)}, u32[]{:S(2)}, u32[]{:S(2)}) collective-permute-start(bf16[768,384]{1,0:T(8,128)(2,1)S(1)} %masked_tiles.1.refs_0_), channel_id=1, source_target_pairs={{9,0},{11,2},{8,1},{10,3},{13,4},{15,6},{12,5},{14,7},{1,8},{3,10}... | collective-permute-start | bytes 1769480 | tf_op jit(solution)/shard_map/ppermute | solution.py:262
  12.1 3.1 %collective-permute-start.3 = (bf16[768,384]{1,0:T(8,128)(2,1)S(1)}, bf16[768,384]{1,0:T(8,128)(2,1)S(1)}, u32[]{:S(2)}, u32[]{:S(2)}) collective-permute-start(bf16[768,384]{1,0:T(8,128)(2,1)S(1)} %masked_tiles.1.refs_0_), channel_id=1, source_target_pairs={{4,0},{6,2},{13,1},{15,3},{8,4},{10,6},{1,5},{3,7},{12,8},{14,10},... | collective-permute-start | bytes 1769480 | tf_op jit(solution)/shard_map/ppermute | solution.py:262
  15.2 4.7 %collective-permute-start.2 = (bf16[768,384]{1,0:T(8,128)(2,1)S(1)}, bf16[768,384]{1,0:T(8,128)(2,1)S(1)}, u32[]{:S(2)}, u32[]{:S(2)}) collective-permute-start(bf16[768,384]{1,0:T(8,128)(2,1)S(1)} %masked_tiles.1.refs_0_), channel_id=1, source_target_pairs={{13,0},{15,2},{4,1},{6,3},{1,4},{3,6},{8,5},{10,7},{5,8},{7,10},{1... | collective-permute-start | bytes 1769480 | tf_op jit(solution)/shard_map/ppermute | solution.py:262
  19.9 14.5 %collective-permute-start.1 = (bf16[2,48,768]{2,1,0:T(8,128)(2,1)}, bf16[2,48,768]{2,1,0:T(8,128)(2,1)S(1)}, u32[]{:S(2)}, u32[]{:S(2)}) collective-permute-start(bf16[2,48,768]{2,1,0:T(8,128)(2,1)} %two_slices.1), channel_id=1, source_target_pairs={{0,640},{16,896},{32,128},{48,384},{64,704},{80,960},{96,192},{112... | collective-permute-start | bytes 442376 | tf_op jit(solution)/shard_map/ppermute | solution.py:259
  34.4 9.5 %collective-permute-start = (bf16[2,48,768]{2,1,0:T(8,128)(2,1)}, bf16[2,48,768]{2,1,0:T(8,128)(2,1)S(1)}, u32[]{:S(2)}, u32[]{:S(2)}) collective-permute-start(bf16[2,48,768]{2,1,0:T(8,128)(2,1)} %two_slices.1), channel_id=1, source_target_pairs={{0,128},{16,384},{32,640},{48,896},{64,192},{80,448},{96,704},{112... | collective-permute-start | bytes 442376 | tf_op jit(solution)/shard_map/ppermute | solution.py:259
  43.9 10.4 %collective-permute-done.1.far = bf16[2,48,768]{2,1,0:T(8,128)(2,1)S(1)} collective-permute-done((bf16[2,48,768]{2,1,0:T(8,128)(2,1)}, bf16[2,48,768]{2,1,0:T(8,128)(2,1)S(1)}, u32[]{:S(2)}, u32[]{:S(2)}) %collective-permute-start.1) | collective-permute-done | bytes 147488 | tf_op jit(solution)/shard_map/ppermute | solution.py:259
  54.3 7.6 %collective-permute-done.near = bf16[2,48,768]{2,1,0:T(8,128)(2,1)S(1)} collective-permute-done((bf16[2,48,768]{2,1,0:T(8,128)(2,1)}, bf16[2,48,768]{2,1,0:T(8,128)(2,1)S(1)}, u32[]{:S(2)}, u32[]{:S(2)}) %collective-permute-start) | collective-permute-done | bytes 147488 | tf_op jit(solution)/shard_map/ppermute | solution.py:259
  62.0 0.7 collect.1
  63.2 18.2 %collective-permute-start.7 = (bf16[2,48,768]{2,1,0:T(8,128)(2,1)S(1)}, bf16[2,48,768]{2,1,0:T(8,128)(2,1)S(1)}, u32[]{:S(2)}, u32[]{:S(2)}) collective-permute-start(bf16[2,48,768]{2,1,0:T(8,128)(2,1)S(1)} %get-tuple-element.27), channel_id=1, source_target_pairs={{128,0},{192,64},{256,128},{320,192},{384,256},{448,320},{512,384}... | collective-permute-start | bytes 442376 | tf_op jit(solution)/shard_map/ppermute | solution.py:267
  81.5 1.9 %collective-permute-start.8 = (bf16[2,48,768]{2,1,0:T(8,128)(2,1)S(1)}, bf16[2,48,768]{2,1,0:T(8,128)(2,1)S(1)}, u32[]{:S(2)}, u32[]{:S(2)}) collective-permute-start(bf16[2,48,768]{2,1,0:T(8,128)(2,1)S(1)} %get-tuple-element.28), channel_id=1, source_target_pairs={{896,0},{960,64},{0,128},{64,192},{128,256},{192,320},{256,384},{3... | collective-permute-start | bytes 442376 | tf_op jit(solution)/shard_map/ppermute | solution.py:267
  83.4 3.4 %collective-permute-start.6 = (bf16[4,48,768]{2,1,0:T(8,128)(2,1)}, bf16[4,48,768]{2,1,0:T(8,128)(2,1)S(1)}, u32[]{:S(2)}, u32[]{:S(2)}) collective-permute-start(bf16[4,48,768]{2,1,0:T(8,128)(2,1)} %get-tuple-element.26.slab), channel_id=1, source_target_pairs={{960,0},{0,64},{64,128},{128,192},{192,256},{256,320},{320,384},{3... | collective-permute-start | bytes 884744 | tf_op jit(solution)/shard_map/ppermute | solution.py:266
  86.8 1.0 collective-permute-done.7.lower
  87.8 0.7 copy-done.3
  88.5 6.8 %collective-permute-done.8.upper = bf16[2,48,768]{2,1,0:T(8,128)(2,1)S(1)} collective-permute-done((bf16[2,48,768]{2,1,0:T(8,128)(2,1)S(1)}, bf16[2,48,768]{2,1,0:T(8,128)(2,1)S(1)}, u32[]{:S(2)}, u32[]{:S(2)}) %collective-permute-start.8) | collective-permute-done | bytes 147488 | tf_op jit(solution)/shard_map/ppermute | solution.py:267
  95.3 0.7 copy-done.5
  95.9 1.9 %collective-permute-start.9 = (bf16[768,384]{1,0:T(8,128)(2,1)S(1)}, bf16[768,384]{1,0:T(8,128)(2,1)S(1)}, u32[]{:S(2)}, u32[]{:S(2)}) collective-permute-start(bf16[768,384]{1,0:T(8,128)(2,1)S(1)} %masked_tiles.1.refs_0_), channel_id=1, source_target_pairs={{0,2},{2,0},{1,3},{3,1},{4,6},{6,4},{5,7},{7,5},{8,10},{10,8},{9,1... | collective-permute-start | bytes 1769480 | tf_op jit(solution)/shard_map/ppermute | solution.py:269
  97.9 2.4 %collective-permute-start.10 = (bf16[768,384]{1,0:T(8,128)(2,1)S(1)}, bf16[768,384]{1,0:T(8,128)(2,1)}, u32[]{:S(2)}, u32[]{:S(2)}) collective-permute-start(bf16[768,384]{1,0:T(8,128)(2,1)S(1)} %collective-permute-done.2.refs_1_), channel_id=1, source_target_pairs={{0,2},{2,0},{1,3},{3,1},{4,6},{6,4},{5,7},{7,5},{8,10},{10,8},{9,1... | collective-permute-start | bytes 1769480 | tf_op jit(solution)/shard_map/ppermute | solution.py:269
  100.3 1.9 %collective-permute-start.11 = (bf16[768,384]{1,0:T(8,128)(2,1)S(1)}, bf16[768,384]{1,0:T(8,128)(2,1)}, u32[]{:S(2)}, u32[]{:S(2)}) collective-permute-start(bf16[768,384]{1,0:T(8,128)(2,1)S(1)} %collective-permute-done.3.refs_2_), channel_id=1, source_target_pairs={{0,2},{2,0},{1,3},{3,1},{4,6},{6,4},{5,7},{7,5},{8,10},{10,8},{9,1... | collective-permute-start | bytes 1769480 | tf_op jit(solution)/shard_map/ppermute | solution.py:269
  102.2 2.4 %collective-permute-start.12 = (bf16[768,384]{1,0:T(8,128)(2,1)S(1)}, bf16[768,384]{1,0:T(8,128)(2,1)}, u32[]{:S(2)}, u32[]{:S(2)}) collective-permute-start(bf16[768,384]{1,0:T(8,128)(2,1)S(1)} %collective-permute-done.4.refs_3_), channel_id=1, source_target_pairs={{0,2},{2,0},{1,3},{3,1},{4,6},{6,4},{5,7},{7,5},{8,10},{10,8},{9,1... | collective-permute-start | bytes 1769480 | tf_op jit(solution)/shard_map/ppermute | solution.py:269
  104.6 0.7 copy-done.1
  105.3 1.9 %collective-permute-start.5 = (bf16[4,48,768]{2,1,0:T(8,128)(2,1)}, bf16[4,48,768]{2,1,0:T(8,128)(2,1)}, u32[]{:S(2)}, u32[]{:S(2)}) collective-permute-start(bf16[4,48,768]{2,1,0:T(8,128)(2,1)} %get-tuple-element.26.slab), channel_id=1, source_target_pairs={{64,0},{128,64},{192,128},{256,192},{320,256},{384,320},{448,384},... | collective-permute-start | bytes 884744 | tf_op jit(solution)/shard_map/ppermute | solution.py:266
  107.5 9.0 %collective-permute-done.5.above = bf16[4,48,768]{2,1,0:T(8,128)(2,1)} collective-permute-done((bf16[4,48,768]{2,1,0:T(8,128)(2,1)}, bf16[4,48,768]{2,1,0:T(8,128)(2,1)}, u32[]{:S(2)}, u32[]{:S(2)}) %collective-permute-start.5) | collective-permute-done | bytes 294944 | tf_op jit(solution)/shard_map/ppermute | solution.py:266
  116.5 1.0 copy-done.2
  117.5 0.9 copy-done.4
  118.4 0.9 copy-done.6
  119.3 3.3 %product.1 = f32[4,48,768]{2,1,0:T(8,128)S(1)} custom-call(s32[17]{0:T(128)S(1)} %concatenate.3.place, bf16[4,48,768]{2,1,0:T(8,128)(2,1)} %get-tuple-element.26.slab, bf16[4,48,768]{2,1,0:T(8,128)(2,1)} %collective-permute-done.5.above, bf16[4,48,768]{2,1,0:T(8,128)(2,1)S(1)} %copy-done.2, bf16[2,48,768]{2,1,0:T(8,128)(2,1)S(1)} %copy-done.4, ...), custom_call_target="tpu_custom_call" | custom-call | tf_op jit(solution)/shard_map/product/pallas_call | solution.py:143
  122.6 12.0 %all_to_all.10.parts = f32[4,48,768]{2,1,0:T(8,128)S(1)} all-to-all(f32[4,48,768]{2,1,0:T(8,128)S(1)} %product.1), channel_id=1, replica_groups=mesh['zh'=4,'zl'=4,'x'=4,'yh'=4,'core'=2,'yl'=2] {'x'}, dimensions={0} | all-to-all | bytes 1179648 | tf_op jit(solution)/shard_map/all_to_all | solution.py:278
  134.6 3.4 %coarse_parts.1 = s16[16,80,128]{2,1,0:T(8,128)(2,1)S(1)} custom-call(s32[4,16]{1,0:T(4,128)S(1)} %copy-done.7, f32[4,48,768]{2,1,0:T(8,128)S(1)} %all_to_all.10.parts, bf16[768,3072]{1,0:T(8,128)(2,1)S(1)} %bitcast.13), custom_call_target="tpu_custom_call" | custom-call | tf_op jit(solution)/shard_map/coarse_parts/pallas_call | solution.py:188
  138.0 22.4 %all_to_all.11.coded = s16[16,80,128]{2,1,0:T(8,128)(2,1)S(1)} all-to-all(s16[16,80,128]{2,1,0:T(8,128)(2,1)S(1)} %coarse_parts.1), channel_id=1, replica_groups=mesh['zh'=4,'zl'=4,'x'=4,'yh'=4,'core'=2,'yl'=2] {'zh','zl'}, dimensions={0} | all-to-all | bytes 655360 | tf_op jit(solution)/shard_map/all_to_all | solution.py:279
  160.4 0.7 summed.1
  (28 shorter events, 2.0 us)
Async XLA Ops:
  1.4 3.1 %copy-start = (bf16[768,384]{1,0:T(8,128)(2,1)S(1)}, bf16[768,384]{1,0:T(8,128)(2,1)}, u32[]{:S(2)}) copy-start(bf16[768,384]{1,0:T(8,128)(2,1)} %tiles.1) | copy-start | bytes 1769476
  4.5 130.1 %slice-start = ((s8[4718592]{0:T(1024)(128)(4,1)}), s8[524288]{0:T(1024)(128)(4,1)S(1)}, s32[]{:S(2)}) async-start(s8[4718592]{0:T(1024)(128)(4,1)} %bitcast.12), calls=%async_computation.2 | async-start | bytes 1048576
  4.5 130.1 %copy-start.7 = (s32[4,16]{1,0:T(4,128)S(1)}, s32[4,16]{1,0:T(4,128)}, u32[]{:S(2)}) copy-start(s32[4,16]{1,0:T(4,128)} %mask.4) | copy-start | bytes 772
  5.1 57.6 %collective-permute-start.4 = (bf16[768,384]{1,0:T(8,128)(2,1)S(1)}, bf16[768,384]{1,0:T(8,128)(2,1)S(1)}, u32[]{:S(2)}, u32[]{:S(2)}) collective-permute-start(bf16[768,384]{1,0:T(8,128)(2,1)S(1)} %masked_tiles.1.refs_0_), channel_id=1, source_target_pairs={{9,0},{11,2},{8,1},{10,3},{13,4},{15,6},{12,5},{14,7},{1,8},{3,10}... | collective-permute-start | bytes 1769480 | tf_op jit(solution)/shard_map/ppermute | solution.py:262
  12.1 50.6 %collective-permute-start.3 = (bf16[768,384]{1,0:T(8,128)(2,1)S(1)}, bf16[768,384]{1,0:T(8,128)(2,1)S(1)}, u32[]{:S(2)}, u32[]{:S(2)}) collective-permute-start(bf16[768,384]{1,0:T(8,128)(2,1)S(1)} %masked_tiles.1.refs_0_), channel_id=1, source_target_pairs={{4,0},{6,2},{13,1},{15,3},{8,4},{10,6},{1,5},{3,7},{12,8},{14,10},... | collective-permute-start | bytes 1769480 | tf_op jit(solution)/shard_map/ppermute | solution.py:262
  15.2 48.0 %collective-permute-start.2 = (bf16[768,384]{1,0:T(8,128)(2,1)S(1)}, bf16[768,384]{1,0:T(8,128)(2,1)S(1)}, u32[]{:S(2)}, u32[]{:S(2)}) collective-permute-start(bf16[768,384]{1,0:T(8,128)(2,1)S(1)} %masked_tiles.1.refs_0_), channel_id=1, source_target_pairs={{13,0},{15,2},{4,1},{6,3},{1,4},{3,6},{8,5},{10,7},{5,8},{7,10},{1... | collective-permute-start | bytes 1769480 | tf_op jit(solution)/shard_map/ppermute | solution.py:262
  19.9 34.4 %collective-permute-start.1 = (bf16[2,48,768]{2,1,0:T(8,128)(2,1)}, bf16[2,48,768]{2,1,0:T(8,128)(2,1)S(1)}, u32[]{:S(2)}, u32[]{:S(2)}) collective-permute-start(bf16[2,48,768]{2,1,0:T(8,128)(2,1)} %two_slices.1), channel_id=1, source_target_pairs={{0,640},{16,896},{32,128},{48,384},{64,704},{80,960},{96,192},{112... | collective-permute-start | bytes 442376 | tf_op jit(solution)/shard_map/ppermute | solution.py:259
  34.4 27.6 %collective-permute-start = (bf16[2,48,768]{2,1,0:T(8,128)(2,1)}, bf16[2,48,768]{2,1,0:T(8,128)(2,1)S(1)}, u32[]{:S(2)}, u32[]{:S(2)}) collective-permute-start(bf16[2,48,768]{2,1,0:T(8,128)(2,1)} %two_slices.1), channel_id=1, source_target_pairs={{0,128},{16,384},{32,640},{48,896},{64,192},{80,448},{96,704},{112... | collective-permute-start | bytes 442376 | tf_op jit(solution)/shard_map/ppermute | solution.py:259
  63.2 24.6 %collective-permute-start.7 = (bf16[2,48,768]{2,1,0:T(8,128)(2,1)S(1)}, bf16[2,48,768]{2,1,0:T(8,128)(2,1)S(1)}, u32[]{:S(2)}, u32[]{:S(2)}) collective-permute-start(bf16[2,48,768]{2,1,0:T(8,128)(2,1)S(1)} %get-tuple-element.27), channel_id=1, source_target_pairs={{128,0},{192,64},{256,128},{320,192},{384,256},{448,320},{512,384}... | collective-permute-start | bytes 442376 | tf_op jit(solution)/shard_map/ppermute | solution.py:267
  81.5 13.8 %collective-permute-start.8 = (bf16[2,48,768]{2,1,0:T(8,128)(2,1)S(1)}, bf16[2,48,768]{2,1,0:T(8,128)(2,1)S(1)}, u32[]{:S(2)}, u32[]{:S(2)}) collective-permute-start(bf16[2,48,768]{2,1,0:T(8,128)(2,1)S(1)} %get-tuple-element.28), channel_id=1, source_target_pairs={{896,0},{960,64},{0,128},{64,192},{128,256},{192,320},{256,384},{3... | collective-permute-start | bytes 442376 | tf_op jit(solution)/shard_map/ppermute | solution.py:267
  83.4 21.2 %collective-permute-start.6 = (bf16[4,48,768]{2,1,0:T(8,128)(2,1)}, bf16[4,48,768]{2,1,0:T(8,128)(2,1)S(1)}, u32[]{:S(2)}, u32[]{:S(2)}) collective-permute-start(bf16[4,48,768]{2,1,0:T(8,128)(2,1)} %get-tuple-element.26.slab), channel_id=1, source_target_pairs={{960,0},{0,64},{64,128},{128,192},{192,256},{256,320},{320,384},{3... | collective-permute-start | bytes 884744 | tf_op jit(solution)/shard_map/ppermute | solution.py:266
  87.8 0.7 copy-start.3
  95.3 0.7 copy-start.5
  95.9 20.5 %collective-permute-start.9 = (bf16[768,384]{1,0:T(8,128)(2,1)S(1)}, bf16[768,384]{1,0:T(8,128)(2,1)S(1)}, u32[]{:S(2)}, u32[]{:S(2)}) collective-permute-start(bf16[768,384]{1,0:T(8,128)(2,1)S(1)} %masked_tiles.1.refs_0_), channel_id=1, source_target_pairs={{0,2},{2,0},{1,3},{3,1},{4,6},{6,4},{5,7},{7,5},{8,10},{10,8},{9,1... | collective-permute-start | bytes 1769480 | tf_op jit(solution)/shard_map/ppermute | solution.py:269
  97.9 18.6 %collective-permute-start.10 = (bf16[768,384]{1,0:T(8,128)(2,1)S(1)}, bf16[768,384]{1,0:T(8,128)(2,1)}, u32[]{:S(2)}, u32[]{:S(2)}) collective-permute-start(bf16[768,384]{1,0:T(8,128)(2,1)S(1)} %collective-permute-done.2.refs_1_), channel_id=1, source_target_pairs={{0,2},{2,0},{1,3},{3,1},{4,6},{6,4},{5,7},{7,5},{8,10},{10,8},{9,1... | collective-permute-start | bytes 1769480 | tf_op jit(solution)/shard_map/ppermute | solution.py:269
  100.3 16.2 %collective-permute-start.11 = (bf16[768,384]{1,0:T(8,128)(2,1)S(1)}, bf16[768,384]{1,0:T(8,128)(2,1)}, u32[]{:S(2)}, u32[]{:S(2)}) collective-permute-start(bf16[768,384]{1,0:T(8,128)(2,1)S(1)} %collective-permute-done.3.refs_2_), channel_id=1, source_target_pairs={{0,2},{2,0},{1,3},{3,1},{4,6},{6,4},{5,7},{7,5},{8,10},{10,8},{9,1... | collective-permute-start | bytes 1769480 | tf_op jit(solution)/shard_map/ppermute | solution.py:269
  102.2 14.3 %collective-permute-start.12 = (bf16[768,384]{1,0:T(8,128)(2,1)S(1)}, bf16[768,384]{1,0:T(8,128)(2,1)}, u32[]{:S(2)}, u32[]{:S(2)}) collective-permute-start(bf16[768,384]{1,0:T(8,128)(2,1)S(1)} %collective-permute-done.4.refs_3_), channel_id=1, source_target_pairs={{0,2},{2,0},{1,3},{3,1},{4,6},{6,4},{5,7},{7,5},{8,10},{10,8},{9,1... | collective-permute-start | bytes 1769480 | tf_op jit(solution)/shard_map/ppermute | solution.py:269
  104.6 0.7 copy-start.1
  105.3 11.1 %collective-permute-start.5 = (bf16[4,48,768]{2,1,0:T(8,128)(2,1)}, bf16[4,48,768]{2,1,0:T(8,128)(2,1)}, u32[]{:S(2)}, u32[]{:S(2)}) collective-permute-start(bf16[4,48,768]{2,1,0:T(8,128)(2,1)} %get-tuple-element.26.slab), channel_id=1, source_target_pairs={{64,0},{128,64},{192,128},{256,192},{320,256},{384,320},{448,384},... | collective-permute-start | bytes 884744 | tf_op jit(solution)/shard_map/ppermute | solution.py:266
  107.5 27.1 %slice-start.1 = ((s8[4718592]{0:T(1024)(128)(4,1)}), s8[4194304]{0:T(1024)(128)(4,1)S(1)}, s32[]{:S(2)}) async-start(s8[4718592]{0:T(1024)(128)(4,1)} %bitcast.12), calls=%async_computation.3 | async-start | bytes 8388608
  116.5 1.0 copy-start.2
  117.5 0.9 copy-start.4
  118.4 0.9 copy-start.6

commit v4 on v3

v4 whole, which is shorter than its diff:
```python
import jax
import jax.numpy as jnp
from jax import lax
from jax.experimental import pallas as pl
from jax.experimental.pallas import tpu as pltpu
from jax.sharding import Mesh
from jax.sharding import PartitionSpec as P

TILE = 192
WIDE = 48
ROWS = 768
HALF = 384
COARSE = 3072
PLANES = 16
LIMIT = 32766.0
STEPS = 128.0
LEAST = 1e-33
CODED = 80
VMEM = 48 * 1024 * 1024
MOST_VMEM = 62 * 1024 * 1024
F32 = jnp.float32
BF16 = jnp.bfloat16


def params():
    return pltpu.CompilerParams(vmem_limit_bytes=VMEM)


def dot_last(left, right):
    return lax.dot_general(left, right, (((1,), (1,)), ((), ())), preferred_element_type=F32)


def stripes_kernel(place, mask, window, out):
    core, tile, yl = place[0], 2 * place[1], place[2]
    row = lax.broadcasted_iota(jnp.int32, (WIDE, HALF), 0)
    lane = lax.broadcasted_iota(jnp.int32, (WIDE, HALF), 1)
    picks = [(lane == row + (2 * s + yl) * WIDE).astype(F32).astype(BF16) for s in range(4)]
    picked = dot_last(jnp.concatenate(picks, axis=0), window[...])
    fine = lax.broadcasted_iota(jnp.int32, (1, HALF), 1)
    for n in range(2):
        upper, lower = mask[2 * core, tile + n], mask[2 * core + 1, tile + n]
        present = jnp.where(fine < TILE, upper.astype(F32), lower.astype(F32))
        rows = slice(2 * WIDE * n, 2 * WIDE * (n + 1))
        out[rows, :] = (picked[rows] * present).astype(BF16)


def stripes(p_tiles, p_mask, core, half, yl):
    place = jnp.stack([core, half, yl]).astype(jnp.int32)
    return pl.pallas_call(
        stripes_kernel,
        out_shape=jax.ShapeDtypeStruct((4 * WIDE, HALF), BF16),
        grid_spec=pltpu.PrefetchScalarGridSpec(
            num_scalar_prefetch=2,
            grid=(1,),
            in_specs=[pl.BlockSpec((HALF, HALF), lambda g, place, mask: (place[0], place[1]))],
            out_specs=pl.BlockSpec((4 * WIDE, HALF), lambda g, place, mask: (0, 0)),
        ),
        compiler_params=pltpu.CompilerParams(vmem_limit_bytes=MOST_VMEM),
        name="stripes",
    )(place, p_mask, p_tiles)


def mask_rows(mask, tiles, out, first):
    width = tiles.shape[1]
    lane = lax.broadcasted_iota(jnp.int32, (1, width), 1)
    for i in range(ROWS // TILE):
        present = jnp.zeros((1, width), F32)
        for k in range(width // TILE):
            inside = (lane >= k * TILE) & (lane < (k + 1) * TILE)
            present = jnp.where(inside, mask(i, first + k).astype(F32), present)
        rows = slice(i * TILE, (i + 1) * TILE)
        out[rows, :] = tiles[rows, :] * present.astype(BF16)


def operator_kernel(mask, tiles, out):
    mask_rows(lambda i, k: mask[k, i], tiles, out, 0)


def masked_operator(a_tiles, a_mask):
    return pl.pallas_call(
        operator_kernel,
        out_shape=jax.ShapeDtypeStruct(a_tiles.shape, BF16),
        in_specs=[pl.BlockSpec(memory_space=pltpu.SMEM), pl.BlockSpec(memory_space=pltpu.VMEM)],
        out_specs=pl.BlockSpec(memory_space=pltpu.VMEM),
        compiler_params=params(),
        name="masked_operator",
    )(a_mask.T, a_tiles)


def collect_kernel(place, near, far, whole, lower, upper):
    @pl.when(place[0] < 2)
    def _():
        lower[...], upper[...] = near[...], far[...]

    @pl.when(place[0] >= 2)
    def _():
        lower[...], upper[...] = far[...], near[...]

    whole[: 4 * WIDE], whole[4 * WIDE :] = lower[...], upper[...]


def collect(near, far, zh):
    return pl.pallas_call(
        collect_kernel,
        out_shape=[jax.ShapeDtypeStruct((n * WIDE, HALF), BF16) for n in (8, 4, 4)],
        in_specs=[pl.BlockSpec(memory_space=pltpu.SMEM)]
        + [pl.BlockSpec(memory_space=pltpu.VMEM)] * 2,
        out_specs=[pl.BlockSpec(memory_space=pltpu.VMEM)] * 3,
        compiler_params=params(),
        name="collect",
    )(zh.reshape(1).astype(jnp.int32), near, far)


def product_kernel(place, slab, above, below, lower, upper, own, after, before, across, out, columns):
    zl, x, core = place[0], place[1], place[2]
    for y in range(4):
        rows = pl.ds(pl.multiple_of((2 * y + core) * WIDE, WIDE), WIDE)
        half = pl.ds(pl.multiple_of((2 * (y % 2) + core) * WIDE, WIDE), WIDE)
        into = slice(y * WIDE, (y + 1) * WIDE)
        columns[zl, into] = slab[rows, :]
        columns[(zl + 1) % 4, into] = above[rows, :]
        columns[(zl + 3) % 4, into] = below[rows, :]
        columns[(zl + 2) % 4, into] = (lower if y < 2 else upper)[half, :]
    total = dot_last(columns[x], own[...]) + dot_last(columns[(x + 1) % 4], after[...])
    total = total + dot_last(columns[(x + 3) % 4], before[...])
    total = total + dot_last(columns[(x + 2) % 4], across[...])
    out[...] = total.reshape(4, WIDE, ROWS)


def product(slabs, blocks, zl, x, core):
    place = jnp.stack([zl, x, core]).astype(jnp.int32)
    return pl.pallas_call(
        product_kernel,
        out_shape=jax.ShapeDtypeStruct((4, WIDE, ROWS), F32),
        in_specs=[pl.BlockSpec(memory_space=pltpu.SMEM)]
        + [pl.BlockSpec(memory_space=pltpu.VMEM)] * (len(slabs) + len(blocks)),
        out_specs=pl.BlockSpec(memory_space=pltpu.VMEM),
        scratch_shapes=[pltpu.VMEM((4, 4 * WIDE, HALF), BF16)],
        compiler_params=params(),
        name="product",
    )(place, *slabs, *blocks)


def scale_code(most):
    return jnp.ceil(jnp.log2(jnp.maximum(most, LEAST)) * STEPS) + 1.0


def encode_kernel(mine, theirs, out):
    lane = lax.broadcasted_iota(jnp.int32, (WIDE, 128), 1)
    for n in range(4):
        codes = jnp.zeros((WIDE, 128), F32)
        for g in range(ROWS // 128):
            lanes = slice(g * 128, (g + 1) * 128)
            values = mine[n, :, lanes] + theirs[n, :, lanes]
            code = scale_code(jnp.max(jnp.abs(values), axis=1, keepdims=True))
            values = jnp.round(values * (LIMIT * jnp.exp2(code * (-1.0 / STEPS))))
            out[n, :, lanes] = values.astype(jnp.int32).astype(jnp.int16)
            codes = jnp.where(lane == g, code, codes)
        out[n, :, ROWS:] = codes.astype(jnp.int32).astype(jnp.int16)


def encode(mine, theirs):
    return pl.pallas_call(
        encode_kernel,
        out_shape=jax.ShapeDtypeStruct((4, WIDE, ROWS + 128), jnp.int16),
        in_specs=[pl.BlockSpec(memory_space=pltpu.VMEM)] * 2,
        out_specs=pl.BlockSpec(memory_space=pltpu.VMEM),
        compiler_params=params(),
        name="encode",
    )(mine, theirs)


def decoded_sum(coded):
    groups = []
    scales = [
        jnp.exp2(coded[n, :, ROWS:].astype(jnp.int32).astype(F32) * (1.0 / STEPS)) * (1.0 / LIMIT)
        for n in range(4)
    ]
    for g in range(ROWS // 128):
        lanes = slice(g * 128, (g + 1) * 128)
        terms = [
            coded[n, :, lanes].astype(jnp.int32).astype(F32) * scales[n][:, g : g + 1]
            for n in range(4)
        ]
        groups.append((terms[0] + terms[1]) + (terms[2] + terms[3]))
    return jnp.concatenate(groups, axis=1)


def pack(values):
    tail = values[:, 128:]
    return jnp.concatenate(
        [values[:, :128], jnp.concatenate([tail[:24], tail[24:]], axis=1)], axis=0
    )


def coarse_kernel(mask, parts, tiles, out, terms, present):
    @pl.when(pl.program_id(0) == 0)
    def _():
        whole = decoded_sum(parts)
        high = whole.astype(BF16)
        rest = whole - high.astype(F32)
        middle = rest.astype(BF16)
        low = (rest - middle.astype(F32)).astype(BF16)
        terms[...] = jnp.concatenate([high, middle, low], axis=0)

    first = pl.program_id(0) * (tiles.shape[1] // TILE)
    mask_rows(lambda i, k: mask[i, k], tiles, present, first)
    full = jnp.dot(terms[...], present[...], preferred_element_type=F32)
    full = (full[2 * WIDE :] + full[WIDE : 2 * WIDE]) + full[:WIDE]
    for k in range(out.shape[0]):
        chunk = full[:, k * TILE : (k + 1) * TILE]
        code = scale_code(jnp.max(jnp.abs(chunk), axis=0, keepdims=True))
        factor = LIMIT * jnp.exp2(code * (-1.0 / STEPS))
        values = pack(jnp.round(chunk * factor))
        scales = pack(jnp.broadcast_to(code, (WIDE, TILE)))
        coded = jnp.concatenate([values, scales[:1], scales[48:49], jnp.zeros((6, 128), F32)], axis=0)
        out[k] = coded.astype(jnp.int32).astype(jnp.int16)


def coarse_parts(parts, p_tiles, p_mask):
    width = COARSE // 4
    return pl.pallas_call(
        coarse_kernel,
        out_shape=jax.ShapeDtypeStruct((PLANES, CODED, 128), jnp.int16),
        grid_spec=pltpu.PrefetchScalarGridSpec(
            num_scalar_prefetch=1,
            grid=(4,),
            in_specs=[
                pl.BlockSpec((4, WIDE, ROWS + 128), lambda g, mask: (0, 0, 0)),
                pl.BlockSpec((ROWS, width), lambda g, mask: (0, g)),
            ],
            out_specs=pl.BlockSpec((width // TILE, CODED, 128), lambda g, mask: (g, 0, 0)),
            scratch_shapes=[pltpu.VMEM((3 * WIDE, ROWS), BF16), pltpu.VMEM((ROWS, width), BF16)],
        ),
        compiler_params=params(),
        name="coarse_parts",
    )(p_mask, parts, p_tiles)


def sum_kernel(coded, out):
    total = jnp.zeros((72, 128), F32)
    for z in range(PLANES):
        block = coded[z].astype(jnp.int32).astype(F32)
        scale = jnp.exp2(block[72:80] * (1.0 / STEPS)) * (1.0 / LIMIT)
        factor = jnp.concatenate(
            [jnp.broadcast_to(scale[:1], (48, 128)), jnp.broadcast_to(scale[1:2], (24, 128))], axis=0
        )
        total = total + block[:72] * factor
    out[:, :128] = total[:48]
    out[:24, 128:] = total[48:, :64]
    out[24:, 128:] = total[48:, 64:]


def summed(coded):
    return pl.pallas_call(
        sum_kernel,
        out_shape=jax.ShapeDtypeStruct((WIDE, TILE), F32),
        in_specs=[pl.BlockSpec(memory_space=pltpu.VMEM)],
        out_specs=pl.BlockSpec(memory_space=pltpu.VMEM),
        compiler_params=params(),
        name="summed",
    )(coded)


def swapped(turn):
    return [
        ((zh * 4 + zl) * 4 + yh, ((yh + turn) % 4 * 4 + zh) * 4 + zl)
        for zh in range(4)
        for zl in range(4)
        for yh in range(4)
    ]


def around(size, near):
    return [((i + near) % size, i) for i in range(size)]


def local(a_tiles, p_tiles, a_mask, p_mask):
    zh, zl, x = lax.axis_index("zh"), lax.axis_index("zl"), lax.axis_index("x")
    yh, core, yl = lax.axis_index("yh"), lax.axis_index("core"), lax.axis_index("yl")
    z = ("zh", "zl")

    mine = stripes(p_tiles, p_mask, core, 2 * x + yh // 2, yl)
    near, far = [lax.ppermute(mine, z + ("yh",), swapped(turn)) for turn in (0, 2)]
    a_tiles, mine = lax.optimization_barrier((a_tiles, mine))
    own = masked_operator(a_tiles, a_mask)
    after, before = [lax.ppermute(own, "x", around(4, turn)) for turn in (1, -1)]

    slab, lower, upper, own, after, before = lax.optimization_barrier(
        (*collect(near, far, zh), own, after, before)
    )
    slabs = [slab, *[lax.ppermute(slab, z, around(PLANES, turn)) for turn in (1, -1)]]
    slabs += [lax.ppermute(lower, z, around(PLANES, 2)), lax.ppermute(upper, z, around(PLANES, -2))]
    blocks = [own, after, before, lax.ppermute(after, "x", around(4, 1))]

    theirs = lax.ppermute(product(slabs, blocks, zl, x, 1 - core), "core", [(0, 1), (1, 0)])
    coded = encode(product(slabs, blocks, zl, x, core), theirs)
    coded = lax.all_to_all(coded, "yh", 0, 0, tiled=True)
    coded = lax.all_to_all(coarse_parts(coded, p_tiles, p_mask), z, 0, 0, tiled=True)
    return summed(coded).T


def solution(mesh):
    fine = Mesh(mesh.devices.reshape(4, 4, 4, 4, 2, 2), ("zh", "zl", "x", "yh", "core", "yl"))
    z, col = ("zh", "zl"), ("x", "yh", "core")
    return jax.shard_map(
        local,
        mesh=fine,
        in_specs=(P(z, col), P(z, None), P(z, col), P(z, None)),
        out_specs=P(z, col + ("yl",)),
        check_vma=False,
    )
```

time: 163 us -> 148 us (0.908)
  waiting for transfers between devices: 35.4 us -> 10.1 us
  blocking collectives: 34.4 us -> 45.2 us
  local copies, waits for them, and re-layouts: 5.76 us -> 0.02 us
  starting transfers between devices: 72.8 us -> 76.2 us
  Pallas kernels: 11.9 us -> 13.7 us
    ppermute x13 -> x10, waiting for transfers between devices: 35.4 us -> 10.1 us  [the longest x1 5.43 us: local(): lax.ppermute(lower, z, around(PLANES, 2))]
    all_to_all x2, blocking collectives: 34.4 us -> 45.2 us  [the longest x1 30.1 us: local(): lax.all_to_all(coarse_parts(coded, p_tiles, p_mask), z, 0, 0, tiled=True)]
    unnamed x21 -> x10, local copies, waits for them, and re-layouts: 5.59 us -> 0.02 us
    ppermute x13 -> x10, starting transfers between devices: 72.8 us -> 76.2 us  [the longest x2 38 us: local(): lax.ppermute(slab, z, around(PLANES, turn))]
    pallas_call x1 -> x2, Pallas kernels: 3.31 us -> 4.99 us  [product(): pl.pallas_call(product_kernel, out_shape=jax.ShapeDtypeStruct((4, WIDE, R...]
    pallas_call x3 -> x4, Pallas kernels: 4.47 us -> 4.43 us  [the longest x1 2.72 us: stripes(): pl.pallas_call(stripes_kernel, out_shape=jax.ShapeDtypeStruct((4 * WIDE,...]
  transfers between devices with their start and end apart: 13 -> 10, of which waited for: 6 -> 3; matrix products, arithmetic and copies ran while one was open for 0% -> 0% of each run, Pallas kernels for 0% -> 2%
where the time goes in v4:
time: 148 us; the launch traced here: 146 us
  starting transfers between devices  76.2 us (51%)
  blocking collectives  45.2 us (31%)
  Pallas kernels  13.7 us (9%)
  waiting for transfers between devices  10.1 us (7%)
    ppermute x2, starting transfers between devices, local(): lax.ppermute(slab, z, around(PLANES, turn))  38 us
    all_to_all x1, blocking collectives, local(): lax.all_to_all(coarse_parts(coded, p_tiles, p_mask), z, 0, 0, tiled=True)  30.1 us
    ppermute x2, starting transfers between devices, local(): lax.ppermute(own, 'x', around(4, turn))  17 us
    all_to_all x1, blocking collectives, local(): coded = lax.all_to_all(coded, 'yh', 0, 0, tiled=True)  15.1 us
    ppermute x2, starting transfers between devices, local(): lax.ppermute(mine, z + ('yh',), swapped(turn))  9.81 us
    ppermute x1, waiting for transfers between devices, local(): lax.ppermute(lower, z, around(PLANES, 2))  5.43 us
    pallas_call x2, Pallas kernels, product(): pl.pallas_call(product_kernel, out_shape=jax.ShapeDtypeStruct((4, WIDE, R...  4.99 us
    pallas_call x1, Pallas kernels, coarse_parts(): pl.pallas_call(coarse_kernel, out_shape=jax.ShapeDtypeStruct((PLANES, COD...  3.56 us
  transfers between devices with their start and end apart: 10, of which 3 were waited for; matrix products, arithmetic and copies ran while one was open for 0% of the time, Pallas kernels for 2%

profile of v4, /device:TPU:6, one launch (start us, length us, event | category | flops | bytes accessed | tf_op | source)
XLA Modules:
  0.0 146.2 jit_solution(5124927485514068610)
XLA Ops:
  0.0 0.7 pad_add_fusion.2.place
  0.7 2.7 %stripes.1 = bf16[192,384]{1,0:T(8,128)(2,1)} custom-call(s32[3]{0:T(128)} %pad_add_fusion.2.place, s32[4,16]{1,0:T(4,128)} %mask.3, bf16[768,3072]{1,0:T(8,128)(2,1)} %tiles.2), custom_call_target="tpu_custom_call" | custom-call | tf_op jit(solution)/shard_map/stripes/pallas_call | solution.py:49
  3.4 0.6 masked_operator.1.own
  4.0 15.0 %collective-permute-start.3 = (bf16[768,384]{1,0:T(8,128)(2,1)S(1)}, bf16[768,384]{1,0:T(8,128)(2,1)S(1)}, u32[]{:S(2)}, u32[]{:S(2)}) collective-permute-start(bf16[768,384]{1,0:T(8,128)(2,1)S(1)} %masked_operator.1.own), channel_id=1, source_target_pairs={{48,0},{0,16},{16,32},{32,48},{49,1},{1,17},{17,33},{33,49},{50,2}... | collective-permute-start | bytes 1769480 | tf_op jit(solution)/shard_map/ppermute | solution.py:287
  19.1 1.9 %collective-permute-start.2 = (bf16[768,384]{1,0:T(8,128)(2,1)S(1)}, bf16[768,384]{1,0:T(8,128)(2,1)}, u32[]{:S(2)}, u32[]{:S(2)}) collective-permute-start(bf16[768,384]{1,0:T(8,128)(2,1)S(1)} %masked_operator.1.own), channel_id=1, source_target_pairs={{16,0},{32,16},{48,32},{0,48},{17,1},{33,17},{49,33},{1,49},{18,2}... | collective-permute-start | bytes 1769480 | tf_op jit(solution)/shard_map/ppermute | solution.py:287
  21.0 8.2 %collective-permute-start.1 = (bf16[192,384]{1,0:T(8,128)(2,1)}, bf16[192,384]{1,0:T(8,128)(2,1)S(1)}, u32[]{:S(2)}, u32[]{:S(2)}) collective-permute-start(bf16[192,384]{1,0:T(8,128)(2,1)} %stripes.1), channel_id=1, source_target_pairs={{0,512},{4,768},{8,0},{12,256},{64,516},{68,772},{72,4},{76,260},{... | collective-permute-start | bytes 442376 | tf_op jit(solution)/shard_map/ppermute | solution.py:284
  29.2 1.6 %collective-permute-start = (bf16[192,384]{1,0:T(8,128)(2,1)}, bf16[192,384]{1,0:T(8,128)(2,1)S(1)}, u32[]{:S(2)}, u32[]{:S(2)}) collective-permute-start(bf16[192,384]{1,0:T(8,128)(2,1)} %stripes.1), channel_id=1, source_target_pairs={{0,0},{4,256},{8,512},{12,768},{64,4},{68,260},{72,516},{76,772},{... | collective-permute-start | bytes 442376 | tf_op jit(solution)/shard_map/ppermute | solution.py:284
  30.8 1.4 collective-permute-done.1.far
  32.2 0.0 collective-permute-done.near
  32.2 0.8 collect.1
  33.0 0.0 collective-permute-done.2.after
  33.0 2.7 %collective-permute-start.8 = (bf16[768,384]{1,0:T(8,128)(2,1)}, bf16[768,384]{1,0:T(8,128)(2,1)}, u32[]{:S(2)}, u32[]{:S(2)}) collective-permute-start(bf16[768,384]{1,0:T(8,128)(2,1)} %collective-permute-done.2.after), channel_id=1, source_target_pairs={{16,0},{32,16},{48,32},{0,48},{17,1},{33,17},{49,33},{1,49},{18,2}... | collective-permute-start | bytes 1769480 | tf_op jit(solution)/shard_map/ppermute | solution.py:294
  35.7 27.7 %collective-permute-start.5 = (bf16[384,384]{1,0:T(8,128)(2,1)S(1)}, bf16[384,384]{1,0:T(8,128)(2,1)}, u32[]{:S(2)}, u32[]{:S(2)}) collective-permute-start(bf16[384,384]{1,0:T(8,128)(2,1)S(1)} %get-tuple-element.19.slab), channel_id=1, source_target_pairs={{960,0},{0,64},{64,128},{128,192},{192,256},{256,320},{320,384},{3... | collective-permute-start | bytes 884744 | tf_op jit(solution)/shard_map/ppermute | solution.py:292
  63.4 10.3 %collective-permute-start.4 = (bf16[384,384]{1,0:T(8,128)(2,1)S(1)}, bf16[384,384]{1,0:T(8,128)(2,1)}, u32[]{:S(2)}, u32[]{:S(2)}) collective-permute-start(bf16[384,384]{1,0:T(8,128)(2,1)S(1)} %get-tuple-element.19.slab), channel_id=1, source_target_pairs={{64,0},{128,64},{192,128},{256,192},{320,256},{384,320},{448,384},... | collective-permute-start | bytes 884744 | tf_op jit(solution)/shard_map/ppermute | solution.py:292
  73.8 3.4 %collective-permute-start.6 = (bf16[192,384]{1,0:T(8,128)(2,1)}, bf16[192,384]{1,0:T(8,128)(2,1)}, u32[]{:S(2)}, u32[]{:S(2)}) collective-permute-start(bf16[192,384]{1,0:T(8,128)(2,1)} %get-tuple-element.20), channel_id=1, source_target_pairs={{128,0},{192,64},{256,128},{320,192},{384,256},{448,320},{512,384}... | collective-permute-start | bytes 442376 | tf_op jit(solution)/shard_map/ppermute | solution.py:293
  77.1 3.4 %collective-permute-start.7 = (bf16[192,384]{1,0:T(8,128)(2,1)}, bf16[192,384]{1,0:T(8,128)(2,1)}, u32[]{:S(2)}, u32[]{:S(2)}) collective-permute-start(bf16[192,384]{1,0:T(8,128)(2,1)} %get-tuple-element.21), channel_id=1, source_target_pairs={{896,0},{960,64},{0,128},{64,192},{128,256},{192,320},{256,384},{3... | collective-permute-start | bytes 442376 | tf_op jit(solution)/shard_map/ppermute | solution.py:293
  80.5 0.1 pad_add_fusion.3.place
  80.6 5.4 %collective-permute-done.6.lower = bf16[192,384]{1,0:T(8,128)(2,1)} collective-permute-done((bf16[192,384]{1,0:T(8,128)(2,1)}, bf16[192,384]{1,0:T(8,128)(2,1)}, u32[]{:S(2)}, u32[]{:S(2)}) %collective-permute-start.6) | collective-permute-done | bytes 147488 | tf_op jit(solution)/shard_map/ppermute | solution.py:293
  86.0 3.2 %collective-permute-done.7.upper = bf16[192,384]{1,0:T(8,128)(2,1)} collective-permute-done((bf16[192,384]{1,0:T(8,128)(2,1)}, bf16[192,384]{1,0:T(8,128)(2,1)}, u32[]{:S(2)}, u32[]{:S(2)}) %collective-permute-start.7) | collective-permute-done | bytes 147488 | tf_op jit(solution)/shard_map/ppermute | solution.py:293
  89.3 0.0 collective-permute-done.5.below
  89.3 0.0 collective-permute-done.4.above
  89.3 0.0 collective-permute-done.8.across
  89.3 2.5 %product.3 = f32[4,48,768]{2,1,0:T(8,128)S(1)} custom-call(s32[3]{0:T(128)S(1)} %pad_add_fusion.3.place, bf16[384,384]{1,0:T(8,128)(2,1)S(1)} %get-tuple-element.19.slab, bf16[384,384]{1,0:T(8,128)(2,1)} %collective-permute-done.4.above, bf16[384,384]{1,0:T(8,128)(2,1)} %collective-permute-done.5.below, bf16[192,384]{1,0:T(8,128)(2,1)} %collective-permute-done.6.lower, ...), custom_call_target="tpu_custom_call" | custom-call | tf_op jit(solution)/shard_map/product/pallas_call | solution.py:132
  91.8 1.9 %collective-permute-start.9 = (f32[4,48,768]{2,1,0:T(8,128)S(1)}, f32[4,48,768]{2,1,0:T(8,128)S(1)}, u32[]{:S(2)}, u32[]{:S(2)}) collective-permute-start(f32[4,48,768]{2,1,0:T(8,128)S(1)} %product.3), channel_id=1, source_target_pairs={{0,2},{2,0},{1,3},{3,1},{4,6},{6,4},{5,7},{7,5},{8,10},{10,8},{9,1... | collective-permute-start | bytes 1769480 | tf_op jit(solution)/shard_map/ppermute | solution.py:296
  93.7 0.1 pad_add_fusion.place
  93.8 2.5 %product.2.mine = f32[4,48,768]{2,1,0:T(8,128)S(1)} custom-call(s32[3]{0:T(128)S(1)} %pad_add_fusion.place, bf16[384,384]{1,0:T(8,128)(2,1)S(1)} %get-tuple-element.19.slab, bf16[384,384]{1,0:T(8,128)(2,1)} %collective-permute-done.4.above, bf16[384,384]{1,0:T(8,128)(2,1)} %collective-permute-done.5.below, bf16[192,384]{1,0:T(8,128)(2,1)} %collective-permute-done.6.lower, ...), custom_call_target="tpu_custom_call" | custom-call | tf_op jit(solution)/shard_map/product/pallas_call | solution.py:132
  96.3 0.0 collective-permute-done.9.theirs
  96.3 0.3 encode.1
  96.6 15.1 %all_to_all.10.parts = s16[4,48,896]{2,1,0:T(8,128)(2,1)S(1)} all-to-all(s16[4,48,896]{2,1,0:T(8,128)(2,1)S(1)} %encode.1), channel_id=1, replica_groups=mesh['zh'=4,'zl'=4,'x'=4,'yh'=4,'core'=2,'yl'=2] {'yh'}, dimensions={0} | all-to-all | bytes 688128 | tf_op jit(solution)/shard_map/all_to_all | solution.py:298
  111.8 3.6 %coarse_parts.1 = s16[16,80,128]{2,1,0:T(8,128)(2,1)S(1)} custom-call(s32[4,16]{1,0:T(4,128)S(1)} %copy-done.1, s16[4,48,896]{2,1,0:T(8,128)(2,1)S(1)} %all_to_all.10.parts, bf16[768,3072]{1,0:T(8,128)(2,1)S(1)} %bitcast.10), custom_call_target="tpu_custom_call" | custom-call | tf_op jit(solution)/shard_map/coarse_parts/pallas_call | solution.py:222
  115.3 30.1 %all_to_all.11.coded = s16[16,80,128]{2,1,0:T(8,128)(2,1)S(1)} all-to-all(s16[16,80,128]{2,1,0:T(8,128)(2,1)S(1)} %coarse_parts.1), channel_id=1, replica_groups=mesh['zh'=4,'zl'=4,'x'=4,'yh'=4,'core'=2,'yl'=2] {'zh','zl'}, dimensions={0} | all-to-all | bytes 655360 | tf_op jit(solution)/shard_map/all_to_all | solution.py:299
  145.4 0.7 summed.1
  (12 shorter events, 0.0 us)
Async XLA Ops:
  0.0 3.4 %copy-start = (bf16[768,384]{1,0:T(8,128)(2,1)S(1)}, bf16[768,384]{1,0:T(8,128)(2,1)}, u32[]{:S(2)}) copy-start(bf16[768,384]{1,0:T(8,128)(2,1)} %tiles.1) | copy-start | bytes 1769476
  0.0 3.4 %copy-start.2 = (s32[4,2]{0,1:T(2,128)S(1)}, s32[4,2]{0,1:T(2,128)}, u32[]{:S(2)}) copy-start(s32[4,2]{0,1:T(2,128)} %param.6) | copy-start | bytes 100
  0.7 111.1 %slice-start = ((s8[4718592]{0:T(1024)(128)(4,1)}), s8[524288]{0:T(1024)(128)(4,1)S(1)}, s32[]{:S(2)}) async-start(s8[4718592]{0:T(1024)(128)(4,1)} %bitcast.9), calls=%async_computation.2 | async-start | bytes 1048576
  4.0 29.0 %collective-permute-start.3 = (bf16[768,384]{1,0:T(8,128)(2,1)S(1)}, bf16[768,384]{1,0:T(8,128)(2,1)S(1)}, u32[]{:S(2)}, u32[]{:S(2)}) collective-permute-start(bf16[768,384]{1,0:T(8,128)(2,1)S(1)} %masked_operator.1.own), channel_id=1, source_target_pairs={{48,0},{0,16},{16,32},{32,48},{49,1},{1,17},{17,33},{33,49},{50,2}... | collective-permute-start | bytes 1769480 | tf_op jit(solution)/shard_map/ppermute | solution.py:287
  19.1 13.9 %collective-permute-start.2 = (bf16[768,384]{1,0:T(8,128)(2,1)S(1)}, bf16[768,384]{1,0:T(8,128)(2,1)}, u32[]{:S(2)}, u32[]{:S(2)}) collective-permute-start(bf16[768,384]{1,0:T(8,128)(2,1)S(1)} %masked_operator.1.own), channel_id=1, source_target_pairs={{16,0},{32,16},{48,32},{0,48},{17,1},{33,17},{49,33},{1,49},{18,2}... | collective-permute-start | bytes 1769480 | tf_op jit(solution)/shard_map/ppermute | solution.py:287
  21.0 11.2 %collective-permute-start.1 = (bf16[192,384]{1,0:T(8,128)(2,1)}, bf16[192,384]{1,0:T(8,128)(2,1)S(1)}, u32[]{:S(2)}, u32[]{:S(2)}) collective-permute-start(bf16[192,384]{1,0:T(8,128)(2,1)} %stripes.1), channel_id=1, source_target_pairs={{0,512},{4,768},{8,0},{12,256},{64,516},{68,772},{72,4},{76,260},{... | collective-permute-start | bytes 442376 | tf_op jit(solution)/shard_map/ppermute | solution.py:284
  29.2 3.0 %collective-permute-start = (bf16[192,384]{1,0:T(8,128)(2,1)}, bf16[192,384]{1,0:T(8,128)(2,1)S(1)}, u32[]{:S(2)}, u32[]{:S(2)}) collective-permute-start(bf16[192,384]{1,0:T(8,128)(2,1)} %stripes.1), channel_id=1, source_target_pairs={{0,0},{4,256},{8,512},{12,768},{64,4},{68,260},{72,516},{76,772},{... | collective-permute-start | bytes 442376 | tf_op jit(solution)/shard_map/ppermute | solution.py:284
  33.0 56.3 %collective-permute-start.8 = (bf16[768,384]{1,0:T(8,128)(2,1)}, bf16[768,384]{1,0:T(8,128)(2,1)}, u32[]{:S(2)}, u32[]{:S(2)}) collective-permute-start(bf16[768,384]{1,0:T(8,128)(2,1)} %collective-permute-done.2.after), channel_id=1, source_target_pairs={{16,0},{32,16},{48,32},{0,48},{17,1},{33,17},{49,33},{1,49},{18,2}... | collective-permute-start | bytes 1769480 | tf_op jit(solution)/shard_map/ppermute | solution.py:294
  35.7 53.5 %collective-permute-start.5 = (bf16[384,384]{1,0:T(8,128)(2,1)S(1)}, bf16[384,384]{1,0:T(8,128)(2,1)}, u32[]{:S(2)}, u32[]{:S(2)}) collective-permute-start(bf16[384,384]{1,0:T(8,128)(2,1)S(1)} %get-tuple-element.19.slab), channel_id=1, source_target_pairs={{960,0},{0,64},{64,128},{128,192},{192,256},{256,320},{320,384},{3... | collective-permute-start | bytes 884744 | tf_op jit(solution)/shard_map/ppermute | solution.py:292
  63.4 25.9 %collective-permute-start.4 = (bf16[384,384]{1,0:T(8,128)(2,1)S(1)}, bf16[384,384]{1,0:T(8,128)(2,1)}, u32[]{:S(2)}, u32[]{:S(2)}) collective-permute-start(bf16[384,384]{1,0:T(8,128)(2,1)S(1)} %get-tuple-element.19.slab), channel_id=1, source_target_pairs={{64,0},{128,64},{192,128},{256,192},{320,256},{384,320},{448,384},... | collective-permute-start | bytes 884744 | tf_op jit(solution)/shard_map/ppermute | solution.py:292
  73.8 12.3 %collective-permute-start.6 = (bf16[192,384]{1,0:T(8,128)(2,1)}, bf16[192,384]{1,0:T(8,128)(2,1)}, u32[]{:S(2)}, u32[]{:S(2)}) collective-permute-start(bf16[192,384]{1,0:T(8,128)(2,1)} %get-tuple-element.20), channel_id=1, source_target_pairs={{128,0},{192,64},{256,128},{320,192},{384,256},{448,320},{512,384}... | collective-permute-start | bytes 442376 | tf_op jit(solution)/shard_map/ppermute | solution.py:293
  77.1 12.1 %collective-permute-start.7 = (bf16[192,384]{1,0:T(8,128)(2,1)}, bf16[192,384]{1,0:T(8,128)(2,1)}, u32[]{:S(2)}, u32[]{:S(2)}) collective-permute-start(bf16[192,384]{1,0:T(8,128)(2,1)} %get-tuple-element.21), channel_id=1, source_target_pairs={{896,0},{960,64},{0,128},{64,192},{128,256},{192,320},{256,384},{3... | collective-permute-start | bytes 442376 | tf_op jit(solution)/shard_map/ppermute | solution.py:293
  80.6 31.1 %slice-start.1 = ((s8[4718592]{0:T(1024)(128)(4,1)}), s8[4194304]{0:T(1024)(128)(4,1)S(1)}, s32[]{:S(2)}) async-start(s8[4718592]{0:T(1024)(128)(4,1)} %bitcast.9), calls=%async_computation.3 | async-start | bytes 8388608
  80.6 31.1 %copy-start.1 = (s32[4,16]{1,0:T(4,128)S(1)}, s32[4,16]{1,0:T(4,128)}, u32[]{:S(2)}) copy-start(s32[4,16]{1,0:T(4,128)} %mask.3) | copy-start | bytes 772
  91.8 4.5 %collective-permute-start.9 = (f32[4,48,768]{2,1,0:T(8,128)S(1)}, f32[4,48,768]{2,1,0:T(8,128)S(1)}, u32[]{:S(2)}, u32[]{:S(2)}) collective-permute-start(f32[4,48,768]{2,1,0:T(8,128)S(1)} %product.3), channel_id=1, source_target_pairs={{0,2},{2,0},{1,3},{3,1},{4,6},{6,4},{5,7},{7,5},{8,10},{10,8},{9,1... | collective-permute-start | bytes 1769480 | tf_op jit(solution)/shard_map/ppermute | solution.py:296

commit v5 on v4

--- a/solution.py
+++ b/solution.py
@@ -31,29 +31,31 @@
 
 
 def stripes_kernel(place, mask, window, out):
-    core, tile, yl = place[0], 2 * place[1], place[2]
+    core, tile, yl = place[0], 4 * place[1], place[2]
     row = lax.broadcasted_iota(jnp.int32, (WIDE, HALF), 0)
     lane = lax.broadcasted_iota(jnp.int32, (WIDE, HALF), 1)
     picks = [(lane == row + (2 * s + yl) * WIDE).astype(F32).astype(BF16) for s in range(4)]
-    picked = dot_last(jnp.concatenate(picks, axis=0), window[...])
+    pick = jnp.concatenate(picks, axis=0)
     fine = lax.broadcasted_iota(jnp.int32, (1, HALF), 1)
-    for n in range(2):
+    for n in range(4):
+        if n % 2 == 0:
+            picked = dot_last(pick, window[:, n * TILE : n * TILE + HALF])
         upper, lower = mask[2 * core, tile + n], mask[2 * core + 1, tile + n]
         present = jnp.where(fine < TILE, upper.astype(F32), lower.astype(F32))
-        rows = slice(2 * WIDE * n, 2 * WIDE * (n + 1))
-        out[rows, :] = (picked[rows] * present).astype(BF16)
-
-
-def stripes(p_tiles, p_mask, core, half, yl):
-    place = jnp.stack([core, half, yl]).astype(jnp.int32)
+        part = picked[: 2 * WIDE] if n % 2 == 0 else picked[2 * WIDE :]
+        out[2 * WIDE * n : 2 * WIDE * (n + 1), :] = (part * present).astype(BF16)
+
+
+def stripes(p_tiles, p_mask, core, x, yl):
+    place = jnp.stack([core, x, yl]).astype(jnp.int32)
     return pl.pallas_call(
         stripes_kernel,
-        out_shape=jax.ShapeDtypeStruct((4 * WIDE, HALF), BF16),
+        out_shape=jax.ShapeDtypeStruct((8 * WIDE, HALF), BF16),
         grid_spec=pltpu.PrefetchScalarGridSpec(
             num_scalar_prefetch=2,
             grid=(1,),
-            in_specs=[pl.BlockSpec((HALF, HALF), lambda g, place, mask: (place[0], place[1]))],
-            out_specs=pl.BlockSpec((4 * WIDE, HALF), lambda g, place, mask: (0, 0)),
+            in_specs=[pl.BlockSpec((HALF, 2 * HALF), lambda g, place, mask: (place[0], place[1]))],
+            out_specs=pl.BlockSpec((8 * WIDE, HALF), lambda g, place, mask: (0, 0)),
         ),
         compiler_params=pltpu.CompilerParams(vmem_limit_bytes=MOST_VMEM),
         name="stripes",
@@ -87,53 +89,25 @@
     )(a_mask.T, a_tiles)
 
 
-def collect_kernel(place, near, far, whole, lower, upper):
-    @pl.when(place[0] < 2)
-    def _():
-        lower[...], upper[...] = near[...], far[...]
-
-    @pl.when(place[0] >= 2)
-    def _():
-        lower[...], upper[...] = far[...], near[...]
-
-    whole[: 4 * WIDE], whole[4 * WIDE :] = lower[...], upper[...]
-
-
-def collect(near, far, zh):
-    return pl.pallas_call(
-        collect_kernel,
-        out_shape=[jax.ShapeDtypeStruct((n * WIDE, HALF), BF16) for n in (8, 4, 4)],
-        in_specs=[pl.BlockSpec(memory_space=pltpu.SMEM)]
-        + [pl.BlockSpec(memory_space=pltpu.VMEM)] * 2,
-        out_specs=[pl.BlockSpec(memory_space=pltpu.VMEM)] * 3,
-        compiler_params=params(),
-        name="collect",
-    )(zh.reshape(1).astype(jnp.int32), near, far)
-
-
-def product_kernel(place, slab, above, below, lower, upper, own, after, before, across, out, columns):
-    zl, x, core = place[0], place[1], place[2]
-    for y in range(4):
-        rows = pl.ds(pl.multiple_of((2 * y + core) * WIDE, WIDE), WIDE)
-        half = pl.ds(pl.multiple_of((2 * (y % 2) + core) * WIDE, WIDE), WIDE)
-        into = slice(y * WIDE, (y + 1) * WIDE)
-        columns[zl, into] = slab[rows, :]
-        columns[(zl + 1) % 4, into] = above[rows, :]
-        columns[(zl + 3) % 4, into] = below[rows, :]
-        columns[(zl + 2) % 4, into] = (lower if y < 2 else upper)[half, :]
-    total = dot_last(columns[x], own[...]) + dot_last(columns[(x + 1) % 4], after[...])
-    total = total + dot_last(columns[(x + 3) % 4], before[...])
-    total = total + dot_last(columns[(x + 2) % 4], across[...])
+def product_kernel(place, *refs):
+    slabs, blocks, out, columns = refs[:4], refs[4:8], refs[8], refs[9]
+    first, x, core = place[0], place[1], place[2]
+    for n, slab in enumerate(slabs):
+        for y in range(4):
+            rows = pl.ds(pl.multiple_of((2 * y + core) * WIDE, WIDE), WIDE)
+            columns[(first + n) % 4, y * WIDE : (y + 1) * WIDE] = slab[rows, :]
+    total = dot_last(columns[x], blocks[0][...])
+    for n in range(1, 4):
+        total = total + dot_last(columns[(x + n) % 4], blocks[n][...])
     out[...] = total.reshape(4, WIDE, ROWS)
 
 
-def product(slabs, blocks, zl, x, core):
-    place = jnp.stack([zl, x, core]).astype(jnp.int32)
+def product(slabs, blocks, first, x, core):
+    place = jnp.stack([first, x, core]).astype(jnp.int32)
     return pl.pallas_call(
         product_kernel,
         out_shape=jax.ShapeDtypeStruct((4, WIDE, ROWS), F32),
-        in_specs=[pl.BlockSpec(memory_space=pltpu.SMEM)]
-        + [pl.BlockSpec(memory_space=pltpu.VMEM)] * (len(slabs) + len(blocks)),
+        in_specs=[pl.BlockSpec(memory_space=pltpu.SMEM)] + [pl.BlockSpec(memory_space=pltpu.VMEM)] * 8,
         out_specs=pl.BlockSpec(memory_space=pltpu.VMEM),
         scratch_shapes=[pltpu.VMEM((4, 4 * WIDE, HALF), BF16)],
         compiler_params=params(),
@@ -262,13 +236,17 @@
     )(coded)
 
 
-def swapped(turn):
-    return [
-        ((zh * 4 + zl) * 4 + yh, ((yh + turn) % 4 * 4 + zh) * 4 + zl)
-        for zh in range(4)
-        for zl in range(4)
-        for yh in range(4)
-    ]
+def shift(yh):
+    return yh // 2 * 2
+
+
+def spread():
+    pairs = []
+    for source in range(4**3 * 4):
+        zh, zl, yh, core, yl = source // 64, source // 16 % 4, source // 4 % 4, source // 2 % 2, source % 2
+        target = ((yh + core + 2 * yl) % 4 * 4 + (zh + shift(zl)) % 4) * 4 + zl
+        pairs.append((source, (target * 2 + core) * 2 + yl))
+    return pairs
 
 
 def around(size, near):
@@ -280,21 +258,19 @@
     yh, core, yl = lax.axis_index("yh"), lax.axis_index("core"), lax.axis_index("yl")
     z = ("zh", "zl")
 
-    mine = stripes(p_tiles, p_mask, core, 2 * x + yh // 2, yl)
-    near, far = [lax.ppermute(mine, z + ("yh",), swapped(turn)) for turn in (0, 2)]
+    mine = stripes(p_tiles, p_mask, core, x, yl)
+    slab = lax.ppermute(mine, z + ("yh", "core", "yl"), spread())
+    first = (zl - shift(yh)) % 4
     a_tiles, mine = lax.optimization_barrier((a_tiles, mine))
     own = masked_operator(a_tiles, a_mask)
     after, before = [lax.ppermute(own, "x", around(4, turn)) for turn in (1, -1)]
 
-    slab, lower, upper, own, after, before = lax.optimization_barrier(
-        (*collect(near, far, zh), own, after, before)
-    )
-    slabs = [slab, *[lax.ppermute(slab, z, around(PLANES, turn)) for turn in (1, -1)]]
-    slabs += [lax.ppermute(lower, z, around(PLANES, 2)), lax.ppermute(upper, z, around(PLANES, -2))]
-    blocks = [own, after, before, lax.ppermute(after, "x", around(4, 1))]
-
-    theirs = lax.ppermute(product(slabs, blocks, zl, x, 1 - core), "core", [(0, 1), (1, 0)])
-    coded = encode(product(slabs, blocks, zl, x, core), theirs)
+    slab, own, after, before = lax.optimization_barrier((slab, own, after, before))
+    slabs = [slab] + [lax.ppermute(slab, z, around(PLANES, turn)) for turn in (1, 2, -1)]
+    blocks = [own, after, lax.ppermute(after, "x", around(4, 1)), before]
+
+    theirs = lax.ppermute(product(slabs, blocks, first, x, 1 - core), "core", [(0, 1), (1, 0)])
+    coded = encode(product(slabs, blocks, first, x, core), theirs)
     coded = lax.all_to_all(coded, "yh", 0, 0, tiled=True)
     coded = lax.all_to_all(coarse_parts(coded, p_tiles, p_mask), z, 0, 0, tiled=True)
     return summed(coded).T

time: 148 us -> 147 us (level)
  starting transfers between devices: 76.2 us -> 57.8 us
  waiting for transfers between devices: 10.1 us -> 21.9 us
  blocking collectives: 45.2 us -> 51.1 us
    ppermute x6 -> x3, starting transfers between devices: 21.2 us -> 5.45 us  [the longest x1 1.92 us: local(): lax.ppermute(product(slabs, blocks, first, x, 1 - core), 'core', [(0, 1),...]
    ppermute x2, waiting for transfers between devices: 0.01 us -> 11.8 us  [local(): lax.ppermute(own, 'x', around(4, turn))]
    ppermute x2 -> x3, waiting for transfers between devices: 0.01 us -> 10.1 us  [local(): lax.ppermute(slab, z, around(PLANES, turn))]
    ppermute x6 -> x3, waiting for transfers between devices: 10.1 us -> 0.01 us  [the longest x1 0.01 us: local(): slab = lax.ppermute(mine, z + ('yh', 'core', 'yl'), spread())]
    all_to_all x1, blocking collectives: 15.1 us -> 18.1 us  [local(): coded = lax.all_to_all(coded, 'yh', 0, 0, tiled=True)]
    all_to_all x1, blocking collectives: 30.1 us -> 33 us  [local(): lax.all_to_all(coarse_parts(coded, p_tiles, p_mask), z, 0, 0, tiled=True)]
    ppermute x2 -> x3, starting transfers between devices: 38 us -> 35.4 us  [local(): lax.ppermute(slab, z, around(PLANES, turn))]
    pallas_call x2 -> x1, Pallas kernels: 3.48 us -> 3 us  [stripes(): pl.pallas_call(stripes_kernel, out_shape=jax.ShapeDtypeStruct((8 * WIDE,...]
  transfers between devices with their start and end apart: 10 -> 8, of which waited for: 3 -> 4; matrix products, arithmetic and copies ran while one was open for 0% -> 0% of each run, Pallas kernels for 2% -> 2%
where the time goes in v5:
time: 147 us; the launch traced here: 145 us
  starting transfers between devices  57.8 us (39%)
  blocking collectives  51.1 us (35%)
  waiting for transfers between devices  21.9 us (15%)
  Pallas kernels  13.2 us (9%)
    ppermute x3, starting transfers between devices, local(): lax.ppermute(slab, z, around(PLANES, turn))  35.4 us
    all_to_all x1, blocking collectives, local(): lax.all_to_all(coarse_parts(coded, p_tiles, p_mask), z, 0, 0, tiled=True)  33 us
    all_to_all x1, blocking collectives, local(): coded = lax.all_to_all(coded, 'yh', 0, 0, tiled=True)  18.1 us
    ppermute x2, starting transfers between devices, local(): lax.ppermute(own, 'x', around(4, turn))  16.9 us
    ppermute x2, waiting for transfers between devices, local(): lax.ppermute(own, 'x', around(4, turn))  11.8 us
    ppermute x3, waiting for transfers between devices, local(): lax.ppermute(slab, z, around(PLANES, turn))  10.1 us
    pallas_call x2, Pallas kernels, product(): pl.pallas_call(product_kernel, out_shape=jax.ShapeDtypeStruct((4, WIDE, R...  4.94 us
    pallas_call x1, Pallas kernels, coarse_parts(): pl.pallas_call(coarse_kernel, out_shape=jax.ShapeDtypeStruct((PLANES, COD...  3.56 us
  transfers between devices with their start and end apart: 8, of which 4 were waited for; matrix products, arithmetic and copies ran while one was open for 0% of the time, Pallas kernels for 2%

profile of v5, /device:TPU:6, one launch (start us, length us, event | category | flops | bytes accessed | tf_op | source)
XLA Modules:
  0.0 145.0 jit_solution(11994848344476962265)
XLA Ops:
  0.0 0.6 pad_add_fusion.2.place
  0.7 3.0 %stripes.1 = bf16[384,384]{1,0:T(8,128)(2,1)} custom-call(s32[3]{0:T(128)} %pad_add_fusion.2.place, s32[4,16]{1,0:T(4,128)} %mask.3, bf16[768,3072]{1,0:T(8,128)(2,1)} %tiles.2), custom_call_target="tpu_custom_call" | custom-call | tf_op jit(solution)/shard_map/stripes/pallas_call | solution.py:51
  3.7 0.0 copy-done
  3.7 0.0 copy-done.2
  3.7 0.6 masked_operator.1.refs_4_
  4.3 15.0 %collective-permute-start.2 = (bf16[768,384]{1,0:T(8,128)(2,1)S(1)}, bf16[768,384]{1,0:T(8,128)(2,1)S(1)}, u32[]{:S(2)}, u32[]{:S(2)}) collective-permute-start(bf16[768,384]{1,0:T(8,128)(2,1)S(1)} %masked_operator.1.refs_4_), channel_id=1, source_target_pairs={{48,0},{0,16},{16,32},{32,48},{49,1},{1,17},{17,33},{33,49},{50,2}... | collective-permute-start | bytes 1769480 | tf_op jit(solution)/shard_map/ppermute | solution.py:266
  19.3 1.9 %collective-permute-start.1 = (bf16[768,384]{1,0:T(8,128)(2,1)S(1)}, bf16[768,384]{1,0:T(8,128)(2,1)}, u32[]{:S(2)}, u32[]{:S(2)}) collective-permute-start(bf16[768,384]{1,0:T(8,128)(2,1)S(1)} %masked_operator.1.refs_4_), channel_id=1, source_target_pairs={{16,0},{32,16},{48,32},{0,48},{17,1},{33,17},{49,33},{1,49},{18,2}... | collective-permute-start | bytes 1769480 | tf_op jit(solution)/shard_map/ppermute | solution.py:266
  21.2 1.6 %collective-permute-start = (bf16[384,384]{1,0:T(8,128)(2,1)}, bf16[384,384]{1,0:T(8,128)(2,1)S(1)}, u32[]{:S(2)}, u32[]{:S(2)}) collective-permute-start(bf16[384,384]{1,0:T(8,128)(2,1)} %stripes.1), channel_id=1, source_target_pairs={{0,0},{1,513},{2,258},{3,771},{4,256},{5,769},{6,514},{7,3},{8,512... | collective-permute-start | bytes 884744 | tf_op jit(solution)/shard_map/ppermute | solution.py:262
  22.9 0.0 collective-permute-done.refs_0_
  22.9 3.8 %collective-permute-done.2.refs_7_ = bf16[768,384]{1,0:T(8,128)(2,1)S(1)} collective-permute-done((bf16[768,384]{1,0:T(8,128)(2,1)S(1)}, bf16[768,384]{1,0:T(8,128)(2,1)S(1)}, u32[]{:S(2)}, u32[]{:S(2)}) %collective-permute-start.2) | collective-permute-done | bytes 589856 | tf_op jit(solution)/shard_map/ppermute | solution.py:266
  26.7 8.0 %collective-permute-done.1.refs_5_ = bf16[768,384]{1,0:T(8,128)(2,1)} collective-permute-done((bf16[768,384]{1,0:T(8,128)(2,1)S(1)}, bf16[768,384]{1,0:T(8,128)(2,1)}, u32[]{:S(2)}, u32[]{:S(2)}) %collective-permute-start.1) | collective-permute-done | bytes 589856 | tf_op jit(solution)/shard_map/ppermute | solution.py:266
  34.7 1.9 %collective-permute-start.6 = (bf16[768,384]{1,0:T(8,128)(2,1)}, bf16[768,384]{1,0:T(8,128)(2,1)}, u32[]{:S(2)}, u32[]{:S(2)}) collective-permute-start(bf16[768,384]{1,0:T(8,128)(2,1)} %collective-permute-done.1.refs_5_), channel_id=1, source_target_pairs={{16,0},{32,16},{48,32},{0,48},{17,1},{33,17},{49,33},{1,49},{18,2}... | collective-permute-start | bytes 1769480 | tf_op jit(solution)/shard_map/ppermute | solution.py:270
  36.6 2.1 %collective-permute-start.5 = (bf16[384,384]{1,0:T(8,128)(2,1)S(1)}, bf16[384,384]{1,0:T(8,128)(2,1)}, u32[]{:S(2)}, u32[]{:S(2)}) collective-permute-start(bf16[384,384]{1,0:T(8,128)(2,1)S(1)} %collective-permute-done.refs_0_), channel_id=1, source_target_pairs={{960,0},{0,64},{64,128},{128,192},{192,256},{256,320},{320,384},{3... | collective-permute-start | bytes 884744 | tf_op jit(solution)/shard_map/ppermute | solution.py:269
  38.7 23.6 %collective-permute-start.4 = (bf16[384,384]{1,0:T(8,128)(2,1)S(1)}, bf16[384,384]{1,0:T(8,128)(2,1)}, u32[]{:S(2)}, u32[]{:S(2)}) collective-permute-start(bf16[384,384]{1,0:T(8,128)(2,1)S(1)} %collective-permute-done.refs_0_), channel_id=1, source_target_pairs={{128,0},{192,64},{256,128},{320,192},{384,256},{448,320},{512,384}... | collective-permute-start | bytes 884744 | tf_op jit(solution)/shard_map/ppermute | solution.py:269
  62.3 9.7 %collective-permute-start.3 = (bf16[384,384]{1,0:T(8,128)(2,1)S(1)}, bf16[384,384]{1,0:T(8,128)(2,1)}, u32[]{:S(2)}, u32[]{:S(2)}) collective-permute-start(bf16[384,384]{1,0:T(8,128)(2,1)S(1)} %collective-permute-done.refs_0_), channel_id=1, source_target_pairs={{64,0},{128,64},{192,128},{256,192},{320,256},{384,320},{448,384},... | collective-permute-start | bytes 884744 | tf_op jit(solution)/shard_map/ppermute | solution.py:269
  72.0 0.1 pad_add_fusion.3.place
  72.1 0.0 collective-permute-done.5.refs_3_
  72.1 2.7 %collective-permute-done.4.refs_2_ = bf16[384,384]{1,0:T(8,128)(2,1)} collective-permute-done((bf16[384,384]{1,0:T(8,128)(2,1)S(1)}, bf16[384,384]{1,0:T(8,128)(2,1)}, u32[]{:S(2)}, u32[]{:S(2)}) %collective-permute-start.4) | collective-permute-done | bytes 294944 | tf_op jit(solution)/shard_map/ppermute | solution.py:269
  74.9 7.4 %collective-permute-done.3.refs_1_ = bf16[384,384]{1,0:T(8,128)(2,1)} collective-permute-done((bf16[384,384]{1,0:T(8,128)(2,1)S(1)}, bf16[384,384]{1,0:T(8,128)(2,1)}, u32[]{:S(2)}, u32[]{:S(2)}) %collective-permute-start.3) | collective-permute-done | bytes 294944 | tf_op jit(solution)/shard_map/ppermute | solution.py:269
  82.2 0.0 collective-permute-done.6.refs_6_
  82.2 2.5 %product.3 = f32[4,48,768]{2,1,0:T(8,128)S(1)} custom-call(s32[3]{0:T(128)S(1)} %pad_add_fusion.3.place, bf16[384,384]{1,0:T(8,128)(2,1)S(1)} %collective-permute-done.refs_0_, bf16[384,384]{1,0:T(8,128)(2,1)} %collective-permute-done.3.refs_1_, bf16[384,384]{1,0:T(8,128)(2,1)} %collective-permute-done.4.refs_2_, ...), custom_call_target="tpu_custom_call" | custom-call | tf_op jit(solution)/shard_map/product/pallas_call | solution.py:107
  84.7 1.9 %collective-permute-start.7 = (f32[4,48,768]{2,1,0:T(8,128)S(1)}, f32[4,48,768]{2,1,0:T(8,128)S(1)}, u32[]{:S(2)}, u32[]{:S(2)}) collective-permute-start(f32[4,48,768]{2,1,0:T(8,128)S(1)} %product.3), channel_id=1, source_target_pairs={{0,2},{2,0},{1,3},{3,1},{4,6},{6,4},{5,7},{7,5},{8,10},{10,8},{9,1... | collective-permute-start | bytes 1769480 | tf_op jit(solution)/shard_map/ppermute | solution.py:272
  86.6 0.1 pad_add_fusion.place
  86.7 2.5 %product.2.mine = f32[4,48,768]{2,1,0:T(8,128)S(1)} custom-call(s32[3]{0:T(128)S(1)} %pad_add_fusion.place, bf16[384,384]{1,0:T(8,128)(2,1)S(1)} %collective-permute-done.refs_0_, bf16[384,384]{1,0:T(8,128)(2,1)} %collective-permute-done.3.refs_1_, bf16[384,384]{1,0:T(8,128)(2,1)} %collective-permute-done.4.refs_2_, ...), custom_call_target="tpu_custom_call" | custom-call | tf_op jit(solution)/shard_map/product/pallas_call | solution.py:107
  89.2 0.0 collective-permute-done.7.theirs
  89.2 0.4 encode.1
  89.6 18.1 %all_to_all.10.parts = s16[4,48,896]{2,1,0:T(8,128)(2,1)S(1)} all-to-all(s16[4,48,896]{2,1,0:T(8,128)(2,1)S(1)} %encode.1), channel_id=1, replica_groups=mesh['zh'=4,'zl'=4,'x'=4,'yh'=4,'core'=2,'yl'=2] {'yh'}, dimensions={0} | all-to-all | bytes 688128 | tf_op jit(solution)/shard_map/all_to_all | solution.py:274
  107.7 0.0 slice-done
  107.7 0.0 slice-done.1
  107.7 3.6 %coarse_parts.1 = s16[16,80,128]{2,1,0:T(8,128)(2,1)S(1)} custom-call(s32[4,16]{1,0:T(4,128)S(1)} %copy-done.1, s16[4,48,896]{2,1,0:T(8,128)(2,1)S(1)} %all_to_all.10.parts, bf16[768,3072]{1,0:T(8,128)(2,1)S(1)} %bitcast.8), custom_call_target="tpu_custom_call" | custom-call | tf_op jit(solution)/shard_map/coarse_parts/pallas_call | solution.py:196
  111.2 33.0 %all_to_all.11.coded = s16[16,80,128]{2,1,0:T(8,128)(2,1)S(1)} all-to-all(s16[16,80,128]{2,1,0:T(8,128)(2,1)S(1)} %coarse_parts.1), channel_id=1, replica_groups=mesh['zh'=4,'zl'=4,'x'=4,'yh'=4,'core'=2,'yl'=2] {'zh','zl'}, dimensions={0} | all-to-all | bytes 655360 | tf_op jit(solution)/shard_map/all_to_all | solution.py:275
  144.2 0.7 summed.1
  (7 shorter events, 0.0 us)
Async XLA Ops:
  0.0 3.7 %copy-start = (bf16[768,384]{1,0:T(8,128)(2,1)S(1)}, bf16[768,384]{1,0:T(8,128)(2,1)}, u32[]{:S(2)}) copy-start(bf16[768,384]{1,0:T(8,128)(2,1)} %tiles.1) | copy-start | bytes 1769476
  0.0 3.7 %copy-start.2 = (s32[4,2]{0,1:T(2,128)S(1)}, s32[4,2]{0,1:T(2,128)}, u32[]{:S(2)}) copy-start(s32[4,2]{0,1:T(2,128)} %param.6) | copy-start | bytes 100
  0.7 107.0 %slice-start = ((s8[4718592]{0:T(1024)(128)(4,1)}), s8[524288]{0:T(1024)(128)(4,1)S(1)}, s32[]{:S(2)}) async-start(s8[4718592]{0:T(1024)(128)(4,1)} %bitcast.7), calls=%async_computation.2 | async-start | bytes 1048576
  4.3 22.4 %collective-permute-start.2 = (bf16[768,384]{1,0:T(8,128)(2,1)S(1)}, bf16[768,384]{1,0:T(8,128)(2,1)S(1)}, u32[]{:S(2)}, u32[]{:S(2)}) collective-permute-start(bf16[768,384]{1,0:T(8,128)(2,1)S(1)} %masked_operator.1.refs_4_), channel_id=1, source_target_pairs={{48,0},{0,16},{16,32},{32,48},{49,1},{1,17},{17,33},{33,49},{50,2}... | collective-permute-start | bytes 1769480 | tf_op jit(solution)/shard_map/ppermute | solution.py:266
  19.3 15.4 %collective-permute-start.1 = (bf16[768,384]{1,0:T(8,128)(2,1)S(1)}, bf16[768,384]{1,0:T(8,128)(2,1)}, u32[]{:S(2)}, u32[]{:S(2)}) collective-permute-start(bf16[768,384]{1,0:T(8,128)(2,1)S(1)} %masked_operator.1.refs_4_), channel_id=1, source_target_pairs={{16,0},{32,16},{48,32},{0,48},{17,1},{33,17},{49,33},{1,49},{18,2}... | collective-permute-start | bytes 1769480 | tf_op jit(solution)/shard_map/ppermute | solution.py:266
  21.2 1.6 %collective-permute-start = (bf16[384,384]{1,0:T(8,128)(2,1)}, bf16[384,384]{1,0:T(8,128)(2,1)S(1)}, u32[]{:S(2)}, u32[]{:S(2)}) collective-permute-start(bf16[384,384]{1,0:T(8,128)(2,1)} %stripes.1), channel_id=1, source_target_pairs={{0,0},{1,513},{2,258},{3,771},{4,256},{5,769},{6,514},{7,3},{8,512... | collective-permute-start | bytes 884744 | tf_op jit(solution)/shard_map/ppermute | solution.py:262
  34.7 47.6 %collective-permute-start.6 = (bf16[768,384]{1,0:T(8,128)(2,1)}, bf16[768,384]{1,0:T(8,128)(2,1)}, u32[]{:S(2)}, u32[]{:S(2)}) collective-permute-start(bf16[768,384]{1,0:T(8,128)(2,1)} %collective-permute-done.1.refs_5_), channel_id=1, source_target_pairs={{16,0},{32,16},{48,32},{0,48},{17,1},{33,17},{49,33},{1,49},{18,2}... | collective-permute-start | bytes 1769480 | tf_op jit(solution)/shard_map/ppermute | solution.py:270
  36.6 35.5 %collective-permute-start.5 = (bf16[384,384]{1,0:T(8,128)(2,1)S(1)}, bf16[384,384]{1,0:T(8,128)(2,1)}, u32[]{:S(2)}, u32[]{:S(2)}) collective-permute-start(bf16[384,384]{1,0:T(8,128)(2,1)S(1)} %collective-permute-done.refs_0_), channel_id=1, source_target_pairs={{960,0},{0,64},{64,128},{128,192},{192,256},{256,320},{320,384},{3... | collective-permute-start | bytes 884744 | tf_op jit(solution)/shard_map/ppermute | solution.py:269
  38.7 36.2 %collective-permute-start.4 = (bf16[384,384]{1,0:T(8,128)(2,1)S(1)}, bf16[384,384]{1,0:T(8,128)(2,1)}, u32[]{:S(2)}, u32[]{:S(2)}) collective-permute-start(bf16[384,384]{1,0:T(8,128)(2,1)S(1)} %collective-permute-done.refs_0_), channel_id=1, source_target_pairs={{128,0},{192,64},{256,128},{320,192},{384,256},{448,320},{512,384}... | collective-permute-start | bytes 884744 | tf_op jit(solution)/shard_map/ppermute | solution.py:269
  62.3 20.0 %collective-permute-start.3 = (bf16[384,384]{1,0:T(8,128)(2,1)S(1)}, bf16[384,384]{1,0:T(8,128)(2,1)}, u32[]{:S(2)}, u32[]{:S(2)}) collective-permute-start(bf16[384,384]{1,0:T(8,128)(2,1)S(1)} %collective-permute-done.refs_0_), channel_id=1, source_target_pairs={{64,0},{128,64},{192,128},{256,192},{320,256},{384,320},{448,384},... | collective-permute-start | bytes 884744 | tf_op jit(solution)/shard_map/ppermute | solution.py:269
  72.1 35.6 %slice-start.1 = ((s8[4718592]{0:T(1024)(128)(4,1)}), s8[4194304]{0:T(1024)(128)(4,1)S(1)}, s32[]{:S(2)}) async-start(s8[4718592]{0:T(1024)(128)(4,1)} %bitcast.7), calls=%async_computation.3 | async-start | bytes 8388608
  72.1 35.6 %copy-start.1 = (s32[4,16]{1,0:T(4,128)S(1)}, s32[4,16]{1,0:T(4,128)}, u32[]{:S(2)}) copy-start(s32[4,16]{1,0:T(4,128)} %mask.3) | copy-start | bytes 772
  84.7 4.5 %collective-permute-start.7 = (f32[4,48,768]{2,1,0:T(8,128)S(1)}, f32[4,48,768]{2,1,0:T(8,128)S(1)}, u32[]{:S(2)}, u32[]{:S(2)}) collective-permute-start(f32[4,48,768]{2,1,0:T(8,128)S(1)} %product.3), channel_id=1, source_target_pairs={{0,2},{2,0},{1,3},{3,1},{4,6},{6,4},{5,7},{7,5},{8,10},{10,8},{9,1... | collective-permute-start | bytes 1769480 | tf_op jit(solution)/shard_map/ppermute | solution.py:272

commit v6 on v5

--- a/solution.py
+++ b/solution.py
@@ -1,3 +1,5 @@
+import functools
+
 import jax
 import jax.numpy as jnp
 from jax import lax
@@ -14,9 +16,10 @@
 PLANES = 16
 LIMIT = 32766.0
 STEPS = 128.0
+EMPTY = 16
 LEAST = 1e-33
 CODED = 80
-VMEM = 48 * 1024 * 1024
+VMEM = 16 * 1024 * 1024
 MOST_VMEM = 62 * 1024 * 1024
 F32 = jnp.float32
 BF16 = jnp.bfloat16
@@ -30,42 +33,48 @@
     return lax.dot_general(left, right, (((1,), (1,)), ((), ())), preferred_element_type=F32)
 
 
-def stripes_kernel(place, mask, window, out):
-    core, tile, yl = place[0], 4 * place[1], place[2]
+def stripes_kernel(mask, tiles, out, window, arrived):
+    core, x, yl = lax.axis_index("core"), lax.axis_index("x"), lax.axis_index("yl")
+    copies = []
+    for n in range(2):
+        rows = pl.ds(pl.multiple_of(core * HALF, HALF), HALF)
+        columns = pl.ds(pl.multiple_of((2 * x + n) * HALF, HALF), HALF)
+        copies.append(pltpu.make_async_copy(tiles.at[rows, columns], window.at[n], arrived.at[n]))
+        copies[n].start()
     row = lax.broadcasted_iota(jnp.int32, (WIDE, HALF), 0)
     lane = lax.broadcasted_iota(jnp.int32, (WIDE, HALF), 1)
     picks = [(lane == row + (2 * s + yl) * WIDE).astype(F32).astype(BF16) for s in range(4)]
     pick = jnp.concatenate(picks, axis=0)
     fine = lax.broadcasted_iota(jnp.int32, (1, HALF), 1)
-    for n in range(4):
-        if n % 2 == 0:
-            picked = dot_last(pick, window[:, n * TILE : n * TILE + HALF])
-        upper, lower = mask[2 * core, tile + n], mask[2 * core + 1, tile + n]
-        present = jnp.where(fine < TILE, upper.astype(F32), lower.astype(F32))
-        part = picked[: 2 * WIDE] if n % 2 == 0 else picked[2 * WIDE :]
-        out[2 * WIDE * n : 2 * WIDE * (n + 1), :] = (part * present).astype(BF16)
-
-
-def stripes(p_tiles, p_mask, core, x, yl):
-    place = jnp.stack([core, x, yl]).astype(jnp.int32)
+    out[8 * WIDE :, :] = jnp.zeros((EMPTY, HALF), BF16)
+    for n in range(2):
+        copies[n].wait()
+        picked = dot_last(pick, window[n])
+        for m in range(2):
+            tile = 4 * x + 2 * n + m
+            upper, lower = mask[2 * core, tile], mask[2 * core + 1, tile]
+            present = jnp.where(fine < TILE, upper.astype(F32), lower.astype(F32))
+            part = picked[2 * WIDE * m : 2 * WIDE * (m + 1)]
+            first = 2 * WIDE * (2 * n + m)
+            out[first : first + 2 * WIDE, :] = (part * present).astype(BF16)
+
+
+def stripes(p_tiles, p_mask):
     return pl.pallas_call(
         stripes_kernel,
-        out_shape=jax.ShapeDtypeStruct((8 * WIDE, HALF), BF16),
-        grid_spec=pltpu.PrefetchScalarGridSpec(
-            num_scalar_prefetch=2,
-            grid=(1,),
-            in_specs=[pl.BlockSpec((HALF, 2 * HALF), lambda g, place, mask: (place[0], place[1]))],
-            out_specs=pl.BlockSpec((8 * WIDE, HALF), lambda g, place, mask: (0, 0)),
-        ),
+        out_shape=jax.ShapeDtypeStruct((8 * WIDE + EMPTY, HALF), BF16),
+        in_specs=[pl.BlockSpec(memory_space=pltpu.SMEM), pl.BlockSpec(memory_space=pltpu.HBM)],
+        out_specs=pl.BlockSpec(memory_space=pltpu.VMEM),
+        scratch_shapes=[pltpu.VMEM((2, HALF, HALF), BF16), pltpu.SemaphoreType.DMA((2,))],
         compiler_params=pltpu.CompilerParams(vmem_limit_bytes=MOST_VMEM),
         name="stripes",
-    )(place, p_mask, p_tiles)
+    )(p_mask, p_tiles)
 
 
 def mask_rows(mask, tiles, out, first):
-    width = tiles.shape[1]
+    height, width = tiles.shape
     lane = lax.broadcasted_iota(jnp.int32, (1, width), 1)
-    for i in range(ROWS // TILE):
+    for i in range(height // TILE):
         present = jnp.zeros((1, width), F32)
         for k in range(width // TILE):
             inside = (lane >= k * TILE) & (lane < (k + 1) * TILE)
@@ -74,45 +83,49 @@
         out[rows, :] = tiles[rows, :] * present.astype(BF16)
 
 
-def operator_kernel(mask, tiles, out):
-    mask_rows(lambda i, k: mask[k, i], tiles, out, 0)
+def operator_kernel(mask, tiles, upper, lower):
+    for half, out in enumerate((upper, lower)):
+        rows = tiles[half * HALF : (half + 1) * HALF, :]
+        mask_rows(lambda i, k: mask[k, 2 * half + i], rows, out, 0)
 
 
 def masked_operator(a_tiles, a_mask):
     return pl.pallas_call(
         operator_kernel,
-        out_shape=jax.ShapeDtypeStruct(a_tiles.shape, BF16),
+        out_shape=[jax.ShapeDtypeStruct((HALF, HALF), BF16)] * 2,
         in_specs=[pl.BlockSpec(memory_space=pltpu.SMEM), pl.BlockSpec(memory_space=pltpu.VMEM)],
-        out_specs=pl.BlockSpec(memory_space=pltpu.VMEM),
+        out_specs=[pl.BlockSpec(memory_space=pltpu.VMEM)] * 2,
         compiler_params=params(),
         name="masked_operator",
     )(a_mask.T, a_tiles)
 
 
-def product_kernel(place, *refs):
-    slabs, blocks, out, columns = refs[:4], refs[4:8], refs[8], refs[9]
-    first, x, core = place[0], place[1], place[2]
+def product_kernel(other, *refs):
+    slabs, blocks, out, columns = refs[:4], refs[4:12], refs[12], refs[13]
+    x, zl, yh = lax.axis_index("x"), lax.axis_index("zl"), lax.axis_index("yh")
+    first = zl + 4 - shift(yh)
+    core = (lax.axis_index("core") + other) % 2
     for n, slab in enumerate(slabs):
         for y in range(4):
             rows = pl.ds(pl.multiple_of((2 * y + core) * WIDE, WIDE), WIDE)
             columns[(first + n) % 4, y * WIDE : (y + 1) * WIDE] = slab[rows, :]
-    total = dot_last(columns[x], blocks[0][...])
-    for n in range(1, 4):
-        total = total + dot_last(columns[(x + n) % 4], blocks[n][...])
-    out[...] = total.reshape(4, WIDE, ROWS)
-
-
-def product(slabs, blocks, first, x, core):
-    place = jnp.stack([first, x, core]).astype(jnp.int32)
-    return pl.pallas_call(
-        product_kernel,
+    for half in range(2):
+        total = dot_last(columns[x], blocks[half][...])
+        for n in range(1, 4):
+            total = total + dot_last(columns[(x + n) % 4], blocks[2 * n + half][...])
+        out[:, :, half * HALF : (half + 1) * HALF] = total.reshape(4, WIDE, HALF)
+
+
+def product(slabs, blocks, other):
+    return pl.pallas_call(
+        functools.partial(product_kernel, other),
         out_shape=jax.ShapeDtypeStruct((4, WIDE, ROWS), F32),
-        in_specs=[pl.BlockSpec(memory_space=pltpu.SMEM)] + [pl.BlockSpec(memory_space=pltpu.VMEM)] * 8,
+        in_specs=[pl.BlockSpec(memory_space=pltpu.VMEM)] * 12,
         out_specs=pl.BlockSpec(memory_space=pltpu.VMEM),
         scratch_shapes=[pltpu.VMEM((4, 4 * WIDE, HALF), BF16)],
         compiler_params=params(),
-        name="product",
-    )(place, *slabs, *blocks)
+        name="product_for_other" if other else "product",
+    )(*slabs, *blocks)
 
 
 def scale_code(most):
@@ -254,23 +267,24 @@
 
 
 def local(a_tiles, p_tiles, a_mask, p_mask):
-    zh, zl, x = lax.axis_index("zh"), lax.axis_index("zl"), lax.axis_index("x")
-    yh, core, yl = lax.axis_index("yh"), lax.axis_index("core"), lax.axis_index("yl")
     z = ("zh", "zl")
-
-    mine = stripes(p_tiles, p_mask, core, x, yl)
+    mine = stripes(p_tiles, p_mask)
     slab = lax.ppermute(mine, z + ("yh", "core", "yl"), spread())
-    first = (zl - shift(yh)) % 4
     a_tiles, mine = lax.optimization_barrier((a_tiles, mine))
     own = masked_operator(a_tiles, a_mask)
-    after, before = [lax.ppermute(own, "x", around(4, turn)) for turn in (1, -1)]
+    after = [lax.ppermute(half, "x", around(4, 1)) for half in own]
+    before = [lax.ppermute(half, "x", around(4, -1)) for half in own]
 
     slab, own, after, before = lax.optimization_barrier((slab, own, after, before))
     slabs = [slab] + [lax.ppermute(slab, z, around(PLANES, turn)) for turn in (1, 2, -1)]
-    blocks = [own, after, lax.ppermute(after, "x", around(4, 1)), before]
-
-    theirs = lax.ppermute(product(slabs, blocks, first, x, 1 - core), "core", [(0, 1), (1, 0)])
-    coded = encode(product(slabs, blocks, first, x, core), theirs)
+    across = [
+        lax.ppermute(after[0], "x", around(4, 1)),
+        lax.ppermute(before[1], "x", around(4, -1)),
+    ]
+    blocks = [*own, *after, *across, *before]
+
+    theirs = lax.ppermute(product(slabs, blocks, 1), "core", [(0, 1), (1, 0)])
+    coded = encode(product(slabs, blocks, 0), theirs)
     coded = lax.all_to_all(coded, "yh", 0, 0, tiled=True)
     coded = lax.all_to_all(coarse_parts(coded, p_tiles, p_mask), z, 0, 0, tiled=True)
     return summed(coded).T

time: 147 us -> 135 us (0.918)
  waiting for transfers between devices: 21.9 us -> 13.1 us
  starting transfers between devices: 57.8 us -> 60.7 us
  Pallas kernels: 13.2 us -> 10.5 us
    ppermute x4 -> x7, starting transfers between devices: 20.8 us -> 33.2 us  [the longest x2 20.4 us: local(): before = [lax.ppermute(half, 'x', around(4, -1)) for half in own]]
    ppermute x3, waiting for transfers between devices: 10.1 us -> 0.01 us  [local(): lax.ppermute(slab, z, around(PLANES, turn))]
    ppermute x3, starting transfers between devices: 35.4 us -> 25.8 us  [local(): lax.ppermute(slab, z, around(PLANES, turn))]
    pallas_call x4, Pallas kernels: 8.54 us -> 5.88 us  [the longest x1 3.12 us: stripes(): pl.pallas_call(stripes_kernel, out_shape=jax.ShapeDtypeStruct((8 * WIDE +...]
    ppermute x4 -> x7, waiting for transfers between devices: 11.8 us -> 13.1 us  [the longest x2 7.45 us: local(): after = [lax.ppermute(half, 'x', around(4, 1)) for half in own]]
  transfers between devices with their start and end apart: 8 -> 11, of which waited for: 4 -> 6; matrix products, arithmetic and copies ran while one was open for 0% -> 0% of each run, Pallas kernels for 2% -> 1%
where the time goes in v6:
time: 135 us; the launch traced here: 134 us
  starting transfers between devices  60.7 us (45%)
  blocking collectives  49.8 us (37%)
  waiting for transfers between devices  13.1 us (10%)
  Pallas kernels  10.5 us (8%)
    all_to_all x1, blocking collectives, local(): lax.all_to_all(coarse_parts(coded, p_tiles, p_mask), z, 0, 0, tiled=True)  32.3 us
    ppermute x3, starting transfers between devices, local(): lax.ppermute(slab, z, around(PLANES, turn))  25.8 us
    ppermute x2, starting transfers between devices, local(): before = [lax.ppermute(half, 'x', around(4, -1)) for half in own]  20.4 us
    all_to_all x1, blocking collectives, local(): coded = lax.all_to_all(coded, 'yh', 0, 0, tiled=True)  17.5 us
    ppermute x2, waiting for transfers between devices, local(): after = [lax.ppermute(half, 'x', around(4, 1)) for half in own]  7.45 us
    ppermute x1, starting transfers between devices, local(): lax.ppermute(before[1], 'x', around(4, -1))  4.32 us
    ppermute x2, starting transfers between devices, local(): after = [lax.ppermute(half, 'x', around(4, 1)) for half in own]  3.84 us
    pallas_call x1, Pallas kernels, coarse_parts(): pl.pallas_call(coarse_kernel, out_shape=jax.ShapeDtypeStruct((PLANES, COD...  3.56 us
  transfers between devices with their start and end apart: 11, of which 6 were waited for; matrix products, arithmetic and copies ran while one was open for 0% of the time, Pallas kernels for 1%

profile of v6, /device:TPU:6, one launch (start us, length us, event | category | flops | bytes accessed | tf_op | source)
XLA Modules:
  0.0 134.3 jit_solution(17563641585920819774)
XLA Ops:
  0.0 3.1 %stripes.1 = bf16[400,384]{1,0:T(8,128)(2,1)} custom-call(s32[4,16]{1,0:T(4,128)} %mask.3, bf16[768,3072]{1,0:T(8,128)(2,1)} %tiles.4), custom_call_target="tpu_custom_call" | custom-call | tf_op jit(solution)/shard_map/stripes/pallas_call | solution.py:63
  3.1 1.6 %collective-permute-start = (bf16[400,384]{1,0:T(8,128)(2,1)}, bf16[400,384]{1,0:T(8,128)(2,1)S(1)}, u32[]{:S(2)}, u32[]{:S(2)}) collective-permute-start(bf16[400,384]{1,0:T(8,128)(2,1)} %stripes.1), channel_id=1, source_target_pairs={{0,0},{1,513},{2,258},{3,771},{4,256},{5,769},{6,514},{7,3},{8,512... | collective-permute-start | bytes 921608 | tf_op jit(solution)/shard_map/ppermute | solution.py:272
  4.8 0.6 masked_operator.1
  5.4 15.0 %collective-permute-start.3 = (bf16[384,384]{1,0:T(8,128)(2,1)S(1)}, bf16[384,384]{1,0:T(8,128)(2,1)S(1)}, u32[]{:S(2)}, u32[]{:S(2)}) collective-permute-start(bf16[384,384]{1,0:T(8,128)(2,1)S(1)} %get-tuple-element.19.refs_4_), channel_id=1, source_target_pairs={{48,0},{0,16},{16,32},{32,48},{49,1},{1,17},{17,33},{33,49},{50,2}... | collective-permute-start | bytes 884744 | tf_op jit(solution)/shard_map/ppermute | solution.py:276
  20.4 1.9 %collective-permute-start.1 = (bf16[384,384]{1,0:T(8,128)(2,1)S(1)}, bf16[384,384]{1,0:T(8,128)(2,1)S(1)}, u32[]{:S(2)}, u32[]{:S(2)}) collective-permute-start(bf16[384,384]{1,0:T(8,128)(2,1)S(1)} %get-tuple-element.19.refs_4_), channel_id=1, source_target_pairs={{16,0},{32,16},{48,32},{0,48},{17,1},{33,17},{49,33},{1,49},{18,2}... | collective-permute-start | bytes 884744 | tf_op jit(solution)/shard_map/ppermute | solution.py:275
  22.3 0.0 slice-start.1
  22.4 0.0 copy-start.1
  22.4 5.4 %collective-permute-start.4 = (bf16[384,384]{1,0:T(8,128)(2,1)S(1)}, bf16[384,384]{1,0:T(8,128)(2,1)S(1)}, u32[]{:S(2)}, u32[]{:S(2)}) collective-permute-start(bf16[384,384]{1,0:T(8,128)(2,1)S(1)} %get-tuple-element.20.refs_5_), channel_id=1, source_target_pairs={{48,0},{0,16},{16,32},{32,48},{49,1},{1,17},{17,33},{33,49},{50,2}... | collective-permute-start | bytes 884744 | tf_op jit(solution)/shard_map/ppermute | solution.py:276
  27.8 1.9 %collective-permute-start.2 = (bf16[384,384]{1,0:T(8,128)(2,1)S(1)}, bf16[384,384]{1,0:T(8,128)(2,1)S(1)}, u32[]{:S(2)}, u32[]{:S(2)}) collective-permute-start(bf16[384,384]{1,0:T(8,128)(2,1)S(1)} %get-tuple-element.20.refs_5_), channel_id=1, source_target_pairs={{16,0},{32,16},{48,32},{0,48},{17,1},{33,17},{49,33},{1,49},{18,2}... | collective-permute-start | bytes 884744 | tf_op jit(solution)/shard_map/ppermute | solution.py:275
  29.7 1.8 %collective-permute-done.1.refs_6_ = bf16[384,384]{1,0:T(8,128)(2,1)S(1)} collective-permute-done((bf16[384,384]{1,0:T(8,128)(2,1)S(1)}, bf16[384,384]{1,0:T(8,128)(2,1)S(1)}, u32[]{:S(2)}, u32[]{:S(2)}) %collective-permute-start.1) | collective-permute-done | bytes 294944 | tf_op jit(solution)/shard_map/ppermute | solution.py:275
  31.6 0.4 collective-permute-done.4.refs_11_
  32.0 5.6 %collective-permute-done.2.refs_7_ = bf16[384,384]{1,0:T(8,128)(2,1)S(1)} collective-permute-done((bf16[384,384]{1,0:T(8,128)(2,1)S(1)}, bf16[384,384]{1,0:T(8,128)(2,1)S(1)}, u32[]{:S(2)}, u32[]{:S(2)}) %collective-permute-start.2) | collective-permute-done | bytes 294944 | tf_op jit(solution)/shard_map/ppermute | solution.py:275
  37.6 0.0 collective-permute-done.refs_0_
  37.6 1.9 %collective-permute-start.7 = (bf16[400,384]{1,0:T(8,128)(2,1)S(1)}, bf16[400,384]{1,0:T(8,128)(2,1)S(1)}, u32[]{:S(2)}, u32[]{:S(2)}) collective-permute-start(bf16[400,384]{1,0:T(8,128)(2,1)S(1)} %collective-permute-done.refs_0_), channel_id=1, source_target_pairs={{960,0},{0,64},{64,128},{128,192},{192,256},{256,320},{320,384},{3... | collective-permute-start | bytes 921608 | tf_op jit(solution)/shard_map/ppermute | solution.py:279
  39.5 14.6 %collective-permute-start.6 = (bf16[400,384]{1,0:T(8,128)(2,1)S(1)}, bf16[400,384]{1,0:T(8,128)(2,1)S(1)}, u32[]{:S(2)}, u32[]{:S(2)}) collective-permute-start(bf16[400,384]{1,0:T(8,128)(2,1)S(1)} %collective-permute-done.refs_0_), channel_id=1, source_target_pairs={{128,0},{192,64},{256,128},{320,192},{384,256},{448,320},{512,384}... | collective-permute-start | bytes 921608 | tf_op jit(solution)/shard_map/ppermute | solution.py:279
  54.1 9.3 %collective-permute-start.5 = (bf16[400,384]{1,0:T(8,128)(2,1)S(1)}, bf16[400,384]{1,0:T(8,128)(2,1)S(1)}, u32[]{:S(2)}, u32[]{:S(2)}) collective-permute-start(bf16[400,384]{1,0:T(8,128)(2,1)S(1)} %collective-permute-done.refs_0_), channel_id=1, source_target_pairs={{64,0},{128,64},{192,128},{256,192},{320,256},{384,320},{448,384},... | collective-permute-start | bytes 921608 | tf_op jit(solution)/shard_map/ppermute | solution.py:279
  63.4 2.7 %collective-permute-start.8 = (bf16[384,384]{1,0:T(8,128)(2,1)S(1)}, bf16[384,384]{1,0:T(8,128)(2,1)S(1)}, u32[]{:S(2)}, u32[]{:S(2)}) collective-permute-start(bf16[384,384]{1,0:T(8,128)(2,1)S(1)} %collective-permute-done.1.refs_6_), channel_id=1, source_target_pairs={{16,0},{32,16},{48,32},{0,48},{17,1},{33,17},{49,33},{1,49},{18,2}... | collective-permute-start | bytes 884744 | tf_op jit(solution)/shard_map/ppermute | solution.py:281
  66.2 4.3 %collective-permute-start.9 = (bf16[384,384]{1,0:T(8,128)(2,1)S(1)}, bf16[384,384]{1,0:T(8,128)(2,1)S(1)}, u32[]{:S(2)}, u32[]{:S(2)}) collective-permute-start(bf16[384,384]{1,0:T(8,128)(2,1)S(1)} %collective-permute-done.4.refs_11_), channel_id=1, source_target_pairs={{48,0},{0,16},{16,32},{32,48},{49,1},{1,17},{17,33},{33,49},{50,2}... | collective-permute-start | bytes 884744 | tf_op jit(solution)/shard_map/ppermute | solution.py:282
  70.5 2.8 %collective-permute-done.8.refs_8_ = bf16[384,384]{1,0:T(8,128)(2,1)S(1)} collective-permute-done((bf16[384,384]{1,0:T(8,128)(2,1)S(1)}, bf16[384,384]{1,0:T(8,128)(2,1)S(1)}, u32[]{:S(2)}, u32[]{:S(2)}) %collective-permute-start.8) | collective-permute-done | bytes 294944 | tf_op jit(solution)/shard_map/ppermute | solution.py:281
  73.3 1.5 %collective-permute-done.9.refs_9_ = bf16[384,384]{1,0:T(8,128)(2,1)S(1)} collective-permute-done((bf16[384,384]{1,0:T(8,128)(2,1)S(1)}, bf16[384,384]{1,0:T(8,128)(2,1)S(1)}, u32[]{:S(2)}, u32[]{:S(2)}) %collective-permute-start.9) | collective-permute-done | bytes 294944 | tf_op jit(solution)/shard_map/ppermute | solution.py:282
  74.8 0.0 collective-permute-done.7.refs_3_
  74.8 0.0 collective-permute-done.6.refs_2_
  74.8 0.0 collective-permute-done.5.refs_1_
  74.8 1.1 product_for_other.1
  75.9 1.9 %collective-permute-start.10 = (f32[4,48,768]{2,1,0:T(8,128)S(1)}, f32[4,48,768]{2,1,0:T(8,128)S(1)}, u32[]{:S(2)}, u32[]{:S(2)}) collective-permute-start(f32[4,48,768]{2,1,0:T(8,128)S(1)} %product_for_other.1), channel_id=1, source_target_pairs={{0,2},{2,0},{1,3},{3,1},{4,6},{6,4},{5,7},{7,5},{8,10},{10,8},{9,1... | collective-permute-start | bytes 1769480 | tf_op jit(solution)/shard_map/ppermute | solution.py:286
  77.8 1.1 product.1.mine
  78.9 0.9 collective-permute-done.10.theirs
  79.8 0.4 encode.1
  80.2 17.5 %all_to_all.10.parts = s16[4,48,896]{2,1,0:T(8,128)(2,1)S(1)} all-to-all(s16[4,48,896]{2,1,0:T(8,128)(2,1)S(1)} %encode.1), channel_id=1, replica_groups=mesh['zh'=4,'zl'=4,'x'=4,'yh'=4,'core'=2,'yl'=2] {'yh'}, dimensions={0} | all-to-all | bytes 688128 | tf_op jit(solution)/shard_map/all_to_all | solution.py:288
  97.7 3.6 %coarse_parts.1 = s16[16,80,128]{2,1,0:T(8,128)(2,1)S(1)} custom-call(s32[4,16]{1,0:T(4,128)S(1)} %copy-done.1, s16[4,48,896]{2,1,0:T(8,128)(2,1)S(1)} %all_to_all.10.parts, bf16[768,3072]{1,0:T(8,128)(2,1)S(1)} %bitcast.3), custom_call_target="tpu_custom_call" | custom-call | tf_op jit(solution)/shard_map/coarse_parts/pallas_call | solution.py:209
  101.2 32.3 %all_to_all.11.coded = s16[16,80,128]{2,1,0:T(8,128)(2,1)S(1)} all-to-all(s16[16,80,128]{2,1,0:T(8,128)(2,1)S(1)} %coarse_parts.1), channel_id=1, replica_groups=mesh['zh'=4,'zl'=4,'x'=4,'yh'=4,'core'=2,'yl'=2] {'zh','zl'}, dimensions={0} | all-to-all | bytes 655360 | tf_op jit(solution)/shard_map/all_to_all | solution.py:289
  133.5 0.7 summed.1
  (10 shorter events, 0.0 us)
Async XLA Ops:
  0.0 4.8 %copy-start = (bf16[768,384]{1,0:T(8,128)(2,1)S(1)}, bf16[768,384]{1,0:T(8,128)(2,1)}, u32[]{:S(2)}) copy-start(bf16[768,384]{1,0:T(8,128)(2,1)} %tiles.3) | copy-start | bytes 1769476
  0.0 4.8 %copy-start.2 = (s32[4,2]{0,1:T(2,128)S(1)}, s32[4,2]{0,1:T(2,128)}, u32[]{:S(2)}) copy-start(s32[4,2]{0,1:T(2,128)} %param.6) | copy-start | bytes 100
  0.0 97.6 %slice-start = ((s8[4718592]{0:T(1024)(128)(4,1)}), s8[524288]{0:T(1024)(128)(4,1)S(1)}, s32[]{:S(2)}) async-start(s8[4718592]{0:T(1024)(128)(4,1)} %bitcast.2), calls=%async_computation.2 | async-start | bytes 1048576
  3.1 34.5 %collective-permute-start = (bf16[400,384]{1,0:T(8,128)(2,1)}, bf16[400,384]{1,0:T(8,128)(2,1)S(1)}, u32[]{:S(2)}, u32[]{:S(2)}) collective-permute-start(bf16[400,384]{1,0:T(8,128)(2,1)} %stripes.1), channel_id=1, source_target_pairs={{0,0},{1,513},{2,258},{3,771},{4,256},{5,769},{6,514},{7,3},{8,512... | collective-permute-start | bytes 921608 | tf_op jit(solution)/shard_map/ppermute | solution.py:272
  5.4 24.3 %collective-permute-start.3 = (bf16[384,384]{1,0:T(8,128)(2,1)S(1)}, bf16[384,384]{1,0:T(8,128)(2,1)S(1)}, u32[]{:S(2)}, u32[]{:S(2)}) collective-permute-start(bf16[384,384]{1,0:T(8,128)(2,1)S(1)} %get-tuple-element.19.refs_4_), channel_id=1, source_target_pairs={{48,0},{0,16},{16,32},{32,48},{49,1},{1,17},{17,33},{33,49},{50,2}... | collective-permute-start | bytes 884744 | tf_op jit(solution)/shard_map/ppermute | solution.py:276
  20.4 11.1 %collective-permute-start.1 = (bf16[384,384]{1,0:T(8,128)(2,1)S(1)}, bf16[384,384]{1,0:T(8,128)(2,1)S(1)}, u32[]{:S(2)}, u32[]{:S(2)}) collective-permute-start(bf16[384,384]{1,0:T(8,128)(2,1)S(1)} %get-tuple-element.19.refs_4_), channel_id=1, source_target_pairs={{16,0},{32,16},{48,32},{0,48},{17,1},{33,17},{49,33},{1,49},{18,2}... | collective-permute-start | bytes 884744 | tf_op jit(solution)/shard_map/ppermute | solution.py:275
  22.3 75.3 %slice-start.1 = ((s8[4718592]{0:T(1024)(128)(4,1)}), s8[4194304]{0:T(1024)(128)(4,1)S(1)}, s32[]{:S(2)}) async-start(s8[4718592]{0:T(1024)(128)(4,1)} %bitcast.2), calls=%async_computation.3 | async-start | bytes 8388608
  22.4 75.3 %copy-start.1 = (s32[4,16]{1,0:T(4,128)S(1)}, s32[4,16]{1,0:T(4,128)}, u32[]{:S(2)}) copy-start(s32[4,16]{1,0:T(4,128)} %mask.3) | copy-start | bytes 772
  22.4 9.6 %collective-permute-start.4 = (bf16[384,384]{1,0:T(8,128)(2,1)S(1)}, bf16[384,384]{1,0:T(8,128)(2,1)S(1)}, u32[]{:S(2)}, u32[]{:S(2)}) collective-permute-start(bf16[384,384]{1,0:T(8,128)(2,1)S(1)} %get-tuple-element.20.refs_5_), channel_id=1, source_target_pairs={{48,0},{0,16},{16,32},{32,48},{49,1},{1,17},{17,33},{33,49},{50,2}... | collective-permute-start | bytes 884744 | tf_op jit(solution)/shard_map/ppermute | solution.py:276
  27.8 9.8 %collective-permute-start.2 = (bf16[384,384]{1,0:T(8,128)(2,1)S(1)}, bf16[384,384]{1,0:T(8,128)(2,1)S(1)}, u32[]{:S(2)}, u32[]{:S(2)}) collective-permute-start(bf16[384,384]{1,0:T(8,128)(2,1)S(1)} %get-tuple-element.20.refs_5_), channel_id=1, source_target_pairs={{16,0},{32,16},{48,32},{0,48},{17,1},{33,17},{49,33},{1,49},{18,2}... | collective-permute-start | bytes 884744 | tf_op jit(solution)/shard_map/ppermute | solution.py:275
  37.6 37.2 %collective-permute-start.7 = (bf16[400,384]{1,0:T(8,128)(2,1)S(1)}, bf16[400,384]{1,0:T(8,128)(2,1)S(1)}, u32[]{:S(2)}, u32[]{:S(2)}) collective-permute-start(bf16[400,384]{1,0:T(8,128)(2,1)S(1)} %collective-permute-done.refs_0_), channel_id=1, source_target_pairs={{960,0},{0,64},{64,128},{128,192},{192,256},{256,320},{320,384},{3... | collective-permute-start | bytes 921608 | tf_op jit(solution)/shard_map/ppermute | solution.py:279
  39.5 35.3 %collective-permute-start.6 = (bf16[400,384]{1,0:T(8,128)(2,1)S(1)}, bf16[400,384]{1,0:T(8,128)(2,1)S(1)}, u32[]{:S(2)}, u32[]{:S(2)}) collective-permute-start(bf16[400,384]{1,0:T(8,128)(2,1)S(1)} %collective-permute-done.refs_0_), channel_id=1, source_target_pairs={{128,0},{192,64},{256,128},{320,192},{384,256},{448,320},{512,384}... | collective-permute-start | bytes 921608 | tf_op jit(solution)/shard_map/ppermute | solution.py:279
  54.1 20.7 %collective-permute-start.5 = (bf16[400,384]{1,0:T(8,128)(2,1)S(1)}, bf16[400,384]{1,0:T(8,128)(2,1)S(1)}, u32[]{:S(2)}, u32[]{:S(2)}) collective-permute-start(bf16[400,384]{1,0:T(8,128)(2,1)S(1)} %collective-permute-done.refs_0_), channel_id=1, source_target_pairs={{64,0},{128,64},{192,128},{256,192},{320,256},{384,320},{448,384},... | collective-permute-start | bytes 921608 | tf_op jit(solution)/shard_map/ppermute | solution.py:279
  63.4 9.8 %collective-permute-start.8 = (bf16[384,384]{1,0:T(8,128)(2,1)S(1)}, bf16[384,384]{1,0:T(8,128)(2,1)S(1)}, u32[]{:S(2)}, u32[]{:S(2)}) collective-permute-start(bf16[384,384]{1,0:T(8,128)(2,1)S(1)} %collective-permute-done.1.refs_6_), channel_id=1, source_target_pairs={{16,0},{32,16},{48,32},{0,48},{17,1},{33,17},{49,33},{1,49},{18,2}... | collective-permute-start | bytes 884744 | tf_op jit(solution)/shard_map/ppermute | solution.py:281
  66.2 8.6 %collective-permute-start.9 = (bf16[384,384]{1,0:T(8,128)(2,1)S(1)}, bf16[384,384]{1,0:T(8,128)(2,1)S(1)}, u32[]{:S(2)}, u32[]{:S(2)}) collective-permute-start(bf16[384,384]{1,0:T(8,128)(2,1)S(1)} %collective-permute-done.4.refs_11_), channel_id=1, source_target_pairs={{48,0},{0,16},{16,32},{32,48},{49,1},{1,17},{17,33},{33,49},{50,2}... | collective-permute-start | bytes 884744 | tf_op jit(solution)/shard_map/ppermute | solution.py:282
  75.9 3.9 %collective-permute-start.10 = (f32[4,48,768]{2,1,0:T(8,128)S(1)}, f32[4,48,768]{2,1,0:T(8,128)S(1)}, u32[]{:S(2)}, u32[]{:S(2)}) collective-permute-start(f32[4,48,768]{2,1,0:T(8,128)S(1)} %product_for_other.1), channel_id=1, source_target_pairs={{0,2},{2,0},{1,3},{3,1},{4,6},{6,4},{5,7},{7,5},{8,10},{10,8},{9,1... | collective-permute-start | bytes 1769480 | tf_op jit(solution)/shard_map/ppermute | solution.py:286

commit v7 on v6

--- a/solution.py
+++ b/solution.py
@@ -34,7 +34,8 @@
 
 
 def stripes_kernel(mask, tiles, out, window, arrived):
-    core, x, yl = lax.axis_index("core"), lax.axis_index("x"), lax.axis_index("yl")
+    core, x = lax.axis_index("core"), lax.axis_index("x")
+    yl, _ = y_target(lax.axis_index("zl"), lax.axis_index("yh"), lax.axis_index("yl"))
     copies = []
     for n in range(2):
         rows = pl.ds(pl.multiple_of(core * HALF, HALF), HALF)
@@ -102,13 +103,12 @@
 
 def product_kernel(other, *refs):
     slabs, blocks, out, columns = refs[:4], refs[4:12], refs[12], refs[13]
-    x, zl, yh = lax.axis_index("x"), lax.axis_index("zl"), lax.axis_index("yh")
-    first = zl + 4 - shift(yh)
+    x, zl = lax.axis_index("x"), lax.axis_index("zl")
     core = (lax.axis_index("core") + other) % 2
     for n, slab in enumerate(slabs):
         for y in range(4):
             rows = pl.ds(pl.multiple_of((2 * y + core) * WIDE, WIDE), WIDE)
-            columns[(first + n) % 4, y * WIDE : (y + 1) * WIDE] = slab[rows, :]
+            columns[(zl + n) % 4, y * WIDE : (y + 1) * WIDE] = slab[rows, :]
     for half in range(2):
         total = dot_last(columns[x], blocks[half][...])
         for n in range(1, 4):
@@ -249,16 +249,19 @@
     )(coded)
 
 
-def shift(yh):
-    return yh // 2 * 2
+def y_target(zl, yh, yl):
+    turn = (2 * yh + yl + 8 - 2 * zl) % 8
+    far = (turn + 3) // 4 % 2
+    return far, far * (turn - 1) + (1 - far) * ((8 - turn) % 8)
 
 
 def spread():
     pairs = []
     for source in range(4**3 * 4):
         zh, zl, yh, core, yl = source // 64, source // 16 % 4, source // 4 % 4, source // 2 % 2, source % 2
-        target = ((yh + core + 2 * yl) % 4 * 4 + (zh + shift(zl)) % 4) * 4 + zl
-        pairs.append((source, (target * 2 + core) * 2 + yl))
+        target_yl, rank = y_target(zl, yh, yl)
+        target = ((rank + 2 * core + zl) % 4 * 4 + zh) * 4 + zl
+        pairs.append((source, (target * 2 + core) * 2 + target_yl))
     return pairs
 
 

time: 135 us -> 129 us (0.956)
  starting transfers between devices: 60.7 us -> 53.2 us
  waiting for transfers between devices: 13.1 us -> 16.5 us
  blocking collectives: 49.8 us -> 48.1 us
    ppermute x3, starting transfers between devices: 25.8 us -> 18.3 us  [local(): lax.ppermute(slab, z, around(PLANES, turn))]
    ppermute x2, waiting for transfers between devices: 0.44 us -> 3.92 us  [local(): before = [lax.ppermute(half, 'x', around(4, -1)) for half in own]]
    ppermute x3, waiting for transfers between devices: 0.01 us -> 3.31 us  [local(): lax.ppermute(slab, z, around(PLANES, turn))]
    ppermute x2, waiting for transfers between devices: 7.45 us -> 4.2 us  [local(): after = [lax.ppermute(half, 'x', around(4, 1)) for half in own]]
  transfers between devices with their start and end apart: 11 -> 11, of which waited for: 6 -> 7; matrix products, arithmetic and copies ran while one was open for 0% -> 0% of each run, Pallas kernels for 1% -> 1%
where the time goes in v7:
time: 129 us
  starting transfers between devices  53.2 us (41%)
  blocking collectives  48.1 us (37%)
  waiting for transfers between devices  16.5 us (13%)
  Pallas kernels  10.5 us (8%)
    all_to_all x1, blocking collectives, local(): lax.all_to_all(coarse_parts(coded, p_tiles, p_mask), z, 0, 0, tiled=True)  31.2 us
    ppermute x2, starting transfers between devices, local(): before = [lax.ppermute(half, 'x', around(4, -1)) for half in own]  20.4 us
    ppermute x3, starting transfers between devices, local(): lax.ppermute(slab, z, around(PLANES, turn))  18.3 us
    all_to_all x1, blocking collectives, local(): coded = lax.all_to_all(coded, 'yh', 0, 0, tiled=True)  16.9 us
    ppermute x1, starting transfers between devices, local(): lax.ppermute(before[1], 'x', around(4, -1))  5.13 us
    ppermute x2, waiting for transfers between devices, local(): after = [lax.ppermute(half, 'x', around(4, 1)) for half in own]  4.2 us
    ppermute x2, waiting for transfers between devices, local(): before = [lax.ppermute(half, 'x', around(4, -1)) for half in own]  3.92 us
    ppermute x2, starting transfers between devices, local(): after = [lax.ppermute(half, 'x', around(4, 1)) for half in own]  3.84 us
  transfers between devices with their start and end apart: 11, of which 7 were waited for; matrix products, arithmetic and copies ran while one was open for 0% of the time, Pallas kernels for 1%

profile of v7, /device:TPU:6, one launch (start us, length us, event | category | flops | bytes accessed | tf_op | source)
XLA Modules:
  0.0 128.6 jit_solution(3632915050801045576)
XLA Ops:
  0.0 3.1 %stripes.1 = bf16[400,384]{1,0:T(8,128)(2,1)} custom-call(s32[4,16]{1,0:T(4,128)} %mask.3, bf16[768,3072]{1,0:T(8,128)(2,1)} %tiles.4), custom_call_target="tpu_custom_call" | custom-call | tf_op jit(solution)/shard_map/stripes/pallas_call | solution.py:64
  3.1 1.6 %collective-permute-start = (bf16[400,384]{1,0:T(8,128)(2,1)}, bf16[400,384]{1,0:T(8,128)(2,1)S(1)}, u32[]{:S(2)}, u32[]{:S(2)}) collective-permute-start(bf16[400,384]{1,0:T(8,128)(2,1)} %stripes.1), channel_id=1, source_target_pairs={{0,0},{1,1},{2,514},{3,515},{4,257},{5,513},{6,771},{7,3},{8,769},... | collective-permute-start | bytes 921608 | tf_op jit(solution)/shard_map/ppermute | solution.py:275
  4.8 0.6 masked_operator.1
  5.4 15.0 %collective-permute-start.3 = (bf16[384,384]{1,0:T(8,128)(2,1)S(1)}, bf16[384,384]{1,0:T(8,128)(2,1)S(1)}, u32[]{:S(2)}, u32[]{:S(2)}) collective-permute-start(bf16[384,384]{1,0:T(8,128)(2,1)S(1)} %get-tuple-element.19.refs_4_), channel_id=1, source_target_pairs={{48,0},{0,16},{16,32},{32,48},{49,1},{1,17},{17,33},{33,49},{50,2}... | collective-permute-start | bytes 884744 | tf_op jit(solution)/shard_map/ppermute | solution.py:279
  20.4 1.9 %collective-permute-start.1 = (bf16[384,384]{1,0:T(8,128)(2,1)S(1)}, bf16[384,384]{1,0:T(8,128)(2,1)S(1)}, u32[]{:S(2)}, u32[]{:S(2)}) collective-permute-start(bf16[384,384]{1,0:T(8,128)(2,1)S(1)} %get-tuple-element.19.refs_4_), channel_id=1, source_target_pairs={{16,0},{32,16},{48,32},{0,48},{17,1},{33,17},{49,33},{1,49},{18,2}... | collective-permute-start | bytes 884744 | tf_op jit(solution)/shard_map/ppermute | solution.py:278
  22.4 0.0 slice-start.1
  22.4 0.0 copy-start.1
  22.4 5.4 %collective-permute-start.4 = (bf16[384,384]{1,0:T(8,128)(2,1)S(1)}, bf16[384,384]{1,0:T(8,128)(2,1)S(1)}, u32[]{:S(2)}, u32[]{:S(2)}) collective-permute-start(bf16[384,384]{1,0:T(8,128)(2,1)S(1)} %get-tuple-element.20.refs_5_), channel_id=1, source_target_pairs={{48,0},{0,16},{16,32},{32,48},{49,1},{1,17},{17,33},{33,49},{50,2}... | collective-permute-start | bytes 884744 | tf_op jit(solution)/shard_map/ppermute | solution.py:279
  27.8 1.9 %collective-permute-start.2 = (bf16[384,384]{1,0:T(8,128)(2,1)S(1)}, bf16[384,384]{1,0:T(8,128)(2,1)S(1)}, u32[]{:S(2)}, u32[]{:S(2)}) collective-permute-start(bf16[384,384]{1,0:T(8,128)(2,1)S(1)} %get-tuple-element.20.refs_5_), channel_id=1, source_target_pairs={{16,0},{32,16},{48,32},{0,48},{17,1},{33,17},{49,33},{1,49},{18,2}... | collective-permute-start | bytes 884744 | tf_op jit(solution)/shard_map/ppermute | solution.py:278
  29.7 0.0 collective-permute-done.3.refs_10_
  29.7 0.5 collective-permute-done.1.refs_6_
  30.3 3.9 %collective-permute-done.4.refs_11_ = bf16[384,384]{1,0:T(8,128)(2,1)S(1)} collective-permute-done((bf16[384,384]{1,0:T(8,128)(2,1)S(1)}, bf16[384,384]{1,0:T(8,128)(2,1)S(1)}, u32[]{:S(2)}, u32[]{:S(2)}) %collective-permute-start.4) | collective-permute-done | bytes 294944 | tf_op jit(solution)/shard_map/ppermute | solution.py:279
  34.2 3.7 %collective-permute-done.2.refs_7_ = bf16[384,384]{1,0:T(8,128)(2,1)S(1)} collective-permute-done((bf16[384,384]{1,0:T(8,128)(2,1)S(1)}, bf16[384,384]{1,0:T(8,128)(2,1)S(1)}, u32[]{:S(2)}, u32[]{:S(2)}) %collective-permute-start.2) | collective-permute-done | bytes 294944 | tf_op jit(solution)/shard_map/ppermute | solution.py:278
  37.8 0.0 collective-permute-done.refs_0_
  37.8 9.1 %collective-permute-start.7 = (bf16[400,384]{1,0:T(8,128)(2,1)S(1)}, bf16[400,384]{1,0:T(8,128)(2,1)S(1)}, u32[]{:S(2)}, u32[]{:S(2)}) collective-permute-start(bf16[400,384]{1,0:T(8,128)(2,1)S(1)} %collective-permute-done.refs_0_), channel_id=1, source_target_pairs={{960,0},{0,64},{64,128},{128,192},{192,256},{256,320},{320,384},{3... | collective-permute-start | bytes 921608 | tf_op jit(solution)/shard_map/ppermute | solution.py:282
  47.0 5.3 %collective-permute-start.6 = (bf16[400,384]{1,0:T(8,128)(2,1)S(1)}, bf16[400,384]{1,0:T(8,128)(2,1)S(1)}, u32[]{:S(2)}, u32[]{:S(2)}) collective-permute-start(bf16[400,384]{1,0:T(8,128)(2,1)S(1)} %collective-permute-done.refs_0_), channel_id=1, source_target_pairs={{128,0},{192,64},{256,128},{320,192},{384,256},{448,320},{512,384}... | collective-permute-start | bytes 921608 | tf_op jit(solution)/shard_map/ppermute | solution.py:282
  52.3 3.9 %collective-permute-start.5 = (bf16[400,384]{1,0:T(8,128)(2,1)S(1)}, bf16[400,384]{1,0:T(8,128)(2,1)S(1)}, u32[]{:S(2)}, u32[]{:S(2)}) collective-permute-start(bf16[400,384]{1,0:T(8,128)(2,1)S(1)} %collective-permute-done.refs_0_), channel_id=1, source_target_pairs={{64,0},{128,64},{192,128},{256,192},{320,256},{384,320},{448,384},... | collective-permute-start | bytes 921608 | tf_op jit(solution)/shard_map/ppermute | solution.py:282
  56.2 1.9 %collective-permute-start.8 = (bf16[384,384]{1,0:T(8,128)(2,1)S(1)}, bf16[384,384]{1,0:T(8,128)(2,1)S(1)}, u32[]{:S(2)}, u32[]{:S(2)}) collective-permute-start(bf16[384,384]{1,0:T(8,128)(2,1)S(1)} %collective-permute-done.1.refs_6_), channel_id=1, source_target_pairs={{16,0},{32,16},{48,32},{0,48},{17,1},{33,17},{49,33},{1,49},{18,2}... | collective-permute-start | bytes 884744 | tf_op jit(solution)/shard_map/ppermute | solution.py:284
  58.1 5.1 %collective-permute-start.9 = (bf16[384,384]{1,0:T(8,128)(2,1)S(1)}, bf16[384,384]{1,0:T(8,128)(2,1)S(1)}, u32[]{:S(2)}, u32[]{:S(2)}) collective-permute-start(bf16[384,384]{1,0:T(8,128)(2,1)S(1)} %collective-permute-done.4.refs_11_), channel_id=1, source_target_pairs={{48,0},{0,16},{16,32},{32,48},{49,1},{1,17},{17,33},{33,49},{50,2}... | collective-permute-start | bytes 884744 | tf_op jit(solution)/shard_map/ppermute | solution.py:285
  63.3 2.8 %collective-permute-done.8.refs_8_ = bf16[384,384]{1,0:T(8,128)(2,1)S(1)} collective-permute-done((bf16[384,384]{1,0:T(8,128)(2,1)S(1)}, bf16[384,384]{1,0:T(8,128)(2,1)S(1)}, u32[]{:S(2)}, u32[]{:S(2)}) %collective-permute-start.8) | collective-permute-done | bytes 294944 | tf_op jit(solution)/shard_map/ppermute | solution.py:284
  66.0 1.5 %collective-permute-done.9.refs_9_ = bf16[384,384]{1,0:T(8,128)(2,1)S(1)} collective-permute-done((bf16[384,384]{1,0:T(8,128)(2,1)S(1)}, bf16[384,384]{1,0:T(8,128)(2,1)S(1)}, u32[]{:S(2)}, u32[]{:S(2)}) %collective-permute-start.9) | collective-permute-done | bytes 294944 | tf_op jit(solution)/shard_map/ppermute | solution.py:285
  67.5 0.0 collective-permute-done.7.refs_3_
  67.5 3.3 %collective-permute-done.5.refs_1_ = bf16[400,384]{1,0:T(8,128)(2,1)S(1)} collective-permute-done((bf16[400,384]{1,0:T(8,128)(2,1)S(1)}, bf16[400,384]{1,0:T(8,128)(2,1)S(1)}, u32[]{:S(2)}, u32[]{:S(2)}) %collective-permute-start.5) | collective-permute-done | bytes 307232 | tf_op jit(solution)/shard_map/ppermute | solution.py:282
  70.8 1.1 product_for_other.1
  71.9 2.0 %collective-permute-start.10 = (f32[4,48,768]{2,1,0:T(8,128)S(1)}, f32[4,48,768]{2,1,0:T(8,128)S(1)}, u32[]{:S(2)}, u32[]{:S(2)}) collective-permute-start(f32[4,48,768]{2,1,0:T(8,128)S(1)} %product_for_other.1), channel_id=1, source_target_pairs={{0,2},{2,0},{1,3},{3,1},{4,6},{6,4},{5,7},{7,5},{8,10},{10,8},{9,1... | collective-permute-start | bytes 1769480 | tf_op jit(solution)/shard_map/ppermute | solution.py:289
  73.8 1.1 product.1.mine
  74.9 0.8 collective-permute-done.10.theirs
  75.8 0.4 encode.1
  76.1 16.9 %all_to_all.10.parts = s16[4,48,896]{2,1,0:T(8,128)(2,1)S(1)} all-to-all(s16[4,48,896]{2,1,0:T(8,128)(2,1)S(1)} %encode.1), channel_id=1, replica_groups=mesh['zh'=4,'zl'=4,'x'=4,'yh'=4,'core'=2,'yl'=2] {'yh'}, dimensions={0} | all-to-all | bytes 688128 | tf_op jit(solution)/shard_map/all_to_all | solution.py:291
  93.1 3.6 %coarse_parts.1 = s16[16,80,128]{2,1,0:T(8,128)(2,1)S(1)} custom-call(s32[4,16]{1,0:T(4,128)S(1)} %copy-done.1, s16[4,48,896]{2,1,0:T(8,128)(2,1)S(1)} %all_to_all.10.parts, bf16[768,3072]{1,0:T(8,128)(2,1)S(1)} %bitcast.3), custom_call_target="tpu_custom_call" | custom-call | tf_op jit(solution)/shard_map/coarse_parts/pallas_call | solution.py:209
  96.6 31.2 %all_to_all.11.coded = s16[16,80,128]{2,1,0:T(8,128)(2,1)S(1)} all-to-all(s16[16,80,128]{2,1,0:T(8,128)(2,1)S(1)} %coarse_parts.1), channel_id=1, replica_groups=mesh['zh'=4,'zl'=4,'x'=4,'yh'=4,'core'=2,'yl'=2] {'zh','zl'}, dimensions={0} | all-to-all | bytes 655360 | tf_op jit(solution)/shard_map/all_to_all | solution.py:292
  127.8 0.7 summed.1
  (10 shorter events, 0.0 us)
Async XLA Ops:
  0.0 4.8 %copy-start = (bf16[768,384]{1,0:T(8,128)(2,1)S(1)}, bf16[768,384]{1,0:T(8,128)(2,1)}, u32[]{:S(2)}) copy-start(bf16[768,384]{1,0:T(8,128)(2,1)} %tiles.3) | copy-start | bytes 1769476
  0.0 4.8 %copy-start.2 = (s32[4,2]{0,1:T(2,128)S(1)}, s32[4,2]{0,1:T(2,128)}, u32[]{:S(2)}) copy-start(s32[4,2]{0,1:T(2,128)} %param.6) | copy-start | bytes 100
  0.0 93.0 %slice-start = ((s8[4718592]{0:T(1024)(128)(4,1)}), s8[524288]{0:T(1024)(128)(4,1)S(1)}, s32[]{:S(2)}) async-start(s8[4718592]{0:T(1024)(128)(4,1)} %bitcast.2), calls=%async_computation.2 | async-start | bytes 1048576
  3.1 34.7 %collective-permute-start = (bf16[400,384]{1,0:T(8,128)(2,1)}, bf16[400,384]{1,0:T(8,128)(2,1)S(1)}, u32[]{:S(2)}, u32[]{:S(2)}) collective-permute-start(bf16[400,384]{1,0:T(8,128)(2,1)} %stripes.1), channel_id=1, source_target_pairs={{0,0},{1,1},{2,514},{3,515},{4,257},{5,513},{6,771},{7,3},{8,769},... | collective-permute-start | bytes 921608 | tf_op jit(solution)/shard_map/ppermute | solution.py:275
  5.4 24.3 %collective-permute-start.3 = (bf16[384,384]{1,0:T(8,128)(2,1)S(1)}, bf16[384,384]{1,0:T(8,128)(2,1)S(1)}, u32[]{:S(2)}, u32[]{:S(2)}) collective-permute-start(bf16[384,384]{1,0:T(8,128)(2,1)S(1)} %get-tuple-element.19.refs_4_), channel_id=1, source_target_pairs={{48,0},{0,16},{16,32},{32,48},{49,1},{1,17},{17,33},{33,49},{50,2}... | collective-permute-start | bytes 884744 | tf_op jit(solution)/shard_map/ppermute | solution.py:279
  20.4 9.8 %collective-permute-start.1 = (bf16[384,384]{1,0:T(8,128)(2,1)S(1)}, bf16[384,384]{1,0:T(8,128)(2,1)S(1)}, u32[]{:S(2)}, u32[]{:S(2)}) collective-permute-start(bf16[384,384]{1,0:T(8,128)(2,1)S(1)} %get-tuple-element.19.refs_4_), channel_id=1, source_target_pairs={{16,0},{32,16},{48,32},{0,48},{17,1},{33,17},{49,33},{1,49},{18,2}... | collective-permute-start | bytes 884744 | tf_op jit(solution)/shard_map/ppermute | solution.py:278
  22.4 70.7 %slice-start.1 = ((s8[4718592]{0:T(1024)(128)(4,1)}), s8[4194304]{0:T(1024)(128)(4,1)S(1)}, s32[]{:S(2)}) async-start(s8[4718592]{0:T(1024)(128)(4,1)} %bitcast.2), calls=%async_computation.3 | async-start | bytes 8388608
  22.4 70.7 %copy-start.1 = (s32[4,16]{1,0:T(4,128)S(1)}, s32[4,16]{1,0:T(4,128)}, u32[]{:S(2)}) copy-start(s32[4,16]{1,0:T(4,128)} %mask.3) | copy-start | bytes 772
  22.4 11.8 %collective-permute-start.4 = (bf16[384,384]{1,0:T(8,128)(2,1)S(1)}, bf16[384,384]{1,0:T(8,128)(2,1)S(1)}, u32[]{:S(2)}, u32[]{:S(2)}) collective-permute-start(bf16[384,384]{1,0:T(8,128)(2,1)S(1)} %get-tuple-element.20.refs_5_), channel_id=1, source_target_pairs={{48,0},{0,16},{16,32},{32,48},{49,1},{1,17},{17,33},{33,49},{50,2}... | collective-permute-start | bytes 884744 | tf_op jit(solution)/shard_map/ppermute | solution.py:279
  27.8 10.1 %collective-permute-start.2 = (bf16[384,384]{1,0:T(8,128)(2,1)S(1)}, bf16[384,384]{1,0:T(8,128)(2,1)S(1)}, u32[]{:S(2)}, u32[]{:S(2)}) collective-permute-start(bf16[384,384]{1,0:T(8,128)(2,1)S(1)} %get-tuple-element.20.refs_5_), channel_id=1, source_target_pairs={{16,0},{32,16},{48,32},{0,48},{17,1},{33,17},{49,33},{1,49},{18,2}... | collective-permute-start | bytes 884744 | tf_op jit(solution)/shard_map/ppermute | solution.py:278
  37.8 29.6 %collective-permute-start.7 = (bf16[400,384]{1,0:T(8,128)(2,1)S(1)}, bf16[400,384]{1,0:T(8,128)(2,1)S(1)}, u32[]{:S(2)}, u32[]{:S(2)}) collective-permute-start(bf16[400,384]{1,0:T(8,128)(2,1)S(1)} %collective-permute-done.refs_0_), channel_id=1, source_target_pairs={{960,0},{0,64},{64,128},{128,192},{192,256},{256,320},{320,384},{3... | collective-permute-start | bytes 921608 | tf_op jit(solution)/shard_map/ppermute | solution.py:282
  47.0 20.5 %collective-permute-start.6 = (bf16[400,384]{1,0:T(8,128)(2,1)S(1)}, bf16[400,384]{1,0:T(8,128)(2,1)S(1)}, u32[]{:S(2)}, u32[]{:S(2)}) collective-permute-start(bf16[400,384]{1,0:T(8,128)(2,1)S(1)} %collective-permute-done.refs_0_), channel_id=1, source_target_pairs={{128,0},{192,64},{256,128},{320,192},{384,256},{448,320},{512,384}... | collective-permute-start | bytes 921608 | tf_op jit(solution)/shard_map/ppermute | solution.py:282
  52.3 18.5 %collective-permute-start.5 = (bf16[400,384]{1,0:T(8,128)(2,1)S(1)}, bf16[400,384]{1,0:T(8,128)(2,1)S(1)}, u32[]{:S(2)}, u32[]{:S(2)}) collective-permute-start(bf16[400,384]{1,0:T(8,128)(2,1)S(1)} %collective-permute-done.refs_0_), channel_id=1, source_target_pairs={{64,0},{128,64},{192,128},{256,192},{320,256},{384,320},{448,384},... | collective-permute-start | bytes 921608 | tf_op jit(solution)/shard_map/ppermute | solution.py:282
  56.2 9.8 %collective-permute-start.8 = (bf16[384,384]{1,0:T(8,128)(2,1)S(1)}, bf16[384,384]{1,0:T(8,128)(2,1)S(1)}, u32[]{:S(2)}, u32[]{:S(2)}) collective-permute-start(bf16[384,384]{1,0:T(8,128)(2,1)S(1)} %collective-permute-done.1.refs_6_), channel_id=1, source_target_pairs={{16,0},{32,16},{48,32},{0,48},{17,1},{33,17},{49,33},{1,49},{18,2}... | collective-permute-start | bytes 884744 | tf_op jit(solution)/shard_map/ppermute | solution.py:284
  58.1 9.4 %collective-permute-start.9 = (bf16[384,384]{1,0:T(8,128)(2,1)S(1)}, bf16[384,384]{1,0:T(8,128)(2,1)S(1)}, u32[]{:S(2)}, u32[]{:S(2)}) collective-permute-start(bf16[384,384]{1,0:T(8,128)(2,1)S(1)} %collective-permute-done.4.refs_11_), channel_id=1, source_target_pairs={{48,0},{0,16},{16,32},{32,48},{49,1},{1,17},{17,33},{33,49},{50,2}... | collective-permute-start | bytes 884744 | tf_op jit(solution)/shard_map/ppermute | solution.py:285
  71.9 3.9 %collective-permute-start.10 = (f32[4,48,768]{2,1,0:T(8,128)S(1)}, f32[4,48,768]{2,1,0:T(8,128)S(1)}, u32[]{:S(2)}, u32[]{:S(2)}) collective-permute-start(f32[4,48,768]{2,1,0:T(8,128)S(1)} %product_for_other.1), channel_id=1, source_target_pairs={{0,2},{2,0},{1,3},{3,1},{4,6},{6,4},{5,7},{7,5},{8,10},{10,8},{9,1... | collective-permute-start | bytes 1769480 | tf_op jit(solution)/shard_map/ppermute | solution.py:289

commit v8 on v7

--- a/solution.py
+++ b/solution.py
@@ -20,7 +20,7 @@
 LEAST = 1e-33
 CODED = 80
 VMEM = 16 * 1024 * 1024
-MOST_VMEM = 62 * 1024 * 1024
+MOST_VMEM = 57 * 1024 * 1024
 F32 = jnp.float32
 BF16 = jnp.bfloat16
 
@@ -33,9 +33,11 @@
     return lax.dot_general(left, right, (((1,), (1,)), ((), ())), preferred_element_type=F32)
 
 
-def stripes_kernel(mask, tiles, out, window, arrived):
+def stripes_kernel(mask_in, tiles, out, window, mask, arrived, mask_arrived):
     core, x = lax.axis_index("core"), lax.axis_index("x")
     yl, _ = y_target(lax.axis_index("zl"), lax.axis_index("yh"), lax.axis_index("yl"))
+    mask_copy = pltpu.make_async_copy(mask_in, mask, mask_arrived)
+    mask_copy.start()
     copies = []
     for n in range(2):
         rows = pl.ds(pl.multiple_of(core * HALF, HALF), HALF)
@@ -48,6 +50,7 @@
     pick = jnp.concatenate(picks, axis=0)
     fine = lax.broadcasted_iota(jnp.int32, (1, HALF), 1)
     out[8 * WIDE :, :] = jnp.zeros((EMPTY, HALF), BF16)
+    mask_copy.wait()
     for n in range(2):
         copies[n].wait()
         picked = dot_last(pick, window[n])
@@ -64,9 +67,14 @@
     return pl.pallas_call(
         stripes_kernel,
         out_shape=jax.ShapeDtypeStruct((8 * WIDE + EMPTY, HALF), BF16),
-        in_specs=[pl.BlockSpec(memory_space=pltpu.SMEM), pl.BlockSpec(memory_space=pltpu.HBM)],
+        in_specs=[pl.BlockSpec(memory_space=pl.ANY)] * 2,
         out_specs=pl.BlockSpec(memory_space=pltpu.VMEM),
-        scratch_shapes=[pltpu.VMEM((2, HALF, HALF), BF16), pltpu.SemaphoreType.DMA((2,))],
+        scratch_shapes=[
+            pltpu.VMEM((2, HALF, HALF), BF16),
+            pltpu.SMEM(p_mask.shape, jnp.int32),
+            pltpu.SemaphoreType.DMA((2,)),
+            pltpu.SemaphoreType.DMA,
+        ],
         compiler_params=pltpu.CompilerParams(vmem_limit_bytes=MOST_VMEM),
         name="stripes",
     )(p_mask, p_tiles)
@@ -269,6 +277,13 @@
     return [((i + near) % size, i) for i in range(size)]
 
 
+def two_away():
+    near = [2, -2]
+    return [
+        ((i + near[core]) % PLANES * 2 + core, i * 2 + core) for i in range(PLANES) for core in range(2)
+    ]
+
+
 def local(a_tiles, p_tiles, a_mask, p_mask):
     z = ("zh", "zl")
     mine = stripes(p_tiles, p_mask)
@@ -279,7 +294,8 @@
     before = [lax.ppermute(half, "x", around(4, -1)) for half in own]
 
     slab, own, after, before = lax.optimization_barrier((slab, own, after, before))
-    slabs = [slab] + [lax.ppermute(slab, z, around(PLANES, turn)) for turn in (1, 2, -1)]
+    above, below = [lax.ppermute(slab, z, around(PLANES, turn)) for turn in (1, -1)]
+    slabs = [slab, above, lax.ppermute(slab, z + ("core",), two_away()), below]
     across = [
         lax.ppermute(after[0], "x", around(4, 1)),
         lax.ppermute(before[1], "x", around(4, -1)),

time: 129 us -> 125 us (0.969); the launches traced: 129 us -> 123 us
  waiting for transfers between devices: 16.5 us -> 13.5 us
  blocking collectives: 48.1 us -> 45.9 us
    ppermute x0 -> x1, starting transfers between devices: none -> 5.31 us  [local(): slabs = [slab, above, lax.ppermute(slab, z + ('core',), two_away()), below]]
    ppermute x3 -> x2, starting transfers between devices: 18.3 us -> 13 us  [local(): lax.ppermute(slab, z, around(PLANES, turn))]
    all_to_all x1, blocking collectives: 31.2 us -> 26 us  [local(): lax.all_to_all(coarse_parts(coded, p_tiles, p_mask), z, 0, 0, tiled=True)]
    ppermute x3 -> x2, waiting for transfers between devices: 3.31 us -> 0.01 us  [local(): lax.ppermute(slab, z, around(PLANES, turn))]
    all_to_all x1, blocking collectives: 16.9 us -> 20 us  [local(): coded = lax.all_to_all(coded, 'yh', 0, 0, tiled=True)]
  transfers between devices with their start and end apart: 11 -> 11, of which waited for: 7 -> 6; matrix products, arithmetic and copies ran while one was open for 0% -> 0% of each run, Pallas kernels for 1% -> 1%
where the time goes in v8:
time: 125 us; the launch traced here: 123 us
  starting transfers between devices  53.2 us (43%)
  blocking collectives  45.9 us (37%)
  waiting for transfers between devices  13.5 us (11%)
  Pallas kernels  9.8 us (8%)
    all_to_all x1, blocking collectives, local(): lax.all_to_all(coarse_parts(coded, p_tiles, p_mask), z, 0, 0, tiled=True)  26 us
    ppermute x2, starting transfers between devices, local(): before = [lax.ppermute(half, 'x', around(4, -1)) for half in own]  20.4 us
    all_to_all x1, blocking collectives, local(): coded = lax.all_to_all(coded, 'yh', 0, 0, tiled=True)  20 us
    ppermute x2, starting transfers between devices, local(): lax.ppermute(slab, z, around(PLANES, turn))  13 us
    ppermute x1, starting transfers between devices, local(): slabs = [slab, above, lax.ppermute(slab, z + ('core',), two_away()), below]  5.31 us
    ppermute x1, starting transfers between devices, local(): lax.ppermute(before[1], 'x', around(4, -1))  5.13 us
    ppermute x2, waiting for transfers between devices, local(): after = [lax.ppermute(half, 'x', around(4, 1)) for half in own]  4.2 us
    ppermute x2, waiting for transfers between devices, local(): before = [lax.ppermute(half, 'x', around(4, -1)) for half in own]  3.92 us
  transfers between devices with their start and end apart: 11, of which 6 were waited for; matrix products, arithmetic and copies ran while one was open for 0% of the time, Pallas kernels for 1%

profile of v8, /device:TPU:6, one launch (start us, length us, event | category | flops | bytes accessed | tf_op | source)
XLA Modules:
  0.0 122.6 jit_solution(15592691079051805201)
XLA Ops:
  0.0 2.4 %stripes.1 = bf16[400,384]{1,0:T(8,128)(2,1)} custom-call(s32[4,16]{1,0:T(4,128)} %mask.1, bf16[768,3072]{1,0:T(8,128)(2,1)} %tiles.4), custom_call_target="tpu_custom_call" | custom-call | tf_op jit(solution)/shard_map/stripes/pallas_call | solution.py:67
  2.4 1.6 %collective-permute-start = (bf16[400,384]{1,0:T(8,128)(2,1)}, bf16[400,384]{1,0:T(8,128)(2,1)S(1)}, u32[]{:S(2)}, u32[]{:S(2)}) collective-permute-start(bf16[400,384]{1,0:T(8,128)(2,1)} %stripes.1), channel_id=1, source_target_pairs={{0,0},{1,1},{2,514},{3,515},{4,257},{5,513},{6,771},{7,3},{8,769},... | collective-permute-start | bytes 921608 | tf_op jit(solution)/shard_map/ppermute | solution.py:290
  4.0 0.6 masked_operator.1
  4.7 15.0 %collective-permute-start.3 = (bf16[384,384]{1,0:T(8,128)(2,1)S(1)}, bf16[384,384]{1,0:T(8,128)(2,1)S(1)}, u32[]{:S(2)}, u32[]{:S(2)}) collective-permute-start(bf16[384,384]{1,0:T(8,128)(2,1)S(1)} %get-tuple-element.19.refs_4_), channel_id=1, source_target_pairs={{48,0},{0,16},{16,32},{32,48},{49,1},{1,17},{17,33},{33,49},{50,2}... | collective-permute-start | bytes 884744 | tf_op jit(solution)/shard_map/ppermute | solution.py:294
  19.7 1.9 %collective-permute-start.1 = (bf16[384,384]{1,0:T(8,128)(2,1)S(1)}, bf16[384,384]{1,0:T(8,128)(2,1)S(1)}, u32[]{:S(2)}, u32[]{:S(2)}) collective-permute-start(bf16[384,384]{1,0:T(8,128)(2,1)S(1)} %get-tuple-element.19.refs_4_), channel_id=1, source_target_pairs={{16,0},{32,16},{48,32},{0,48},{17,1},{33,17},{49,33},{1,49},{18,2}... | collective-permute-start | bytes 884744 | tf_op jit(solution)/shard_map/ppermute | solution.py:293
  21.6 0.0 slice-start.1
  21.6 0.0 copy-start.1
  21.7 5.4 %collective-permute-start.4 = (bf16[384,384]{1,0:T(8,128)(2,1)S(1)}, bf16[384,384]{1,0:T(8,128)(2,1)S(1)}, u32[]{:S(2)}, u32[]{:S(2)}) collective-permute-start(bf16[384,384]{1,0:T(8,128)(2,1)S(1)} %get-tuple-element.20.refs_5_), channel_id=1, source_target_pairs={{48,0},{0,16},{16,32},{32,48},{49,1},{1,17},{17,33},{33,49},{50,2}... | collective-permute-start | bytes 884744 | tf_op jit(solution)/shard_map/ppermute | solution.py:294
  27.1 1.9 %collective-permute-start.2 = (bf16[384,384]{1,0:T(8,128)(2,1)S(1)}, bf16[384,384]{1,0:T(8,128)(2,1)S(1)}, u32[]{:S(2)}, u32[]{:S(2)}) collective-permute-start(bf16[384,384]{1,0:T(8,128)(2,1)S(1)} %get-tuple-element.20.refs_5_), channel_id=1, source_target_pairs={{16,0},{32,16},{48,32},{0,48},{17,1},{33,17},{49,33},{1,49},{18,2}... | collective-permute-start | bytes 884744 | tf_op jit(solution)/shard_map/ppermute | solution.py:293
  29.0 0.0 collective-permute-done.3.refs_10_
  29.0 0.5 collective-permute-done.1.refs_6_
  29.5 3.9 %collective-permute-done.4.refs_11_ = bf16[384,384]{1,0:T(8,128)(2,1)S(1)} collective-permute-done((bf16[384,384]{1,0:T(8,128)(2,1)S(1)}, bf16[384,384]{1,0:T(8,128)(2,1)S(1)}, u32[]{:S(2)}, u32[]{:S(2)}) %collective-permute-start.4) | collective-permute-done | bytes 294944 | tf_op jit(solution)/shard_map/ppermute | solution.py:294
  33.4 3.7 %collective-permute-done.2.refs_7_ = bf16[384,384]{1,0:T(8,128)(2,1)S(1)} collective-permute-done((bf16[384,384]{1,0:T(8,128)(2,1)S(1)}, bf16[384,384]{1,0:T(8,128)(2,1)S(1)}, u32[]{:S(2)}, u32[]{:S(2)}) %collective-permute-start.2) | collective-permute-done | bytes 294944 | tf_op jit(solution)/shard_map/ppermute | solution.py:293
  37.1 0.0 collective-permute-done.refs_0_
  37.1 9.1 %collective-permute-start.7 = (bf16[400,384]{1,0:T(8,128)(2,1)S(1)}, bf16[400,384]{1,0:T(8,128)(2,1)S(1)}, u32[]{:S(2)}, u32[]{:S(2)}) collective-permute-start(bf16[400,384]{1,0:T(8,128)(2,1)S(1)} %collective-permute-done.refs_0_), channel_id=1, source_target_pairs={{960,0},{0,64},{64,128},{128,192},{192,256},{256,320},{320,384},{3... | collective-permute-start | bytes 921608 | tf_op jit(solution)/shard_map/ppermute | solution.py:297
  46.2 5.3 %collective-permute-start.6 = (bf16[400,384]{1,0:T(8,128)(2,1)S(1)}, bf16[400,384]{1,0:T(8,128)(2,1)S(1)}, u32[]{:S(2)}, u32[]{:S(2)}) collective-permute-start(bf16[400,384]{1,0:T(8,128)(2,1)S(1)} %collective-permute-done.refs_0_), channel_id=1, source_target_pairs={{128,0},{898,2},{192,64},{962,66},{256,128},{2,130},{320,192},{66,... | collective-permute-start | bytes 921608 | tf_op jit(solution)/shard_map/ppermute | solution.py:298
  51.5 3.9 %collective-permute-start.5 = (bf16[400,384]{1,0:T(8,128)(2,1)S(1)}, bf16[400,384]{1,0:T(8,128)(2,1)S(1)}, u32[]{:S(2)}, u32[]{:S(2)}) collective-permute-start(bf16[400,384]{1,0:T(8,128)(2,1)S(1)} %collective-permute-done.refs_0_), channel_id=1, source_target_pairs={{64,0},{128,64},{192,128},{256,192},{320,256},{384,320},{448,384},... | collective-permute-start | bytes 921608 | tf_op jit(solution)/shard_map/ppermute | solution.py:297
  55.5 1.9 %collective-permute-start.8 = (bf16[384,384]{1,0:T(8,128)(2,1)S(1)}, bf16[384,384]{1,0:T(8,128)(2,1)S(1)}, u32[]{:S(2)}, u32[]{:S(2)}) collective-permute-start(bf16[384,384]{1,0:T(8,128)(2,1)S(1)} %collective-permute-done.1.refs_6_), channel_id=1, source_target_pairs={{16,0},{32,16},{48,32},{0,48},{17,1},{33,17},{49,33},{1,49},{18,2}... | collective-permute-start | bytes 884744 | tf_op jit(solution)/shard_map/ppermute | solution.py:300
  57.4 5.1 %collective-permute-start.9 = (bf16[384,384]{1,0:T(8,128)(2,1)S(1)}, bf16[384,384]{1,0:T(8,128)(2,1)S(1)}, u32[]{:S(2)}, u32[]{:S(2)}) collective-permute-start(bf16[384,384]{1,0:T(8,128)(2,1)S(1)} %collective-permute-done.4.refs_11_), channel_id=1, source_target_pairs={{48,0},{0,16},{16,32},{32,48},{49,1},{1,17},{17,33},{33,49},{50,2}... | collective-permute-start | bytes 884744 | tf_op jit(solution)/shard_map/ppermute | solution.py:301
  62.5 3.2 %collective-permute-done.8.refs_8_ = bf16[384,384]{1,0:T(8,128)(2,1)S(1)} collective-permute-done((bf16[384,384]{1,0:T(8,128)(2,1)S(1)}, bf16[384,384]{1,0:T(8,128)(2,1)S(1)}, u32[]{:S(2)}, u32[]{:S(2)}) %collective-permute-start.8) | collective-permute-done | bytes 294944 | tf_op jit(solution)/shard_map/ppermute | solution.py:300
  65.8 1.2 %collective-permute-done.9.refs_9_ = bf16[384,384]{1,0:T(8,128)(2,1)S(1)} collective-permute-done((bf16[384,384]{1,0:T(8,128)(2,1)S(1)}, bf16[384,384]{1,0:T(8,128)(2,1)S(1)}, u32[]{:S(2)}, u32[]{:S(2)}) %collective-permute-start.9) | collective-permute-done | bytes 294944 | tf_op jit(solution)/shard_map/ppermute | solution.py:301
  67.0 0.0 collective-permute-done.7.refs_3_
  67.0 0.0 collective-permute-done.6.refs_2_
  67.0 1.1 product_for_other.1
  68.1 1.9 %collective-permute-start.10 = (f32[4,48,768]{2,1,0:T(8,128)S(1)}, f32[4,48,768]{2,1,0:T(8,128)S(1)}, u32[]{:S(2)}, u32[]{:S(2)}) collective-permute-start(f32[4,48,768]{2,1,0:T(8,128)S(1)} %product_for_other.1), channel_id=1, source_target_pairs={{0,2},{2,0},{1,3},{3,1},{4,6},{6,4},{5,7},{7,5},{8,10},{10,8},{9,1... | collective-permute-start | bytes 1769480 | tf_op jit(solution)/shard_map/ppermute | solution.py:305
  70.0 1.1 product.1.mine
  71.1 0.9 collective-permute-done.10.theirs
  72.0 0.3 encode.1
  72.4 20.0 %all_to_all.10.parts = s16[4,48,896]{2,1,0:T(8,128)(2,1)S(1)} all-to-all(s16[4,48,896]{2,1,0:T(8,128)(2,1)S(1)} %encode.1), channel_id=1, replica_groups=mesh['zh'=4,'zl'=4,'x'=4,'yh'=4,'core'=2,'yl'=2] {'yh'}, dimensions={0} | all-to-all | bytes 688128 | tf_op jit(solution)/shard_map/all_to_all | solution.py:307
  92.3 3.6 %coarse_parts.1 = s16[16,80,128]{2,1,0:T(8,128)(2,1)S(1)} custom-call(s32[4,16]{1,0:T(4,128)S(1)} %copy-done.1, s16[4,48,896]{2,1,0:T(8,128)(2,1)S(1)} %all_to_all.10.parts, bf16[768,3072]{1,0:T(8,128)(2,1)S(1)} %bitcast.3), custom_call_target="tpu_custom_call" | custom-call | tf_op jit(solution)/shard_map/coarse_parts/pallas_call | solution.py:217
  95.9 26.0 %all_to_all.11.coded = s16[16,80,128]{2,1,0:T(8,128)(2,1)S(1)} all-to-all(s16[16,80,128]{2,1,0:T(8,128)(2,1)S(1)} %coarse_parts.1), channel_id=1, replica_groups=mesh['zh'=4,'zl'=4,'x'=4,'yh'=4,'core'=2,'yl'=2] {'zh','zl'}, dimensions={0} | all-to-all | bytes 655360 | tf_op jit(solution)/shard_map/all_to_all | solution.py:308
  121.9 0.7 summed.1
  (10 shorter events, 0.0 us)
Async XLA Ops:
  0.0 4.0 %copy-start = (bf16[768,384]{1,0:T(8,128)(2,1)S(1)}, bf16[768,384]{1,0:T(8,128)(2,1)}, u32[]{:S(2)}) copy-start(bf16[768,384]{1,0:T(8,128)(2,1)} %tiles.3) | copy-start | bytes 1769476
  0.0 4.0 %copy-start.2 = (s32[4,2]{0,1:T(2,128)S(1)}, s32[4,2]{0,1:T(2,128)}, u32[]{:S(2)}) copy-start(s32[4,2]{0,1:T(2,128)} %param.6) | copy-start | bytes 100
  0.0 92.3 %slice-start = ((s8[4718592]{0:T(1024)(128)(4,1)}), s8[524288]{0:T(1024)(128)(4,1)S(1)}, s32[]{:S(2)}) async-start(s8[4718592]{0:T(1024)(128)(4,1)} %bitcast.2), calls=%async_computation.2 | async-start | bytes 1048576
  2.4 34.7 %collective-permute-start = (bf16[400,384]{1,0:T(8,128)(2,1)}, bf16[400,384]{1,0:T(8,128)(2,1)S(1)}, u32[]{:S(2)}, u32[]{:S(2)}) collective-permute-start(bf16[400,384]{1,0:T(8,128)(2,1)} %stripes.1), channel_id=1, source_target_pairs={{0,0},{1,1},{2,514},{3,515},{4,257},{5,513},{6,771},{7,3},{8,769},... | collective-permute-start | bytes 921608 | tf_op jit(solution)/shard_map/ppermute | solution.py:290
  4.7 24.3 %collective-permute-start.3 = (bf16[384,384]{1,0:T(8,128)(2,1)S(1)}, bf16[384,384]{1,0:T(8,128)(2,1)S(1)}, u32[]{:S(2)}, u32[]{:S(2)}) collective-permute-start(bf16[384,384]{1,0:T(8,128)(2,1)S(1)} %get-tuple-element.19.refs_4_), channel_id=1, source_target_pairs={{48,0},{0,16},{16,32},{32,48},{49,1},{1,17},{17,33},{33,49},{50,2}... | collective-permute-start | bytes 884744 | tf_op jit(solution)/shard_map/ppermute | solution.py:294
  19.7 9.8 %collective-permute-start.1 = (bf16[384,384]{1,0:T(8,128)(2,1)S(1)}, bf16[384,384]{1,0:T(8,128)(2,1)S(1)}, u32[]{:S(2)}, u32[]{:S(2)}) collective-permute-start(bf16[384,384]{1,0:T(8,128)(2,1)S(1)} %get-tuple-element.19.refs_4_), channel_id=1, source_target_pairs={{16,0},{32,16},{48,32},{0,48},{17,1},{33,17},{49,33},{1,49},{18,2}... | collective-permute-start | bytes 884744 | tf_op jit(solution)/shard_map/ppermute | solution.py:293
  21.6 70.7 %slice-start.1 = ((s8[4718592]{0:T(1024)(128)(4,1)}), s8[4194304]{0:T(1024)(128)(4,1)S(1)}, s32[]{:S(2)}) async-start(s8[4718592]{0:T(1024)(128)(4,1)} %bitcast.2), calls=%async_computation.3 | async-start | bytes 8388608
  21.6 70.7 %copy-start.1 = (s32[4,16]{1,0:T(4,128)S(1)}, s32[4,16]{1,0:T(4,128)}, u32[]{:S(2)}) copy-start(s32[4,16]{1,0:T(4,128)} %mask.1) | copy-start | bytes 772
  21.7 11.8 %collective-permute-start.4 = (bf16[384,384]{1,0:T(8,128)(2,1)S(1)}, bf16[384,384]{1,0:T(8,128)(2,1)S(1)}, u32[]{:S(2)}, u32[]{:S(2)}) collective-permute-start(bf16[384,384]{1,0:T(8,128)(2,1)S(1)} %get-tuple-element.20.refs_5_), channel_id=1, source_target_pairs={{48,0},{0,16},{16,32},{32,48},{49,1},{1,17},{17,33},{33,49},{50,2}... | collective-permute-start | bytes 884744 | tf_op jit(solution)/shard_map/ppermute | solution.py:294
  27.1 10.1 %collective-permute-start.2 = (bf16[384,384]{1,0:T(8,128)(2,1)S(1)}, bf16[384,384]{1,0:T(8,128)(2,1)S(1)}, u32[]{:S(2)}, u32[]{:S(2)}) collective-permute-start(bf16[384,384]{1,0:T(8,128)(2,1)S(1)} %get-tuple-element.20.refs_5_), channel_id=1, source_target_pairs={{16,0},{32,16},{48,32},{0,48},{17,1},{33,17},{49,33},{1,49},{18,2}... | collective-permute-start | bytes 884744 | tf_op jit(solution)/shard_map/ppermute | solution.py:293
  37.1 29.9 %collective-permute-start.7 = (bf16[400,384]{1,0:T(8,128)(2,1)S(1)}, bf16[400,384]{1,0:T(8,128)(2,1)S(1)}, u32[]{:S(2)}, u32[]{:S(2)}) collective-permute-start(bf16[400,384]{1,0:T(8,128)(2,1)S(1)} %collective-permute-done.refs_0_), channel_id=1, source_target_pairs={{960,0},{0,64},{64,128},{128,192},{192,256},{256,320},{320,384},{3... | collective-permute-start | bytes 921608 | tf_op jit(solution)/shard_map/ppermute | solution.py:297
  46.2 20.8 %collective-permute-start.6 = (bf16[400,384]{1,0:T(8,128)(2,1)S(1)}, bf16[400,384]{1,0:T(8,128)(2,1)S(1)}, u32[]{:S(2)}, u32[]{:S(2)}) collective-permute-start(bf16[400,384]{1,0:T(8,128)(2,1)S(1)} %collective-permute-done.refs_0_), channel_id=1, source_target_pairs={{128,0},{898,2},{192,64},{962,66},{256,128},{2,130},{320,192},{66,... | collective-permute-start | bytes 921608 | tf_op jit(solution)/shard_map/ppermute | solution.py:298
  51.5 15.5 %collective-permute-start.5 = (bf16[400,384]{1,0:T(8,128)(2,1)S(1)}, bf16[400,384]{1,0:T(8,128)(2,1)S(1)}, u32[]{:S(2)}, u32[]{:S(2)}) collective-permute-start(bf16[400,384]{1,0:T(8,128)(2,1)S(1)} %collective-permute-done.refs_0_), channel_id=1, source_target_pairs={{64,0},{128,64},{192,128},{256,192},{320,256},{384,320},{448,384},... | collective-permute-start | bytes 921608 | tf_op jit(solution)/shard_map/ppermute | solution.py:297
  55.5 10.3 %collective-permute-start.8 = (bf16[384,384]{1,0:T(8,128)(2,1)S(1)}, bf16[384,384]{1,0:T(8,128)(2,1)S(1)}, u32[]{:S(2)}, u32[]{:S(2)}) collective-permute-start(bf16[384,384]{1,0:T(8,128)(2,1)S(1)} %collective-permute-done.1.refs_6_), channel_id=1, source_target_pairs={{16,0},{32,16},{48,32},{0,48},{17,1},{33,17},{49,33},{1,49},{18,2}... | collective-permute-start | bytes 884744 | tf_op jit(solution)/shard_map/ppermute | solution.py:300
  57.4 9.6 %collective-permute-start.9 = (bf16[384,384]{1,0:T(8,128)(2,1)S(1)}, bf16[384,384]{1,0:T(8,128)(2,1)S(1)}, u32[]{:S(2)}, u32[]{:S(2)}) collective-permute-start(bf16[384,384]{1,0:T(8,128)(2,1)S(1)} %collective-permute-done.4.refs_11_), channel_id=1, source_target_pairs={{48,0},{0,16},{16,32},{32,48},{49,1},{1,17},{17,33},{33,49},{50,2}... | collective-permute-start | bytes 884744 | tf_op jit(solution)/shard_map/ppermute | solution.py:301
  68.1 3.9 %collective-permute-start.10 = (f32[4,48,768]{2,1,0:T(8,128)S(1)}, f32[4,48,768]{2,1,0:T(8,128)S(1)}, u32[]{:S(2)}, u32[]{:S(2)}) collective-permute-start(f32[4,48,768]{2,1,0:T(8,128)S(1)} %product_for_other.1), channel_id=1, source_target_pairs={{0,2},{2,0},{1,3},{3,1},{4,6},{6,4},{5,7},{7,5},{8,10},{10,8},{9,1... | collective-permute-start | bytes 1769480 | tf_op jit(solution)/shard_map/ppermute | solution.py:305

commit v9 on v8

--- a/solution.py
+++ b/solution.py
@@ -293,7 +293,6 @@
     after = [lax.ppermute(half, "x", around(4, 1)) for half in own]
     before = [lax.ppermute(half, "x", around(4, -1)) for half in own]
 
-    slab, own, after, before = lax.optimization_barrier((slab, own, after, before))
     above, below = [lax.ppermute(slab, z, around(PLANES, turn)) for turn in (1, -1)]
     slabs = [slab, above, lax.ppermute(slab, z + ("core",), two_away()), below]
     across = [

time: 125 us -> 125 us (level)
  waiting for transfers between devices: 13.5 us -> 7.1 us
  starting transfers between devices: 53.2 us -> 58.4 us
  blocking collectives: 45.9 us -> 47.2 us
    ppermute x1, starting transfers between devices: 5.31 us -> 11 us  [local(): slabs = [slab, above, lax.ppermute(slab, z + ('core',), two_away()), below]]
    ppermute x2, waiting for transfers between devices: 4.2 us -> 0.01 us  [local(): after = [lax.ppermute(half, 'x', around(4, 1)) for half in own]]
    ppermute x2, waiting for transfers between devices: 3.92 us -> 0.01 us  [local(): before = [lax.ppermute(half, 'x', around(4, -1)) for half in own]]
    ppermute x1, waiting for transfers between devices: 3.22 us -> 4.7 us  [local(): lax.ppermute(after[0], 'x', around(4, 1))]
    ppermute x2, starting transfers between devices: 13 us -> 11.6 us  [local(): lax.ppermute(slab, z, around(PLANES, turn))]
  transfers between devices with their start and end apart: 11 -> 11, of which waited for: 6 -> 3; matrix products, arithmetic and copies ran while one was open for 0% -> 0% of each run, Pallas kernels for 1% -> 1%
where the time goes in v9:
time: 125 us; the launch traced here: 123 us
  starting transfers between devices  58.4 us (47%)
  blocking collectives  47.2 us (38%)
  Pallas kernels  9.8 us (8%)
  waiting for transfers between devices  7.1 us (6%)
    all_to_all x1, blocking collectives, local(): lax.all_to_all(coarse_parts(coded, p_tiles, p_mask), z, 0, 0, tiled=True)  26.1 us
    all_to_all x1, blocking collectives, local(): coded = lax.all_to_all(coded, 'yh', 0, 0, tiled=True)  21.2 us
    ppermute x2, starting transfers between devices, local(): before = [lax.ppermute(half, 'x', around(4, -1)) for half in own]  20.4 us
    ppermute x2, starting transfers between devices, local(): lax.ppermute(slab, z, around(PLANES, turn))  11.6 us
    ppermute x1, starting transfers between devices, local(): slabs = [slab, above, lax.ppermute(slab, z + ('core',), two_away()), below]  11 us
    ppermute x1, waiting for transfers between devices, local(): lax.ppermute(after[0], 'x', around(4, 1))  4.7 us
    ppermute x1, starting transfers between devices, local(): lax.ppermute(before[1], 'x', around(4, -1))  4.32 us
    ppermute x2, starting transfers between devices, local(): after = [lax.ppermute(half, 'x', around(4, 1)) for half in own]  3.84 us
  transfers between devices with their start and end apart: 11, of which 3 were waited for; matrix products, arithmetic and copies ran while one was open for 0% of the time, Pallas kernels for 1%

profile of v9, /device:TPU:6, one launch (start us, length us, event | category | flops | bytes accessed | tf_op | source)
XLA Modules:
  0.0 122.7 jit_solution(15327733014975714535)
XLA Ops:
  0.0 2.4 %stripes.1 = bf16[400,384]{1,0:T(8,128)(2,1)} custom-call(s32[4,16]{1,0:T(4,128)} %mask.1, bf16[768,3072]{1,0:T(8,128)(2,1)} %tiles.4), custom_call_target="tpu_custom_call" | custom-call | tf_op jit(solution)/shard_map/stripes/pallas_call | solution.py:67
  2.4 1.6 %collective-permute-start = (bf16[400,384]{1,0:T(8,128)(2,1)}, bf16[400,384]{1,0:T(8,128)(2,1)S(1)}, u32[]{:S(2)}, u32[]{:S(2)}) collective-permute-start(bf16[400,384]{1,0:T(8,128)(2,1)} %stripes.1), channel_id=1, source_target_pairs={{0,0},{1,1},{2,514},{3,515},{4,257},{5,513},{6,771},{7,3},{8,769},... | collective-permute-start | bytes 921608 | tf_op jit(solution)/shard_map/ppermute | solution.py:290
  4.0 0.6 masked_operator.1
  4.7 15.0 %collective-permute-start.9 = (bf16[384,384]{1,0:T(8,128)(2,1)S(1)}, bf16[384,384]{1,0:T(8,128)(2,1)S(1)}, u32[]{:S(2)}, u32[]{:S(2)}) collective-permute-start(bf16[384,384]{1,0:T(8,128)(2,1)S(1)} %get-tuple-element.9.refs_4_), channel_id=1, source_target_pairs={{48,0},{0,16},{16,32},{32,48},{49,1},{1,17},{17,33},{33,49},{50,2}... | collective-permute-start | bytes 884744 | tf_op jit(solution)/shard_map/ppermute | solution.py:294
  19.7 1.9 %collective-permute-start.4 = (bf16[384,384]{1,0:T(8,128)(2,1)S(1)}, bf16[384,384]{1,0:T(8,128)(2,1)S(1)}, u32[]{:S(2)}, u32[]{:S(2)}) collective-permute-start(bf16[384,384]{1,0:T(8,128)(2,1)S(1)} %get-tuple-element.9.refs_4_), channel_id=1, source_target_pairs={{16,0},{32,16},{48,32},{0,48},{17,1},{33,17},{49,33},{1,49},{18,2}... | collective-permute-start | bytes 884744 | tf_op jit(solution)/shard_map/ppermute | solution.py:293
  21.6 0.0 slice-start.1
  21.6 0.0 copy-start.1
  21.7 5.4 %collective-permute-start.7 = (bf16[384,384]{1,0:T(8,128)(2,1)S(1)}, bf16[384,384]{1,0:T(8,128)(2,1)S(1)}, u32[]{:S(2)}, u32[]{:S(2)}) collective-permute-start(bf16[384,384]{1,0:T(8,128)(2,1)S(1)} %get-tuple-element.10.refs_5_), channel_id=1, source_target_pairs={{48,0},{0,16},{16,32},{32,48},{49,1},{1,17},{17,33},{33,49},{50,2}... | collective-permute-start | bytes 884744 | tf_op jit(solution)/shard_map/ppermute | solution.py:294
  27.1 1.9 %collective-permute-start.5 = (bf16[384,384]{1,0:T(8,128)(2,1)S(1)}, bf16[384,384]{1,0:T(8,128)(2,1)S(1)}, u32[]{:S(2)}, u32[]{:S(2)}) collective-permute-start(bf16[384,384]{1,0:T(8,128)(2,1)S(1)} %get-tuple-element.10.refs_5_), channel_id=1, source_target_pairs={{16,0},{32,16},{48,32},{0,48},{17,1},{33,17},{49,33},{1,49},{18,2}... | collective-permute-start | bytes 884744 | tf_op jit(solution)/shard_map/ppermute | solution.py:293
  29.0 0.0 collective-permute-done.refs_0_
  29.0 9.7 %collective-permute-start.3 = (bf16[400,384]{1,0:T(8,128)(2,1)S(1)}, bf16[400,384]{1,0:T(8,128)(2,1)S(1)}, u32[]{:S(2)}, u32[]{:S(2)}) collective-permute-start(bf16[400,384]{1,0:T(8,128)(2,1)S(1)} %collective-permute-done.refs_0_), channel_id=1, source_target_pairs={{960,0},{0,64},{64,128},{128,192},{192,256},{256,320},{320,384},{3... | collective-permute-start | bytes 921608 | tf_op jit(solution)/shard_map/ppermute | solution.py:296
  38.7 0.0 collective-permute-done.9.refs_10_
  38.7 11.0 %collective-permute-start.2 = (bf16[400,384]{1,0:T(8,128)(2,1)S(1)}, bf16[400,384]{1,0:T(8,128)(2,1)S(1)}, u32[]{:S(2)}, u32[]{:S(2)}) collective-permute-start(bf16[400,384]{1,0:T(8,128)(2,1)S(1)} %collective-permute-done.refs_0_), channel_id=1, source_target_pairs={{128,0},{898,2},{192,64},{962,66},{256,128},{2,130},{320,192},{66,... | collective-permute-start | bytes 921608 | tf_op jit(solution)/shard_map/ppermute | solution.py:297
  49.7 0.0 collective-permute-done.4.refs_6_
  49.7 1.9 %collective-permute-start.1 = (bf16[400,384]{1,0:T(8,128)(2,1)S(1)}, bf16[400,384]{1,0:T(8,128)(2,1)S(1)}, u32[]{:S(2)}, u32[]{:S(2)}) collective-permute-start(bf16[400,384]{1,0:T(8,128)(2,1)S(1)} %collective-permute-done.refs_0_), channel_id=1, source_target_pairs={{64,0},{128,64},{192,128},{256,192},{320,256},{384,320},{448,384},... | collective-permute-start | bytes 921608 | tf_op jit(solution)/shard_map/ppermute | solution.py:296
  51.6 2.7 %collective-permute-start.6 = (bf16[384,384]{1,0:T(8,128)(2,1)S(1)}, bf16[384,384]{1,0:T(8,128)(2,1)S(1)}, u32[]{:S(2)}, u32[]{:S(2)}) collective-permute-start(bf16[384,384]{1,0:T(8,128)(2,1)S(1)} %collective-permute-done.4.refs_6_), channel_id=1, source_target_pairs={{16,0},{32,16},{48,32},{0,48},{17,1},{33,17},{49,33},{1,49},{18,2}... | collective-permute-start | bytes 884744 | tf_op jit(solution)/shard_map/ppermute | solution.py:299
  54.4 0.0 collective-permute-done.5.refs_7_
  54.4 4.3 %collective-permute-start.8 = (bf16[384,384]{1,0:T(8,128)(2,1)S(1)}, bf16[384,384]{1,0:T(8,128)(2,1)S(1)}, u32[]{:S(2)}, u32[]{:S(2)}) collective-permute-start(bf16[384,384]{1,0:T(8,128)(2,1)S(1)} %collective-permute-done.7.refs_11_), channel_id=1, source_target_pairs={{48,0},{0,16},{16,32},{32,48},{49,1},{1,17},{17,33},{33,49},{50,2}... | collective-permute-start | bytes 884744 | tf_op jit(solution)/shard_map/ppermute | solution.py:300
  58.7 4.7 %collective-permute-done.6.refs_8_ = bf16[384,384]{1,0:T(8,128)(2,1)S(1)} collective-permute-done((bf16[384,384]{1,0:T(8,128)(2,1)S(1)}, bf16[384,384]{1,0:T(8,128)(2,1)S(1)}, u32[]{:S(2)}, u32[]{:S(2)}) %collective-permute-start.6) | collective-permute-done | bytes 294944 | tf_op jit(solution)/shard_map/ppermute | solution.py:299
  63.4 1.9 %collective-permute-done.8.refs_9_ = bf16[384,384]{1,0:T(8,128)(2,1)S(1)} collective-permute-done((bf16[384,384]{1,0:T(8,128)(2,1)S(1)}, bf16[384,384]{1,0:T(8,128)(2,1)S(1)}, u32[]{:S(2)}, u32[]{:S(2)}) %collective-permute-start.8) | collective-permute-done | bytes 294944 | tf_op jit(solution)/shard_map/ppermute | solution.py:300
  65.3 0.0 collective-permute-done.3.refs_3_
  65.3 0.0 collective-permute-done.2.refs_2_
  65.3 0.0 collective-permute-done.1.refs_1_
  65.3 1.1 product_for_other.1
  66.3 2.8 %collective-permute-start.10 = (f32[4,48,768]{2,1,0:T(8,128)S(1)}, f32[4,48,768]{2,1,0:T(8,128)S(1)}, u32[]{:S(2)}, u32[]{:S(2)}) collective-permute-start(f32[4,48,768]{2,1,0:T(8,128)S(1)} %product_for_other.1), channel_id=1, source_target_pairs={{0,2},{2,0},{1,3},{3,1},{4,6},{6,4},{5,7},{7,5},{8,10},{10,8},{9,1... | collective-permute-start | bytes 1769480 | tf_op jit(solution)/shard_map/ppermute | solution.py:304
  69.2 1.1 product.1.mine
  70.3 0.5 collective-permute-done.10.theirs
  70.8 0.3 encode.1
  71.2 21.2 %all_to_all.10.parts = s16[4,48,896]{2,1,0:T(8,128)(2,1)S(1)} all-to-all(s16[4,48,896]{2,1,0:T(8,128)(2,1)S(1)} %encode.1), channel_id=1, replica_groups=mesh['zh'=4,'zl'=4,'x'=4,'yh'=4,'core'=2,'yl'=2] {'yh'}, dimensions={0} | all-to-all | bytes 688128 | tf_op jit(solution)/shard_map/all_to_all | solution.py:306
  92.4 3.6 %coarse_parts.1 = s16[16,80,128]{2,1,0:T(8,128)(2,1)S(1)} custom-call(s32[4,16]{1,0:T(4,128)S(1)} %copy-done.1, s16[4,48,896]{2,1,0:T(8,128)(2,1)S(1)} %all_to_all.10.parts, bf16[768,3072]{1,0:T(8,128)(2,1)S(1)} %bitcast.3), custom_call_target="tpu_custom_call" | custom-call | tf_op jit(solution)/shard_map/coarse_parts/pallas_call | solution.py:217
  95.9 26.1 %all_to_all.11.coded = s16[16,80,128]{2,1,0:T(8,128)(2,1)S(1)} all-to-all(s16[16,80,128]{2,1,0:T(8,128)(2,1)S(1)} %coarse_parts.1), channel_id=1, replica_groups=mesh['zh'=4,'zl'=4,'x'=4,'yh'=4,'core'=2,'yl'=2] {'zh','zl'}, dimensions={0} | all-to-all | bytes 655360 | tf_op jit(solution)/shard_map/all_to_all | solution.py:307
  122.0 0.7 summed.1
  (10 shorter events, 0.0 us)
Async XLA Ops:
  0.0 4.0 %copy-start = (bf16[768,384]{1,0:T(8,128)(2,1)S(1)}, bf16[768,384]{1,0:T(8,128)(2,1)}, u32[]{:S(2)}) copy-start(bf16[768,384]{1,0:T(8,128)(2,1)} %tiles.3) | copy-start | bytes 1769476
  0.0 4.0 %copy-start.2 = (s32[4,2]{0,1:T(2,128)S(1)}, s32[4,2]{0,1:T(2,128)}, u32[]{:S(2)}) copy-start(s32[4,2]{0,1:T(2,128)} %param.6) | copy-start | bytes 100
  0.0 92.4 %slice-start = ((s8[4718592]{0:T(1024)(128)(4,1)}), s8[524288]{0:T(1024)(128)(4,1)S(1)}, s32[]{:S(2)}) async-start(s8[4718592]{0:T(1024)(128)(4,1)} %bitcast.2), calls=%async_computation.2 | async-start | bytes 1048576
  2.4 26.6 %collective-permute-start = (bf16[400,384]{1,0:T(8,128)(2,1)}, bf16[400,384]{1,0:T(8,128)(2,1)S(1)}, u32[]{:S(2)}, u32[]{:S(2)}) collective-permute-start(bf16[400,384]{1,0:T(8,128)(2,1)} %stripes.1), channel_id=1, source_target_pairs={{0,0},{1,1},{2,514},{3,515},{4,257},{5,513},{6,771},{7,3},{8,769},... | collective-permute-start | bytes 921608 | tf_op jit(solution)/shard_map/ppermute | solution.py:290
  4.7 34.0 %collective-permute-start.9 = (bf16[384,384]{1,0:T(8,128)(2,1)S(1)}, bf16[384,384]{1,0:T(8,128)(2,1)S(1)}, u32[]{:S(2)}, u32[]{:S(2)}) collective-permute-start(bf16[384,384]{1,0:T(8,128)(2,1)S(1)} %get-tuple-element.9.refs_4_), channel_id=1, source_target_pairs={{48,0},{0,16},{16,32},{32,48},{49,1},{1,17},{17,33},{33,49},{50,2}... | collective-permute-start | bytes 884744 | tf_op jit(solution)/shard_map/ppermute | solution.py:294
  19.7 30.0 %collective-permute-start.4 = (bf16[384,384]{1,0:T(8,128)(2,1)S(1)}, bf16[384,384]{1,0:T(8,128)(2,1)S(1)}, u32[]{:S(2)}, u32[]{:S(2)}) collective-permute-start(bf16[384,384]{1,0:T(8,128)(2,1)S(1)} %get-tuple-element.9.refs_4_), channel_id=1, source_target_pairs={{16,0},{32,16},{48,32},{0,48},{17,1},{33,17},{49,33},{1,49},{18,2}... | collective-permute-start | bytes 884744 | tf_op jit(solution)/shard_map/ppermute | solution.py:293
  21.6 70.7 %slice-start.1 = ((s8[4718592]{0:T(1024)(128)(4,1)}), s8[4194304]{0:T(1024)(128)(4,1)S(1)}, s32[]{:S(2)}) async-start(s8[4718592]{0:T(1024)(128)(4,1)} %bitcast.2), calls=%async_computation.3 | async-start | bytes 8388608
  21.6 70.7 %copy-start.1 = (s32[4,16]{1,0:T(4,128)S(1)}, s32[4,16]{1,0:T(4,128)}, u32[]{:S(2)}) copy-start(s32[4,16]{1,0:T(4,128)} %mask.1) | copy-start | bytes 772
  21.7 30.0 %collective-permute-start.7 = (bf16[384,384]{1,0:T(8,128)(2,1)S(1)}, bf16[384,384]{1,0:T(8,128)(2,1)S(1)}, u32[]{:S(2)}, u32[]{:S(2)}) collective-permute-start(bf16[384,384]{1,0:T(8,128)(2,1)S(1)} %get-tuple-element.10.refs_5_), channel_id=1, source_target_pairs={{48,0},{0,16},{16,32},{32,48},{49,1},{1,17},{17,33},{33,49},{50,2}... | collective-permute-start | bytes 884744 | tf_op jit(solution)/shard_map/ppermute | solution.py:294
  27.1 27.3 %collective-permute-start.5 = (bf16[384,384]{1,0:T(8,128)(2,1)S(1)}, bf16[384,384]{1,0:T(8,128)(2,1)S(1)}, u32[]{:S(2)}, u32[]{:S(2)}) collective-permute-start(bf16[384,384]{1,0:T(8,128)(2,1)S(1)} %get-tuple-element.10.refs_5_), channel_id=1, source_target_pairs={{16,0},{32,16},{48,32},{0,48},{17,1},{33,17},{49,33},{1,49},{18,2}... | collective-permute-start | bytes 884744 | tf_op jit(solution)/shard_map/ppermute | solution.py:293
  29.0 36.3 %collective-permute-start.3 = (bf16[400,384]{1,0:T(8,128)(2,1)S(1)}, bf16[400,384]{1,0:T(8,128)(2,1)S(1)}, u32[]{:S(2)}, u32[]{:S(2)}) collective-permute-start(bf16[400,384]{1,0:T(8,128)(2,1)S(1)} %collective-permute-done.refs_0_), channel_id=1, source_target_pairs={{960,0},{0,64},{64,128},{128,192},{192,256},{256,320},{320,384},{3... | collective-permute-start | bytes 921608 | tf_op jit(solution)/shard_map/ppermute | solution.py:296
  38.7 26.6 %collective-permute-start.2 = (bf16[400,384]{1,0:T(8,128)(2,1)S(1)}, bf16[400,384]{1,0:T(8,128)(2,1)S(1)}, u32[]{:S(2)}, u32[]{:S(2)}) collective-permute-start(bf16[400,384]{1,0:T(8,128)(2,1)S(1)} %collective-permute-done.refs_0_), channel_id=1, source_target_pairs={{128,0},{898,2},{192,64},{962,66},{256,128},{2,130},{320,192},{66,... | collective-permute-start | bytes 921608 | tf_op jit(solution)/shard_map/ppermute | solution.py:297
  49.7 15.6 %collective-permute-start.1 = (bf16[400,384]{1,0:T(8,128)(2,1)S(1)}, bf16[400,384]{1,0:T(8,128)(2,1)S(1)}, u32[]{:S(2)}, u32[]{:S(2)}) collective-permute-start(bf16[400,384]{1,0:T(8,128)(2,1)S(1)} %collective-permute-done.refs_0_), channel_id=1, source_target_pairs={{64,0},{128,64},{192,128},{256,192},{320,256},{384,320},{448,384},... | collective-permute-start | bytes 921608 | tf_op jit(solution)/shard_map/ppermute | solution.py:296
  51.6 11.8 %collective-permute-start.6 = (bf16[384,384]{1,0:T(8,128)(2,1)S(1)}, bf16[384,384]{1,0:T(8,128)(2,1)S(1)}, u32[]{:S(2)}, u32[]{:S(2)}) collective-permute-start(bf16[384,384]{1,0:T(8,128)(2,1)S(1)} %collective-permute-done.4.refs_6_), channel_id=1, source_target_pairs={{16,0},{32,16},{48,32},{0,48},{17,1},{33,17},{49,33},{1,49},{18,2}... | collective-permute-start | bytes 884744 | tf_op jit(solution)/shard_map/ppermute | solution.py:299
  54.4 10.9 %collective-permute-start.8 = (bf16[384,384]{1,0:T(8,128)(2,1)S(1)}, bf16[384,384]{1,0:T(8,128)(2,1)S(1)}, u32[]{:S(2)}, u32[]{:S(2)}) collective-permute-start(bf16[384,384]{1,0:T(8,128)(2,1)S(1)} %collective-permute-done.7.refs_11_), channel_id=1, source_target_pairs={{48,0},{0,16},{16,32},{32,48},{49,1},{1,17},{17,33},{33,49},{50,2}... | collective-permute-start | bytes 884744 | tf_op jit(solution)/shard_map/ppermute | solution.py:300
  66.3 4.5 %collective-permute-start.10 = (f32[4,48,768]{2,1,0:T(8,128)S(1)}, f32[4,48,768]{2,1,0:T(8,128)S(1)}, u32[]{:S(2)}, u32[]{:S(2)}) collective-permute-start(f32[4,48,768]{2,1,0:T(8,128)S(1)} %product_for_other.1), channel_id=1, source_target_pairs={{0,2},{2,0},{1,3},{3,1},{4,6},{6,4},{5,7},{7,5},{8,10},{10,8},{9,1... | collective-permute-start | bytes 1769480 | tf_op jit(solution)/shard_map/ppermute | solution.py:304

commit v10 on v9

--- a/solution.py
+++ b/solution.py
@@ -18,6 +18,7 @@
 STEPS = 128.0
 EMPTY = 16
 LEAST = 1e-33
+GROUPS = ROWS // 128
 CODED = 80
 VMEM = 16 * 1024 * 1024
 MOST_VMEM = 57 * 1024 * 1024
@@ -109,6 +110,21 @@
     )(a_mask.T, a_tiles)
 
 
+def trim_kernel(padded, out):
+    out[...] = padded[: 8 * WIDE, :]
+
+
+def trim(padded):
+    return pl.pallas_call(
+        trim_kernel,
+        out_shape=jax.ShapeDtypeStruct((8 * WIDE, HALF), BF16),
+        in_specs=[pl.BlockSpec(memory_space=pltpu.VMEM)],
+        out_specs=pl.BlockSpec(memory_space=pltpu.VMEM),
+        compiler_params=params(),
+        name="trim",
+    )(padded)
+
+
 def product_kernel(other, *refs):
     slabs, blocks, out, columns = refs[:4], refs[4:12], refs[12], refs[13]
     x, zl = lax.axis_index("x"), lax.axis_index("zl")
@@ -141,23 +157,22 @@
 
 
 def encode_kernel(mine, theirs, out):
-    lane = lax.broadcasted_iota(jnp.int32, (WIDE, 128), 1)
     for n in range(4):
-        codes = jnp.zeros((WIDE, 128), F32)
-        for g in range(ROWS // 128):
+        codes = []
+        for g in range(GROUPS):
             lanes = slice(g * 128, (g + 1) * 128)
             values = mine[n, :, lanes] + theirs[n, :, lanes]
-            code = scale_code(jnp.max(jnp.abs(values), axis=1, keepdims=True))
-            values = jnp.round(values * (LIMIT * jnp.exp2(code * (-1.0 / STEPS))))
-            out[n, :, lanes] = values.astype(jnp.int32).astype(jnp.int16)
-            codes = jnp.where(lane == g, code, codes)
-        out[n, :, ROWS:] = codes.astype(jnp.int32).astype(jnp.int16)
+            codes.append(scale_code(jnp.max(jnp.abs(values), axis=0, keepdims=True)))
+            values = jnp.round(values * (LIMIT * jnp.exp2(codes[g] * (-1.0 / STEPS))))
+            out[n, g * WIDE : (g + 1) * WIDE, :] = values.astype(jnp.int32).astype(jnp.int16)
+        codes = jnp.concatenate(codes + [jnp.zeros((8 - GROUPS, 128), F32)], axis=0)
+        out[n, GROUPS * WIDE :, :] = codes.astype(jnp.int32).astype(jnp.int16)
 
 
 def encode(mine, theirs):
     return pl.pallas_call(
         encode_kernel,
-        out_shape=jax.ShapeDtypeStruct((4, WIDE, ROWS + 128), jnp.int16),
+        out_shape=jax.ShapeDtypeStruct((4, GROUPS * WIDE + 8, 128), jnp.int16),
         in_specs=[pl.BlockSpec(memory_space=pltpu.VMEM)] * 2,
         out_specs=pl.BlockSpec(memory_space=pltpu.VMEM),
         compiler_params=params(),
@@ -166,19 +181,14 @@
 
 
 def decoded_sum(coded):
-    groups = []
-    scales = [
-        jnp.exp2(coded[n, :, ROWS:].astype(jnp.int32).astype(F32) * (1.0 / STEPS)) * (1.0 / LIMIT)
-        for n in range(4)
-    ]
-    for g in range(ROWS // 128):
-        lanes = slice(g * 128, (g + 1) * 128)
-        terms = [
-            coded[n, :, lanes].astype(jnp.int32).astype(F32) * scales[n][:, g : g + 1]
-            for n in range(4)
-        ]
-        groups.append((terms[0] + terms[1]) + (terms[2] + terms[3]))
-    return jnp.concatenate(groups, axis=1)
+    total = [jnp.zeros((WIDE, 128), F32)] * GROUPS
+    for n in range(4):
+        codes = coded[n, GROUPS * WIDE :, :].astype(jnp.int32).astype(F32)
+        scales = jnp.exp2(codes * (1.0 / STEPS)) * (1.0 / LIMIT)
+        for g in range(GROUPS):
+            values = coded[n, g * WIDE : (g + 1) * WIDE, :].astype(jnp.int32).astype(F32)
+            total[g] = total[g] + values * scales[g : g + 1]
+    return jnp.concatenate(total, axis=1)
 
 
 def pack(values):
@@ -188,45 +198,36 @@
     )
 
 
-def coarse_kernel(mask, parts, tiles, out, terms, present):
-    @pl.when(pl.program_id(0) == 0)
-    def _():
-        whole = decoded_sum(parts)
-        high = whole.astype(BF16)
-        rest = whole - high.astype(F32)
-        middle = rest.astype(BF16)
-        low = (rest - middle.astype(F32)).astype(BF16)
-        terms[...] = jnp.concatenate([high, middle, low], axis=0)
-
-    first = pl.program_id(0) * (tiles.shape[1] // TILE)
-    mask_rows(lambda i, k: mask[i, k], tiles, present, first)
-    full = jnp.dot(terms[...], present[...], preferred_element_type=F32)
-    full = (full[2 * WIDE :] + full[WIDE : 2 * WIDE]) + full[:WIDE]
-    for k in range(out.shape[0]):
-        chunk = full[:, k * TILE : (k + 1) * TILE]
-        code = scale_code(jnp.max(jnp.abs(chunk), axis=0, keepdims=True))
-        factor = LIMIT * jnp.exp2(code * (-1.0 / STEPS))
-        values = pack(jnp.round(chunk * factor))
-        scales = pack(jnp.broadcast_to(code, (WIDE, TILE)))
-        coded = jnp.concatenate([values, scales[:1], scales[48:49], jnp.zeros((6, 128), F32)], axis=0)
-        out[k] = coded.astype(jnp.int32).astype(jnp.int16)
+def coarse_kernel(mask, parts, tiles, out, present):
+    whole = decoded_sum(parts)
+    high = whole.astype(BF16)
+    terms = jnp.concatenate([high, (whole - high.astype(F32)).astype(BF16)], axis=0)
+    width = present.shape[1]
+    for n in range(COARSE // width):
+        first = n * (width // TILE)
+        block = tiles.at[:, n * width : (n + 1) * width]
+        mask_rows(lambda i, k: mask[i, k], block, present, first)
+        full = jnp.dot(terms, present[...], preferred_element_type=F32)
+        full = full[:WIDE] + full[WIDE:]
+        for k in range(width // TILE):
+            chunk = full[:, k * TILE : (k + 1) * TILE]
+            code = scale_code(jnp.max(jnp.abs(chunk), axis=0, keepdims=True))
+            factor = LIMIT * jnp.exp2(code * (-1.0 / STEPS))
+            values = pack(jnp.round(chunk * factor))
+            scales = pack(jnp.broadcast_to(code, (WIDE, TILE)))
+            empty = jnp.zeros((6, 128), F32)
+            coded = jnp.concatenate([values, scales[:1], scales[48:49], empty], axis=0)
+            out[first + k] = coded.astype(jnp.int32).astype(jnp.int16)
 
 
 def coarse_parts(parts, p_tiles, p_mask):
-    width = COARSE // 4
+    vmem = pl.BlockSpec(memory_space=pltpu.VMEM)
     return pl.pallas_call(
         coarse_kernel,
         out_shape=jax.ShapeDtypeStruct((PLANES, CODED, 128), jnp.int16),
-        grid_spec=pltpu.PrefetchScalarGridSpec(
-            num_scalar_prefetch=1,
-            grid=(4,),
-            in_specs=[
-                pl.BlockSpec((4, WIDE, ROWS + 128), lambda g, mask: (0, 0, 0)),
-                pl.BlockSpec((ROWS, width), lambda g, mask: (0, g)),
-            ],
-            out_specs=pl.BlockSpec((width // TILE, CODED, 128), lambda g, mask: (g, 0, 0)),
-            scratch_shapes=[pltpu.VMEM((3 * WIDE, ROWS), BF16), pltpu.VMEM((ROWS, width), BF16)],
-        ),
+        in_specs=[pl.BlockSpec(memory_space=pltpu.SMEM), vmem, vmem],
+        out_specs=vmem,
+        scratch_shapes=[pltpu.VMEM((ROWS, COARSE // 4), BF16)],
         compiler_params=params(),
         name="coarse_parts",
     )(p_mask, parts, p_tiles)
@@ -287,7 +288,7 @@
 def local(a_tiles, p_tiles, a_mask, p_mask):
     z = ("zh", "zl")
     mine = stripes(p_tiles, p_mask)
-    slab = lax.ppermute(mine, z + ("yh", "core", "yl"), spread())
+    slab = trim(lax.ppermute(mine, z + ("yh", "core", "yl"), spread()))
     a_tiles, mine = lax.optimization_barrier((a_tiles, mine))
     own = masked_operator(a_tiles, a_mask)
     after = [lax.ppermute(half, "x", around(4, 1)) for half in own]

time: 125 us -> 120 us (0.960); the launches traced: 123 us -> 119 us
  starting transfers between devices: 58.4 us -> 53.4 us
  waiting for transfers between devices: 7.1 us -> 10.3 us
  Pallas kernels: 9.8 us -> 7.86 us
    ppermute x1, waiting for transfers between devices: 0.01 us -> 7.5 us  [local(): slabs = [slab, above, lax.ppermute(slab, z + ('core',), two_away()), below]]
    ppermute x1, starting transfers between devices: 11 us -> 3.69 us  [local(): slabs = [slab, above, lax.ppermute(slab, z + ('core',), two_away()), below]]
    ppermute x2, starting transfers between devices: 11.6 us -> 16.3 us  [local(): lax.ppermute(slab, z, around(PLANES, turn))]
    ppermute x1, waiting for transfers between devices: 4.7 us -> 0.01 us  [local(): lax.ppermute(after[0], 'x', around(4, 1))]
    all_to_all x1, blocking collectives: 26.1 us -> 29.3 us  [local(): lax.all_to_all(coarse_parts(coded, p_tiles, p_mask), z, 0, 0, tiled=True)]
    all_to_all x1, blocking collectives: 21.2 us -> 18 us  [local(): coded = lax.all_to_all(coded, 'yh', 0, 0, tiled=True)]
    ppermute x2, starting transfers between devices: 20.4 us -> 18.1 us  [local(): before = [lax.ppermute(half, 'x', around(4, -1)) for half in own]]
    ppermute x2, waiting for transfers between devices: 0.01 us -> 1.93 us  [local(): lax.ppermute(slab, z, around(PLANES, turn))]
where the time goes in v10:
time: 120 us; the launch traced here: 119 us
  starting transfers between devices  53.4 us (44%)
  blocking collectives  47.3 us (39%)
  waiting for transfers between devices  10.3 us (9%)
  Pallas kernels  7.86 us (7%)
    all_to_all x1, blocking collectives, local(): lax.all_to_all(coarse_parts(coded, p_tiles, p_mask), z, 0, 0, tiled=True)  29.3 us
    ppermute x2, starting transfers between devices, local(): before = [lax.ppermute(half, 'x', around(4, -1)) for half in own]  18.1 us
    all_to_all x1, blocking collectives, local(): coded = lax.all_to_all(coded, 'yh', 0, 0, tiled=True)  18 us
    ppermute x2, starting transfers between devices, local(): lax.ppermute(slab, z, around(PLANES, turn))  16.3 us
    ppermute x1, waiting for transfers between devices, local(): slabs = [slab, above, lax.ppermute(slab, z + ('core',), two_away()), below]  7.5 us
    ppermute x1, starting transfers between devices, local(): lax.ppermute(before[1], 'x', around(4, -1))  5.13 us
    ppermute x2, starting transfers between devices, local(): after = [lax.ppermute(half, 'x', around(4, 1)) for half in own]  4.66 us
    ppermute x1, starting transfers between devices, local(): slabs = [slab, above, lax.ppermute(slab, z + ('core',), two_away()), below]  3.69 us
  transfers between devices with their start and end apart: 11, of which 3 were waited for; matrix products, arithmetic and copies ran while one was open for 0% of the time, Pallas kernels for 1%

profile of v10, /device:TPU:6, one launch (start us, length us, event | category | flops | bytes accessed | tf_op | source)
XLA Modules:
  0.0 119.2 jit_solution(12125722834145213903)
XLA Ops:
  0.0 2.4 %stripes.1 = bf16[400,384]{1,0:T(8,128)(2,1)} custom-call(s32[4,16]{1,0:T(4,128)} %mask.1, bf16[768,3072]{1,0:T(8,128)(2,1)} %tiles.4), custom_call_target="tpu_custom_call" | custom-call | tf_op jit(solution)/shard_map/stripes/pallas_call | solution.py:68
  2.4 1.6 %collective-permute-start = (bf16[400,384]{1,0:T(8,128)(2,1)}, bf16[400,384]{1,0:T(8,128)(2,1)S(1)}, u32[]{:S(2)}, u32[]{:S(2)}) collective-permute-start(bf16[400,384]{1,0:T(8,128)(2,1)} %stripes.1), channel_id=1, source_target_pairs={{0,0},{1,1},{2,514},{3,515},{4,257},{5,513},{6,771},{7,3},{8,769},... | collective-permute-start | bytes 921608 | tf_op jit(solution)/shard_map/ppermute | solution.py:291
  4.0 0.6 masked_operator.1
  4.7 2.7 %collective-permute-start.4 = (bf16[384,384]{1,0:T(8,128)(2,1)S(1)}, bf16[384,384]{1,0:T(8,128)(2,1)S(1)}, u32[]{:S(2)}, u32[]{:S(2)}) collective-permute-start(bf16[384,384]{1,0:T(8,128)(2,1)S(1)} %get-tuple-element.9.refs_4_), channel_id=1, source_target_pairs={{16,0},{32,16},{48,32},{0,48},{17,1},{33,17},{49,33},{1,49},{18,2}... | collective-permute-start | bytes 884744 | tf_op jit(solution)/shard_map/ppermute | solution.py:294
  7.4 14.2 %collective-permute-start.7 = (bf16[384,384]{1,0:T(8,128)(2,1)S(1)}, bf16[384,384]{1,0:T(8,128)(2,1)S(1)}, u32[]{:S(2)}, u32[]{:S(2)}) collective-permute-start(bf16[384,384]{1,0:T(8,128)(2,1)S(1)} %get-tuple-element.10.refs_5_), channel_id=1, source_target_pairs={{48,0},{0,16},{16,32},{32,48},{49,1},{1,17},{17,33},{33,49},{50,2}... | collective-permute-start | bytes 884744 | tf_op jit(solution)/shard_map/ppermute | solution.py:295
  21.6 3.9 %collective-permute-start.9 = (bf16[384,384]{1,0:T(8,128)(2,1)S(1)}, bf16[384,384]{1,0:T(8,128)(2,1)S(1)}, u32[]{:S(2)}, u32[]{:S(2)}) collective-permute-start(bf16[384,384]{1,0:T(8,128)(2,1)S(1)} %get-tuple-element.9.refs_4_), channel_id=1, source_target_pairs={{48,0},{0,16},{16,32},{32,48},{49,1},{1,17},{17,33},{33,49},{50,2}... | collective-permute-start | bytes 884744 | tf_op jit(solution)/shard_map/ppermute | solution.py:295
  25.6 1.9 %collective-permute-start.5 = (bf16[384,384]{1,0:T(8,128)(2,1)S(1)}, bf16[384,384]{1,0:T(8,128)(2,1)S(1)}, u32[]{:S(2)}, u32[]{:S(2)}) collective-permute-start(bf16[384,384]{1,0:T(8,128)(2,1)S(1)} %get-tuple-element.10.refs_5_), channel_id=1, source_target_pairs={{16,0},{32,16},{48,32},{0,48},{17,1},{33,17},{49,33},{1,49},{18,2}... | collective-permute-start | bytes 884744 | tf_op jit(solution)/shard_map/ppermute | solution.py:294
  27.5 0.0 collective-permute-done.4.refs_6_
  27.5 1.9 %collective-permute-start.6 = (bf16[384,384]{1,0:T(8,128)(2,1)S(1)}, bf16[384,384]{1,0:T(8,128)(2,1)S(1)}, u32[]{:S(2)}, u32[]{:S(2)}) collective-permute-start(bf16[384,384]{1,0:T(8,128)(2,1)S(1)} %collective-permute-done.4.refs_6_), channel_id=1, source_target_pairs={{16,0},{32,16},{48,32},{0,48},{17,1},{33,17},{49,33},{1,49},{18,2}... | collective-permute-start | bytes 884744 | tf_op jit(solution)/shard_map/ppermute | solution.py:300
  29.4 0.0 collective-permute-done.7.refs_11_
  29.4 5.1 %collective-permute-start.8 = (bf16[384,384]{1,0:T(8,128)(2,1)S(1)}, bf16[384,384]{1,0:T(8,128)(2,1)S(1)}, u32[]{:S(2)}, u32[]{:S(2)}) collective-permute-start(bf16[384,384]{1,0:T(8,128)(2,1)S(1)} %collective-permute-done.7.refs_11_), channel_id=1, source_target_pairs={{48,0},{0,16},{16,32},{32,48},{49,1},{1,17},{17,33},{33,49},{50,2}... | collective-permute-start | bytes 884744 | tf_op jit(solution)/shard_map/ppermute | solution.py:301
  34.6 0.0 collective-permute-done.padded
  34.6 0.0 slice-start.1
  34.6 0.0 copy-start.1
  34.6 12.4 %collective-permute-start.3 = (bf16[384,384]{1,0:T(8,128)(2,1)S(1)}, bf16[384,384]{1,0:T(8,128)(2,1)S(1)}, u32[]{:S(2)}, u32[]{:S(2)}) collective-permute-start(bf16[384,384]{1,0:T(8,128)(2,1)S(1)} %trim.1.refs_0_), channel_id=1, source_target_pairs={{960,0},{0,64},{64,128},{128,192},{192,256},{256,320},{320,384},{3... | collective-permute-start | bytes 884744 | tf_op jit(solution)/shard_map/ppermute | solution.py:297
  47.1 0.0 collective-permute-done.9.refs_10_
  47.1 3.7 %collective-permute-start.2 = (bf16[384,384]{1,0:T(8,128)(2,1)S(1)}, bf16[384,384]{1,0:T(8,128)(2,1)S(1)}, u32[]{:S(2)}, u32[]{:S(2)}) collective-permute-start(bf16[384,384]{1,0:T(8,128)(2,1)S(1)} %trim.1.refs_0_), channel_id=1, source_target_pairs={{128,0},{898,2},{192,64},{962,66},{256,128},{2,130},{320,192},{66,... | collective-permute-start | bytes 884744 | tf_op jit(solution)/shard_map/ppermute | solution.py:298
  50.8 0.0 collective-permute-done.5.refs_7_
  50.8 3.9 %collective-permute-start.1 = (bf16[384,384]{1,0:T(8,128)(2,1)S(1)}, bf16[384,384]{1,0:T(8,128)(2,1)S(1)}, u32[]{:S(2)}, u32[]{:S(2)}) collective-permute-start(bf16[384,384]{1,0:T(8,128)(2,1)S(1)} %trim.1.refs_0_), channel_id=1, source_target_pairs={{64,0},{128,64},{192,128},{256,192},{320,256},{384,320},{448,384},... | collective-permute-start | bytes 884744 | tf_op jit(solution)/shard_map/ppermute | solution.py:297
  54.7 0.0 collective-permute-done.8.refs_9_
  54.7 0.0 collective-permute-done.3.refs_3_
  54.8 7.5 %collective-permute-done.2.refs_2_ = bf16[384,384]{1,0:T(8,128)(2,1)S(1)} collective-permute-done((bf16[384,384]{1,0:T(8,128)(2,1)S(1)}, bf16[384,384]{1,0:T(8,128)(2,1)S(1)}, u32[]{:S(2)}, u32[]{:S(2)}) %collective-permute-start.2) | collective-permute-done | bytes 294944 | tf_op jit(solution)/shard_map/ppermute | solution.py:298
  62.3 1.9 %collective-permute-done.1.refs_1_ = bf16[384,384]{1,0:T(8,128)(2,1)S(1)} collective-permute-done((bf16[384,384]{1,0:T(8,128)(2,1)S(1)}, bf16[384,384]{1,0:T(8,128)(2,1)S(1)}, u32[]{:S(2)}, u32[]{:S(2)}) %collective-permute-start.1) | collective-permute-done | bytes 294944 | tf_op jit(solution)/shard_map/ppermute | solution.py:297
  64.2 1.1 product_for_other.1
  65.2 1.9 %collective-permute-start.10 = (f32[4,48,768]{2,1,0:T(8,128)S(1)}, f32[4,48,768]{2,1,0:T(8,128)S(1)}, u32[]{:S(2)}, u32[]{:S(2)}) collective-permute-start(f32[4,48,768]{2,1,0:T(8,128)S(1)} %product_for_other.1), channel_id=1, source_target_pairs={{0,2},{2,0},{1,3},{3,1},{4,6},{6,4},{5,7},{7,5},{8,10},{10,8},{9,1... | collective-permute-start | bytes 1769480 | tf_op jit(solution)/shard_map/ppermute | solution.py:305
  67.2 1.1 product.1.mine
  68.2 0.9 collective-permute-done.10.theirs
  69.1 0.2 encode.1
  69.3 18.0 %all_to_all.10.parts = s16[4,296,128]{2,1,0:T(8,128)(2,1)S(1)} all-to-all(s16[4,296,128]{2,1,0:T(8,128)(2,1)S(1)} %encode.1), channel_id=1, replica_groups=mesh['zh'=4,'zl'=4,'x'=4,'yh'=4,'core'=2,'yl'=2] {'yh'}, dimensions={0} | all-to-all | bytes 606208 | tf_op jit(solution)/shard_map/all_to_all | solution.py:307
  87.3 1.8 %coarse_parts.1 = s16[16,80,128]{2,1,0:T(8,128)(2,1)S(1)} custom-call(s32[4,16]{1,0:T(4,128)S(1)} %copy-done.1, s16[4,296,128]{2,1,0:T(8,128)(2,1)S(1)} %all_to_all.10.parts, bf16[768,3072]{1,0:T(8,128)(2,1)S(1)} %bitcast.3), custom_call_target="tpu_custom_call" | custom-call | tf_op jit(solution)/shard_map/coarse_parts/pallas_call | solution.py:225
  89.1 29.3 %all_to_all.11.coded = s16[16,80,128]{2,1,0:T(8,128)(2,1)S(1)} all-to-all(s16[16,80,128]{2,1,0:T(8,128)(2,1)S(1)} %coarse_parts.1), channel_id=1, replica_groups=mesh['zh'=4,'zl'=4,'x'=4,'yh'=4,'core'=2,'yl'=2] {'zh','zl'}, dimensions={0} | all-to-all | bytes 655360 | tf_op jit(solution)/shard_map/all_to_all | solution.py:308
  118.4 0.7 summed.1
  (11 shorter events, 0.0 us)
Async XLA Ops:
  0.0 4.0 %copy-start = (bf16[768,384]{1,0:T(8,128)(2,1)S(1)}, bf16[768,384]{1,0:T(8,128)(2,1)}, u32[]{:S(2)}) copy-start(bf16[768,384]{1,0:T(8,128)(2,1)} %tiles.3) | copy-start | bytes 1769476
  0.0 4.0 %copy-start.2 = (s32[4,2]{0,1:T(2,128)S(1)}, s32[4,2]{0,1:T(2,128)}, u32[]{:S(2)}) copy-start(s32[4,2]{0,1:T(2,128)} %param.6) | copy-start | bytes 100
  0.0 87.3 %slice-start = ((s8[4718592]{0:T(1024)(128)(4,1)}), s8[524288]{0:T(1024)(128)(4,1)S(1)}, s32[]{:S(2)}) async-start(s8[4718592]{0:T(1024)(128)(4,1)} %bitcast.2), calls=%async_computation.2 | async-start | bytes 1048576
  2.4 32.2 %collective-permute-start = (bf16[400,384]{1,0:T(8,128)(2,1)}, bf16[400,384]{1,0:T(8,128)(2,1)S(1)}, u32[]{:S(2)}, u32[]{:S(2)}) collective-permute-start(bf16[400,384]{1,0:T(8,128)(2,1)} %stripes.1), channel_id=1, source_target_pairs={{0,0},{1,1},{2,514},{3,515},{4,257},{5,513},{6,771},{7,3},{8,769},... | collective-permute-start | bytes 921608 | tf_op jit(solution)/shard_map/ppermute | solution.py:291
  4.7 22.8 %collective-permute-start.4 = (bf16[384,384]{1,0:T(8,128)(2,1)S(1)}, bf16[384,384]{1,0:T(8,128)(2,1)S(1)}, u32[]{:S(2)}, u32[]{:S(2)}) collective-permute-start(bf16[384,384]{1,0:T(8,128)(2,1)S(1)} %get-tuple-element.9.refs_4_), channel_id=1, source_target_pairs={{16,0},{32,16},{48,32},{0,48},{17,1},{33,17},{49,33},{1,49},{18,2}... | collective-permute-start | bytes 884744 | tf_op jit(solution)/shard_map/ppermute | solution.py:294
  7.4 22.0 %collective-permute-start.7 = (bf16[384,384]{1,0:T(8,128)(2,1)S(1)}, bf16[384,384]{1,0:T(8,128)(2,1)S(1)}, u32[]{:S(2)}, u32[]{:S(2)}) collective-permute-start(bf16[384,384]{1,0:T(8,128)(2,1)S(1)} %get-tuple-element.10.refs_5_), channel_id=1, source_target_pairs={{48,0},{0,16},{16,32},{32,48},{49,1},{1,17},{17,33},{33,49},{50,2}... | collective-permute-start | bytes 884744 | tf_op jit(solution)/shard_map/ppermute | solution.py:295
  21.6 25.4 %collective-permute-start.9 = (bf16[384,384]{1,0:T(8,128)(2,1)S(1)}, bf16[384,384]{1,0:T(8,128)(2,1)S(1)}, u32[]{:S(2)}, u32[]{:S(2)}) collective-permute-start(bf16[384,384]{1,0:T(8,128)(2,1)S(1)} %get-tuple-element.9.refs_4_), channel_id=1, source_target_pairs={{48,0},{0,16},{16,32},{32,48},{49,1},{1,17},{17,33},{33,49},{50,2}... | collective-permute-start | bytes 884744 | tf_op jit(solution)/shard_map/ppermute | solution.py:295
  25.6 25.2 %collective-permute-start.5 = (bf16[384,384]{1,0:T(8,128)(2,1)S(1)}, bf16[384,384]{1,0:T(8,128)(2,1)S(1)}, u32[]{:S(2)}, u32[]{:S(2)}) collective-permute-start(bf16[384,384]{1,0:T(8,128)(2,1)S(1)} %get-tuple-element.10.refs_5_), channel_id=1, source_target_pairs={{16,0},{32,16},{48,32},{0,48},{17,1},{33,17},{49,33},{1,49},{18,2}... | collective-permute-start | bytes 884744 | tf_op jit(solution)/shard_map/ppermute | solution.py:294
  27.5 27.2 %collective-permute-start.6 = (bf16[384,384]{1,0:T(8,128)(2,1)S(1)}, bf16[384,384]{1,0:T(8,128)(2,1)S(1)}, u32[]{:S(2)}, u32[]{:S(2)}) collective-permute-start(bf16[384,384]{1,0:T(8,128)(2,1)S(1)} %collective-permute-done.4.refs_6_), channel_id=1, source_target_pairs={{16,0},{32,16},{48,32},{0,48},{17,1},{33,17},{49,33},{1,49},{18,2}... | collective-permute-start | bytes 884744 | tf_op jit(solution)/shard_map/ppermute | solution.py:300
  29.4 25.3 %collective-permute-start.8 = (bf16[384,384]{1,0:T(8,128)(2,1)S(1)}, bf16[384,384]{1,0:T(8,128)(2,1)S(1)}, u32[]{:S(2)}, u32[]{:S(2)}) collective-permute-start(bf16[384,384]{1,0:T(8,128)(2,1)S(1)} %collective-permute-done.7.refs_11_), channel_id=1, source_target_pairs={{48,0},{0,16},{16,32},{32,48},{49,1},{1,17},{17,33},{33,49},{50,2}... | collective-permute-start | bytes 884744 | tf_op jit(solution)/shard_map/ppermute | solution.py:301
  34.6 52.7 %slice-start.1 = ((s8[4718592]{0:T(1024)(128)(4,1)}), s8[4194304]{0:T(1024)(128)(4,1)S(1)}, s32[]{:S(2)}) async-start(s8[4718592]{0:T(1024)(128)(4,1)} %bitcast.2), calls=%async_computation.3 | async-start | bytes 8388608
  34.6 52.7 %copy-start.1 = (s32[4,16]{1,0:T(4,128)S(1)}, s32[4,16]{1,0:T(4,128)}, u32[]{:S(2)}) copy-start(s32[4,16]{1,0:T(4,128)} %mask.1) | copy-start | bytes 772
  34.6 20.1 %collective-permute-start.3 = (bf16[384,384]{1,0:T(8,128)(2,1)S(1)}, bf16[384,384]{1,0:T(8,128)(2,1)S(1)}, u32[]{:S(2)}, u32[]{:S(2)}) collective-permute-start(bf16[384,384]{1,0:T(8,128)(2,1)S(1)} %trim.1.refs_0_), channel_id=1, source_target_pairs={{960,0},{0,64},{64,128},{128,192},{192,256},{256,320},{320,384},{3... | collective-permute-start | bytes 884744 | tf_op jit(solution)/shard_map/ppermute | solution.py:297
  47.1 15.2 %collective-permute-start.2 = (bf16[384,384]{1,0:T(8,128)(2,1)S(1)}, bf16[384,384]{1,0:T(8,128)(2,1)S(1)}, u32[]{:S(2)}, u32[]{:S(2)}) collective-permute-start(bf16[384,384]{1,0:T(8,128)(2,1)S(1)} %trim.1.refs_0_), channel_id=1, source_target_pairs={{128,0},{898,2},{192,64},{962,66},{256,128},{2,130},{320,192},{66,... | collective-permute-start | bytes 884744 | tf_op jit(solution)/shard_map/ppermute | solution.py:298
  50.8 13.4 %collective-permute-start.1 = (bf16[384,384]{1,0:T(8,128)(2,1)S(1)}, bf16[384,384]{1,0:T(8,128)(2,1)S(1)}, u32[]{:S(2)}, u32[]{:S(2)}) collective-permute-start(bf16[384,384]{1,0:T(8,128)(2,1)S(1)} %trim.1.refs_0_), channel_id=1, source_target_pairs={{64,0},{128,64},{192,128},{256,192},{320,256},{384,320},{448,384},... | collective-permute-start | bytes 884744 | tf_op jit(solution)/shard_map/ppermute | solution.py:297
  65.2 3.9 %collective-permute-start.10 = (f32[4,48,768]{2,1,0:T(8,128)S(1)}, f32[4,48,768]{2,1,0:T(8,128)S(1)}, u32[]{:S(2)}, u32[]{:S(2)}) collective-permute-start(f32[4,48,768]{2,1,0:T(8,128)S(1)} %product_for_other.1), channel_id=1, source_target_pairs={{0,2},{2,0},{1,3},{3,1},{4,6},{6,4},{5,7},{7,5},{8,10},{10,8},{9,1... | collective-permute-start | bytes 1769480 | tf_op jit(solution)/shard_map/ppermute | solution.py:305

commit v11 on v10

--- a/solution.py
+++ b/solution.py
@@ -129,7 +129,7 @@
     slabs, blocks, out, columns = refs[:4], refs[4:12], refs[12], refs[13]
     x, zl = lax.axis_index("x"), lax.axis_index("zl")
     core = (lax.axis_index("core") + other) % 2
-    for n, slab in enumerate(slabs):
+    for n, slab in zip((0, 1, 3, 2), slabs):
         for y in range(4):
             rows = pl.ds(pl.multiple_of((2 * y + core) * WIDE, WIDE), WIDE)
             columns[(zl + n) % 4, y * WIDE : (y + 1) * WIDE] = slab[rows, :]
@@ -295,7 +295,7 @@
     before = [lax.ppermute(half, "x", around(4, -1)) for half in own]
 
     above, below = [lax.ppermute(slab, z, around(PLANES, turn)) for turn in (1, -1)]
-    slabs = [slab, above, lax.ppermute(slab, z + ("core",), two_away()), below]
+    slabs = [slab, above, below, lax.ppermute(slab, z + ("core",), two_away())]
     across = [
         lax.ppermute(after[0], "x", around(4, 1)),
         lax.ppermute(before[1], "x", around(4, -1)),

time: 120 us -> 117 us (0.975)
  waiting for transfers between devices: 10.3 us -> 6.17 us
  starting transfers between devices: 53.4 us -> 54.6 us
    ppermute x1, starting transfers between devices: 3.69 us -> 14.2 us  [local(): slabs = [slab, above, below, lax.ppermute(slab, z + ('core',), two_away())]]
    ppermute x2, starting transfers between devices: 16.3 us -> 7.05 us  [local(): lax.ppermute(slab, z, around(PLANES, turn))]
    ppermute x1, waiting for transfers between devices: 7.5 us -> 0.01 us  [local(): slabs = [slab, above, below, lax.ppermute(slab, z + ('core',), two_away())]]
    ppermute x2, waiting for transfers between devices: 1.93 us -> 5.25 us  [local(): lax.ppermute(slab, z, around(PLANES, turn))]
    all_to_all x1, blocking collectives: 29.3 us -> 27.3 us  [local(): lax.all_to_all(coarse_parts(coded, p_tiles, p_mask), z, 0, 0, tiled=True)]
    all_to_all x1, blocking collectives: 18 us -> 19.6 us  [local(): coded = lax.all_to_all(coded, 'yh', 0, 0, tiled=True)]
where the time goes in v11:
time: 117 us; the launch traced here: 116 us
  starting transfers between devices  54.6 us (47%)
  blocking collectives  46.9 us (40%)
  Pallas kernels  7.86 us (7%)
  waiting for transfers between devices  6.17 us (5%)
    all_to_all x1, blocking collectives, local(): lax.all_to_all(coarse_parts(coded, p_tiles, p_mask), z, 0, 0, tiled=True)  27.3 us
    all_to_all x1, blocking collectives, local(): coded = lax.all_to_all(coded, 'yh', 0, 0, tiled=True)  19.6 us
    ppermute x2, starting transfers between devices, local(): before = [lax.ppermute(half, 'x', around(4, -1)) for half in own]  18.1 us
    ppermute x1, starting transfers between devices, local(): slabs = [slab, above, below, lax.ppermute(slab, z + ('core',), two_away())]  14.2 us
    ppermute x2, starting transfers between devices, local(): lax.ppermute(slab, z, around(PLANES, turn))  7.05 us
    ppermute x2, waiting for transfers between devices, local(): lax.ppermute(slab, z, around(PLANES, turn))  5.25 us
    ppermute x1, starting transfers between devices, local(): lax.ppermute(before[1], 'x', around(4, -1))  5.13 us
    ppermute x2, starting transfers between devices, local(): after = [lax.ppermute(half, 'x', around(4, 1)) for half in own]  4.66 us
  transfers between devices with their start and end apart: 11, of which 3 were waited for; matrix products, arithmetic and copies ran while one was open for 0% of the time, Pallas kernels for 1%

profile of v11, /device:TPU:6, one launch (start us, length us, event | category | flops | bytes accessed | tf_op | source)
XLA Modules:
  0.0 115.8 jit_solution(14923853863675380851)
XLA Ops:
  0.0 2.4 %stripes.1 = bf16[400,384]{1,0:T(8,128)(2,1)} custom-call(s32[4,16]{1,0:T(4,128)} %mask.1, bf16[768,3072]{1,0:T(8,128)(2,1)} %tiles.4), custom_call_target="tpu_custom_call" | custom-call | tf_op jit(solution)/shard_map/stripes/pallas_call | solution.py:68
  2.4 1.6 %collective-permute-start = (bf16[400,384]{1,0:T(8,128)(2,1)}, bf16[400,384]{1,0:T(8,128)(2,1)S(1)}, u32[]{:S(2)}, u32[]{:S(2)}) collective-permute-start(bf16[400,384]{1,0:T(8,128)(2,1)} %stripes.1), channel_id=1, source_target_pairs={{0,0},{1,1},{2,514},{3,515},{4,257},{5,513},{6,771},{7,3},{8,769},... | collective-permute-start | bytes 921608 | tf_op jit(solution)/shard_map/ppermute | solution.py:291
  4.0 0.6 masked_operator.1
  4.7 2.7 %collective-permute-start.4 = (bf16[384,384]{1,0:T(8,128)(2,1)S(1)}, bf16[384,384]{1,0:T(8,128)(2,1)S(1)}, u32[]{:S(2)}, u32[]{:S(2)}) collective-permute-start(bf16[384,384]{1,0:T(8,128)(2,1)S(1)} %get-tuple-element.9.refs_4_), channel_id=1, source_target_pairs={{16,0},{32,16},{48,32},{0,48},{17,1},{33,17},{49,33},{1,49},{18,2}... | collective-permute-start | bytes 884744 | tf_op jit(solution)/shard_map/ppermute | solution.py:294
  7.4 14.2 %collective-permute-start.7 = (bf16[384,384]{1,0:T(8,128)(2,1)S(1)}, bf16[384,384]{1,0:T(8,128)(2,1)S(1)}, u32[]{:S(2)}, u32[]{:S(2)}) collective-permute-start(bf16[384,384]{1,0:T(8,128)(2,1)S(1)} %get-tuple-element.10.refs_5_), channel_id=1, source_target_pairs={{48,0},{0,16},{16,32},{32,48},{49,1},{1,17},{17,33},{33,49},{50,2}... | collective-permute-start | bytes 884744 | tf_op jit(solution)/shard_map/ppermute | solution.py:295
  21.6 3.9 %collective-permute-start.9 = (bf16[384,384]{1,0:T(8,128)(2,1)S(1)}, bf16[384,384]{1,0:T(8,128)(2,1)S(1)}, u32[]{:S(2)}, u32[]{:S(2)}) collective-permute-start(bf16[384,384]{1,0:T(8,128)(2,1)S(1)} %get-tuple-element.9.refs_4_), channel_id=1, source_target_pairs={{48,0},{0,16},{16,32},{32,48},{49,1},{1,17},{17,33},{33,49},{50,2}... | collective-permute-start | bytes 884744 | tf_op jit(solution)/shard_map/ppermute | solution.py:295
  25.6 1.9 %collective-permute-start.5 = (bf16[384,384]{1,0:T(8,128)(2,1)S(1)}, bf16[384,384]{1,0:T(8,128)(2,1)S(1)}, u32[]{:S(2)}, u32[]{:S(2)}) collective-permute-start(bf16[384,384]{1,0:T(8,128)(2,1)S(1)} %get-tuple-element.10.refs_5_), channel_id=1, source_target_pairs={{16,0},{32,16},{48,32},{0,48},{17,1},{33,17},{49,33},{1,49},{18,2}... | collective-permute-start | bytes 884744 | tf_op jit(solution)/shard_map/ppermute | solution.py:294
  27.5 0.0 collective-permute-done.4.refs_6_
  27.5 1.9 %collective-permute-start.6 = (bf16[384,384]{1,0:T(8,128)(2,1)S(1)}, bf16[384,384]{1,0:T(8,128)(2,1)S(1)}, u32[]{:S(2)}, u32[]{:S(2)}) collective-permute-start(bf16[384,384]{1,0:T(8,128)(2,1)S(1)} %collective-permute-done.4.refs_6_), channel_id=1, source_target_pairs={{16,0},{32,16},{48,32},{0,48},{17,1},{33,17},{49,33},{1,49},{18,2}... | collective-permute-start | bytes 884744 | tf_op jit(solution)/shard_map/ppermute | solution.py:300
  29.4 0.0 collective-permute-done.7.refs_11_
  29.4 5.1 %collective-permute-start.8 = (bf16[384,384]{1,0:T(8,128)(2,1)S(1)}, bf16[384,384]{1,0:T(8,128)(2,1)S(1)}, u32[]{:S(2)}, u32[]{:S(2)}) collective-permute-start(bf16[384,384]{1,0:T(8,128)(2,1)S(1)} %collective-permute-done.7.refs_11_), channel_id=1, source_target_pairs={{48,0},{0,16},{16,32},{32,48},{49,1},{1,17},{17,33},{33,49},{50,2}... | collective-permute-start | bytes 884744 | tf_op jit(solution)/shard_map/ppermute | solution.py:301
  34.6 0.0 collective-permute-done.padded
  34.6 0.0 slice-start.1
  34.6 0.0 copy-start.1
  34.6 14.2 %collective-permute-start.3 = (bf16[384,384]{1,0:T(8,128)(2,1)S(1)}, bf16[384,384]{1,0:T(8,128)(2,1)S(1)}, u32[]{:S(2)}, u32[]{:S(2)}) collective-permute-start(bf16[384,384]{1,0:T(8,128)(2,1)S(1)} %trim.1.refs_0_), channel_id=1, source_target_pairs={{128,0},{898,2},{192,64},{962,66},{256,128},{2,130},{320,192},{66,... | collective-permute-start | bytes 884744 | tf_op jit(solution)/shard_map/ppermute | solution.py:298
  48.8 0.0 collective-permute-done.9.refs_10_
  48.8 1.9 %collective-permute-start.2 = (bf16[384,384]{1,0:T(8,128)(2,1)S(1)}, bf16[384,384]{1,0:T(8,128)(2,1)S(1)}, u32[]{:S(2)}, u32[]{:S(2)}) collective-permute-start(bf16[384,384]{1,0:T(8,128)(2,1)S(1)} %trim.1.refs_0_), channel_id=1, source_target_pairs={{960,0},{0,64},{64,128},{128,192},{192,256},{256,320},{320,384},{3... | collective-permute-start | bytes 884744 | tf_op jit(solution)/shard_map/ppermute | solution.py:297
  50.8 0.0 collective-permute-done.5.refs_7_
  50.8 5.1 %collective-permute-start.1 = (bf16[384,384]{1,0:T(8,128)(2,1)S(1)}, bf16[384,384]{1,0:T(8,128)(2,1)S(1)}, u32[]{:S(2)}, u32[]{:S(2)}) collective-permute-start(bf16[384,384]{1,0:T(8,128)(2,1)S(1)} %trim.1.refs_0_), channel_id=1, source_target_pairs={{64,0},{128,64},{192,128},{256,192},{320,256},{384,320},{448,384},... | collective-permute-start | bytes 884744 | tf_op jit(solution)/shard_map/ppermute | solution.py:297
  55.9 0.0 collective-permute-done.6.refs_8_
  55.9 0.0 collective-permute-done.8.refs_9_
  56.0 4.3 %collective-permute-done.2.refs_2_ = bf16[384,384]{1,0:T(8,128)(2,1)S(1)} collective-permute-done((bf16[384,384]{1,0:T(8,128)(2,1)S(1)}, bf16[384,384]{1,0:T(8,128)(2,1)S(1)}, u32[]{:S(2)}, u32[]{:S(2)}) %collective-permute-start.2) | collective-permute-done | bytes 294944 | tf_op jit(solution)/shard_map/ppermute | solution.py:297
  60.3 0.9 collective-permute-done.1.refs_1_
  61.2 1.1 product_for_other.1
  62.3 1.9 %collective-permute-start.10 = (f32[4,48,768]{2,1,0:T(8,128)S(1)}, f32[4,48,768]{2,1,0:T(8,128)S(1)}, u32[]{:S(2)}, u32[]{:S(2)}) collective-permute-start(f32[4,48,768]{2,1,0:T(8,128)S(1)} %product_for_other.1), channel_id=1, source_target_pairs={{0,2},{2,0},{1,3},{3,1},{4,6},{6,4},{5,7},{7,5},{8,10},{10,8},{9,1... | collective-permute-start | bytes 1769480 | tf_op jit(solution)/shard_map/ppermute | solution.py:305
  64.2 1.1 product.1.mine
  65.3 0.9 collective-permute-done.10.theirs
  66.2 0.2 encode.1
  66.3 19.6 %all_to_all.10.parts = s16[4,296,128]{2,1,0:T(8,128)(2,1)S(1)} all-to-all(s16[4,296,128]{2,1,0:T(8,128)(2,1)S(1)} %encode.1), channel_id=1, replica_groups=mesh['zh'=4,'zl'=4,'x'=4,'yh'=4,'core'=2,'yl'=2] {'yh'}, dimensions={0} | all-to-all | bytes 606208 | tf_op jit(solution)/shard_map/all_to_all | solution.py:307
  85.9 1.8 %coarse_parts.1 = s16[16,80,128]{2,1,0:T(8,128)(2,1)S(1)} custom-call(s32[4,16]{1,0:T(4,128)S(1)} %copy-done.1, s16[4,296,128]{2,1,0:T(8,128)(2,1)S(1)} %all_to_all.10.parts, bf16[768,3072]{1,0:T(8,128)(2,1)S(1)} %bitcast.3), custom_call_target="tpu_custom_call" | custom-call | tf_op jit(solution)/shard_map/coarse_parts/pallas_call | solution.py:225
  87.7 27.3 %all_to_all.11.coded = s16[16,80,128]{2,1,0:T(8,128)(2,1)S(1)} all-to-all(s16[16,80,128]{2,1,0:T(8,128)(2,1)S(1)} %coarse_parts.1), channel_id=1, replica_groups=mesh['zh'=4,'zl'=4,'x'=4,'yh'=4,'core'=2,'yl'=2] {'zh','zl'}, dimensions={0} | all-to-all | bytes 655360 | tf_op jit(solution)/shard_map/all_to_all | solution.py:308
  115.1 0.7 summed.1
  (11 shorter events, 0.0 us)
Async XLA Ops:
  0.0 4.0 %copy-start = (bf16[768,384]{1,0:T(8,128)(2,1)S(1)}, bf16[768,384]{1,0:T(8,128)(2,1)}, u32[]{:S(2)}) copy-start(bf16[768,384]{1,0:T(8,128)(2,1)} %tiles.3) | copy-start | bytes 1769476
  0.0 4.0 %copy-start.2 = (s32[4,2]{0,1:T(2,128)S(1)}, s32[4,2]{0,1:T(2,128)}, u32[]{:S(2)}) copy-start(s32[4,2]{0,1:T(2,128)} %param.6) | copy-start | bytes 100
  0.0 85.9 %slice-start = ((s8[4718592]{0:T(1024)(128)(4,1)}), s8[524288]{0:T(1024)(128)(4,1)S(1)}, s32[]{:S(2)}) async-start(s8[4718592]{0:T(1024)(128)(4,1)} %bitcast.2), calls=%async_computation.2 | async-start | bytes 1048576
  2.4 32.2 %collective-permute-start = (bf16[400,384]{1,0:T(8,128)(2,1)}, bf16[400,384]{1,0:T(8,128)(2,1)S(1)}, u32[]{:S(2)}, u32[]{:S(2)}) collective-permute-start(bf16[400,384]{1,0:T(8,128)(2,1)} %stripes.1), channel_id=1, source_target_pairs={{0,0},{1,1},{2,514},{3,515},{4,257},{5,513},{6,771},{7,3},{8,769},... | collective-permute-start | bytes 921608 | tf_op jit(solution)/shard_map/ppermute | solution.py:291
  4.7 22.8 %collective-permute-start.4 = (bf16[384,384]{1,0:T(8,128)(2,1)S(1)}, bf16[384,384]{1,0:T(8,128)(2,1)S(1)}, u32[]{:S(2)}, u32[]{:S(2)}) collective-permute-start(bf16[384,384]{1,0:T(8,128)(2,1)S(1)} %get-tuple-element.9.refs_4_), channel_id=1, source_target_pairs={{16,0},{32,16},{48,32},{0,48},{17,1},{33,17},{49,33},{1,49},{18,2}... | collective-permute-start | bytes 884744 | tf_op jit(solution)/shard_map/ppermute | solution.py:294
  7.4 22.0 %collective-permute-start.7 = (bf16[384,384]{1,0:T(8,128)(2,1)S(1)}, bf16[384,384]{1,0:T(8,128)(2,1)S(1)}, u32[]{:S(2)}, u32[]{:S(2)}) collective-permute-start(bf16[384,384]{1,0:T(8,128)(2,1)S(1)} %get-tuple-element.10.refs_5_), channel_id=1, source_target_pairs={{48,0},{0,16},{16,32},{32,48},{49,1},{1,17},{17,33},{33,49},{50,2}... | collective-permute-start | bytes 884744 | tf_op jit(solution)/shard_map/ppermute | solution.py:295
  21.6 27.2 %collective-permute-start.9 = (bf16[384,384]{1,0:T(8,128)(2,1)S(1)}, bf16[384,384]{1,0:T(8,128)(2,1)S(1)}, u32[]{:S(2)}, u32[]{:S(2)}) collective-permute-start(bf16[384,384]{1,0:T(8,128)(2,1)S(1)} %get-tuple-element.9.refs_4_), channel_id=1, source_target_pairs={{48,0},{0,16},{16,32},{32,48},{49,1},{1,17},{17,33},{33,49},{50,2}... | collective-permute-start | bytes 884744 | tf_op jit(solution)/shard_map/ppermute | solution.py:295
  25.6 25.2 %collective-permute-start.5 = (bf16[384,384]{1,0:T(8,128)(2,1)S(1)}, bf16[384,384]{1,0:T(8,128)(2,1)S(1)}, u32[]{:S(2)}, u32[]{:S(2)}) collective-permute-start(bf16[384,384]{1,0:T(8,128)(2,1)S(1)} %get-tuple-element.10.refs_5_), channel_id=1, source_target_pairs={{16,0},{32,16},{48,32},{0,48},{17,1},{33,17},{49,33},{1,49},{18,2}... | collective-permute-start | bytes 884744 | tf_op jit(solution)/shard_map/ppermute | solution.py:294
  27.5 28.4 %collective-permute-start.6 = (bf16[384,384]{1,0:T(8,128)(2,1)S(1)}, bf16[384,384]{1,0:T(8,128)(2,1)S(1)}, u32[]{:S(2)}, u32[]{:S(2)}) collective-permute-start(bf16[384,384]{1,0:T(8,128)(2,1)S(1)} %collective-permute-done.4.refs_6_), channel_id=1, source_target_pairs={{16,0},{32,16},{48,32},{0,48},{17,1},{33,17},{49,33},{1,49},{18,2}... | collective-permute-start | bytes 884744 | tf_op jit(solution)/shard_map/ppermute | solution.py:300
  29.4 26.5 %collective-permute-start.8 = (bf16[384,384]{1,0:T(8,128)(2,1)S(1)}, bf16[384,384]{1,0:T(8,128)(2,1)S(1)}, u32[]{:S(2)}, u32[]{:S(2)}) collective-permute-start(bf16[384,384]{1,0:T(8,128)(2,1)S(1)} %collective-permute-done.7.refs_11_), channel_id=1, source_target_pairs={{48,0},{0,16},{16,32},{32,48},{49,1},{1,17},{17,33},{33,49},{50,2}... | collective-permute-start | bytes 884744 | tf_op jit(solution)/shard_map/ppermute | solution.py:301
  34.6 51.3 %slice-start.1 = ((s8[4718592]{0:T(1024)(128)(4,1)}), s8[4194304]{0:T(1024)(128)(4,1)S(1)}, s32[]{:S(2)}) async-start(s8[4718592]{0:T(1024)(128)(4,1)} %bitcast.2), calls=%async_computation.3 | async-start | bytes 8388608
  34.6 51.3 %copy-start.1 = (s32[4,16]{1,0:T(4,128)S(1)}, s32[4,16]{1,0:T(4,128)}, u32[]{:S(2)}) copy-start(s32[4,16]{1,0:T(4,128)} %mask.1) | copy-start | bytes 772
  34.6 21.3 %collective-permute-start.3 = (bf16[384,384]{1,0:T(8,128)(2,1)S(1)}, bf16[384,384]{1,0:T(8,128)(2,1)S(1)}, u32[]{:S(2)}, u32[]{:S(2)}) collective-permute-start(bf16[384,384]{1,0:T(8,128)(2,1)S(1)} %trim.1.refs_0_), channel_id=1, source_target_pairs={{128,0},{898,2},{192,64},{962,66},{256,128},{2,130},{320,192},{66,... | collective-permute-start | bytes 884744 | tf_op jit(solution)/shard_map/ppermute | solution.py:298
  48.8 11.4 %collective-permute-start.2 = (bf16[384,384]{1,0:T(8,128)(2,1)S(1)}, bf16[384,384]{1,0:T(8,128)(2,1)S(1)}, u32[]{:S(2)}, u32[]{:S(2)}) collective-permute-start(bf16[384,384]{1,0:T(8,128)(2,1)S(1)} %trim.1.refs_0_), channel_id=1, source_target_pairs={{960,0},{0,64},{64,128},{128,192},{192,256},{256,320},{320,384},{3... | collective-permute-start | bytes 884744 | tf_op jit(solution)/shard_map/ppermute | solution.py:297
  50.8 10.4 %collective-permute-start.1 = (bf16[384,384]{1,0:T(8,128)(2,1)S(1)}, bf16[384,384]{1,0:T(8,128)(2,1)S(1)}, u32[]{:S(2)}, u32[]{:S(2)}) collective-permute-start(bf16[384,384]{1,0:T(8,128)(2,1)S(1)} %trim.1.refs_0_), channel_id=1, source_target_pairs={{64,0},{128,64},{192,128},{256,192},{320,256},{384,320},{448,384},... | collective-permute-start | bytes 884744 | tf_op jit(solution)/shard_map/ppermute | solution.py:297
  62.3 3.9 %collective-permute-start.10 = (f32[4,48,768]{2,1,0:T(8,128)S(1)}, f32[4,48,768]{2,1,0:T(8,128)S(1)}, u32[]{:S(2)}, u32[]{:S(2)}) collective-permute-start(f32[4,48,768]{2,1,0:T(8,128)S(1)} %product_for_other.1), channel_id=1, source_target_pairs={{0,2},{2,0},{1,3},{3,1},{4,6},{6,4},{5,7},{7,5},{8,10},{10,8},{9,1... | collective-permute-start | bytes 1769480 | tf_op jit(solution)/shard_map/ppermute | solution.py:305

commit v12 on v11

--- a/solution.py
+++ b/solution.py
@@ -36,7 +36,7 @@
 
 def stripes_kernel(mask_in, tiles, out, window, mask, arrived, mask_arrived):
     core, x = lax.axis_index("core"), lax.axis_index("x")
-    yl, _ = y_target(lax.axis_index("zl"), lax.axis_index("yh"), lax.axis_index("yl"))
+    yl = y_target(lax.axis_index("zl"), lax.axis_index("yh"), lax.axis_index("yl"))
     mask_copy = pltpu.make_async_copy(mask_in, mask, mask_arrived)
     mask_copy.start()
     copies = []
@@ -127,12 +127,13 @@
 
 def product_kernel(other, *refs):
     slabs, blocks, out, columns = refs[:4], refs[4:12], refs[12], refs[13]
-    x, zl = lax.axis_index("x"), lax.axis_index("zl")
+    x, zl, yh = lax.axis_index("x"), lax.axis_index("zl"), lax.axis_index("yh")
     core = (lax.axis_index("core") + other) % 2
     for n, slab in zip((0, 1, 3, 2), slabs):
+        block = block_of(yh, (zl + n) % 4)
         for y in range(4):
             rows = pl.ds(pl.multiple_of((2 * y + core) * WIDE, WIDE), WIDE)
-            columns[(zl + n) % 4, y * WIDE : (y + 1) * WIDE] = slab[rows, :]
+            columns[block, y * WIDE : (y + 1) * WIDE] = slab[rows, :]
     for half in range(2):
         total = dot_last(columns[x], blocks[half][...])
         for n in range(1, 4):
@@ -258,18 +259,34 @@
     )(coded)
 
 
+PLACE = ((0, 1, 2, 3), (2, 0, 1, 3), (1, 3, 0, 2), (3, 2, 1, 0))
+TURNS = (
+    0x8D28D637, 0x778E1D82, 0xD87D2782, 0x22D4B87D,
+    0x2D8278D7, 0x727D88D2, 0x7D8E1782, 0x7872D1E8,
+    0x8D24EB17, 0xDD8722B4, 0x8D28D727, 0x82D8771E,
+    0x8728D72D, 0x72D788D2, 0x287D287D, 0xD2D78368,
+)
+
+
+def block_of(yh, zl):
+    block = jnp.int32(0)
+    for y in range(4):
+        for n in range(4):
+            block = jnp.where((yh == y) & (zl == PLACE[y][n]), n, block)
+    return block
+
+
 def y_target(zl, yh, yl):
-    turn = (2 * yh + yl + 8 - 2 * zl) % 8
-    far = (turn + 3) // 4 % 2
-    return far, far * (turn - 1) + (1 - far) * ((8 - turn) % 8)
+    return ((2 * yh + yl + 8 - 2 * zl) % 8 + 3) // 4 % 2
 
 
 def spread():
     pairs = []
     for source in range(4**3 * 4):
         zh, zl, yh, core, yl = source // 64, source // 16 % 4, source // 4 % 4, source // 2 % 2, source % 2
-        target_yl, rank = y_target(zl, yh, yl)
-        target = ((rank + 2 * core + zl) % 4 * 4 + zh) * 4 + zl
+        target_yl = y_target(zl, yh, yl)
+        turn = TURNS[zh * 4 + zl] >> (yh * 8 + yl * 4 + core * 2) & 3
+        target = (turn * 4 + PLACE[zl][zh]) * 4 + zl
         pairs.append((source, (target * 2 + core) * 2 + target_yl))
     return pairs
 

time: 117 us -> 115 us (0.983)
  blocking collectives: 46.9 us -> 41.6 us
  waiting for transfers between devices: 6.17 us -> 9.63 us
    ppermute x1, starting transfers between devices: 1.62 us -> 18.2 us  [local(): slab = trim(lax.ppermute(mine, z + ('yh', 'core', 'yl'), spread()))]
    ppermute x2, starting transfers between devices: 18.1 us -> 6.24 us  [local(): before = [lax.ppermute(half, 'x', around(4, -1)) for half in own]]
    ppermute x1, starting transfers between devices: 14.2 us -> 6.55 us  [local(): slabs = [slab, above, below, lax.ppermute(slab, z + ('core',), two_away())]]
    ppermute x1, waiting for transfers between devices: 0.01 us -> 6.41 us  [local(): slabs = [slab, above, below, lax.ppermute(slab, z + ('core',), two_away())]]
    all_to_all x1, blocking collectives: 19.6 us -> 15.5 us  [local(): coded = lax.all_to_all(coded, 'yh', 0, 0, tiled=True)]
    ppermute x2, waiting for transfers between devices: 5.25 us -> 2.28 us  [local(): lax.ppermute(slab, z, around(PLANES, turn))]
    ppermute x2, starting transfers between devices: 4.66 us -> 6.65 us  [local(): after = [lax.ppermute(half, 'x', around(4, 1)) for half in own]]
    all_to_all x1, blocking collectives: 27.3 us -> 26.1 us  [local(): lax.all_to_all(coarse_parts(coded, p_tiles, p_mask), z, 0, 0, tiled=True)]
  transfers between devices with their start and end apart: 11 -> 11, of which waited for: 3 -> 4; matrix products, arithmetic and copies ran while one was open for 0% -> 0% of each run, Pallas kernels for 1% -> 2%
where the time goes in v12:
time: 115 us; the launch traced here: 113 us
  starting transfers between devices  53.7 us (47%)
  blocking collectives  41.6 us (36%)
  waiting for transfers between devices  9.63 us (8%)
  Pallas kernels  7.92 us (7%)
    all_to_all x1, blocking collectives, local(): lax.all_to_all(coarse_parts(coded, p_tiles, p_mask), z, 0, 0, tiled=True)  26.1 us
    ppermute x1, starting transfers between devices, local(): slab = trim(lax.ppermute(mine, z + ('yh', 'core', 'yl'), spread()))  18.2 us
    all_to_all x1, blocking collectives, local(): coded = lax.all_to_all(coded, 'yh', 0, 0, tiled=True)  15.5 us
    ppermute x2, starting transfers between devices, local(): lax.ppermute(slab, z, around(PLANES, turn))  7.05 us
    ppermute x2, starting transfers between devices, local(): after = [lax.ppermute(half, 'x', around(4, 1)) for half in own]  6.65 us
    ppermute x1, starting transfers between devices, local(): slabs = [slab, above, below, lax.ppermute(slab, z + ('core',), two_away())]  6.55 us
    ppermute x1, waiting for transfers between devices, local(): slabs = [slab, above, below, lax.ppermute(slab, z + ('core',), two_away())]  6.41 us
    ppermute x2, starting transfers between devices, local(): before = [lax.ppermute(half, 'x', around(4, -1)) for half in own]  6.24 us
  transfers between devices with their start and end apart: 11, of which 4 were waited for; matrix products, arithmetic and copies ran while one was open for 0% of the time, Pallas kernels for 2%

profile of v12, /device:TPU:6, one launch (start us, length us, event | category | flops | bytes accessed | tf_op | source)
XLA Modules:
  0.0 113.0 jit_solution(5223101723555409183)
XLA Ops:
  0.0 2.4 %stripes.1 = bf16[400,384]{1,0:T(8,128)(2,1)} custom-call(s32[4,16]{1,0:T(4,128)} %mask.1, bf16[768,3072]{1,0:T(8,128)(2,1)} %tiles.4), custom_call_target="tpu_custom_call" | custom-call | tf_op jit(solution)/shard_map/stripes/pallas_call | solution.py:68
  2.4 18.2 %collective-permute-start = (bf16[400,384]{1,0:T(8,128)(2,1)}, bf16[400,384]{1,0:T(8,128)(2,1)S(1)}, u32[]{:S(2)}, u32[]{:S(2)}) collective-permute-start(bf16[400,384]{1,0:T(8,128)(2,1)} %stripes.1), channel_id=1, source_target_pairs={{0,768},{1,769},{2,258},{3,3},{4,513},{5,257},{6,259},{7,771},{8,1... | collective-permute-start | bytes 921608 | tf_op jit(solution)/shard_map/ppermute | solution.py:308
  20.6 0.6 masked_operator.1
  21.3 2.7 %collective-permute-start.4 = (bf16[384,384]{1,0:T(8,128)(2,1)S(1)}, bf16[384,384]{1,0:T(8,128)(2,1)S(1)}, u32[]{:S(2)}, u32[]{:S(2)}) collective-permute-start(bf16[384,384]{1,0:T(8,128)(2,1)S(1)} %get-tuple-element.9.refs_4_), channel_id=1, source_target_pairs={{16,0},{32,16},{48,32},{0,48},{17,1},{33,17},{49,33},{1,49},{18,2}... | collective-permute-start | bytes 884744 | tf_op jit(solution)/shard_map/ppermute | solution.py:311
  24.0 4.3 %collective-permute-start.7 = (bf16[384,384]{1,0:T(8,128)(2,1)S(1)}, bf16[384,384]{1,0:T(8,128)(2,1)S(1)}, u32[]{:S(2)}, u32[]{:S(2)}) collective-permute-start(bf16[384,384]{1,0:T(8,128)(2,1)S(1)} %get-tuple-element.10.refs_5_), channel_id=1, source_target_pairs={{48,0},{0,16},{16,32},{32,48},{49,1},{1,17},{17,33},{33,49},{50,2}... | collective-permute-start | bytes 884744 | tf_op jit(solution)/shard_map/ppermute | solution.py:312
  28.3 1.9 %collective-permute-start.9 = (bf16[384,384]{1,0:T(8,128)(2,1)S(1)}, bf16[384,384]{1,0:T(8,128)(2,1)S(1)}, u32[]{:S(2)}, u32[]{:S(2)}) collective-permute-start(bf16[384,384]{1,0:T(8,128)(2,1)S(1)} %get-tuple-element.9.refs_4_), channel_id=1, source_target_pairs={{48,0},{0,16},{16,32},{32,48},{49,1},{1,17},{17,33},{33,49},{50,2}... | collective-permute-start | bytes 884744 | tf_op jit(solution)/shard_map/ppermute | solution.py:312
  30.2 3.9 %collective-permute-start.5 = (bf16[384,384]{1,0:T(8,128)(2,1)S(1)}, bf16[384,384]{1,0:T(8,128)(2,1)S(1)}, u32[]{:S(2)}, u32[]{:S(2)}) collective-permute-start(bf16[384,384]{1,0:T(8,128)(2,1)S(1)} %get-tuple-element.10.refs_5_), channel_id=1, source_target_pairs={{16,0},{32,16},{48,32},{0,48},{17,1},{33,17},{49,33},{1,49},{18,2}... | collective-permute-start | bytes 884744 | tf_op jit(solution)/shard_map/ppermute | solution.py:311
  34.2 0.1 collective-permute-done.4.refs_6_
  34.2 1.9 %collective-permute-start.6 = (bf16[384,384]{1,0:T(8,128)(2,1)S(1)}, bf16[384,384]{1,0:T(8,128)(2,1)S(1)}, u32[]{:S(2)}, u32[]{:S(2)}) collective-permute-start(bf16[384,384]{1,0:T(8,128)(2,1)S(1)} %collective-permute-done.4.refs_6_), channel_id=1, source_target_pairs={{16,0},{32,16},{48,32},{0,48},{17,1},{33,17},{49,33},{1,49},{18,2}... | collective-permute-start | bytes 884744 | tf_op jit(solution)/shard_map/ppermute | solution.py:317
  36.2 0.0 collective-permute-done.7.refs_11_
  36.2 5.1 %collective-permute-start.8 = (bf16[384,384]{1,0:T(8,128)(2,1)S(1)}, bf16[384,384]{1,0:T(8,128)(2,1)S(1)}, u32[]{:S(2)}, u32[]{:S(2)}) collective-permute-start(bf16[384,384]{1,0:T(8,128)(2,1)S(1)} %collective-permute-done.7.refs_11_), channel_id=1, source_target_pairs={{48,0},{0,16},{16,32},{32,48},{49,1},{1,17},{17,33},{33,49},{50,2}... | collective-permute-start | bytes 884744 | tf_op jit(solution)/shard_map/ppermute | solution.py:318
  41.3 0.0 collective-permute-done.padded
  41.4 0.0 slice-start.1
  41.4 0.0 copy-start.1
  41.4 6.5 %collective-permute-start.3 = (bf16[384,384]{1,0:T(8,128)(2,1)S(1)}, bf16[384,384]{1,0:T(8,128)(2,1)S(1)}, u32[]{:S(2)}, u32[]{:S(2)}) collective-permute-start(bf16[384,384]{1,0:T(8,128)(2,1)S(1)} %trim.1.refs_0_), channel_id=1, source_target_pairs={{128,0},{898,2},{192,64},{962,66},{256,128},{2,130},{320,192},{66,... | collective-permute-start | bytes 884744 | tf_op jit(solution)/shard_map/ppermute | solution.py:315
  47.9 0.0 collective-permute-done.9.refs_10_
  47.9 2.2 %collective-permute-start.2 = (bf16[384,384]{1,0:T(8,128)(2,1)S(1)}, bf16[384,384]{1,0:T(8,128)(2,1)S(1)}, u32[]{:S(2)}, u32[]{:S(2)}) collective-permute-start(bf16[384,384]{1,0:T(8,128)(2,1)S(1)} %trim.1.refs_0_), channel_id=1, source_target_pairs={{960,0},{0,64},{64,128},{128,192},{192,256},{256,320},{320,384},{3... | collective-permute-start | bytes 884744 | tf_op jit(solution)/shard_map/ppermute | solution.py:314
  50.1 0.0 collective-permute-done.5.refs_7_
  50.1 4.9 %collective-permute-start.1 = (bf16[384,384]{1,0:T(8,128)(2,1)S(1)}, bf16[384,384]{1,0:T(8,128)(2,1)S(1)}, u32[]{:S(2)}, u32[]{:S(2)}) collective-permute-start(bf16[384,384]{1,0:T(8,128)(2,1)S(1)} %trim.1.refs_0_), channel_id=1, source_target_pairs={{64,0},{128,64},{192,128},{256,192},{320,256},{384,320},{448,384},... | collective-permute-start | bytes 884744 | tf_op jit(solution)/shard_map/ppermute | solution.py:314
  55.0 0.0 collective-permute-done.6.refs_8_
  55.0 0.0 collective-permute-done.8.refs_9_
  55.0 6.4 %collective-permute-done.3.refs_3_ = bf16[384,384]{1,0:T(8,128)(2,1)S(1)} collective-permute-done((bf16[384,384]{1,0:T(8,128)(2,1)S(1)}, bf16[384,384]{1,0:T(8,128)(2,1)S(1)}, u32[]{:S(2)}, u32[]{:S(2)}) %collective-permute-start.3) | collective-permute-done | bytes 294944 | tf_op jit(solution)/shard_map/ppermute | solution.py:315
  61.5 2.3 %collective-permute-done.1.refs_1_ = bf16[384,384]{1,0:T(8,128)(2,1)S(1)} collective-permute-done((bf16[384,384]{1,0:T(8,128)(2,1)S(1)}, bf16[384,384]{1,0:T(8,128)(2,1)S(1)}, u32[]{:S(2)}, u32[]{:S(2)}) %collective-permute-start.1) | collective-permute-done | bytes 294944 | tf_op jit(solution)/shard_map/ppermute | solution.py:314
  63.7 1.1 product_for_other.1
  64.8 1.9 %collective-permute-start.10 = (f32[4,48,768]{2,1,0:T(8,128)S(1)}, f32[4,48,768]{2,1,0:T(8,128)S(1)}, u32[]{:S(2)}, u32[]{:S(2)}) collective-permute-start(f32[4,48,768]{2,1,0:T(8,128)S(1)} %product_for_other.1), channel_id=1, source_target_pairs={{0,2},{2,0},{1,3},{3,1},{4,6},{6,4},{5,7},{7,5},{8,10},{10,8},{9,1... | collective-permute-start | bytes 1769480 | tf_op jit(solution)/shard_map/ppermute | solution.py:322
  66.8 1.1 product.1.mine
  67.9 0.9 collective-permute-done.10.theirs
  68.7 0.2 encode.1
  68.9 15.5 %all_to_all.10.parts = s16[4,296,128]{2,1,0:T(8,128)(2,1)S(1)} all-to-all(s16[4,296,128]{2,1,0:T(8,128)(2,1)S(1)} %encode.1), channel_id=1, replica_groups=mesh['zh'=4,'zl'=4,'x'=4,'yh'=4,'core'=2,'yl'=2] {'yh'}, dimensions={0} | all-to-all | bytes 606208 | tf_op jit(solution)/shard_map/all_to_all | solution.py:324
  84.4 1.8 %coarse_parts.1 = s16[16,80,128]{2,1,0:T(8,128)(2,1)S(1)} custom-call(s32[4,16]{1,0:T(4,128)S(1)} %copy-done.1, s16[4,296,128]{2,1,0:T(8,128)(2,1)S(1)} %all_to_all.10.parts, bf16[768,3072]{1,0:T(8,128)(2,1)S(1)} %bitcast.3), custom_call_target="tpu_custom_call" | custom-call | tf_op jit(solution)/shard_map/coarse_parts/pallas_call | solution.py:226
  86.2 26.1 %all_to_all.11.coded = s16[16,80,128]{2,1,0:T(8,128)(2,1)S(1)} all-to-all(s16[16,80,128]{2,1,0:T(8,128)(2,1)S(1)} %coarse_parts.1), channel_id=1, replica_groups=mesh['zh'=4,'zl'=4,'x'=4,'yh'=4,'core'=2,'yl'=2] {'zh','zl'}, dimensions={0} | all-to-all | bytes 655360 | tf_op jit(solution)/shard_map/all_to_all | solution.py:325
  112.3 0.7 summed.1
  (11 shorter events, 0.0 us)
Async XLA Ops:
  0.0 20.6 %copy-start = (bf16[768,384]{1,0:T(8,128)(2,1)S(1)}, bf16[768,384]{1,0:T(8,128)(2,1)}, u32[]{:S(2)}) copy-start(bf16[768,384]{1,0:T(8,128)(2,1)} %tiles.3) | copy-start | bytes 1769476
  0.0 20.6 %copy-start.2 = (s32[4,2]{0,1:T(2,128)S(1)}, s32[4,2]{0,1:T(2,128)}, u32[]{:S(2)}) copy-start(s32[4,2]{0,1:T(2,128)} %param.6) | copy-start | bytes 100
  0.0 84.4 %slice-start = ((s8[4718592]{0:T(1024)(128)(4,1)}), s8[524288]{0:T(1024)(128)(4,1)S(1)}, s32[]{:S(2)}) async-start(s8[4718592]{0:T(1024)(128)(4,1)} %bitcast.2), calls=%async_computation.2 | async-start | bytes 1048576
  2.4 38.9 %collective-permute-start = (bf16[400,384]{1,0:T(8,128)(2,1)}, bf16[400,384]{1,0:T(8,128)(2,1)S(1)}, u32[]{:S(2)}, u32[]{:S(2)}) collective-permute-start(bf16[400,384]{1,0:T(8,128)(2,1)} %stripes.1), channel_id=1, source_target_pairs={{0,768},{1,769},{2,258},{3,3},{4,513},{5,257},{6,259},{7,771},{8,1... | collective-permute-start | bytes 921608 | tf_op jit(solution)/shard_map/ppermute | solution.py:308
  21.3 13.0 %collective-permute-start.4 = (bf16[384,384]{1,0:T(8,128)(2,1)S(1)}, bf16[384,384]{1,0:T(8,128)(2,1)S(1)}, u32[]{:S(2)}, u32[]{:S(2)}) collective-permute-start(bf16[384,384]{1,0:T(8,128)(2,1)S(1)} %get-tuple-element.9.refs_4_), channel_id=1, source_target_pairs={{16,0},{32,16},{48,32},{0,48},{17,1},{33,17},{49,33},{1,49},{18,2}... | collective-permute-start | bytes 884744 | tf_op jit(solution)/shard_map/ppermute | solution.py:311
  24.0 12.2 %collective-permute-start.7 = (bf16[384,384]{1,0:T(8,128)(2,1)S(1)}, bf16[384,384]{1,0:T(8,128)(2,1)S(1)}, u32[]{:S(2)}, u32[]{:S(2)}) collective-permute-start(bf16[384,384]{1,0:T(8,128)(2,1)S(1)} %get-tuple-element.10.refs_5_), channel_id=1, source_target_pairs={{48,0},{0,16},{16,32},{32,48},{49,1},{1,17},{17,33},{33,49},{50,2}... | collective-permute-start | bytes 884744 | tf_op jit(solution)/shard_map/ppermute | solution.py:312
  28.3 19.6 %collective-permute-start.9 = (bf16[384,384]{1,0:T(8,128)(2,1)S(1)}, bf16[384,384]{1,0:T(8,128)(2,1)S(1)}, u32[]{:S(2)}, u32[]{:S(2)}) collective-permute-start(bf16[384,384]{1,0:T(8,128)(2,1)S(1)} %get-tuple-element.9.refs_4_), channel_id=1, source_target_pairs={{48,0},{0,16},{16,32},{32,48},{49,1},{1,17},{17,33},{33,49},{50,2}... | collective-permute-start | bytes 884744 | tf_op jit(solution)/shard_map/ppermute | solution.py:312
  30.2 19.9 %collective-permute-start.5 = (bf16[384,384]{1,0:T(8,128)(2,1)S(1)}, bf16[384,384]{1,0:T(8,128)(2,1)S(1)}, u32[]{:S(2)}, u32[]{:S(2)}) collective-permute-start(bf16[384,384]{1,0:T(8,128)(2,1)S(1)} %get-tuple-element.10.refs_5_), channel_id=1, source_target_pairs={{16,0},{32,16},{48,32},{0,48},{17,1},{33,17},{49,33},{1,49},{18,2}... | collective-permute-start | bytes 884744 | tf_op jit(solution)/shard_map/ppermute | solution.py:311
  34.2 20.8 %collective-permute-start.6 = (bf16[384,384]{1,0:T(8,128)(2,1)S(1)}, bf16[384,384]{1,0:T(8,128)(2,1)S(1)}, u32[]{:S(2)}, u32[]{:S(2)}) collective-permute-start(bf16[384,384]{1,0:T(8,128)(2,1)S(1)} %collective-permute-done.4.refs_6_), channel_id=1, source_target_pairs={{16,0},{32,16},{48,32},{0,48},{17,1},{33,17},{49,33},{1,49},{18,2}... | collective-permute-start | bytes 884744 | tf_op jit(solution)/shard_map/ppermute | solution.py:317
  36.2 18.9 %collective-permute-start.8 = (bf16[384,384]{1,0:T(8,128)(2,1)S(1)}, bf16[384,384]{1,0:T(8,128)(2,1)S(1)}, u32[]{:S(2)}, u32[]{:S(2)}) collective-permute-start(bf16[384,384]{1,0:T(8,128)(2,1)S(1)} %collective-permute-done.7.refs_11_), channel_id=1, source_target_pairs={{48,0},{0,16},{16,32},{32,48},{49,1},{1,17},{17,33},{33,49},{50,2}... | collective-permute-start | bytes 884744 | tf_op jit(solution)/shard_map/ppermute | solution.py:318
  41.4 43.0 %slice-start.1 = ((s8[4718592]{0:T(1024)(128)(4,1)}), s8[4194304]{0:T(1024)(128)(4,1)S(1)}, s32[]{:S(2)}) async-start(s8[4718592]{0:T(1024)(128)(4,1)} %bitcast.2), calls=%async_computation.3 | async-start | bytes 8388608
  41.4 43.0 %copy-start.1 = (s32[4,16]{1,0:T(4,128)S(1)}, s32[4,16]{1,0:T(4,128)}, u32[]{:S(2)}) copy-start(s32[4,16]{1,0:T(4,128)} %mask.1) | copy-start | bytes 772
  41.4 20.1 %collective-permute-start.3 = (bf16[384,384]{1,0:T(8,128)(2,1)S(1)}, bf16[384,384]{1,0:T(8,128)(2,1)S(1)}, u32[]{:S(2)}, u32[]{:S(2)}) collective-permute-start(bf16[384,384]{1,0:T(8,128)(2,1)S(1)} %trim.1.refs_0_), channel_id=1, source_target_pairs={{128,0},{898,2},{192,64},{962,66},{256,128},{2,130},{320,192},{66,... | collective-permute-start | bytes 884744 | tf_op jit(solution)/shard_map/ppermute | solution.py:315
  47.9 13.5 %collective-permute-start.2 = (bf16[384,384]{1,0:T(8,128)(2,1)S(1)}, bf16[384,384]{1,0:T(8,128)(2,1)S(1)}, u32[]{:S(2)}, u32[]{:S(2)}) collective-permute-start(bf16[384,384]{1,0:T(8,128)(2,1)S(1)} %trim.1.refs_0_), channel_id=1, source_target_pairs={{960,0},{0,64},{64,128},{128,192},{192,256},{256,320},{320,384},{3... | collective-permute-start | bytes 884744 | tf_op jit(solution)/shard_map/ppermute | solution.py:314
  50.1 13.6 %collective-permute-start.1 = (bf16[384,384]{1,0:T(8,128)(2,1)S(1)}, bf16[384,384]{1,0:T(8,128)(2,1)S(1)}, u32[]{:S(2)}, u32[]{:S(2)}) collective-permute-start(bf16[384,384]{1,0:T(8,128)(2,1)S(1)} %trim.1.refs_0_), channel_id=1, source_target_pairs={{64,0},{128,64},{192,128},{256,192},{320,256},{384,320},{448,384},... | collective-permute-start | bytes 884744 | tf_op jit(solution)/shard_map/ppermute | solution.py:314
  64.8 3.9 %collective-permute-start.10 = (f32[4,48,768]{2,1,0:T(8,128)S(1)}, f32[4,48,768]{2,1,0:T(8,128)S(1)}, u32[]{:S(2)}, u32[]{:S(2)}) collective-permute-start(f32[4,48,768]{2,1,0:T(8,128)S(1)} %product_for_other.1), channel_id=1, source_target_pairs={{0,2},{2,0},{1,3},{3,1},{4,6},{6,4},{5,7},{7,5},{8,10},{10,8},{9,1... | collective-permute-start | bytes 1769480 | tf_op jit(solution)/shard_map/ppermute | solution.py:322

commit v13 on v12

--- a/solution.py
+++ b/solution.py
@@ -305,14 +305,15 @@
 def local(a_tiles, p_tiles, a_mask, p_mask):
     z = ("zh", "zl")
     mine = stripes(p_tiles, p_mask)
-    slab = trim(lax.ppermute(mine, z + ("yh", "core", "yl"), spread()))
+    padded = lax.ppermute(mine, z + ("yh", "core", "yl"), spread())
     a_tiles, mine = lax.optimization_barrier((a_tiles, mine))
     own = masked_operator(a_tiles, a_mask)
     after = [lax.ppermute(half, "x", around(4, 1)) for half in own]
     before = [lax.ppermute(half, "x", around(4, -1)) for half in own]
 
+    slab = trim(padded)
     above, below = [lax.ppermute(slab, z, around(PLANES, turn)) for turn in (1, -1)]
-    slabs = [slab, above, below, lax.ppermute(slab, z + ("core",), two_away())]
+    slabs = [slab, above, below, lax.ppermute(padded, z + ("core",), two_away())]
     across = [
         lax.ppermute(after[0], "x", around(4, 1)),
         lax.ppermute(before[1], "x", around(4, -1)),

time: 115 us -> 120 us (1.043); the launches traced: 113 us -> 120 us
  blocking collectives: 41.6 us -> 50.7 us
  waiting for transfers between devices: 9.63 us -> 7.07 us
    all_to_all x1, blocking collectives: 15.5 us -> 26.1 us  [local(): coded = lax.all_to_all(coded, 'yh', 0, 0, tiled=True)]
    ppermute x2, waiting for transfers between devices: 6.41 us -> 0.01 us  [the longest x1 0.01 us: local(): lax.ppermute(padded, z + ('core',), two_away())]
    ppermute x2, waiting for transfers between devices: 2.28 us -> 6.19 us  [local(): lax.ppermute(slab, z, around(PLANES, turn))]
    all_to_all x1, blocking collectives: 26.1 us -> 24.5 us  [local(): lax.all_to_all(coarse_parts(coded, p_tiles, p_mask), z, 0, 0, tiled=True)]
  transfers between devices with their start and end apart: 11 -> 11, of which waited for: 4 -> 3; matrix products, arithmetic and copies ran while one was open for 0% -> 0% of each run, Pallas kernels for 2% -> 1%
where the time goes in v13:
time: 120 us
  starting transfers between devices  53.7 us (45%)
  blocking collectives  50.7 us (42%)
  Pallas kernels  7.94 us (7%)
  waiting for transfers between devices  7.07 us (6%)
    all_to_all x1, blocking collectives, local(): coded = lax.all_to_all(coded, 'yh', 0, 0, tiled=True)  26.1 us
    all_to_all x1, blocking collectives, local(): lax.all_to_all(coarse_parts(coded, p_tiles, p_mask), z, 0, 0, tiled=True)  24.5 us
    ppermute x1, starting transfers between devices, local(): padded = lax.ppermute(mine, z + ('yh', 'core', 'yl'), spread())  18.2 us
    ppermute x2, starting transfers between devices, local(): lax.ppermute(slab, z, around(PLANES, turn))  7.32 us
    ppermute x2, starting transfers between devices, local(): after = [lax.ppermute(half, 'x', around(4, 1)) for half in own]  6.65 us
    ppermute x1, starting transfers between devices, local(): lax.ppermute(padded, z + ('core',), two_away())  6.3 us
    ppermute x2, starting transfers between devices, local(): before = [lax.ppermute(half, 'x', around(4, -1)) for half in own]  6.24 us
    ppermute x2, waiting for transfers between devices, local(): lax.ppermute(slab, z, around(PLANES, turn))  6.19 us
  transfers between devices with their start and end apart: 11, of which 3 were waited for; matrix products, arithmetic and copies ran while one was open for 0% of the time, Pallas kernels for 1%

profile of v13, /device:TPU:6, one launch (start us, length us, event | category | flops | bytes accessed | tf_op | source)
XLA Modules:
  0.0 119.6 jit_solution(10249491257907237372)
XLA Ops:
  0.0 2.4 %stripes.1 = bf16[400,384]{1,0:T(8,128)(2,1)} custom-call(s32[4,16]{1,0:T(4,128)} %mask.1, bf16[768,3072]{1,0:T(8,128)(2,1)} %tiles.4), custom_call_target="tpu_custom_call" | custom-call | tf_op jit(solution)/shard_map/stripes/pallas_call | solution.py:68
  2.4 18.2 %collective-permute-start = (bf16[400,384]{1,0:T(8,128)(2,1)}, bf16[400,384]{1,0:T(8,128)(2,1)S(1)}, u32[]{:S(2)}, u32[]{:S(2)}) collective-permute-start(bf16[400,384]{1,0:T(8,128)(2,1)} %stripes.1), channel_id=1, source_target_pairs={{0,768},{1,769},{2,258},{3,3},{4,513},{5,257},{6,259},{7,771},{8,1... | collective-permute-start | bytes 921608 | tf_op jit(solution)/shard_map/ppermute | solution.py:308
  20.6 0.6 masked_operator.1
  21.3 2.7 %collective-permute-start.4 = (bf16[384,384]{1,0:T(8,128)(2,1)S(1)}, bf16[384,384]{1,0:T(8,128)(2,1)S(1)}, u32[]{:S(2)}, u32[]{:S(2)}) collective-permute-start(bf16[384,384]{1,0:T(8,128)(2,1)S(1)} %get-tuple-element.9.refs_4_), channel_id=1, source_target_pairs={{16,0},{32,16},{48,32},{0,48},{17,1},{33,17},{49,33},{1,49},{18,2}... | collective-permute-start | bytes 884744 | tf_op jit(solution)/shard_map/ppermute | solution.py:311
  24.0 4.3 %collective-permute-start.7 = (bf16[384,384]{1,0:T(8,128)(2,1)S(1)}, bf16[384,384]{1,0:T(8,128)(2,1)S(1)}, u32[]{:S(2)}, u32[]{:S(2)}) collective-permute-start(bf16[384,384]{1,0:T(8,128)(2,1)S(1)} %get-tuple-element.10.refs_5_), channel_id=1, source_target_pairs={{48,0},{0,16},{16,32},{32,48},{49,1},{1,17},{17,33},{33,49},{50,2}... | collective-permute-start | bytes 884744 | tf_op jit(solution)/shard_map/ppermute | solution.py:312
  28.3 1.9 %collective-permute-start.9 = (bf16[384,384]{1,0:T(8,128)(2,1)S(1)}, bf16[384,384]{1,0:T(8,128)(2,1)S(1)}, u32[]{:S(2)}, u32[]{:S(2)}) collective-permute-start(bf16[384,384]{1,0:T(8,128)(2,1)S(1)} %get-tuple-element.9.refs_4_), channel_id=1, source_target_pairs={{48,0},{0,16},{16,32},{32,48},{49,1},{1,17},{17,33},{33,49},{50,2}... | collective-permute-start | bytes 884744 | tf_op jit(solution)/shard_map/ppermute | solution.py:312
  30.2 3.9 %collective-permute-start.5 = (bf16[384,384]{1,0:T(8,128)(2,1)S(1)}, bf16[384,384]{1,0:T(8,128)(2,1)S(1)}, u32[]{:S(2)}, u32[]{:S(2)}) collective-permute-start(bf16[384,384]{1,0:T(8,128)(2,1)S(1)} %get-tuple-element.10.refs_5_), channel_id=1, source_target_pairs={{16,0},{32,16},{48,32},{0,48},{17,1},{33,17},{49,33},{1,49},{18,2}... | collective-permute-start | bytes 884744 | tf_op jit(solution)/shard_map/ppermute | solution.py:311
  34.2 0.0 collective-permute-done.padded
  34.2 6.3 %collective-permute-start.3 = (bf16[400,384]{1,0:T(8,128)(2,1)S(1)}, bf16[400,384]{1,0:T(8,128)(2,1)S(1)}, u32[]{:S(2)}, u32[]{:S(2)}) collective-permute-start(bf16[400,384]{1,0:T(8,128)(2,1)S(1)} %collective-permute-done.padded), channel_id=1, source_target_pairs={{128,0},{898,2},{192,64},{962,66},{256,128},{2,130},{320,192},{66,... | collective-permute-start | bytes 921608 | tf_op jit(solution)/shard_map/ppermute | solution.py:316
  40.5 0.0 collective-permute-done.4.refs_6_
  40.5 2.4 %collective-permute-start.6 = (bf16[384,384]{1,0:T(8,128)(2,1)S(1)}, bf16[384,384]{1,0:T(8,128)(2,1)S(1)}, u32[]{:S(2)}, u32[]{:S(2)}) collective-permute-start(bf16[384,384]{1,0:T(8,128)(2,1)S(1)} %collective-permute-done.4.refs_6_), channel_id=1, source_target_pairs={{16,0},{32,16},{48,32},{0,48},{17,1},{33,17},{49,33},{1,49},{18,2}... | collective-permute-start | bytes 884744 | tf_op jit(solution)/shard_map/ppermute | solution.py:318
  42.9 0.0 collective-permute-done.7.refs_11_
  42.9 4.6 %collective-permute-start.8 = (bf16[384,384]{1,0:T(8,128)(2,1)S(1)}, bf16[384,384]{1,0:T(8,128)(2,1)S(1)}, u32[]{:S(2)}, u32[]{:S(2)}) collective-permute-start(bf16[384,384]{1,0:T(8,128)(2,1)S(1)} %collective-permute-done.7.refs_11_), channel_id=1, source_target_pairs={{48,0},{0,16},{16,32},{32,48},{49,1},{1,17},{17,33},{33,49},{50,2}... | collective-permute-start | bytes 884744 | tf_op jit(solution)/shard_map/ppermute | solution.py:319
  47.6 0.0 slice-start.1
  47.6 0.0 copy-start.1
  47.6 0.0 collective-permute-done.9.refs_10_
  47.7 2.5 %collective-permute-start.2 = (bf16[384,384]{1,0:T(8,128)(2,1)S(1)}, bf16[384,384]{1,0:T(8,128)(2,1)S(1)}, u32[]{:S(2)}, u32[]{:S(2)}) collective-permute-start(bf16[384,384]{1,0:T(8,128)(2,1)S(1)} %trim.1.refs_0_), channel_id=1, source_target_pairs={{960,0},{0,64},{64,128},{128,192},{192,256},{256,320},{320,384},{3... | collective-permute-start | bytes 884744 | tf_op jit(solution)/shard_map/ppermute | solution.py:315
  50.1 0.0 collective-permute-done.5.refs_7_
  50.1 4.8 %collective-permute-start.1 = (bf16[384,384]{1,0:T(8,128)(2,1)S(1)}, bf16[384,384]{1,0:T(8,128)(2,1)S(1)}, u32[]{:S(2)}, u32[]{:S(2)}) collective-permute-start(bf16[384,384]{1,0:T(8,128)(2,1)S(1)} %trim.1.refs_0_), channel_id=1, source_target_pairs={{64,0},{128,64},{192,128},{256,192},{320,256},{384,320},{448,384},... | collective-permute-start | bytes 884744 | tf_op jit(solution)/shard_map/ppermute | solution.py:315
  55.0 0.0 collective-permute-done.8.refs_9_
  55.0 2.7 %collective-permute-done.2.refs_2_ = bf16[384,384]{1,0:T(8,128)(2,1)S(1)} collective-permute-done((bf16[384,384]{1,0:T(8,128)(2,1)S(1)}, bf16[384,384]{1,0:T(8,128)(2,1)S(1)}, u32[]{:S(2)}, u32[]{:S(2)}) %collective-permute-start.2) | collective-permute-done | bytes 294944 | tf_op jit(solution)/shard_map/ppermute | solution.py:315
  57.7 3.5 %collective-permute-done.1.refs_1_ = bf16[384,384]{1,0:T(8,128)(2,1)S(1)} collective-permute-done((bf16[384,384]{1,0:T(8,128)(2,1)S(1)}, bf16[384,384]{1,0:T(8,128)(2,1)S(1)}, u32[]{:S(2)}, u32[]{:S(2)}) %collective-permute-start.1) | collective-permute-done | bytes 294944 | tf_op jit(solution)/shard_map/ppermute | solution.py:315
  61.2 0.0 collective-permute-done.3.refs_3_
  61.2 1.1 product_for_other.1
  62.3 1.9 %collective-permute-start.10 = (f32[4,48,768]{2,1,0:T(8,128)S(1)}, f32[4,48,768]{2,1,0:T(8,128)S(1)}, u32[]{:S(2)}, u32[]{:S(2)}) collective-permute-start(f32[4,48,768]{2,1,0:T(8,128)S(1)} %product_for_other.1), channel_id=1, source_target_pairs={{0,2},{2,0},{1,3},{3,1},{4,6},{6,4},{5,7},{7,5},{8,10},{10,8},{9,1... | collective-permute-start | bytes 1769480 | tf_op jit(solution)/shard_map/ppermute | solution.py:323
  64.3 1.1 product.1.mine
  65.4 0.9 collective-permute-done.10.theirs
  66.2 0.2 encode.1
  66.4 26.1 %all_to_all.10.parts = s16[4,296,128]{2,1,0:T(8,128)(2,1)S(1)} all-to-all(s16[4,296,128]{2,1,0:T(8,128)(2,1)S(1)} %encode.1), channel_id=1, replica_groups=mesh['zh'=4,'zl'=4,'x'=4,'yh'=4,'core'=2,'yl'=2] {'yh'}, dimensions={0} | all-to-all | bytes 606208 | tf_op jit(solution)/shard_map/all_to_all | solution.py:325
  92.5 1.8 %coarse_parts.1 = s16[16,80,128]{2,1,0:T(8,128)(2,1)S(1)} custom-call(s32[4,16]{1,0:T(4,128)S(1)} %copy-done.1, s16[4,296,128]{2,1,0:T(8,128)(2,1)S(1)} %all_to_all.10.parts, bf16[768,3072]{1,0:T(8,128)(2,1)S(1)} %bitcast.3), custom_call_target="tpu_custom_call" | custom-call | tf_op jit(solution)/shard_map/coarse_parts/pallas_call | solution.py:226
  94.3 24.5 %all_to_all.11.coded = s16[16,80,128]{2,1,0:T(8,128)(2,1)S(1)} all-to-all(s16[16,80,128]{2,1,0:T(8,128)(2,1)S(1)} %coarse_parts.1), channel_id=1, replica_groups=mesh['zh'=4,'zl'=4,'x'=4,'yh'=4,'core'=2,'yl'=2] {'zh','zl'}, dimensions={0} | all-to-all | bytes 655360 | tf_op jit(solution)/shard_map/all_to_all | solution.py:326
  118.9 0.7 summed.1
  (11 shorter events, 0.0 us)
Async XLA Ops:
  0.0 20.6 %copy-start = (bf16[768,384]{1,0:T(8,128)(2,1)S(1)}, bf16[768,384]{1,0:T(8,128)(2,1)}, u32[]{:S(2)}) copy-start(bf16[768,384]{1,0:T(8,128)(2,1)} %tiles.3) | copy-start | bytes 1769476
  0.0 20.6 %copy-start.2 = (s32[4,2]{0,1:T(2,128)S(1)}, s32[4,2]{0,1:T(2,128)}, u32[]{:S(2)}) copy-start(s32[4,2]{0,1:T(2,128)} %param.6) | copy-start | bytes 100
  0.0 92.5 %slice-start = ((s8[4718592]{0:T(1024)(128)(4,1)}), s8[524288]{0:T(1024)(128)(4,1)S(1)}, s32[]{:S(2)}) async-start(s8[4718592]{0:T(1024)(128)(4,1)} %bitcast.2), calls=%async_computation.2 | async-start | bytes 1048576
  2.4 31.8 %collective-permute-start = (bf16[400,384]{1,0:T(8,128)(2,1)}, bf16[400,384]{1,0:T(8,128)(2,1)S(1)}, u32[]{:S(2)}, u32[]{:S(2)}) collective-permute-start(bf16[400,384]{1,0:T(8,128)(2,1)} %stripes.1), channel_id=1, source_target_pairs={{0,768},{1,769},{2,258},{3,3},{4,513},{5,257},{6,259},{7,771},{8,1... | collective-permute-start | bytes 921608 | tf_op jit(solution)/shard_map/ppermute | solution.py:308
  21.3 19.2 %collective-permute-start.4 = (bf16[384,384]{1,0:T(8,128)(2,1)S(1)}, bf16[384,384]{1,0:T(8,128)(2,1)S(1)}, u32[]{:S(2)}, u32[]{:S(2)}) collective-permute-start(bf16[384,384]{1,0:T(8,128)(2,1)S(1)} %get-tuple-element.9.refs_4_), channel_id=1, source_target_pairs={{16,0},{32,16},{48,32},{0,48},{17,1},{33,17},{49,33},{1,49},{18,2}... | collective-permute-start | bytes 884744 | tf_op jit(solution)/shard_map/ppermute | solution.py:311
  24.0 18.9 %collective-permute-start.7 = (bf16[384,384]{1,0:T(8,128)(2,1)S(1)}, bf16[384,384]{1,0:T(8,128)(2,1)S(1)}, u32[]{:S(2)}, u32[]{:S(2)}) collective-permute-start(bf16[384,384]{1,0:T(8,128)(2,1)S(1)} %get-tuple-element.10.refs_5_), channel_id=1, source_target_pairs={{48,0},{0,16},{16,32},{32,48},{49,1},{1,17},{17,33},{33,49},{50,2}... | collective-permute-start | bytes 884744 | tf_op jit(solution)/shard_map/ppermute | solution.py:312
  28.3 19.3 %collective-permute-start.9 = (bf16[384,384]{1,0:T(8,128)(2,1)S(1)}, bf16[384,384]{1,0:T(8,128)(2,1)S(1)}, u32[]{:S(2)}, u32[]{:S(2)}) collective-permute-start(bf16[384,384]{1,0:T(8,128)(2,1)S(1)} %get-tuple-element.9.refs_4_), channel_id=1, source_target_pairs={{48,0},{0,16},{16,32},{32,48},{49,1},{1,17},{17,33},{33,49},{50,2}... | collective-permute-start | bytes 884744 | tf_op jit(solution)/shard_map/ppermute | solution.py:312
  30.2 19.9 %collective-permute-start.5 = (bf16[384,384]{1,0:T(8,128)(2,1)S(1)}, bf16[384,384]{1,0:T(8,128)(2,1)S(1)}, u32[]{:S(2)}, u32[]{:S(2)}) collective-permute-start(bf16[384,384]{1,0:T(8,128)(2,1)S(1)} %get-tuple-element.10.refs_5_), channel_id=1, source_target_pairs={{16,0},{32,16},{48,32},{0,48},{17,1},{33,17},{49,33},{1,49},{18,2}... | collective-permute-start | bytes 884744 | tf_op jit(solution)/shard_map/ppermute | solution.py:311
  34.2 27.0 %collective-permute-start.3 = (bf16[400,384]{1,0:T(8,128)(2,1)S(1)}, bf16[400,384]{1,0:T(8,128)(2,1)S(1)}, u32[]{:S(2)}, u32[]{:S(2)}) collective-permute-start(bf16[400,384]{1,0:T(8,128)(2,1)S(1)} %collective-permute-done.padded), channel_id=1, source_target_pairs={{128,0},{898,2},{192,64},{962,66},{256,128},{2,130},{320,192},{66,... | collective-permute-start | bytes 921608 | tf_op jit(solution)/shard_map/ppermute | solution.py:316
  40.5 14.5 %collective-permute-start.6 = (bf16[384,384]{1,0:T(8,128)(2,1)S(1)}, bf16[384,384]{1,0:T(8,128)(2,1)S(1)}, u32[]{:S(2)}, u32[]{:S(2)}) collective-permute-start(bf16[384,384]{1,0:T(8,128)(2,1)S(1)} %collective-permute-done.4.refs_6_), channel_id=1, source_target_pairs={{16,0},{32,16},{48,32},{0,48},{17,1},{33,17},{49,33},{1,49},{18,2}... | collective-permute-start | bytes 884744 | tf_op jit(solution)/shard_map/ppermute | solution.py:318
  42.9 12.1 %collective-permute-start.8 = (bf16[384,384]{1,0:T(8,128)(2,1)S(1)}, bf16[384,384]{1,0:T(8,128)(2,1)S(1)}, u32[]{:S(2)}, u32[]{:S(2)}) collective-permute-start(bf16[384,384]{1,0:T(8,128)(2,1)S(1)} %collective-permute-done.7.refs_11_), channel_id=1, source_target_pairs={{48,0},{0,16},{16,32},{32,48},{49,1},{1,17},{17,33},{33,49},{50,2}... | collective-permute-start | bytes 884744 | tf_op jit(solution)/shard_map/ppermute | solution.py:319
  47.6 44.9 %slice-start.1 = ((s8[4718592]{0:T(1024)(128)(4,1)}), s8[4194304]{0:T(1024)(128)(4,1)S(1)}, s32[]{:S(2)}) async-start(s8[4718592]{0:T(1024)(128)(4,1)} %bitcast.2), calls=%async_computation.3 | async-start | bytes 8388608
  47.6 44.9 %copy-start.1 = (s32[4,16]{1,0:T(4,128)S(1)}, s32[4,16]{1,0:T(4,128)}, u32[]{:S(2)}) copy-start(s32[4,16]{1,0:T(4,128)} %mask.1) | copy-start | bytes 772
  47.7 10.1 %collective-permute-start.2 = (bf16[384,384]{1,0:T(8,128)(2,1)S(1)}, bf16[384,384]{1,0:T(8,128)(2,1)S(1)}, u32[]{:S(2)}, u32[]{:S(2)}) collective-permute-start(bf16[384,384]{1,0:T(8,128)(2,1)S(1)} %trim.1.refs_0_), channel_id=1, source_target_pairs={{960,0},{0,64},{64,128},{128,192},{192,256},{256,320},{320,384},{3... | collective-permute-start | bytes 884744 | tf_op jit(solution)/shard_map/ppermute | solution.py:315
  50.1 11.1 %collective-permute-start.1 = (bf16[384,384]{1,0:T(8,128)(2,1)S(1)}, bf16[384,384]{1,0:T(8,128)(2,1)S(1)}, u32[]{:S(2)}, u32[]{:S(2)}) collective-permute-start(bf16[384,384]{1,0:T(8,128)(2,1)S(1)} %trim.1.refs_0_), channel_id=1, source_target_pairs={{64,0},{128,64},{192,128},{256,192},{320,256},{384,320},{448,384},... | collective-permute-start | bytes 884744 | tf_op jit(solution)/shard_map/ppermute | solution.py:315
  62.3 3.9 %collective-permute-start.10 = (f32[4,48,768]{2,1,0:T(8,128)S(1)}, f32[4,48,768]{2,1,0:T(8,128)S(1)}, u32[]{:S(2)}, u32[]{:S(2)}) collective-permute-start(f32[4,48,768]{2,1,0:T(8,128)S(1)} %product_for_other.1), channel_id=1, source_target_pairs={{0,2},{2,0},{1,3},{3,1},{4,6},{6,4},{5,7},{7,5},{8,10},{10,8},{9,1... | collective-permute-start | bytes 1769480 | tf_op jit(solution)/shard_map/ppermute | solution.py:323

commit v14 on v12

--- a/solution.py
+++ b/solution.py
@@ -93,18 +93,17 @@
         out[rows, :] = tiles[rows, :] * present.astype(BF16)
 
 
-def operator_kernel(mask, tiles, upper, lower):
-    for half, out in enumerate((upper, lower)):
-        rows = tiles[half * HALF : (half + 1) * HALF, :]
-        mask_rows(lambda i, k: mask[k, 2 * half + i], rows, out, 0)
+def operator_kernel(mask, tiles, whole, upper, lower):
+    mask_rows(lambda i, k: mask[k, i], tiles, whole, 0)
+    upper[...], lower[...] = whole[:HALF], whole[HALF:]
 
 
 def masked_operator(a_tiles, a_mask):
     return pl.pallas_call(
         operator_kernel,
-        out_shape=[jax.ShapeDtypeStruct((HALF, HALF), BF16)] * 2,
+        out_shape=[jax.ShapeDtypeStruct((n * HALF, HALF), BF16) for n in (2, 1, 1)],
         in_specs=[pl.BlockSpec(memory_space=pltpu.SMEM), pl.BlockSpec(memory_space=pltpu.VMEM)],
-        out_specs=[pl.BlockSpec(memory_space=pltpu.VMEM)] * 2,
+        out_specs=[pl.BlockSpec(memory_space=pltpu.VMEM)] * 3,
         compiler_params=params(),
         name="masked_operator",
     )(a_mask.T, a_tiles)
@@ -126,7 +125,7 @@
 
 
 def product_kernel(other, *refs):
-    slabs, blocks, out, columns = refs[:4], refs[4:12], refs[12], refs[13]
+    slabs, (own, behind), halves, out, columns = refs[:4], refs[4:6], refs[6:10], refs[10], refs[11]
     x, zl, yh = lax.axis_index("x"), lax.axis_index("zl"), lax.axis_index("yh")
     core = (lax.axis_index("core") + other) % 2
     for n, slab in zip((0, 1, 3, 2), slabs):
@@ -135,17 +134,19 @@
             rows = pl.ds(pl.multiple_of((2 * y + core) * WIDE, WIDE), WIDE)
             columns[block, y * WIDE : (y + 1) * WIDE] = slab[rows, :]
     for half in range(2):
-        total = dot_last(columns[x], blocks[half][...])
-        for n in range(1, 4):
-            total = total + dot_last(columns[(x + n) % 4], blocks[2 * n + half][...])
-        out[:, :, half * HALF : (half + 1) * HALF] = total.reshape(4, WIDE, HALF)
+        rows = slice(half * HALF, (half + 1) * HALF)
+        total = dot_last(columns[x], own[rows, :])
+        total = total + dot_last(columns[(x + 1) % 4], halves[half][...])
+        total = total + dot_last(columns[(x + 2) % 4], halves[2 + half][...])
+        total = total + dot_last(columns[(x + 3) % 4], behind[rows, :])
+        out[:, :, rows] = total.reshape(4, WIDE, HALF)
 
 
 def product(slabs, blocks, other):
     return pl.pallas_call(
         functools.partial(product_kernel, other),
         out_shape=jax.ShapeDtypeStruct((4, WIDE, ROWS), F32),
-        in_specs=[pl.BlockSpec(memory_space=pltpu.VMEM)] * 12,
+        in_specs=[pl.BlockSpec(memory_space=pltpu.VMEM)] * 10,
         out_specs=pl.BlockSpec(memory_space=pltpu.VMEM),
         scratch_shapes=[pltpu.VMEM((4, 4 * WIDE, HALF), BF16)],
         compiler_params=params(),
@@ -307,17 +308,14 @@
     mine = stripes(p_tiles, p_mask)
     slab = trim(lax.ppermute(mine, z + ("yh", "core", "yl"), spread()))
     a_tiles, mine = lax.optimization_barrier((a_tiles, mine))
-    own = masked_operator(a_tiles, a_mask)
-    after = [lax.ppermute(half, "x", around(4, 1)) for half in own]
-    before = [lax.ppermute(half, "x", around(4, -1)) for half in own]
+    own, *own_halves = masked_operator(a_tiles, a_mask)
+    after = [lax.ppermute(half, "x", around(4, 1)) for half in own_halves]
+    before = lax.ppermute(own, "x", around(4, -1))
 
     above, below = [lax.ppermute(slab, z, around(PLANES, turn)) for turn in (1, -1)]
     slabs = [slab, above, below, lax.ppermute(slab, z + ("core",), two_away())]
-    across = [
-        lax.ppermute(after[0], "x", around(4, 1)),
-        lax.ppermute(before[1], "x", around(4, -1)),
-    ]
-    blocks = [*own, *after, *across, *before]
+    across = [lax.ppermute(half, "x", around(4, 1)) for half in after]
+    blocks = [own, before, *after, *across]
 
     theirs = lax.ppermute(product(slabs, blocks, 1), "core", [(0, 1), (1, 0)])
     coded = encode(product(slabs, blocks, 0), theirs)

time: 115 us -> 120 us (1.043)
  the two profiles are of different devices: /device:TPU:6 before, /device:TPU:128 now
where the time goes in v14:
time: 120 us; the launch traced here: 119 us
  starting transfers between devices  50 us (42%)
  blocking collectives  50 us (42%)
  waiting for transfers between devices  11.2 us (9%)
  Pallas kernels  7.97 us (7%)
    all_to_all x1, blocking collectives, local(): lax.all_to_all(coarse_parts(coded, p_tiles, p_mask), z, 0, 0, tiled=True)  34.5 us
    ppermute x1, starting transfers between devices, local(): slab = trim(lax.ppermute(mine, z + ('yh', 'core', 'yl'), spread()))  21.1 us
    all_to_all x1, blocking collectives, local(): coded = lax.all_to_all(coded, 'yh', 0, 0, tiled=True)  15.6 us
    ppermute x2, waiting for transfers between devices, local(): lax.ppermute(slab, z, around(PLANES, turn))  7.79 us
    ppermute x2, starting transfers between devices, local(): lax.ppermute(slab, z, around(PLANES, turn))  7.6 us
    ppermute x2, starting transfers between devices, local(): after = [lax.ppermute(half, 'x', around(4, 1)) for half in own_halves]  7.41 us
    ppermute x2, starting transfers between devices, local(): across = [lax.ppermute(half, 'x', around(4, 1)) for half in after]  6.67 us
    ppermute x1, starting transfers between devices, local(): before = lax.ppermute(own, 'x', around(4, -1))  3.1 us
  transfers between devices with their start and end apart: 10, of which 4 were waited for; matrix products, arithmetic and copies ran while one was open for 0% of the time, Pallas kernels for 1%

profile of v14, /device:TPU:128, one launch (start us, length us, event | category | flops | bytes accessed | tf_op | source)
XLA Modules:
  0.0 119.4 jit_solution(16545312729860930785)
XLA Ops:
  0.0 2.4 %stripes.1 = bf16[400,384]{1,0:T(8,128)(2,1)} custom-call(s32[4,16]{1,0:T(4,128)} %mask.1, bf16[768,3072]{1,0:T(8,128)(2,1)} %tiles.4), custom_call_target="tpu_custom_call" | custom-call | tf_op jit(solution)/shard_map/stripes/pallas_call | solution.py:68
  2.4 0.0 copy-done
  2.4 0.7 masked_operator.1
  3.1 4.7 %collective-permute-start.5 = (bf16[384,384]{1,0:T(8,128)(2,1)S(1)}, bf16[384,384]{1,0:T(8,128)(2,1)S(1)}, u32[]{:S(2)}, u32[]{:S(2)}) collective-permute-start(bf16[384,384]{1,0:T(8,128)(2,1)S(1)} %get-tuple-element.11), channel_id=1, source_target_pairs={{16,0},{32,16},{48,32},{0,48},{17,1},{33,17},{49,33},{1,49},{18,2}... | collective-permute-start | bytes 884744 | tf_op jit(solution)/shard_map/ppermute | solution.py:312
  7.8 21.1 %collective-permute-start = (bf16[400,384]{1,0:T(8,128)(2,1)}, bf16[400,384]{1,0:T(8,128)(2,1)S(1)}, u32[]{:S(2)}, u32[]{:S(2)}) collective-permute-start(bf16[400,384]{1,0:T(8,128)(2,1)} %stripes.1), channel_id=1, source_target_pairs={{0,768},{1,769},{2,258},{3,3},{4,513},{5,257},{6,259},{7,771},{8,1... | collective-permute-start | bytes 921608 | tf_op jit(solution)/shard_map/ppermute | solution.py:309
  28.9 2.7 %collective-permute-start.6 = (bf16[384,384]{1,0:T(8,128)(2,1)S(1)}, bf16[384,384]{1,0:T(8,128)(2,1)S(1)}, u32[]{:S(2)}, u32[]{:S(2)}) collective-permute-start(bf16[384,384]{1,0:T(8,128)(2,1)S(1)} %get-tuple-element.12), channel_id=1, source_target_pairs={{16,0},{32,16},{48,32},{0,48},{17,1},{33,17},{49,33},{1,49},{18,2}... | collective-permute-start | bytes 884744 | tf_op jit(solution)/shard_map/ppermute | solution.py:312
  31.7 3.1 %collective-permute-start.4 = (bf16[768,384]{1,0:T(8,128)(2,1)S(1)}, bf16[768,384]{1,0:T(8,128)(2,1)S(1)}, u32[]{:S(2)}, u32[]{:S(2)}) collective-permute-start(bf16[768,384]{1,0:T(8,128)(2,1)S(1)} %get-tuple-element.10.refs_4_), channel_id=1, source_target_pairs={{48,0},{0,16},{16,32},{32,48},{49,1},{1,17},{17,33},{33,49},{50,2}... | collective-permute-start | bytes 1769480 | tf_op jit(solution)/shard_map/ppermute | solution.py:313
  34.8 0.0 collective-permute-done.5.refs_6_
  34.8 4.0 %collective-permute-start.7 = (bf16[384,384]{1,0:T(8,128)(2,1)S(1)}, bf16[384,384]{1,0:T(8,128)(2,1)S(1)}, u32[]{:S(2)}, u32[]{:S(2)}) collective-permute-start(bf16[384,384]{1,0:T(8,128)(2,1)S(1)} %collective-permute-done.5.refs_6_), channel_id=1, source_target_pairs={{16,0},{32,16},{48,32},{0,48},{17,1},{33,17},{49,33},{1,49},{18,2}... | collective-permute-start | bytes 884744 | tf_op jit(solution)/shard_map/ppermute | solution.py:317
  38.7 0.0 collective-permute-done.6.refs_7_
  38.8 2.7 %collective-permute-start.8 = (bf16[384,384]{1,0:T(8,128)(2,1)S(1)}, bf16[384,384]{1,0:T(8,128)(2,1)S(1)}, u32[]{:S(2)}, u32[]{:S(2)}) collective-permute-start(bf16[384,384]{1,0:T(8,128)(2,1)S(1)} %collective-permute-done.6.refs_7_), channel_id=1, source_target_pairs={{16,0},{32,16},{48,32},{0,48},{17,1},{33,17},{49,33},{1,49},{18,2}... | collective-permute-start | bytes 884744 | tf_op jit(solution)/shard_map/ppermute | solution.py:317
  41.5 0.0 collective-permute-done.padded
  41.5 0.0 slice-start.1
  41.5 0.0 copy-start.1
  41.5 2.2 %collective-permute-start.3 = (bf16[384,384]{1,0:T(8,128)(2,1)S(1)}, bf16[384,384]{1,0:T(8,128)(2,1)S(1)}, u32[]{:S(2)}, u32[]{:S(2)}) collective-permute-start(bf16[384,384]{1,0:T(8,128)(2,1)S(1)} %trim.1.refs_0_), channel_id=1, source_target_pairs={{128,0},{898,2},{192,64},{962,66},{256,128},{2,130},{320,192},{66,... | collective-permute-start | bytes 884744 | tf_op jit(solution)/shard_map/ppermute | solution.py:316
  43.7 5.7 %collective-permute-start.2 = (bf16[384,384]{1,0:T(8,128)(2,1)S(1)}, bf16[384,384]{1,0:T(8,128)(2,1)S(1)}, u32[]{:S(2)}, u32[]{:S(2)}) collective-permute-start(bf16[384,384]{1,0:T(8,128)(2,1)S(1)} %trim.1.refs_0_), channel_id=1, source_target_pairs={{960,0},{0,64},{64,128},{128,192},{192,256},{256,320},{320,384},{3... | collective-permute-start | bytes 884744 | tf_op jit(solution)/shard_map/ppermute | solution.py:315
  49.4 0.0 collective-permute-done.7.refs_8_
  49.4 1.9 %collective-permute-start.1 = (bf16[384,384]{1,0:T(8,128)(2,1)S(1)}, bf16[384,384]{1,0:T(8,128)(2,1)S(1)}, u32[]{:S(2)}, u32[]{:S(2)}) collective-permute-start(bf16[384,384]{1,0:T(8,128)(2,1)S(1)} %trim.1.refs_0_), channel_id=1, source_target_pairs={{64,0},{128,64},{192,128},{256,192},{320,256},{384,320},{448,384},... | collective-permute-start | bytes 884744 | tf_op jit(solution)/shard_map/ppermute | solution.py:315
  51.4 0.0 collective-permute-done.8.refs_9_
  51.4 0.0 collective-permute-done.4.refs_5_
  51.4 2.5 %collective-permute-done.3.refs_3_ = bf16[384,384]{1,0:T(8,128)(2,1)S(1)} collective-permute-done((bf16[384,384]{1,0:T(8,128)(2,1)S(1)}, bf16[384,384]{1,0:T(8,128)(2,1)S(1)}, u32[]{:S(2)}, u32[]{:S(2)}) %collective-permute-start.3) | collective-permute-done | bytes 294944 | tf_op jit(solution)/shard_map/ppermute | solution.py:316
  53.9 1.8 %collective-permute-done.2.refs_2_ = bf16[384,384]{1,0:T(8,128)(2,1)S(1)} collective-permute-done((bf16[384,384]{1,0:T(8,128)(2,1)S(1)}, bf16[384,384]{1,0:T(8,128)(2,1)S(1)}, u32[]{:S(2)}, u32[]{:S(2)}) %collective-permute-start.2) | collective-permute-done | bytes 294944 | tf_op jit(solution)/shard_map/ppermute | solution.py:315
  55.7 5.9 %collective-permute-done.1.refs_1_ = bf16[384,384]{1,0:T(8,128)(2,1)S(1)} collective-permute-done((bf16[384,384]{1,0:T(8,128)(2,1)S(1)}, bf16[384,384]{1,0:T(8,128)(2,1)S(1)}, u32[]{:S(2)}, u32[]{:S(2)}) %collective-permute-start.1) | collective-permute-done | bytes 294944 | tf_op jit(solution)/shard_map/ppermute | solution.py:315
  61.7 1.1 product_for_other.1
  62.8 1.9 %collective-permute-start.9 = (f32[4,48,768]{2,1,0:T(8,128)S(1)}, f32[4,48,768]{2,1,0:T(8,128)S(1)}, u32[]{:S(2)}, u32[]{:S(2)}) collective-permute-start(f32[4,48,768]{2,1,0:T(8,128)S(1)} %product_for_other.1), channel_id=1, source_target_pairs={{0,2},{2,0},{1,3},{3,1},{4,6},{6,4},{5,7},{7,5},{8,10},{10,8},{9,1... | collective-permute-start | bytes 1769480 | tf_op jit(solution)/shard_map/ppermute | solution.py:320
  64.7 1.1 product.1.mine
  65.8 0.9 collective-permute-done.9.theirs
  66.7 0.2 encode.1
  66.8 15.6 %all_to_all.10.parts = s16[4,296,128]{2,1,0:T(8,128)(2,1)S(1)} all-to-all(s16[4,296,128]{2,1,0:T(8,128)(2,1)S(1)} %encode.1), channel_id=1, replica_groups=mesh['zh'=4,'zl'=4,'x'=4,'yh'=4,'core'=2,'yl'=2] {'yh'}, dimensions={0} | all-to-all | bytes 606208 | tf_op jit(solution)/shard_map/all_to_all | solution.py:322
  82.4 1.8 %coarse_parts.1 = s16[16,80,128]{2,1,0:T(8,128)(2,1)S(1)} custom-call(s32[4,16]{1,0:T(4,128)S(1)} %copy-done.1, s16[4,296,128]{2,1,0:T(8,128)(2,1)S(1)} %all_to_all.10.parts, bf16[768,3072]{1,0:T(8,128)(2,1)S(1)} %bitcast.3), custom_call_target="tpu_custom_call" | custom-call | tf_op jit(solution)/shard_map/coarse_parts/pallas_call | solution.py:227
  84.2 34.5 %all_to_all.11.coded = s16[16,80,128]{2,1,0:T(8,128)(2,1)S(1)} all-to-all(s16[16,80,128]{2,1,0:T(8,128)(2,1)S(1)} %coarse_parts.1), channel_id=1, replica_groups=mesh['zh'=4,'zl'=4,'x'=4,'yh'=4,'core'=2,'yl'=2] {'zh','zl'}, dimensions={0} | all-to-all | bytes 655360 | tf_op jit(solution)/shard_map/all_to_all | solution.py:323
  118.7 0.7 summed.1
  (9 shorter events, 0.0 us)
Async XLA Ops:
  0.0 2.4 %copy-start = (bf16[768,384]{1,0:T(8,128)(2,1)S(1)}, bf16[768,384]{1,0:T(8,128)(2,1)}, u32[]{:S(2)}) copy-start(bf16[768,384]{1,0:T(8,128)(2,1)} %tiles.3) | copy-start | bytes 1769476
  0.0 2.4 %copy-start.2 = (s32[4,2]{0,1:T(2,128)S(1)}, s32[4,2]{0,1:T(2,128)}, u32[]{:S(2)}) copy-start(s32[4,2]{0,1:T(2,128)} %param.6) | copy-start | bytes 100
  0.0 82.4 %slice-start = ((s8[4718592]{0:T(1024)(128)(4,1)}), s8[524288]{0:T(1024)(128)(4,1)S(1)}, s32[]{:S(2)}) async-start(s8[4718592]{0:T(1024)(128)(4,1)} %bitcast.2), calls=%async_computation.2 | async-start | bytes 1048576
  3.1 31.7 %collective-permute-start.5 = (bf16[384,384]{1,0:T(8,128)(2,1)S(1)}, bf16[384,384]{1,0:T(8,128)(2,1)S(1)}, u32[]{:S(2)}, u32[]{:S(2)}) collective-permute-start(bf16[384,384]{1,0:T(8,128)(2,1)S(1)} %get-tuple-element.11), channel_id=1, source_target_pairs={{16,0},{32,16},{48,32},{0,48},{17,1},{33,17},{49,33},{1,49},{18,2}... | collective-permute-start | bytes 884744 | tf_op jit(solution)/shard_map/ppermute | solution.py:312
  7.8 33.7 %collective-permute-start = (bf16[400,384]{1,0:T(8,128)(2,1)}, bf16[400,384]{1,0:T(8,128)(2,1)S(1)}, u32[]{:S(2)}, u32[]{:S(2)}) collective-permute-start(bf16[400,384]{1,0:T(8,128)(2,1)} %stripes.1), channel_id=1, source_target_pairs={{0,768},{1,769},{2,258},{3,3},{4,513},{5,257},{6,259},{7,771},{8,1... | collective-permute-start | bytes 921608 | tf_op jit(solution)/shard_map/ppermute | solution.py:309
  28.9 9.8 %collective-permute-start.6 = (bf16[384,384]{1,0:T(8,128)(2,1)S(1)}, bf16[384,384]{1,0:T(8,128)(2,1)S(1)}, u32[]{:S(2)}, u32[]{:S(2)}) collective-permute-start(bf16[384,384]{1,0:T(8,128)(2,1)S(1)} %get-tuple-element.12), channel_id=1, source_target_pairs={{16,0},{32,16},{48,32},{0,48},{17,1},{33,17},{49,33},{1,49},{18,2}... | collective-permute-start | bytes 884744 | tf_op jit(solution)/shard_map/ppermute | solution.py:312
  31.7 19.7 %collective-permute-start.4 = (bf16[768,384]{1,0:T(8,128)(2,1)S(1)}, bf16[768,384]{1,0:T(8,128)(2,1)S(1)}, u32[]{:S(2)}, u32[]{:S(2)}) collective-permute-start(bf16[768,384]{1,0:T(8,128)(2,1)S(1)} %get-tuple-element.10.refs_4_), channel_id=1, source_target_pairs={{48,0},{0,16},{16,32},{32,48},{49,1},{1,17},{17,33},{33,49},{50,2}... | collective-permute-start | bytes 1769480 | tf_op jit(solution)/shard_map/ppermute | solution.py:313
  34.8 14.7 %collective-permute-start.7 = (bf16[384,384]{1,0:T(8,128)(2,1)S(1)}, bf16[384,384]{1,0:T(8,128)(2,1)S(1)}, u32[]{:S(2)}, u32[]{:S(2)}) collective-permute-start(bf16[384,384]{1,0:T(8,128)(2,1)S(1)} %collective-permute-done.5.refs_6_), channel_id=1, source_target_pairs={{16,0},{32,16},{48,32},{0,48},{17,1},{33,17},{49,33},{1,49},{18,2}... | collective-permute-start | bytes 884744 | tf_op jit(solution)/shard_map/ppermute | solution.py:317
  38.8 12.6 %collective-permute-start.8 = (bf16[384,384]{1,0:T(8,128)(2,1)S(1)}, bf16[384,384]{1,0:T(8,128)(2,1)S(1)}, u32[]{:S(2)}, u32[]{:S(2)}) collective-permute-start(bf16[384,384]{1,0:T(8,128)(2,1)S(1)} %collective-permute-done.6.refs_7_), channel_id=1, source_target_pairs={{16,0},{32,16},{48,32},{0,48},{17,1},{33,17},{49,33},{1,49},{18,2}... | collective-permute-start | bytes 884744 | tf_op jit(solution)/shard_map/ppermute | solution.py:317
  41.5 40.9 %slice-start.1 = ((s8[4718592]{0:T(1024)(128)(4,1)}), s8[4194304]{0:T(1024)(128)(4,1)S(1)}, s32[]{:S(2)}) async-start(s8[4718592]{0:T(1024)(128)(4,1)} %bitcast.2), calls=%async_computation.3 | async-start | bytes 8388608
  41.5 40.9 %copy-start.1 = (s32[4,16]{1,0:T(4,128)S(1)}, s32[4,16]{1,0:T(4,128)}, u32[]{:S(2)}) copy-start(s32[4,16]{1,0:T(4,128)} %mask.1) | copy-start | bytes 772
  41.5 12.3 %collective-permute-start.3 = (bf16[384,384]{1,0:T(8,128)(2,1)S(1)}, bf16[384,384]{1,0:T(8,128)(2,1)S(1)}, u32[]{:S(2)}, u32[]{:S(2)}) collective-permute-start(bf16[384,384]{1,0:T(8,128)(2,1)S(1)} %trim.1.refs_0_), channel_id=1, source_target_pairs={{128,0},{898,2},{192,64},{962,66},{256,128},{2,130},{320,192},{66,... | collective-permute-start | bytes 884744 | tf_op jit(solution)/shard_map/ppermute | solution.py:316
  43.7 12.0 %collective-permute-start.2 = (bf16[384,384]{1,0:T(8,128)(2,1)S(1)}, bf16[384,384]{1,0:T(8,128)(2,1)S(1)}, u32[]{:S(2)}, u32[]{:S(2)}) collective-permute-start(bf16[384,384]{1,0:T(8,128)(2,1)S(1)} %trim.1.refs_0_), channel_id=1, source_target_pairs={{960,0},{0,64},{64,128},{128,192},{192,256},{256,320},{320,384},{3... | collective-permute-start | bytes 884744 | tf_op jit(solution)/shard_map/ppermute | solution.py:315
  49.4 12.2 %collective-permute-start.1 = (bf16[384,384]{1,0:T(8,128)(2,1)S(1)}, bf16[384,384]{1,0:T(8,128)(2,1)S(1)}, u32[]{:S(2)}, u32[]{:S(2)}) collective-permute-start(bf16[384,384]{1,0:T(8,128)(2,1)S(1)} %trim.1.refs_0_), channel_id=1, source_target_pairs={{64,0},{128,64},{192,128},{256,192},{320,256},{384,320},{448,384},... | collective-permute-start | bytes 884744 | tf_op jit(solution)/shard_map/ppermute | solution.py:315
  62.8 3.9 %collective-permute-start.9 = (f32[4,48,768]{2,1,0:T(8,128)S(1)}, f32[4,48,768]{2,1,0:T(8,128)S(1)}, u32[]{:S(2)}, u32[]{:S(2)}) collective-permute-start(f32[4,48,768]{2,1,0:T(8,128)S(1)} %product_for_other.1), channel_id=1, source_target_pairs={{0,2},{2,0},{1,3},{3,1},{4,6},{6,4},{5,7},{7,5},{8,10},{10,8},{9,1... | collective-permute-start | bytes 1769480 | tf_op jit(solution)/shard_map/ppermute | solution.py:320

commit v15 on v14

--- a/solution.py
+++ b/solution.py
@@ -93,17 +93,18 @@
         out[rows, :] = tiles[rows, :] * present.astype(BF16)
 
 
-def operator_kernel(mask, tiles, whole, upper, lower):
-    mask_rows(lambda i, k: mask[k, i], tiles, whole, 0)
-    upper[...], lower[...] = whole[:HALF], whole[HALF:]
+def operator_kernel(mask, tiles, out):
+    mask_rows(lambda i, k: mask[k, i], tiles, out.at[0], 0)
+    for n in range(1, 4):
+        out[n] = out[0]
 
 
 def masked_operator(a_tiles, a_mask):
     return pl.pallas_call(
         operator_kernel,
-        out_shape=[jax.ShapeDtypeStruct((n * HALF, HALF), BF16) for n in (2, 1, 1)],
+        out_shape=jax.ShapeDtypeStruct((4,) + a_tiles.shape, BF16),
         in_specs=[pl.BlockSpec(memory_space=pltpu.SMEM), pl.BlockSpec(memory_space=pltpu.VMEM)],
-        out_specs=[pl.BlockSpec(memory_space=pltpu.VMEM)] * 3,
+        out_specs=pl.BlockSpec(memory_space=pltpu.VMEM),
         compiler_params=params(),
         name="masked_operator",
     )(a_mask.T, a_tiles)
@@ -125,33 +126,30 @@
 
 
 def product_kernel(other, *refs):
-    slabs, (own, behind), halves, out, columns = refs[:4], refs[4:6], refs[6:10], refs[10], refs[11]
-    x, zl, yh = lax.axis_index("x"), lax.axis_index("zl"), lax.axis_index("yh")
+    slabs, blocks, out, columns = refs[:4], refs[4], refs[5], refs[6]
+    zl, yh = lax.axis_index("zl"), lax.axis_index("yh")
     core = (lax.axis_index("core") + other) % 2
     for n, slab in zip((0, 1, 3, 2), slabs):
         block = block_of(yh, (zl + n) % 4)
         for y in range(4):
             rows = pl.ds(pl.multiple_of((2 * y + core) * WIDE, WIDE), WIDE)
             columns[block, y * WIDE : (y + 1) * WIDE] = slab[rows, :]
-    for half in range(2):
-        rows = slice(half * HALF, (half + 1) * HALF)
-        total = dot_last(columns[x], own[rows, :])
-        total = total + dot_last(columns[(x + 1) % 4], halves[half][...])
-        total = total + dot_last(columns[(x + 2) % 4], halves[2 + half][...])
-        total = total + dot_last(columns[(x + 3) % 4], behind[rows, :])
-        out[:, :, rows] = total.reshape(4, WIDE, HALF)
+    total = dot_last(columns[0], blocks[0])
+    for n in range(1, 4):
+        total = total + dot_last(columns[n], blocks[n])
+    out[...] = total.reshape(4, WIDE, ROWS)
 
 
 def product(slabs, blocks, other):
     return pl.pallas_call(
         functools.partial(product_kernel, other),
         out_shape=jax.ShapeDtypeStruct((4, WIDE, ROWS), F32),
-        in_specs=[pl.BlockSpec(memory_space=pltpu.VMEM)] * 10,
+        in_specs=[pl.BlockSpec(memory_space=pltpu.VMEM)] * 5,
         out_specs=pl.BlockSpec(memory_space=pltpu.VMEM),
         scratch_shapes=[pltpu.VMEM((4, 4 * WIDE, HALF), BF16)],
         compiler_params=params(),
         name="product_for_other" if other else "product",
-    )(*slabs, *blocks)
+    )(*slabs, blocks)
 
 
 def scale_code(most):
@@ -308,14 +306,10 @@
     mine = stripes(p_tiles, p_mask)
     slab = trim(lax.ppermute(mine, z + ("yh", "core", "yl"), spread()))
     a_tiles, mine = lax.optimization_barrier((a_tiles, mine))
-    own, *own_halves = masked_operator(a_tiles, a_mask)
-    after = [lax.ppermute(half, "x", around(4, 1)) for half in own_halves]
-    before = lax.ppermute(own, "x", around(4, -1))
+    blocks = lax.all_to_all(masked_operator(a_tiles, a_mask), "x", 0, 0, tiled=True)
 
     above, below = [lax.ppermute(slab, z, around(PLANES, turn)) for turn in (1, -1)]
     slabs = [slab, above, below, lax.ppermute(slab, z + ("core",), two_away())]
-    across = [lax.ppermute(half, "x", around(4, 1)) for half in after]
-    blocks = [own, before, *after, *across]
 
     theirs = lax.ppermute(product(slabs, blocks, 1), "core", [(0, 1), (1, 0)])
     coded = encode(product(slabs, blocks, 0), theirs)

time: 120 us -> 123 us (1.025)
  the two profiles are of different devices: /device:TPU:128 before, /device:TPU:6 now
where the time goes in v15:
time: 123 us; the launch traced here: 122 us
  blocking collectives  52 us (42%)
  starting transfers between devices  47 us (38%)
  waiting for transfers between devices  11.5 us (9%)
  Pallas kernels  7.9 us (6%)
  local copies, waits for them, and re-layouts  3.77 us (3%)
    all_to_all x1, blocking collectives, local(): lax.all_to_all(coarse_parts(coded, p_tiles, p_mask), z, 0, 0, tiled=True)  26.3 us
    all_to_all x1, blocking collectives, local(): coded = lax.all_to_all(coded, 'yh', 0, 0, tiled=True)  25.7 us
    all_to_all x1, starting transfers between devices, local(): lax.all_to_all(masked_operator(a_tiles, a_mask), 'x', 0, 0, tiled=True)  16.9 us
    ppermute x1, starting transfers between devices, local(): slabs = [slab, above, below, lax.ppermute(slab, z + ('core',), two_away())]  14.5 us
    ppermute x2, starting transfers between devices, local(): lax.ppermute(slab, z, around(PLANES, turn))  7.39 us
    ppermute x1, starting transfers between devices, local(): slab = trim(lax.ppermute(mine, z + ('yh', 'core', 'yl'), spread()))  6.22 us
    ppermute x2, waiting for transfers between devices, local(): lax.ppermute(slab, z, around(PLANES, turn))  4.41 us
    ppermute x1, waiting for transfers between devices, local(): slab = trim(lax.ppermute(mine, z + ('yh', 'core', 'yl'), spread()))  4.38 us
  transfers between devices with their start and end apart: 6, of which 5 were waited for; matrix products, arithmetic and copies ran while one was open for 0% of the time, Pallas kernels for 1%

profile of v15, /device:TPU:6, one launch (start us, length us, event | category | flops | bytes accessed | tf_op | source)
XLA Modules:
  0.0 122.3 jit_solution(10886581783583491602)
XLA Ops:
  0.0 0.0 copy-start.2
  0.0 0.0 copy-start.4
  0.0 2.4 %stripes.1 = bf16[400,384]{1,0:T(8,128)(2,1)} custom-call(s32[4,16]{1,0:T(4,128)} %mask.1, bf16[768,3072]{1,0:T(8,128)(2,1)} %tiles.4), custom_call_target="tpu_custom_call" | custom-call | tf_op jit(solution)/shard_map/stripes/pallas_call | solution.py:68
  2.4 0.0 copy-done.2
  2.4 0.0 copy-done.4
  2.4 0.8 masked_operator.1
  3.2 0.0 copy-start.1
  3.2 1.4 %copy-done.1 = bf16[4,768,384]{2,1,0:T(8,128)(2,1)} copy-done((bf16[4,768,384]{2,1,0:T(8,128)(2,1)}, bf16[4,768,384]{2,1,0:T(8,128)(2,1)S(1)}, u32[]{:S(2)}) %copy-start.1) | copy-done | bytes 2359320
  4.6 0.0 copy-start.5
  4.6 16.9 %all-to-all-start = ((bf16[4,768,384]{2,1,0:T(8,128)(2,1)}), bf16[4,768,384]{2,1,0:T(8,128)(2,1)S(1)}, u32[]{:S(2)}, u32[]{:S(2)}) async-start(bf16[4,768,384]{2,1,0:T(8,128)(2,1)} %copy-done.1), calls=%async_computation | async-start | bytes 4718592 | tf_op jit(solution)/shard_map/all_to_all | solution.py:309
  21.5 0.0 copy-done.5
  21.5 6.2 %collective-permute-start = (bf16[400,384]{1,0:T(8,128)(2,1)S(1)}, bf16[400,384]{1,0:T(8,128)(2,1)S(1)}, u32[]{:S(2)}, u32[]{:S(2)}) collective-permute-start(bf16[400,384]{1,0:T(8,128)(2,1)S(1)} %copy-done.5), channel_id=1, source_target_pairs={{0,768},{1,769},{2,258},{3,3},{4,513},{5,257},{6,259},{7,771},{8,1... | collective-permute-start | bytes 921608 | tf_op jit(solution)/shard_map/ppermute | solution.py:307
  27.7 4.4 %collective-permute-done.padded = bf16[400,384]{1,0:T(8,128)(2,1)S(1)} collective-permute-done((bf16[400,384]{1,0:T(8,128)(2,1)S(1)}, bf16[400,384]{1,0:T(8,128)(2,1)S(1)}, u32[]{:S(2)}, u32[]{:S(2)}) %collective-permute-start) | collective-permute-done | bytes 307232 | tf_op jit(solution)/shard_map/ppermute | solution.py:307
  32.1 14.5 %collective-permute-start.3 = (bf16[384,384]{1,0:T(8,128)(2,1)S(1)}, bf16[384,384]{1,0:T(8,128)(2,1)S(1)}, u32[]{:S(2)}, u32[]{:S(2)}) collective-permute-start(bf16[384,384]{1,0:T(8,128)(2,1)S(1)} %trim.1.refs_0_), channel_id=1, source_target_pairs={{128,0},{898,2},{192,64},{962,66},{256,128},{2,130},{320,192},{66,... | collective-permute-start | bytes 884744 | tf_op jit(solution)/shard_map/ppermute | solution.py:312
  46.6 1.9 %collective-permute-start.2 = (bf16[384,384]{1,0:T(8,128)(2,1)S(1)}, bf16[384,384]{1,0:T(8,128)(2,1)S(1)}, u32[]{:S(2)}, u32[]{:S(2)}) collective-permute-start(bf16[384,384]{1,0:T(8,128)(2,1)S(1)} %trim.1.refs_0_), channel_id=1, source_target_pairs={{960,0},{0,64},{64,128},{128,192},{192,256},{256,320},{320,384},{3... | collective-permute-start | bytes 884744 | tf_op jit(solution)/shard_map/ppermute | solution.py:311
  48.6 5.5 %collective-permute-start.1 = (bf16[384,384]{1,0:T(8,128)(2,1)S(1)}, bf16[384,384]{1,0:T(8,128)(2,1)S(1)}, u32[]{:S(2)}, u32[]{:S(2)}) collective-permute-start(bf16[384,384]{1,0:T(8,128)(2,1)S(1)} %trim.1.refs_0_), channel_id=1, source_target_pairs={{64,0},{128,64},{192,128},{256,192},{320,256},{384,320},{448,384},... | collective-permute-start | bytes 884744 | tf_op jit(solution)/shard_map/ppermute | solution.py:311
  54.0 1.9 %collective-permute-done.3.refs_3_ = bf16[384,384]{1,0:T(8,128)(2,1)S(1)} collective-permute-done((bf16[384,384]{1,0:T(8,128)(2,1)S(1)}, bf16[384,384]{1,0:T(8,128)(2,1)S(1)}, u32[]{:S(2)}, u32[]{:S(2)}) %collective-permute-start.3) | collective-permute-done | bytes 294944 | tf_op jit(solution)/shard_map/ppermute | solution.py:312
  55.9 4.2 %collective-permute-done.2.refs_2_ = bf16[384,384]{1,0:T(8,128)(2,1)S(1)} collective-permute-done((bf16[384,384]{1,0:T(8,128)(2,1)S(1)}, bf16[384,384]{1,0:T(8,128)(2,1)S(1)}, u32[]{:S(2)}, u32[]{:S(2)}) %collective-permute-start.2) | collective-permute-done | bytes 294944 | tf_op jit(solution)/shard_map/ppermute | solution.py:311
  60.1 0.3 collective-permute-done.1.refs_1_
  60.3 0.0 all-to-all-done.refs_4_
  60.3 1.0 product_for_other.1
  61.3 0.0 copy-start.3
  61.4 2.0 %collective-permute-start.4 = (f32[4,48,768]{2,1,0:T(8,128)S(1)}, f32[4,48,768]{2,1,0:T(8,128)S(1)}, u32[]{:S(2)}, u32[]{:S(2)}) collective-permute-start(f32[4,48,768]{2,1,0:T(8,128)S(1)} %product_for_other.1), channel_id=1, source_target_pairs={{0,2},{2,0},{1,3},{3,1},{4,6},{6,4},{5,7},{7,5},{8,10},{10,8},{9,1... | collective-permute-start | bytes 1769480 | tf_op jit(solution)/shard_map/ppermute | solution.py:314
  63.4 1.0 product.1.mine
  64.4 0.8 collective-permute-done.4.theirs
  65.3 0.2 encode.1
  65.4 25.7 %all_to_all.15.parts = s16[4,296,128]{2,1,0:T(8,128)(2,1)S(1)} all-to-all(s16[4,296,128]{2,1,0:T(8,128)(2,1)S(1)} %encode.1), channel_id=1, replica_groups=mesh['zh'=4,'zl'=4,'x'=4,'yh'=4,'core'=2,'yl'=2] {'yh'}, dimensions={0} | all-to-all | bytes 606208 | tf_op jit(solution)/shard_map/all_to_all | solution.py:316
  91.1 0.0 copy-done.3
  91.1 2.3 %copy-done = bf16[768,3072]{1,0:T(8,128)(2,1)S(1)} copy-done((bf16[768,3072]{1,0:T(8,128)(2,1)S(1)}, bf16[768,3072]{1,0:T(8,128)(2,1)}, u32[]{:S(2)}) %copy-start) | copy-done | bytes 4718616
  93.5 1.8 %coarse_parts.1 = s16[16,80,128]{2,1,0:T(8,128)(2,1)S(1)} custom-call(s32[4,16]{1,0:T(4,128)S(1)} %copy-done.3, s16[4,296,128]{2,1,0:T(8,128)(2,1)S(1)} %all_to_all.15.parts, bf16[768,3072]{1,0:T(8,128)(2,1)S(1)} %copy-done), custom_call_target="tpu_custom_call" | custom-call | tf_op jit(solution)/shard_map/coarse_parts/pallas_call | solution.py:225
  95.3 26.3 %all_to_all.16.coded = s16[16,80,128]{2,1,0:T(8,128)(2,1)S(1)} all-to-all(s16[16,80,128]{2,1,0:T(8,128)(2,1)S(1)} %coarse_parts.1), channel_id=1, replica_groups=mesh['zh'=4,'zl'=4,'x'=4,'yh'=4,'core'=2,'yl'=2] {'zh','zl'}, dimensions={0} | all-to-all | bytes 655360 | tf_op jit(solution)/shard_map/all_to_all | solution.py:317
  121.5 0.7 summed.1
  (2 shorter events, 0.0 us)
Async XLA Ops:
  0.0 2.4 %copy-start.2 = (bf16[768,384]{1,0:T(8,128)(2,1)S(1)}, bf16[768,384]{1,0:T(8,128)(2,1)}, u32[]{:S(2)}) copy-start(bf16[768,384]{1,0:T(8,128)(2,1)} %tiles.3) | copy-start | bytes 1769476
  0.0 2.4 %copy-start.4 = (s32[4,2]{0,1:T(2,128)S(1)}, s32[4,2]{0,1:T(2,128)}, u32[]{:S(2)}) copy-start(s32[4,2]{0,1:T(2,128)} %param.6) | copy-start | bytes 100
  3.2 1.4 %copy-start.1 = (bf16[4,768,384]{2,1,0:T(8,128)(2,1)}, bf16[4,768,384]{2,1,0:T(8,128)(2,1)S(1)}, u32[]{:S(2)}) copy-start(bf16[4,768,384]{2,1,0:T(8,128)(2,1)S(1)} %masked_operator.1) | copy-start | bytes 7077892
  4.6 16.9 %copy-start.5 = (bf16[400,384]{1,0:T(8,128)(2,1)S(1)}, bf16[400,384]{1,0:T(8,128)(2,1)}, u32[]{:S(2)}) copy-start(bf16[400,384]{1,0:T(8,128)(2,1)} %stripes.1) | copy-start | bytes 921604
  4.6 55.7 %all-to-all-start = ((bf16[4,768,384]{2,1,0:T(8,128)(2,1)}), bf16[4,768,384]{2,1,0:T(8,128)(2,1)S(1)}, u32[]{:S(2)}, u32[]{:S(2)}) async-start(bf16[4,768,384]{2,1,0:T(8,128)(2,1)} %copy-done.1), calls=%async_computation | async-start | bytes 4718592 | tf_op jit(solution)/shard_map/all_to_all | solution.py:309
  21.5 10.6 %collective-permute-start = (bf16[400,384]{1,0:T(8,128)(2,1)S(1)}, bf16[400,384]{1,0:T(8,128)(2,1)S(1)}, u32[]{:S(2)}, u32[]{:S(2)}) collective-permute-start(bf16[400,384]{1,0:T(8,128)(2,1)S(1)} %copy-done.5), channel_id=1, source_target_pairs={{0,768},{1,769},{2,258},{3,3},{4,513},{5,257},{6,259},{7,771},{8,1... | collective-permute-start | bytes 921608 | tf_op jit(solution)/shard_map/ppermute | solution.py:307
  32.1 23.8 %collective-permute-start.3 = (bf16[384,384]{1,0:T(8,128)(2,1)S(1)}, bf16[384,384]{1,0:T(8,128)(2,1)S(1)}, u32[]{:S(2)}, u32[]{:S(2)}) collective-permute-start(bf16[384,384]{1,0:T(8,128)(2,1)S(1)} %trim.1.refs_0_), channel_id=1, source_target_pairs={{128,0},{898,2},{192,64},{962,66},{256,128},{2,130},{320,192},{66,... | collective-permute-start | bytes 884744 | tf_op jit(solution)/shard_map/ppermute | solution.py:312
  46.6 13.4 %collective-permute-start.2 = (bf16[384,384]{1,0:T(8,128)(2,1)S(1)}, bf16[384,384]{1,0:T(8,128)(2,1)S(1)}, u32[]{:S(2)}, u32[]{:S(2)}) collective-permute-start(bf16[384,384]{1,0:T(8,128)(2,1)S(1)} %trim.1.refs_0_), channel_id=1, source_target_pairs={{960,0},{0,64},{64,128},{128,192},{192,256},{256,320},{320,384},{3... | collective-permute-start | bytes 884744 | tf_op jit(solution)/shard_map/ppermute | solution.py:311
  48.6 11.8 %collective-permute-start.1 = (bf16[384,384]{1,0:T(8,128)(2,1)S(1)}, bf16[384,384]{1,0:T(8,128)(2,1)S(1)}, u32[]{:S(2)}, u32[]{:S(2)}) collective-permute-start(bf16[384,384]{1,0:T(8,128)(2,1)S(1)} %trim.1.refs_0_), channel_id=1, source_target_pairs={{64,0},{128,64},{192,128},{256,192},{320,256},{384,320},{448,384},... | collective-permute-start | bytes 884744 | tf_op jit(solution)/shard_map/ppermute | solution.py:311
  61.3 29.8 %copy-start.3 = (s32[4,16]{1,0:T(4,128)S(1)}, s32[4,16]{1,0:T(4,128)}, u32[]{:S(2)}) copy-start(s32[4,16]{1,0:T(4,128)} %mask.1) | copy-start | bytes 772
  61.4 3.9 %collective-permute-start.4 = (f32[4,48,768]{2,1,0:T(8,128)S(1)}, f32[4,48,768]{2,1,0:T(8,128)S(1)}, u32[]{:S(2)}, u32[]{:S(2)}) collective-permute-start(f32[4,48,768]{2,1,0:T(8,128)S(1)} %product_for_other.1), channel_id=1, source_target_pairs={{0,2},{2,0},{1,3},{3,1},{4,6},{6,4},{5,7},{7,5},{8,10},{10,8},{9,1... | collective-permute-start | bytes 1769480 | tf_op jit(solution)/shard_map/ppermute | solution.py:314
  91.1 2.3 %copy-start = (bf16[768,3072]{1,0:T(8,128)(2,1)S(1)}, bf16[768,3072]{1,0:T(8,128)(2,1)}, u32[]{:S(2)}) copy-start(bf16[768,3072]{1,0:T(8,128)(2,1)} %tiles.4) | copy-start | bytes 14155780

commit v16 on v12

--- a/solution.py
+++ b/solution.py
@@ -125,32 +125,59 @@
     )(padded)
 
 
-def product_kernel(other, *refs):
-    slabs, blocks, out, columns = refs[:4], refs[4:12], refs[12], refs[13]
+def add_terms(total, left, blocks, number, x):
+    for n in range(4):
+
+        @pl.when((number - x + 4) % 4 == n)
+        def _():
+            for half in range(2):
+                lanes = slice(half * HALF, (half + 1) * HALF)
+                total[:, lanes] += dot_last(left, blocks[2 * n + half][...])
+
+
+def early_kernel(slab, two_away, *refs):
+    blocks, out = refs[:8], refs[8]
+    x, zl, yh = lax.axis_index("x"), lax.axis_index("zl"), lax.axis_index("yh")
+    out[...] = jnp.zeros_like(out)
+    add_terms(out, slab[...], blocks, block_of(yh, zl), x)
+    add_terms(out, two_away[: 8 * WIDE, :], blocks, block_of(yh, (zl + 2) % 4), x)
+
+
+def early_terms(slab, two_away, blocks):
+    vmem = pl.BlockSpec(memory_space=pltpu.VMEM)
+    return pl.pallas_call(
+        early_kernel,
+        out_shape=jax.ShapeDtypeStruct((8 * WIDE, ROWS), F32),
+        in_specs=[vmem] * 10,
+        out_specs=vmem,
+        compiler_params=params(),
+        name="early_terms",
+    )(slab, two_away, *blocks)
+
+
+def product_kernel(other, early, above, below, *refs):
+    blocks, out, left, total = refs[:8], refs[8], refs[9], refs[10]
     x, zl, yh = lax.axis_index("x"), lax.axis_index("zl"), lax.axis_index("yh")
     core = (lax.axis_index("core") + other) % 2
-    for n, slab in zip((0, 1, 3, 2), slabs):
-        block = block_of(yh, (zl + n) % 4)
-        for y in range(4):
-            rows = pl.ds(pl.multiple_of((2 * y + core) * WIDE, WIDE), WIDE)
-            columns[block, y * WIDE : (y + 1) * WIDE] = slab[rows, :]
-    for half in range(2):
-        total = dot_last(columns[x], blocks[half][...])
-        for n in range(1, 4):
-            total = total + dot_last(columns[(x + n) % 4], blocks[2 * n + half][...])
-        out[:, :, half * HALF : (half + 1) * HALF] = total.reshape(4, WIDE, HALF)
-
-
-def product(slabs, blocks, other):
+    for y in range(4):
+        rows = pl.ds(pl.multiple_of((2 * y + core) * WIDE, WIDE), WIDE)
+        into = slice(y * WIDE, (y + 1) * WIDE)
+        left[0, into], left[1, into], total[into] = above[rows, :], below[rows, :], early[rows, :]
+    add_terms(total, left[0], blocks, block_of(yh, (zl + 1) % 4), x)
+    add_terms(total, left[1], blocks, block_of(yh, (zl + 3) % 4), x)
+    out[...] = total[...].reshape(4, WIDE, ROWS)
+
+
+def product(early, above, below, blocks, other):
     return pl.pallas_call(
         functools.partial(product_kernel, other),
         out_shape=jax.ShapeDtypeStruct((4, WIDE, ROWS), F32),
-        in_specs=[pl.BlockSpec(memory_space=pltpu.VMEM)] * 12,
-        out_specs=pl.BlockSpec(memory_space=pltpu.VMEM),
-        scratch_shapes=[pltpu.VMEM((4, 4 * WIDE, HALF), BF16)],
+        in_specs=[pl.BlockSpec(memory_space=pltpu.VMEM)] * 11,
+        out_specs=pl.BlockSpec(memory_space=pltpu.VMEM),
+        scratch_shapes=[pltpu.VMEM((2, 4 * WIDE, HALF), BF16), pltpu.VMEM((4 * WIDE, ROWS), F32)],
         compiler_params=params(),
         name="product_for_other" if other else "product",
-    )(*slabs, *blocks)
+    )(early, above, below, *blocks)
 
 
 def scale_code(most):
@@ -312,15 +339,16 @@
     before = [lax.ppermute(half, "x", around(4, -1)) for half in own]
 
     above, below = [lax.ppermute(slab, z, around(PLANES, turn)) for turn in (1, -1)]
-    slabs = [slab, above, below, lax.ppermute(slab, z + ("core",), two_away())]
+    far = lax.ppermute(slab, z + ("core",), two_away())
     across = [
         lax.ppermute(after[0], "x", around(4, 1)),
         lax.ppermute(before[1], "x", around(4, -1)),
     ]
     blocks = [*own, *after, *across, *before]
 
-    theirs = lax.ppermute(product(slabs, blocks, 1), "core", [(0, 1), (1, 0)])
-    coded = encode(product(slabs, blocks, 0), theirs)
+    early = early_terms(slab, far, blocks)
+    theirs = lax.ppermute(product(early, above, below, blocks, 1), "core", [(0, 1), (1, 0)])
+    coded = encode(product(early, above, below, blocks, 0), theirs)
     coded = lax.all_to_all(coded, "yh", 0, 0, tiled=True)
     coded = lax.all_to_all(coarse_parts(coded, p_tiles, p_mask), z, 0, 0, tiled=True)
     return summed(coded).T

time: 115 us -> 115 us (level)
  the two profiles are of different devices: /device:TPU:6 before, /device:TPU:4 now
where the time goes in v16:
time: 115 us
  starting transfers between devices  51.4 us (45%)
  blocking collectives  45.8 us (40%)
  Pallas kernels  8.8 us (8%)
  waiting for transfers between devices  8.39 us (7%)
    all_to_all x1, blocking collectives, local(): lax.all_to_all(coarse_parts(coded, p_tiles, p_mask), z, 0, 0, tiled=True)  23.7 us
    all_to_all x1, blocking collectives, local(): coded = lax.all_to_all(coded, 'yh', 0, 0, tiled=True)  22 us
    ppermute x1, starting transfers between devices, local(): slab = trim(lax.ppermute(mine, z + ('yh', 'core', 'yl'), spread()))  18.2 us
    ppermute x2, starting transfers between devices, local(): before = [lax.ppermute(half, 'x', around(4, -1)) for half in own]  7.72 us
    ppermute x2, starting transfers between devices, local(): lax.ppermute(slab, z, around(PLANES, turn))  7.05 us
    ppermute x1, waiting for transfers between devices, local(): far = lax.ppermute(slab, z + ('core',), two_away())  6.44 us
    ppermute x1, starting transfers between devices, local(): far = lax.ppermute(slab, z + ('core',), two_away())  6.25 us
    ppermute x2, starting transfers between devices, local(): after = [lax.ppermute(half, 'x', around(4, 1)) for half in own]  4.36 us
  transfers between devices with their start and end apart: 11, of which 3 were waited for; matrix products, arithmetic and copies ran while one was open for 0% of the time, Pallas kernels for 2%

profile of v16, /device:TPU:4, one launch (start us, length us, event | category | flops | bytes accessed | tf_op | source)
XLA Modules:
  0.0 114.6 jit_solution(9522060389622161108)
XLA Ops:
  0.0 2.4 %stripes.1 = bf16[400,384]{1,0:T(8,128)(2,1)} custom-call(s32[4,16]{1,0:T(4,128)} %mask.1, bf16[768,3072]{1,0:T(8,128)(2,1)} %tiles.4), custom_call_target="tpu_custom_call" | custom-call | tf_op jit(solution)/shard_map/stripes/pallas_call | solution.py:68
  2.4 18.2 %collective-permute-start = (bf16[400,384]{1,0:T(8,128)(2,1)}, bf16[400,384]{1,0:T(8,128)(2,1)S(1)}, u32[]{:S(2)}, u32[]{:S(2)}) collective-permute-start(bf16[400,384]{1,0:T(8,128)(2,1)} %stripes.1), channel_id=1, source_target_pairs={{0,768},{1,769},{2,258},{3,3},{4,513},{5,257},{6,259},{7,771},{8,1... | collective-permute-start | bytes 921608 | tf_op jit(solution)/shard_map/ppermute | solution.py:335
  20.6 0.6 masked_operator.1
  21.2 2.4 %collective-permute-start.2 = (bf16[384,384]{1,0:T(8,128)(2,1)S(1)}, bf16[384,384]{1,0:T(8,128)(2,1)S(1)}, u32[]{:S(2)}, u32[]{:S(2)}) collective-permute-start(bf16[384,384]{1,0:T(8,128)(2,1)S(1)} %get-tuple-element.9.refs_0_), channel_id=1, source_target_pairs={{16,0},{32,16},{48,32},{0,48},{17,1},{33,17},{49,33},{1,49},{18,2}... | collective-permute-start | bytes 884744 | tf_op jit(solution)/shard_map/ppermute | solution.py:338
  23.7 3.4 %collective-permute-start.5 = (bf16[384,384]{1,0:T(8,128)(2,1)S(1)}, bf16[384,384]{1,0:T(8,128)(2,1)S(1)}, u32[]{:S(2)}, u32[]{:S(2)}) collective-permute-start(bf16[384,384]{1,0:T(8,128)(2,1)S(1)} %get-tuple-element.10.refs_1_), channel_id=1, source_target_pairs={{48,0},{0,16},{16,32},{32,48},{49,1},{1,17},{17,33},{33,49},{50,2}... | collective-permute-start | bytes 884744 | tf_op jit(solution)/shard_map/ppermute | solution.py:339
  27.1 4.3 %collective-permute-start.7 = (bf16[384,384]{1,0:T(8,128)(2,1)S(1)}, bf16[384,384]{1,0:T(8,128)(2,1)S(1)}, u32[]{:S(2)}, u32[]{:S(2)}) collective-permute-start(bf16[384,384]{1,0:T(8,128)(2,1)S(1)} %get-tuple-element.9.refs_0_), channel_id=1, source_target_pairs={{48,0},{0,16},{16,32},{32,48},{49,1},{1,17},{17,33},{33,49},{50,2}... | collective-permute-start | bytes 884744 | tf_op jit(solution)/shard_map/ppermute | solution.py:339
  31.4 1.9 %collective-permute-start.3 = (bf16[384,384]{1,0:T(8,128)(2,1)S(1)}, bf16[384,384]{1,0:T(8,128)(2,1)S(1)}, u32[]{:S(2)}, u32[]{:S(2)}) collective-permute-start(bf16[384,384]{1,0:T(8,128)(2,1)S(1)} %get-tuple-element.10.refs_1_), channel_id=1, source_target_pairs={{16,0},{32,16},{48,32},{0,48},{17,1},{33,17},{49,33},{1,49},{18,2}... | collective-permute-start | bytes 884744 | tf_op jit(solution)/shard_map/ppermute | solution.py:338
  33.3 0.0 collective-permute-done.2.refs_2_
  33.3 2.0 %collective-permute-start.4 = (bf16[384,384]{1,0:T(8,128)(2,1)S(1)}, bf16[384,384]{1,0:T(8,128)(2,1)S(1)}, u32[]{:S(2)}, u32[]{:S(2)}) collective-permute-start(bf16[384,384]{1,0:T(8,128)(2,1)S(1)} %collective-permute-done.2.refs_2_), channel_id=1, source_target_pairs={{16,0},{32,16},{48,32},{0,48},{17,1},{33,17},{49,33},{1,49},{18,2}... | collective-permute-start | bytes 884744 | tf_op jit(solution)/shard_map/ppermute | solution.py:344
  35.4 0.0 collective-permute-done.5.refs_7_
  35.4 3.8 %collective-permute-start.6 = (bf16[384,384]{1,0:T(8,128)(2,1)S(1)}, bf16[384,384]{1,0:T(8,128)(2,1)S(1)}, u32[]{:S(2)}, u32[]{:S(2)}) collective-permute-start(bf16[384,384]{1,0:T(8,128)(2,1)S(1)} %collective-permute-done.5.refs_7_), channel_id=1, source_target_pairs={{48,0},{0,16},{16,32},{32,48},{49,1},{1,17},{17,33},{33,49},{50,2}... | collective-permute-start | bytes 884744 | tf_op jit(solution)/shard_map/ppermute | solution.py:345
  39.3 6.3 %collective-permute-start.1 = (bf16[384,384]{1,0:T(8,128)(2,1)S(1)}, bf16[384,384]{1,0:T(8,128)(2,1)S(1)}, u32[]{:S(2)}, u32[]{:S(2)}) collective-permute-start(bf16[384,384]{1,0:T(8,128)(2,1)S(1)} %trim.1.slab), channel_id=1, source_target_pairs={{128,0},{898,2},{192,64},{962,66},{256,128},{2,130},{320,192},{66,... | collective-permute-start | bytes 884744 | tf_op jit(solution)/shard_map/ppermute | solution.py:342
  45.5 0.0 collective-permute-done.7.refs_6_
  45.6 2.2 %collective-permute-start.9 = (bf16[384,384]{1,0:T(8,128)(2,1)S(1)}, bf16[384,384]{1,0:T(8,128)(2,1)S(1)}, u32[]{:S(2)}, u32[]{:S(2)}) collective-permute-start(bf16[384,384]{1,0:T(8,128)(2,1)S(1)} %trim.1.slab), channel_id=1, source_target_pairs={{960,0},{0,64},{64,128},{128,192},{192,256},{256,320},{320,384},{3... | collective-permute-start | bytes 884744 | tf_op jit(solution)/shard_map/ppermute | solution.py:341
  47.8 4.8 %collective-permute-start.8 = (bf16[384,384]{1,0:T(8,128)(2,1)S(1)}, bf16[384,384]{1,0:T(8,128)(2,1)S(1)}, u32[]{:S(2)}, u32[]{:S(2)}) collective-permute-start(bf16[384,384]{1,0:T(8,128)(2,1)S(1)} %trim.1.slab), channel_id=1, source_target_pairs={{64,0},{128,64},{192,128},{256,192},{320,256},{384,320},{448,384},... | collective-permute-start | bytes 884744 | tf_op jit(solution)/shard_map/ppermute | solution.py:341
  52.6 0.0 collective-permute-done.4.refs_4_
  52.6 0.0 collective-permute-done.6.refs_5_
  52.7 6.4 %collective-permute-done.1.two_away = bf16[384,384]{1,0:T(8,128)(2,1)S(1)} collective-permute-done((bf16[384,384]{1,0:T(8,128)(2,1)S(1)}, bf16[384,384]{1,0:T(8,128)(2,1)S(1)}, u32[]{:S(2)}, u32[]{:S(2)}) %collective-permute-start.1) | collective-permute-done | bytes 294944 | tf_op jit(solution)/shard_map/ppermute | solution.py:342
  59.1 1.3 %early_terms.1.early = f32[384,768]{1,0:T(8,128)S(1)} custom-call(bf16[384,384]{1,0:T(8,128)(2,1)S(1)} %trim.1.slab, bf16[384,384]{1,0:T(8,128)(2,1)S(1)} %collective-permute-done.1.two_away, bf16[384,384]{1,0:T(8,128)(2,1)S(1)} %get-tuple-element.9.refs_0_, bf16[384,384]{1,0:T(8,128)(2,1)S(1)} %get-tuple-element.10.refs_1_, ...), custom_call_target="tpu_custom_call" | custom-call | tf_op jit(solution)/shard_map/early_terms/pallas_call | solution.py:148
  60.4 0.0 slice-start.1
  60.4 0.0 copy-start.1
  60.4 0.0 collective-permute-done.9.below
  60.4 0.9 collective-permute-done.8.above
  61.3 0.9 product_for_other.1
  62.2 1.9 %collective-permute-start.10 = (f32[4,48,768]{2,1,0:T(8,128)S(1)}, f32[4,48,768]{2,1,0:T(8,128)S(1)}, u32[]{:S(2)}, u32[]{:S(2)}) collective-permute-start(f32[4,48,768]{2,1,0:T(8,128)S(1)} %product_for_other.1), channel_id=1, source_target_pairs={{0,2},{2,0},{1,3},{3,1},{4,6},{6,4},{5,7},{7,5},{8,10},{10,8},{9,1... | collective-permute-start | bytes 1769480 | tf_op jit(solution)/shard_map/ppermute | solution.py:350
  64.1 0.9 product.1.mine
  65.1 1.0 collective-permute-done.10.theirs
  66.1 0.2 encode.1
  66.3 22.0 %all_to_all.10.parts = s16[4,296,128]{2,1,0:T(8,128)(2,1)S(1)} all-to-all(s16[4,296,128]{2,1,0:T(8,128)(2,1)S(1)} %encode.1), channel_id=1, replica_groups=mesh['zh'=4,'zl'=4,'x'=4,'yh'=4,'core'=2,'yl'=2] {'yh'}, dimensions={0} | all-to-all | bytes 606208 | tf_op jit(solution)/shard_map/all_to_all | solution.py:352
  88.3 1.8 %coarse_parts.1 = s16[16,80,128]{2,1,0:T(8,128)(2,1)S(1)} custom-call(s32[4,16]{1,0:T(4,128)S(1)} %copy-done.1, s16[4,296,128]{2,1,0:T(8,128)(2,1)S(1)} %all_to_all.10.parts, bf16[768,3072]{1,0:T(8,128)(2,1)S(1)} %bitcast.3), custom_call_target="tpu_custom_call" | custom-call | tf_op jit(solution)/shard_map/coarse_parts/pallas_call | solution.py:253
  90.1 23.7 %all_to_all.11.coded = s16[16,80,128]{2,1,0:T(8,128)(2,1)S(1)} all-to-all(s16[16,80,128]{2,1,0:T(8,128)(2,1)S(1)} %coarse_parts.1), channel_id=1, replica_groups=mesh['zh'=4,'zl'=4,'x'=4,'yh'=4,'core'=2,'yl'=2] {'zh','zl'}, dimensions={0} | all-to-all | bytes 655360 | tf_op jit(solution)/shard_map/all_to_all | solution.py:353
  113.9 0.7 summed.1
  (12 shorter events, 0.0 us)
Async XLA Ops:
  0.0 20.6 %copy-start = (bf16[768,384]{1,0:T(8,128)(2,1)S(1)}, bf16[768,384]{1,0:T(8,128)(2,1)}, u32[]{:S(2)}) copy-start(bf16[768,384]{1,0:T(8,128)(2,1)} %tiles.3) | copy-start | bytes 1769476
  0.0 20.6 %copy-start.2 = (s32[4,2]{0,1:T(2,128)S(1)}, s32[4,2]{0,1:T(2,128)}, u32[]{:S(2)}) copy-start(s32[4,2]{0,1:T(2,128)} %param.6) | copy-start | bytes 100
  2.4 36.9 %collective-permute-start = (bf16[400,384]{1,0:T(8,128)(2,1)}, bf16[400,384]{1,0:T(8,128)(2,1)S(1)}, u32[]{:S(2)}, u32[]{:S(2)}) collective-permute-start(bf16[400,384]{1,0:T(8,128)(2,1)} %stripes.1), channel_id=1, source_target_pairs={{0,768},{1,769},{2,258},{3,3},{4,513},{5,257},{6,259},{7,771},{8,1... | collective-permute-start | bytes 921608 | tf_op jit(solution)/shard_map/ppermute | solution.py:335
  21.2 12.1 %collective-permute-start.2 = (bf16[384,384]{1,0:T(8,128)(2,1)S(1)}, bf16[384,384]{1,0:T(8,128)(2,1)S(1)}, u32[]{:S(2)}, u32[]{:S(2)}) collective-permute-start(bf16[384,384]{1,0:T(8,128)(2,1)S(1)} %get-tuple-element.9.refs_0_), channel_id=1, source_target_pairs={{16,0},{32,16},{48,32},{0,48},{17,1},{33,17},{49,33},{1,49},{18,2}... | collective-permute-start | bytes 884744 | tf_op jit(solution)/shard_map/ppermute | solution.py:338
  23.7 11.7 %collective-permute-start.5 = (bf16[384,384]{1,0:T(8,128)(2,1)S(1)}, bf16[384,384]{1,0:T(8,128)(2,1)S(1)}, u32[]{:S(2)}, u32[]{:S(2)}) collective-permute-start(bf16[384,384]{1,0:T(8,128)(2,1)S(1)} %get-tuple-element.10.refs_1_), channel_id=1, source_target_pairs={{48,0},{0,16},{16,32},{32,48},{49,1},{1,17},{17,33},{33,49},{50,2}... | collective-permute-start | bytes 884744 | tf_op jit(solution)/shard_map/ppermute | solution.py:339
  27.1 18.5 %collective-permute-start.7 = (bf16[384,384]{1,0:T(8,128)(2,1)S(1)}, bf16[384,384]{1,0:T(8,128)(2,1)S(1)}, u32[]{:S(2)}, u32[]{:S(2)}) collective-permute-start(bf16[384,384]{1,0:T(8,128)(2,1)S(1)} %get-tuple-element.9.refs_0_), channel_id=1, source_target_pairs={{48,0},{0,16},{16,32},{32,48},{49,1},{1,17},{17,33},{33,49},{50,2}... | collective-permute-start | bytes 884744 | tf_op jit(solution)/shard_map/ppermute | solution.py:339
  31.4 16.4 %collective-permute-start.3 = (bf16[384,384]{1,0:T(8,128)(2,1)S(1)}, bf16[384,384]{1,0:T(8,128)(2,1)S(1)}, u32[]{:S(2)}, u32[]{:S(2)}) collective-permute-start(bf16[384,384]{1,0:T(8,128)(2,1)S(1)} %get-tuple-element.10.refs_1_), channel_id=1, source_target_pairs={{16,0},{32,16},{48,32},{0,48},{17,1},{33,17},{49,33},{1,49},{18,2}... | collective-permute-start | bytes 884744 | tf_op jit(solution)/shard_map/ppermute | solution.py:338
  33.3 19.3 %collective-permute-start.4 = (bf16[384,384]{1,0:T(8,128)(2,1)S(1)}, bf16[384,384]{1,0:T(8,128)(2,1)S(1)}, u32[]{:S(2)}, u32[]{:S(2)}) collective-permute-start(bf16[384,384]{1,0:T(8,128)(2,1)S(1)} %collective-permute-done.2.refs_2_), channel_id=1, source_target_pairs={{16,0},{32,16},{48,32},{0,48},{17,1},{33,17},{49,33},{1,49},{18,2}... | collective-permute-start | bytes 884744 | tf_op jit(solution)/shard_map/ppermute | solution.py:344
  35.4 17.3 %collective-permute-start.6 = (bf16[384,384]{1,0:T(8,128)(2,1)S(1)}, bf16[384,384]{1,0:T(8,128)(2,1)S(1)}, u32[]{:S(2)}, u32[]{:S(2)}) collective-permute-start(bf16[384,384]{1,0:T(8,128)(2,1)S(1)} %collective-permute-done.5.refs_7_), channel_id=1, source_target_pairs={{48,0},{0,16},{16,32},{32,48},{49,1},{1,17},{17,33},{33,49},{50,2}... | collective-permute-start | bytes 884744 | tf_op jit(solution)/shard_map/ppermute | solution.py:345
  39.3 19.8 %collective-permute-start.1 = (bf16[384,384]{1,0:T(8,128)(2,1)S(1)}, bf16[384,384]{1,0:T(8,128)(2,1)S(1)}, u32[]{:S(2)}, u32[]{:S(2)}) collective-permute-start(bf16[384,384]{1,0:T(8,128)(2,1)S(1)} %trim.1.slab), channel_id=1, source_target_pairs={{128,0},{898,2},{192,64},{962,66},{256,128},{2,130},{320,192},{66,... | collective-permute-start | bytes 884744 | tf_op jit(solution)/shard_map/ppermute | solution.py:342
  45.6 14.8 %collective-permute-start.9 = (bf16[384,384]{1,0:T(8,128)(2,1)S(1)}, bf16[384,384]{1,0:T(8,128)(2,1)S(1)}, u32[]{:S(2)}, u32[]{:S(2)}) collective-permute-start(bf16[384,384]{1,0:T(8,128)(2,1)S(1)} %trim.1.slab), channel_id=1, source_target_pairs={{960,0},{0,64},{64,128},{128,192},{192,256},{256,320},{320,384},{3... | collective-permute-start | bytes 884744 | tf_op jit(solution)/shard_map/ppermute | solution.py:341
  47.8 13.5 %collective-permute-start.8 = (bf16[384,384]{1,0:T(8,128)(2,1)S(1)}, bf16[384,384]{1,0:T(8,128)(2,1)S(1)}, u32[]{:S(2)}, u32[]{:S(2)}) collective-permute-start(bf16[384,384]{1,0:T(8,128)(2,1)S(1)} %trim.1.slab), channel_id=1, source_target_pairs={{64,0},{128,64},{192,128},{256,192},{320,256},{384,320},{448,384},... | collective-permute-start | bytes 884744 | tf_op jit(solution)/shard_map/ppermute | solution.py:341
  59.1 29.2 %slice-start = ((s8[4718592]{0:T(1024)(128)(4,1)}), s8[4194304]{0:T(1024)(128)(4,1)S(1)}, s32[]{:S(2)}) async-start(s8[4718592]{0:T(1024)(128)(4,1)} %bitcast.2), calls=%async_computation.2 | async-start | bytes 8388608
  60.4 28.0 %slice-start.1 = ((s8[4718592]{0:T(1024)(128)(4,1)}), s8[524288]{0:T(1024)(128)(4,1)S(1)}, s32[]{:S(2)}) async-start(s8[4718592]{0:T(1024)(128)(4,1)} %bitcast.2), calls=%async_computation.3 | async-start | bytes 1048576
  60.4 27.9 %copy-start.1 = (s32[4,16]{1,0:T(4,128)S(1)}, s32[4,16]{1,0:T(4,128)}, u32[]{:S(2)}) copy-start(s32[4,16]{1,0:T(4,128)} %mask.1) | copy-start | bytes 772
  62.2 3.9 %collective-permute-start.10 = (f32[4,48,768]{2,1,0:T(8,128)S(1)}, f32[4,48,768]{2,1,0:T(8,128)S(1)}, u32[]{:S(2)}, u32[]{:S(2)}) collective-permute-start(f32[4,48,768]{2,1,0:T(8,128)S(1)} %product_for_other.1), channel_id=1, source_target_pairs={{0,2},{2,0},{1,3},{3,1},{4,6},{6,4},{5,7},{7,5},{8,10},{10,8},{9,1... | collective-permute-start | bytes 1769480 | tf_op jit(solution)/shard_map/ppermute | solution.py:350

commit v17 on v12

--- a/solution.py
+++ b/solution.py
@@ -199,16 +199,35 @@
     )
 
 
-def coarse_kernel(mask, parts, tiles, out, present):
+def prolongator_kernel(mask, tiles, out):
+    width = COARSE // 4
+    for n in range(4):
+        columns = slice(n * width, (n + 1) * width)
+        first = n * (width // TILE)
+        mask_rows(lambda i, k: mask[i, k], tiles.at[:, columns], out.at[:, columns], first)
+
+
+def masked_prolongator(p_tiles, p_mask):
+    vmem = pl.BlockSpec(memory_space=pltpu.VMEM)
+    return pl.pallas_call(
+        prolongator_kernel,
+        out_shape=jax.ShapeDtypeStruct(p_tiles.shape, BF16),
+        in_specs=[pl.BlockSpec(memory_space=pltpu.SMEM), vmem],
+        out_specs=vmem,
+        compiler_params=params(),
+        name="masked_prolongator",
+    )(p_mask, p_tiles)
+
+
+def coarse_kernel(parts, tiles, out):
     whole = decoded_sum(parts)
     high = whole.astype(BF16)
     terms = jnp.concatenate([high, (whole - high.astype(F32)).astype(BF16)], axis=0)
-    width = present.shape[1]
-    for n in range(COARSE // width):
+    width = COARSE // 4
+    for n in range(4):
         first = n * (width // TILE)
-        block = tiles.at[:, n * width : (n + 1) * width]
-        mask_rows(lambda i, k: mask[i, k], block, present, first)
-        full = jnp.dot(terms, present[...], preferred_element_type=F32)
+        block = tiles[:, n * width : (n + 1) * width]
+        full = jnp.dot(terms, block, preferred_element_type=F32)
         full = full[:WIDE] + full[WIDE:]
         for k in range(width // TILE):
             chunk = full[:, k * TILE : (k + 1) * TILE]
@@ -221,17 +240,15 @@
             out[first + k] = coded.astype(jnp.int32).astype(jnp.int16)
 
 
-def coarse_parts(parts, p_tiles, p_mask):
-    vmem = pl.BlockSpec(memory_space=pltpu.VMEM)
+def coarse_parts(parts, p_masked):
     return pl.pallas_call(
         coarse_kernel,
         out_shape=jax.ShapeDtypeStruct((PLANES, CODED, 128), jnp.int16),
-        in_specs=[pl.BlockSpec(memory_space=pltpu.SMEM), vmem, vmem],
-        out_specs=vmem,
-        scratch_shapes=[pltpu.VMEM((ROWS, COARSE // 4), BF16)],
+        in_specs=[pl.BlockSpec(memory_space=pltpu.VMEM)] * 2,
+        out_specs=pl.BlockSpec(memory_space=pltpu.VMEM),
         compiler_params=params(),
         name="coarse_parts",
-    )(p_mask, parts, p_tiles)
+    )(parts, p_masked)
 
 
 def sum_kernel(coded, out):
@@ -321,8 +338,10 @@
 
     theirs = lax.ppermute(product(slabs, blocks, 1), "core", [(0, 1), (1, 0)])
     coded = encode(product(slabs, blocks, 0), theirs)
+    p_tiles, theirs = lax.optimization_barrier((p_tiles, theirs))
+    p_masked = masked_prolongator(p_tiles, p_mask)
     coded = lax.all_to_all(coded, "yh", 0, 0, tiled=True)
-    coded = lax.all_to_all(coarse_parts(coded, p_tiles, p_mask), z, 0, 0, tiled=True)
+    coded = lax.all_to_all(coarse_parts(coded, p_masked), z, 0, 0, tiled=True)
     return summed(coded).T
 
 

time: 115 us -> 118 us (1.026)
  the two profiles are of different devices: /device:TPU:6 before, /device:TPU:4 now
where the time goes in v17:
time: 118 us; the launch traced here: 117 us
  starting transfers between devices  62.2 us (53%)
  blocking collectives  24.1 us (20%)
  waiting for transfers between devices  14.8 us (13%)
  Pallas kernels  8.88 us (8%)
  local copies, waits for them, and re-layouts  6.8 us (6%)
    all_to_all x1, blocking collectives, local(): coded = lax.all_to_all(coarse_parts(coded, p_masked), z, 0, 0, tiled=True)  24.1 us
    ppermute x1, starting transfers between devices, local(): slab = trim(lax.ppermute(mine, z + ('yh', 'core', 'yl'), spread()))  18.2 us
    all_to_all x1, starting transfers between devices, local(): coded = lax.all_to_all(coded, 'yh', 0, 0, tiled=True)  10.8 us
    ppermute x2, starting transfers between devices, local(): before = [lax.ppermute(half, 'x', around(4, -1)) for half in own]  7.72 us
    ppermute x2, starting transfers between devices, local(): lax.ppermute(slab, z, around(PLANES, turn))  7.05 us
    unnamed x12, local copies, waits for them, and re-layouts  6.8 us
    ppermute x1, waiting for transfers between devices, local(): slabs = [slab, above, below, lax.ppermute(slab, z + ('core',), two_away())]  6.44 us
    ppermute x1, starting transfers between devices, local(): slabs = [slab, above, below, lax.ppermute(slab, z + ('core',), two_away())]  6.25 us
  transfers between devices with their start and end apart: 12, of which 4 were waited for; matrix products, arithmetic and copies ran while one was open for 0% of the time, Pallas kernels for 2%

profile of v17, /device:TPU:4, one launch (start us, length us, event | category | flops | bytes accessed | tf_op | source)
XLA Modules:
  0.0 117.0 jit_solution(10249576630998910424)
XLA Ops:
  0.0 2.4 %stripes.1 = bf16[400,384]{1,0:T(8,128)(2,1)} custom-call(s32[4,16]{1,0:T(4,128)} %mask.1, bf16[768,3072]{1,0:T(8,128)(2,1)} %tiles.3), custom_call_target="tpu_custom_call" | custom-call | tf_op jit(solution)/shard_map/stripes/pallas_call | solution.py:68
  2.4 18.2 %collective-permute-start = (bf16[400,384]{1,0:T(8,128)(2,1)}, bf16[400,384]{1,0:T(8,128)(2,1)S(1)}, u32[]{:S(2)}, u32[]{:S(2)}) collective-permute-start(bf16[400,384]{1,0:T(8,128)(2,1)} %stripes.1), channel_id=1, source_target_pairs={{0,768},{1,769},{2,258},{3,3},{4,513},{5,257},{6,259},{7,771},{8,1... | collective-permute-start | bytes 921608 | tf_op jit(solution)/shard_map/ppermute | solution.py:325
  20.6 0.6 masked_operator.1
  21.2 2.4 %collective-permute-start.4 = (bf16[384,384]{1,0:T(8,128)(2,1)S(1)}, bf16[384,384]{1,0:T(8,128)(2,1)S(1)}, u32[]{:S(2)}, u32[]{:S(2)}) collective-permute-start(bf16[384,384]{1,0:T(8,128)(2,1)S(1)} %get-tuple-element.10.refs_4_), channel_id=1, source_target_pairs={{16,0},{32,16},{48,32},{0,48},{17,1},{33,17},{49,33},{1,49},{18,2}... | collective-permute-start | bytes 884744 | tf_op jit(solution)/shard_map/ppermute | solution.py:328
  23.7 3.4 %collective-permute-start.7 = (bf16[384,384]{1,0:T(8,128)(2,1)S(1)}, bf16[384,384]{1,0:T(8,128)(2,1)S(1)}, u32[]{:S(2)}, u32[]{:S(2)}) collective-permute-start(bf16[384,384]{1,0:T(8,128)(2,1)S(1)} %get-tuple-element.11.refs_5_), channel_id=1, source_target_pairs={{48,0},{0,16},{16,32},{32,48},{49,1},{1,17},{17,33},{33,49},{50,2}... | collective-permute-start | bytes 884744 | tf_op jit(solution)/shard_map/ppermute | solution.py:329
  27.1 4.3 %collective-permute-start.9 = (bf16[384,384]{1,0:T(8,128)(2,1)S(1)}, bf16[384,384]{1,0:T(8,128)(2,1)S(1)}, u32[]{:S(2)}, u32[]{:S(2)}) collective-permute-start(bf16[384,384]{1,0:T(8,128)(2,1)S(1)} %get-tuple-element.10.refs_4_), channel_id=1, source_target_pairs={{48,0},{0,16},{16,32},{32,48},{49,1},{1,17},{17,33},{33,49},{50,2}... | collective-permute-start | bytes 884744 | tf_op jit(solution)/shard_map/ppermute | solution.py:329
  31.4 1.9 %collective-permute-start.5 = (bf16[384,384]{1,0:T(8,128)(2,1)S(1)}, bf16[384,384]{1,0:T(8,128)(2,1)S(1)}, u32[]{:S(2)}, u32[]{:S(2)}) collective-permute-start(bf16[384,384]{1,0:T(8,128)(2,1)S(1)} %get-tuple-element.11.refs_5_), channel_id=1, source_target_pairs={{16,0},{32,16},{48,32},{0,48},{17,1},{33,17},{49,33},{1,49},{18,2}... | collective-permute-start | bytes 884744 | tf_op jit(solution)/shard_map/ppermute | solution.py:328
  33.3 0.0 collective-permute-done.4.refs_6_
  33.3 2.0 %collective-permute-start.6 = (bf16[384,384]{1,0:T(8,128)(2,1)S(1)}, bf16[384,384]{1,0:T(8,128)(2,1)S(1)}, u32[]{:S(2)}, u32[]{:S(2)}) collective-permute-start(bf16[384,384]{1,0:T(8,128)(2,1)S(1)} %collective-permute-done.4.refs_6_), channel_id=1, source_target_pairs={{16,0},{32,16},{48,32},{0,48},{17,1},{33,17},{49,33},{1,49},{18,2}... | collective-permute-start | bytes 884744 | tf_op jit(solution)/shard_map/ppermute | solution.py:334
  35.4 0.0 collective-permute-done.7.refs_11_
  35.4 3.8 %collective-permute-start.8 = (bf16[384,384]{1,0:T(8,128)(2,1)S(1)}, bf16[384,384]{1,0:T(8,128)(2,1)S(1)}, u32[]{:S(2)}, u32[]{:S(2)}) collective-permute-start(bf16[384,384]{1,0:T(8,128)(2,1)S(1)} %collective-permute-done.7.refs_11_), channel_id=1, source_target_pairs={{48,0},{0,16},{16,32},{32,48},{49,1},{1,17},{17,33},{33,49},{50,2}... | collective-permute-start | bytes 884744 | tf_op jit(solution)/shard_map/ppermute | solution.py:335
  39.2 0.0 collective-permute-done.padded
  39.3 0.0 copy-start.4
  39.3 6.3 %collective-permute-start.3 = (bf16[384,384]{1,0:T(8,128)(2,1)S(1)}, bf16[384,384]{1,0:T(8,128)(2,1)S(1)}, u32[]{:S(2)}, u32[]{:S(2)}) collective-permute-start(bf16[384,384]{1,0:T(8,128)(2,1)S(1)} %trim.1.refs_0_), channel_id=1, source_target_pairs={{128,0},{898,2},{192,64},{962,66},{256,128},{2,130},{320,192},{66,... | collective-permute-start | bytes 884744 | tf_op jit(solution)/shard_map/ppermute | solution.py:332
  45.6 2.2 %collective-permute-start.2 = (bf16[384,384]{1,0:T(8,128)(2,1)S(1)}, bf16[384,384]{1,0:T(8,128)(2,1)S(1)}, u32[]{:S(2)}, u32[]{:S(2)}) collective-permute-start(bf16[384,384]{1,0:T(8,128)(2,1)S(1)} %trim.1.refs_0_), channel_id=1, source_target_pairs={{960,0},{0,64},{64,128},{128,192},{192,256},{256,320},{320,384},{3... | collective-permute-start | bytes 884744 | tf_op jit(solution)/shard_map/ppermute | solution.py:331
  47.8 4.8 %collective-permute-start.1 = (bf16[384,384]{1,0:T(8,128)(2,1)S(1)}, bf16[384,384]{1,0:T(8,128)(2,1)S(1)}, u32[]{:S(2)}, u32[]{:S(2)}) collective-permute-start(bf16[384,384]{1,0:T(8,128)(2,1)S(1)} %trim.1.refs_0_), channel_id=1, source_target_pairs={{64,0},{128,64},{192,128},{256,192},{320,256},{384,320},{448,384},... | collective-permute-start | bytes 884744 | tf_op jit(solution)/shard_map/ppermute | solution.py:331
  52.7 6.4 %collective-permute-done.3.refs_3_ = bf16[384,384]{1,0:T(8,128)(2,1)S(1)} collective-permute-done((bf16[384,384]{1,0:T(8,128)(2,1)S(1)}, bf16[384,384]{1,0:T(8,128)(2,1)S(1)}, u32[]{:S(2)}, u32[]{:S(2)}) %collective-permute-start.3) | collective-permute-done | bytes 294944 | tf_op jit(solution)/shard_map/ppermute | solution.py:332
  59.1 2.2 %collective-permute-done.1.refs_1_ = bf16[384,384]{1,0:T(8,128)(2,1)S(1)} collective-permute-done((bf16[384,384]{1,0:T(8,128)(2,1)S(1)}, bf16[384,384]{1,0:T(8,128)(2,1)S(1)}, u32[]{:S(2)}, u32[]{:S(2)}) %collective-permute-start.1) | collective-permute-done | bytes 294944 | tf_op jit(solution)/shard_map/ppermute | solution.py:331
  61.3 1.1 product_for_other.1
  62.4 1.9 %collective-permute-start.10 = (f32[4,48,768]{2,1,0:T(8,128)S(1)}, f32[4,48,768]{2,1,0:T(8,128)S(1)}, u32[]{:S(2)}, u32[]{:S(2)}) collective-permute-start(f32[4,48,768]{2,1,0:T(8,128)S(1)} %product_for_other.1), channel_id=1, source_target_pairs={{0,2},{2,0},{1,3},{3,1},{4,6},{6,4},{5,7},{7,5},{8,10},{10,8},{9,1... | collective-permute-start | bytes 1769480 | tf_op jit(solution)/shard_map/ppermute | solution.py:339
  64.3 1.1 product.1.mine
  65.4 0.9 collective-permute-done.10.theirs
  66.3 0.9 encode.1
  67.2 10.8 %all-to-all-start = ((s16[4,296,128]{2,1,0:T(8,128)(2,1)}), s16[4,296,128]{2,1,0:T(8,128)(2,1)S(1)}, u32[]{:S(2)}, u32[]{:S(2)}) async-start(s16[4,296,128]{2,1,0:T(8,128)(2,1)} %encode.1), calls=%async_computation | async-start | bytes 606208 | tf_op jit(solution)/shard_map/all_to_all | solution.py:343
  78.0 2.3 %copy-done = bf16[768,3072]{1,0:T(8,128)(2,1)S(1)} copy-done((bf16[768,3072]{1,0:T(8,128)(2,1)S(1)}, bf16[768,3072]{1,0:T(8,128)(2,1)}, u32[]{:S(2)}) %copy-start) | copy-done | bytes 4718616
  80.3 0.9 masked_prolongator.1.tiles
  81.2 2.1 %copy-done.1 = bf16[768,3072]{1,0:T(8,128)(2,1)} copy-done((bf16[768,3072]{1,0:T(8,128)(2,1)}, bf16[768,3072]{1,0:T(8,128)(2,1)S(1)}, u32[]{:S(2)}) %copy-start.1) | copy-done | bytes 4718616
  83.3 5.3 %all-to-all-done.parts = s16[4,296,128]{2,1,0:T(8,128)(2,1)S(1)} async-done(((s16[4,296,128]{2,1,0:T(8,128)(2,1)}), s16[4,296,128]{2,1,0:T(8,128)(2,1)S(1)}, u32[]{:S(2)}, u32[]{:S(2)}) %all-to-all-start) | async-done | bytes 303136 | tf_op jit(solution)/shard_map/all_to_all | solution.py:343
  88.6 2.3 %copy-done.2 = bf16[768,3072]{1,0:T(8,128)(2,1)S(1)} copy-done((bf16[768,3072]{1,0:T(8,128)(2,1)S(1)}, bf16[768,3072]{1,0:T(8,128)(2,1)}, u32[]{:S(2)}) %copy-start.2) | copy-done | bytes 4718616
  90.9 1.2 %coarse_parts.1 = s16[16,80,128]{2,1,0:T(8,128)(2,1)S(1)} custom-call(s16[4,296,128]{2,1,0:T(8,128)(2,1)S(1)} %all-to-all-done.parts, bf16[768,3072]{1,0:T(8,128)(2,1)S(1)} %copy-done.2), custom_call_target="tpu_custom_call" | custom-call | tf_op jit(solution)/shard_map/coarse_parts/pallas_call | solution.py:244
  92.1 24.1 %all_to_all.10.coded = s16[16,80,128]{2,1,0:T(8,128)(2,1)S(1)} all-to-all(s16[16,80,128]{2,1,0:T(8,128)(2,1)S(1)} %coarse_parts.1), channel_id=1, replica_groups=mesh['zh'=4,'zl'=4,'x'=4,'yh'=4,'core'=2,'yl'=2] {'zh','zl'}, dimensions={0} | all-to-all | bytes 655360 | tf_op jit(solution)/shard_map/all_to_all | solution.py:344
  116.3 0.7 summed.1
  (14 shorter events, 0.1 us)
Async XLA Ops:
  0.0 20.6 %copy-start.3 = (bf16[768,384]{1,0:T(8,128)(2,1)S(1)}, bf16[768,384]{1,0:T(8,128)(2,1)}, u32[]{:S(2)}) copy-start(bf16[768,384]{1,0:T(8,128)(2,1)} %tiles.2) | copy-start | bytes 1769476
  0.0 20.6 %copy-start.5 = (s32[4,2]{0,1:T(2,128)S(1)}, s32[4,2]{0,1:T(2,128)}, u32[]{:S(2)}) copy-start(s32[4,2]{0,1:T(2,128)} %param.6) | copy-start | bytes 100
  2.4 36.9 %collective-permute-start = (bf16[400,384]{1,0:T(8,128)(2,1)}, bf16[400,384]{1,0:T(8,128)(2,1)S(1)}, u32[]{:S(2)}, u32[]{:S(2)}) collective-permute-start(bf16[400,384]{1,0:T(8,128)(2,1)} %stripes.1), channel_id=1, source_target_pairs={{0,768},{1,769},{2,258},{3,3},{4,513},{5,257},{6,259},{7,771},{8,1... | collective-permute-start | bytes 921608 | tf_op jit(solution)/shard_map/ppermute | solution.py:325
  21.2 12.1 %collective-permute-start.4 = (bf16[384,384]{1,0:T(8,128)(2,1)S(1)}, bf16[384,384]{1,0:T(8,128)(2,1)S(1)}, u32[]{:S(2)}, u32[]{:S(2)}) collective-permute-start(bf16[384,384]{1,0:T(8,128)(2,1)S(1)} %get-tuple-element.10.refs_4_), channel_id=1, source_target_pairs={{16,0},{32,16},{48,32},{0,48},{17,1},{33,17},{49,33},{1,49},{18,2}... | collective-permute-start | bytes 884744 | tf_op jit(solution)/shard_map/ppermute | solution.py:328
  23.7 11.7 %collective-permute-start.7 = (bf16[384,384]{1,0:T(8,128)(2,1)S(1)}, bf16[384,384]{1,0:T(8,128)(2,1)S(1)}, u32[]{:S(2)}, u32[]{:S(2)}) collective-permute-start(bf16[384,384]{1,0:T(8,128)(2,1)S(1)} %get-tuple-element.11.refs_5_), channel_id=1, source_target_pairs={{48,0},{0,16},{16,32},{32,48},{49,1},{1,17},{17,33},{33,49},{50,2}... | collective-permute-start | bytes 884744 | tf_op jit(solution)/shard_map/ppermute | solution.py:329
  27.1 18.5 %collective-permute-start.9 = (bf16[384,384]{1,0:T(8,128)(2,1)S(1)}, bf16[384,384]{1,0:T(8,128)(2,1)S(1)}, u32[]{:S(2)}, u32[]{:S(2)}) collective-permute-start(bf16[384,384]{1,0:T(8,128)(2,1)S(1)} %get-tuple-element.10.refs_4_), channel_id=1, source_target_pairs={{48,0},{0,16},{16,32},{32,48},{49,1},{1,17},{17,33},{33,49},{50,2}... | collective-permute-start | bytes 884744 | tf_op jit(solution)/shard_map/ppermute | solution.py:329
  31.4 16.4 %collective-permute-start.5 = (bf16[384,384]{1,0:T(8,128)(2,1)S(1)}, bf16[384,384]{1,0:T(8,128)(2,1)S(1)}, u32[]{:S(2)}, u32[]{:S(2)}) collective-permute-start(bf16[384,384]{1,0:T(8,128)(2,1)S(1)} %get-tuple-element.11.refs_5_), channel_id=1, source_target_pairs={{16,0},{32,16},{48,32},{0,48},{17,1},{33,17},{49,33},{1,49},{18,2}... | collective-permute-start | bytes 884744 | tf_op jit(solution)/shard_map/ppermute | solution.py:328
  33.3 19.3 %collective-permute-start.6 = (bf16[384,384]{1,0:T(8,128)(2,1)S(1)}, bf16[384,384]{1,0:T(8,128)(2,1)S(1)}, u32[]{:S(2)}, u32[]{:S(2)}) collective-permute-start(bf16[384,384]{1,0:T(8,128)(2,1)S(1)} %collective-permute-done.4.refs_6_), channel_id=1, source_target_pairs={{16,0},{32,16},{48,32},{0,48},{17,1},{33,17},{49,33},{1,49},{18,2}... | collective-permute-start | bytes 884744 | tf_op jit(solution)/shard_map/ppermute | solution.py:334
  35.4 17.3 %collective-permute-start.8 = (bf16[384,384]{1,0:T(8,128)(2,1)S(1)}, bf16[384,384]{1,0:T(8,128)(2,1)S(1)}, u32[]{:S(2)}, u32[]{:S(2)}) collective-permute-start(bf16[384,384]{1,0:T(8,128)(2,1)S(1)} %collective-permute-done.7.refs_11_), channel_id=1, source_target_pairs={{48,0},{0,16},{16,32},{32,48},{49,1},{1,17},{17,33},{33,49},{50,2}... | collective-permute-start | bytes 884744 | tf_op jit(solution)/shard_map/ppermute | solution.py:335
  39.3 38.7 %copy-start.4 = (s32[4,16]{1,0:T(4,128)S(1)}, s32[4,16]{1,0:T(4,128)}, u32[]{:S(2)}) copy-start(s32[4,16]{1,0:T(4,128)} %mask.1) | copy-start | bytes 772
  39.3 19.8 %collective-permute-start.3 = (bf16[384,384]{1,0:T(8,128)(2,1)S(1)}, bf16[384,384]{1,0:T(8,128)(2,1)S(1)}, u32[]{:S(2)}, u32[]{:S(2)}) collective-permute-start(bf16[384,384]{1,0:T(8,128)(2,1)S(1)} %trim.1.refs_0_), channel_id=1, source_target_pairs={{128,0},{898,2},{192,64},{962,66},{256,128},{2,130},{320,192},{66,... | collective-permute-start | bytes 884744 | tf_op jit(solution)/shard_map/ppermute | solution.py:332
  45.6 13.5 %collective-permute-start.2 = (bf16[384,384]{1,0:T(8,128)(2,1)S(1)}, bf16[384,384]{1,0:T(8,128)(2,1)S(1)}, u32[]{:S(2)}, u32[]{:S(2)}) collective-permute-start(bf16[384,384]{1,0:T(8,128)(2,1)S(1)} %trim.1.refs_0_), channel_id=1, source_target_pairs={{960,0},{0,64},{64,128},{128,192},{192,256},{256,320},{320,384},{3... | collective-permute-start | bytes 884744 | tf_op jit(solution)/shard_map/ppermute | solution.py:331
  47.8 13.5 %collective-permute-start.1 = (bf16[384,384]{1,0:T(8,128)(2,1)S(1)}, bf16[384,384]{1,0:T(8,128)(2,1)S(1)}, u32[]{:S(2)}, u32[]{:S(2)}) collective-permute-start(bf16[384,384]{1,0:T(8,128)(2,1)S(1)} %trim.1.refs_0_), channel_id=1, source_target_pairs={{64,0},{128,64},{192,128},{256,192},{320,256},{384,320},{448,384},... | collective-permute-start | bytes 884744 | tf_op jit(solution)/shard_map/ppermute | solution.py:331
  62.4 3.9 %collective-permute-start.10 = (f32[4,48,768]{2,1,0:T(8,128)S(1)}, f32[4,48,768]{2,1,0:T(8,128)S(1)}, u32[]{:S(2)}, u32[]{:S(2)}) collective-permute-start(f32[4,48,768]{2,1,0:T(8,128)S(1)} %product_for_other.1), channel_id=1, source_target_pairs={{0,2},{2,0},{1,3},{3,1},{4,6},{6,4},{5,7},{7,5},{8,10},{10,8},{9,1... | collective-permute-start | bytes 1769480 | tf_op jit(solution)/shard_map/ppermute | solution.py:339
  67.2 21.4 %all-to-all-start = ((s16[4,296,128]{2,1,0:T(8,128)(2,1)}), s16[4,296,128]{2,1,0:T(8,128)(2,1)S(1)}, u32[]{:S(2)}, u32[]{:S(2)}) async-start(s16[4,296,128]{2,1,0:T(8,128)(2,1)} %encode.1), calls=%async_computation | async-start | bytes 606208 | tf_op jit(solution)/shard_map/all_to_all | solution.py:343
  78.0 2.3 %copy-start = (bf16[768,3072]{1,0:T(8,128)(2,1)S(1)}, bf16[768,3072]{1,0:T(8,128)(2,1)}, u32[]{:S(2)}) copy-start(bf16[768,3072]{1,0:T(8,128)(2,1)} %tiles.3) | copy-start | bytes 14155780
  81.2 2.1 %copy-start.1 = (bf16[768,3072]{1,0:T(8,128)(2,1)}, bf16[768,3072]{1,0:T(8,128)(2,1)S(1)}, u32[]{:S(2)}) copy-start(bf16[768,3072]{1,0:T(8,128)(2,1)S(1)} %masked_prolongator.1.tiles) | copy-start | bytes 14155780
  88.6 2.3 %copy-start.2 = (bf16[768,3072]{1,0:T(8,128)(2,1)S(1)}, bf16[768,3072]{1,0:T(8,128)(2,1)}, u32[]{:S(2)}) copy-start(bf16[768,3072]{1,0:T(8,128)(2,1)} %copy-done.1) | copy-start | bytes 14155780
